TPU v7x, 128 devices: a whole 4x4x4 slice. The times are simulated.
128 devices in a mesh: comp: 2 (over x_hi), gx: 8 (over z, core), gy: 8 (over x_lo, y).
Axes of the slice: x: 4 (x_hi: 2, x_lo: 2; x = x_hi * 2 + x_lo), y: 4, z: 4, core: 2. Of those that a mesh axis runs over, the one named last changes fastest.
Arguments:
- state: float32 [2, 4, 16, 1024, 1024], P('comp', None, None, 'gx', 'gy'), may hold values from -6 to 6
- horiz_coef: float32 [2, 4], P('comp'), may hold values from 0.03 to 0.12
- vert_coef: float32 [2, 1024, 1024], P('comp', 'gx', 'gy'), may hold values from 0.02 to 0.3
- couple_rate: float32 [2, 4], P('comp'), may hold values from 0.2 to 0.8
- sea_mask: int32 [2, 1024, 1024], P('comp', 'gx', 'gy'), may hold values 0 or 1
- dest_block: int32 [2, 1024, 8, 4], P('comp', 'gx', 'gy'), may hold values from 0 to 8191, as said below
- entry_count: int32 [2, 1024, 8], P('comp', 'gx', 'gy'), may hold values from 1 to 4
- remap_weight: bfloat16 [2, 1024, 8, 4, 128, 128], P('comp', 'gx', 'gy'), may hold values from -0.375 to 0.375
Outputs:
- advanced: float32 [2, 4, 16, 1024, 1024], P('comp', None, None, 'gx', 'gy')
Inputs may be any that keep to these rules, and one draw needn't show every extreme that they name: `dest_block`: each list entry names a block of the other component: id // 128 is a device of that component's 8 x 8 tiles in row-major order and id % 128 a tile row on it. Over the live entries of one device, at most 8 name blocks of any one device of the other component, and in every draw some pair of devices has exactly 8. Padded entries hold arbitrary ids.
All inputs are finite; a program needn't handle non-finite values. No bound on the sum of `sea_mask` on one device may be relied on, other than what follows from the above.
Results may differ from a plain program's by a relative error of at most 0.0011.
Values sent between devices are 32-bit elements; how exact they have to be, the bound alone decides.
No kernel may reach another device: no remote copies, remote signals or barrier semaphores. Data moves between devices by JAX's collectives and lax.ppermute only.
A program may use at most 128 MiB of HBM per device.

v0:
```python
import jax
import jax.numpy as jnp
from jax import lax
from jax.sharding import PartitionSpec as P

STEPS = 2


def from_partner(block, axis, apart):
    count = lax.axis_size(axis)
    route = []
    for low in range(count):
        high = low | 1 << apart
        if high != low and high < count:
            route += [(low, high), (high, low)]
    return lax.ppermute(block, axis, route)


def extended(cells, sides, width):
    for axis, dim in sides:
        count = lax.axis_size(axis)
        ends = count - 1
        head = lax.slice_in_dim(cells, 0, width, axis=dim)
        tail = lax.slice_in_dim(cells, cells.shape[dim] - width, cells.shape[dim], axis=dim)
        cells = jnp.concatenate(
            [
                lax.ppermute(tail, axis, [(i, (i + 1) % count) for i in range(ends)]),
                cells,
                lax.ppermute(head, axis, [((i + 1) % count, i) for i in range(ends)]),
            ],
            axis=dim,
        )
    return cells


def mix_levels(values, coef, axis):
    count = values.shape[axis]
    upper = lax.slice_in_dim(values, 1, count, axis=axis)
    lower = lax.slice_in_dim(values, 0, count - 1, axis=axis)
    zero_plane = jnp.zeros_like(lax.slice_in_dim(values, 0, 1, axis=axis))
    from_above = jnp.concatenate([upper - lower, zero_plane], axis=axis)
    from_below = jnp.concatenate([zero_plane, lower - upper], axis=axis)
    return values + coef * (from_above + from_below)


def local(
    state, horiz_coef, vert_coef, couple_rate, sea_mask, dest_block, entry_count, remap_weight
):
    values = state[0]
    var_count, level_count, tile_rows, block_width = values.shape
    fan_width = dest_block.shape[-1]
    peer_count = lax.axis_size("gx") * lax.axis_size("gy")
    slot_count = (tile_rows * fan_width + peer_count - 1) // peer_count
    entries_all = tile_rows * fan_width
    field_width = var_count * block_width
    surface = values[:, 0].astype(jnp.bfloat16)
    partial_value = jnp.einsum(
        "vrk,rfkj->rfvj", surface, remap_weight[0, :, 0], preferred_element_type=jnp.float32
    )
    payload = partial_value.reshape(entries_all, field_width)
    targets = dest_block[0, :, 0].reshape(entries_all)
    usable = (jnp.arange(fan_width)[None, :] < entry_count[0, :, 0][:, None]).reshape(entries_all)
    target_dev = targets // tile_rows
    target_row = targets % tile_rows
    matches_peer = jnp.logical_and(
        target_dev[:, None] == jnp.arange(peer_count)[None, :], usable[:, None]
    ).astype(jnp.int32)
    before = jnp.cumsum(matches_peer, axis=0) - matches_peer
    position = jnp.sum(before * matches_peer, axis=1)
    placement = target_dev * slot_count + position
    total_slots = peer_count * slot_count
    placement = jnp.where(usable, placement, total_slots)
    packed = (
        jnp.zeros((total_slots, field_width), jnp.float32).at[placement].set(payload, mode="drop")
    )
    labels = jnp.full((total_slots,), -1, jnp.int32).at[placement].set(target_row, mode="drop")
    packed = packed.reshape(peer_count, slot_count, field_width)
    labels = labels.reshape(peer_count, slot_count)
    packed, labels = (
        lax.all_to_all(packed, ("gx", "gy"), split_axis=0, concat_axis=0, tiled=True),
        lax.all_to_all(labels, ("gx", "gy"), split_axis=0, concat_axis=0, tiled=True),
    )
    packed, labels = from_partner((packed, labels), "comp", 0)
    packed = packed.reshape(total_slots, field_width)
    labels = labels.reshape(total_slots)
    selector = (labels[None, :] == jnp.arange(tile_rows)[:, None]).astype(jnp.float32)
    gathered = jnp.dot(
        selector, packed, precision=lax.Precision.HIGHEST, preferred_element_type=jnp.float32
    )
    imported = gathered.reshape(tile_rows, var_count, block_width).transpose(1, 0, 2)
    horiz_rate = horiz_coef[0][:, None, None, None]
    vert_rate = vert_coef[0][None, None, :, :]
    relax_rate = couple_rate[0][:, None, None] * sea_mask[0].astype(jnp.float32)[None, :, :]
    for substep in range(STEPS):
        padded = extended(values, (("gx", 2), ("gy", 3)), 1)
        laplace = padded[:, :, 2:, 1:-1] + padded[:, :, :-2, 1:-1]
        laplace = laplace + padded[:, :, 1:-1, 2:] + padded[:, :, 1:-1, :-2] - 4.0 * values
        values = values + horiz_rate * laplace
        values = mix_levels(values, vert_rate, 1)
        bottom = values[:, 0]
        bottom = bottom + relax_rate * (imported - bottom)
        values = jnp.concatenate([bottom[:, None], values[:, 1:]], axis=1)
    return values[None]


def solution(mesh):
    in_specs = (
        P("comp", None, None, "gx", "gy"),
        P("comp", None),
        P("comp", "gx", "gy"),
        P("comp", None),
        P("comp", "gx", "gy"),
        P("comp", "gx", "gy", None),
        P("comp", "gx", "gy"),
        P("comp", "gx", "gy", None, None, None),
    )
    out_specs = P("comp", None, None, "gx", "gy")
    return jax.shard_map(local, mesh=mesh, in_specs=in_specs, out_specs=out_specs, check_vma=False)
```

profile of v0, /device:TPU:1, one launch (start us, length us, event | category | flops | bytes accessed | tf_op | source)
XLA Modules:
  0.0 214.9 jit_solution(1913131404523635879)
XLA Ops:
  9.2 10.9 %all-to-all-start = ((s32[64,1,8]{2,1,0:T(1,128)}), s32[64,1,8]{2,1,0:T(1,128)S(1)}, u32[]{:S(2)}, u32[]{:S(2)}) async-start(s32[64,1,8]{2,1,0:T(1,128)} %bitcast.10), calls=%async_computation | async-start | bytes 65536 | tf_op jit(solution)/shard_map/all_to_all | solution.py:81
  20.1 5.0 %copy.48 = f32[1,4,16,128,128]{4,1,3,2,0:T(4,128)S(1)} copy(f32[1,4,16,128,128]{4,3,2,1,0:T(8,128)} %param.8) | data formatting | bytes 8388608 | tf_op args[0]
  25.1 3.5 %collective-permute-start.1 = (f32[4,16,1,128]{3,0,2,1:T(4,128)S(1)}, f32[4,16,1,128]{3,0,2,1:T(4,128)S(1)}, u32[]{:S(2)}, u32[]{:S(2)}) collective-permute-start(f32[4,16,1,128]{3,0,2,1:T(4,128)S(1)} %get-tuple-element.15), channel_id=1, source_target_pairs={{0,8},{8,16},{16,24},{24,32},{32,40},{40,48},{48,56},{1,9},{9,17},... | collective-permute-start | bytes 98312 | tf_op jit(solution)/shard_map/ppermute | solution.py:27
  30.6 7.0 %fusion = f32[128,4,128,4]{2,3,1,0:T(4,128)S(1)} fusion(bf16[1,128,1,4,128,128]{5,4,3,2,1,0:T(8,128)(2,1)} %param.15, f32[4,16,128,128]{3,0,2,1:T(4,128)S(1)} %bitcast.93), kind=kOutput, calls=%fused_computation.2 | convolution fusion | flops 67108864 | bytes 17956864 | tf_op jit(solution)/shard_map/vrk,rfkj->rfvj/dot_general | solution.py:57
  37.6 3.3 %scatter_custom_fusion.1 = f32[512,512]{1,0:T(8,128)} fusion(s32[512]{0:T(512)S(1)} %bitcast.113, f32[64,8,4,128]{3,2,1,0:T(4,128)S(1)} %bitcast.99, f32[]{:T(128)} %constant.36.clone.1), kind=kCustom, calls=%fused_computation.51 | custom fusion | bytes 2097156 | tf_op jit(solution)/shard_map/scatter | solution.py:74
  40.9 8.9 %all-to-all-start.1 = ((f32[64,8,512]{2,1,0:T(8,128)}), f32[64,8,512]{2,1,0:T(8,128)S(1)}, u32[]{:S(2)}, u32[]{:S(2)}) async-start(f32[64,8,512]{2,1,0:T(8,128)} %bitcast.18), calls=%async_computation.1 | async-start | bytes 2097152 | tf_op jit(solution)/shard_map/all_to_all | solution.py:80
  55.2 5.7 %fusion.42 = (f32[4,16,130,1]{3,0,2,1:T(4,128)}, f32[4,16,130,1]{3,0,2,1:T(4,128)}) fusion(f32[4,16,130,128]{3,0,2,1:T(4,128)S(1)} %pad_maximum_fusion.1), kind=kLoop, calls=%fused_computation.109 | loop fusion | bytes 133120 | tf_op jit(solution)/shard_map/slice | solution.py:23
  61.0 5.1 %copy.21 = f32[4,16,130,1]{2,1,3,0:T(8,128)S(1)} copy(f32[4,16,130,1]{3,0,2,1:T(4,128)} %get-tuple-element.7) | data formatting | bytes 66560 | tf_op jit(solution)/shard_map/slice | solution.py:23
  66.0 5.1 %copy.23 = f32[4,16,130,1]{2,1,3,0:T(8,128)S(1)} copy(f32[4,16,130,1]{3,0,2,1:T(4,128)} %get-tuple-element.8) | data formatting | bytes 66560 | tf_op jit(solution)/shard_map/slice | solution.py:24
  75.8 3.6 %collective-permute-done.2 = f32[4,16,130,1]{2,1,3,0:T(8,128)S(1)} collective-permute-done((f32[4,16,130,1]{2,1,3,0:T(8,128)S(1)}, f32[4,16,130,1]{2,1,3,0:T(8,128)S(1)}, u32[]{:S(2)}, u32[]{:S(2)}) %collective-permute-start.2) | collective-permute-done | bytes 33312 | tf_op jit(solution)/shard_map/ppermute | solution.py:29
  79.4 4.0 %copy.22 = f32[4,16,130,1]{3,0,2,1:T(4,128)} copy(f32[4,16,130,1]{2,1,3,0:T(8,128)S(1)} %collective-permute-done.2) | data formatting | bytes 66560 | tf_op jit(solution)/shard_map/ppermute | solution.py:29
  83.4 4.0 %copy.24 = f32[4,16,130,1]{3,0,2,1:T(4,128)} copy(f32[4,16,130,1]{2,1,3,0:T(8,128)S(1)} %collective-permute-done.3) | data formatting | bytes 66560 | tf_op jit(solution)/shard_map/ppermute | solution.py:27
  87.4 17.7 %fusion.11 = f32[4,16,128,128]{3,0,2,1:T(4,128)S(1)} fusion(f32[4,16,128,128]{3,0,2,1:T(4,128)} %bitcast.95, f32[4,16,130,1]{3,0,2,1:T(4,128)} %copy.24, f32[4,16,1,128]{3,0,2,1:T(4,128)S(1)} %collective-permute-done, f32[4,16,1,128]{3,0,2,1:T(4,128)S(1)} %collective-permute-done.1, f32[4,16,130,1]{3,0,2,1:T(4,128)} %copy.22, f32[4]{0:T(128)S(1)} %bitcast.105), kind=kLoop, calls=%fused_computation.31 | loop fusion | flops 15728640 | bytes 8520720 | tf_op jit(solution)/shard_map/add | solution.py:98
  105.1 3.8 %slice_subtract_fusion.3 = (f32[4,15,128,128]{3,0,2,1:T(4,128)}, f32[4,15,128,128]{3,0,2,1:T(4,128)}) fusion(f32[4,16,128,128]{3,0,2,1:T(4,128)S(1)} %fusion.11), kind=kLoop, calls=%fused_computation.48 | loop fusion | flops 1966080 | bytes 15728640 | tf_op jit(solution)/shard_map/sub | solution.py:41
  109.4 17.2 %multiply_add_fusion.1 = f32[4,16,128,128]{3,0,2,1:T(4,128)S(1)} fusion(f32[4,15,128,128]{3,0,2,1:T(4,128)} %get-tuple-element.14, f32[4,15,128,128]{3,0,2,1:T(4,128)} %get-tuple-element.13, f32[128,128]{1,0:T(8,128)S(1)} %bitcast.102, f32[4,16,128,128]{3,0,2,1:T(4,128)} %bitcast.96, f32[4,16,1,128]{3,0,2,1:T(4,128)S(1)} %collective-permute-done, ...), kind=kLoop, calls=%fused_computation.44 | loop fusion | flops 18874368 | bytes 16450576 | tf_op jit(solution)/shard_map/add | solution.py:43
  136.4 6.0 %collective-permute-start.7 = (f32[4,16,1,128]{3,0,2,1:T(4,128)S(1)}, f32[4,16,1,128]{3,0,2,1:T(4,128)S(1)}, u32[]{:S(2)}, u32[]{:S(2)}) collective-permute-start(f32[4,16,1,128]{3,0,2,1:T(4,128)S(1)} %get-tuple-element.11), channel_id=1, source_target_pairs={{0,8},{8,16},{16,24},{24,32},{32,40},{40,48},{48,56},{1,9},{9,17},... | collective-permute-start | bytes 98312 | tf_op jit(solution)/shard_map/ppermute | solution.py:27
  149.1 5.7 %fusion.41 = (f32[4,16,130,1]{3,0,2,1:T(4,128)}, f32[4,16,130,1]{3,0,2,1:T(4,128)}) fusion(f32[4,16,130,128]{3,0,2,1:T(4,128)S(1)} %pad_maximum_fusion.2), kind=kLoop, calls=%fused_computation.108 | loop fusion | bytes 133120 | tf_op jit(solution)/shard_map/slice | solution.py:23
  154.8 5.0 %copy.32 = f32[4,16,130,1]{2,1,3,0:T(8,128)S(1)} copy(f32[4,16,130,1]{3,0,2,1:T(4,128)} %get-tuple-element.5) | data formatting | bytes 66560 | tf_op jit(solution)/shard_map/slice | solution.py:23
  161.2 5.1 %copy.34 = f32[4,16,130,1]{2,1,3,0:T(8,128)S(1)} copy(f32[4,16,130,1]{3,0,2,1:T(4,128)} %get-tuple-element.6) | data formatting | bytes 66560 | tf_op jit(solution)/shard_map/slice | solution.py:24
  166.2 4.3 %collective-permute-start.9 = (f32[4,16,130,1]{2,1,3,0:T(8,128)S(1)}, f32[4,16,130,1]{2,1,3,0:T(8,128)S(1)}, u32[]{:S(2)}, u32[]{:S(2)}) collective-permute-start(f32[4,16,130,1]{2,1,3,0:T(8,128)S(1)} %copy.34), channel_id=1, source_target_pairs={{0,1},{1,2},{2,3},{3,4},{4,5},{5,6},{6,7},{8,9},{9,10},{10,11},{11... | collective-permute-start | bytes 99848 | tf_op jit(solution)/shard_map/ppermute | solution.py:27
  170.5 4.0 %copy.33 = f32[4,16,130,1]{3,0,2,1:T(4,128)} copy(f32[4,16,130,1]{2,1,3,0:T(8,128)S(1)} %collective-permute-done.8) | data formatting | bytes 66560 | tf_op jit(solution)/shard_map/ppermute | solution.py:29
  174.5 4.0 %copy.35 = f32[4,16,130,1]{3,0,2,1:T(4,128)} copy(f32[4,16,130,1]{2,1,3,0:T(8,128)S(1)} %collective-permute-done.9) | data formatting | bytes 66560 | tf_op jit(solution)/shard_map/ppermute | solution.py:27
  178.5 16.6 %fusion.5 = f32[4,16,128,128]{3,0,2,1:T(4,128)S(1)} fusion(f32[4,16,130,1]{3,0,2,1:T(4,128)} %copy.35, f32[4,16,1,128]{3,0,2,1:T(4,128)S(1)} %collective-permute-done.6, f32[4,16,1,128]{3,0,2,1:T(4,128)S(1)} %collective-permute-done.7, f32[4,15,128,128]{3,0,2,1:T(4,128)} %slice.126, f32[4,1,128,128]{3,0,2,1:T(4,128)S(1)} %fusion.19, ...), kind=kLoop, calls=%fused_computation.13 | loop fusion | flops 20971520 | bytes 8520720 | tf_op jit(solution)/shard_map/add | solution.py:98
  198.5 12.1 %multiply_add_fusion = f32[4,16,128,128]{3,0,2,1:T(4,128)S(1)} fusion(f32[4,15,128,128]{3,0,2,1:T(4,128)S(1)} %get-tuple-element.10, f32[4,15,128,128]{3,0,2,1:T(4,128)S(1)} %get-tuple-element.9, f32[128,128]{1,0:T(8,128)S(1)} %bitcast.103, f32[4,16,1,128]{3,0,2,1:T(4,128)S(1)} %collective-permute-done.6, f32[4,15,128,128]{3,0,2,1:T(4,128)S(1)} %copy-done.1, ...), kind=kLoop, calls=%fused_computation.43 | loop fusion | flops 24117248 | bytes 16450576 | tf_op jit(solution)/shard_map/add | solution.py:43
  (82 shorter events, 47.0 us)
Async XLA Ops:
  9.2 31.7 %all-to-all-start = ((s32[64,1,8]{2,1,0:T(1,128)}), s32[64,1,8]{2,1,0:T(1,128)S(1)}, u32[]{:S(2)}, u32[]{:S(2)}) async-start(s32[64,1,8]{2,1,0:T(1,128)} %bitcast.10), calls=%async_computation | async-start | bytes 65536 | tf_op jit(solution)/shard_map/all_to_all | solution.py:81
  25.1 12.5 %copy-start.2 = (f32[1,4,16,128,128]{4,1,3,2,0:T(4,128)}, f32[1,4,16,128,128]{4,1,3,2,0:T(4,128)S(1)}, u32[]{:S(2)}) copy-start(f32[1,4,16,128,128]{4,1,3,2,0:T(4,128)S(1)} %copy.48) | copy-start | bytes 12582916
  25.1 27.4 %collective-permute-start.1 = (f32[4,16,1,128]{3,0,2,1:T(4,128)S(1)}, f32[4,16,1,128]{3,0,2,1:T(4,128)S(1)}, u32[]{:S(2)}, u32[]{:S(2)}) collective-permute-start(f32[4,16,1,128]{3,0,2,1:T(4,128)S(1)} %get-tuple-element.15), channel_id=1, source_target_pairs={{0,8},{8,16},{16,24},{24,32},{32,40},{40,48},{48,56},{1,9},{9,17},... | collective-permute-start | bytes 98312 | tf_op jit(solution)/shard_map/ppermute | solution.py:27
  28.7 23.9 %collective-permute-start = (f32[4,16,1,128]{3,0,2,1:T(4,128)S(1)}, f32[4,16,1,128]{3,0,2,1:T(4,128)S(1)}, u32[]{:S(2)}, u32[]{:S(2)}) collective-permute-start(f32[4,16,1,128]{3,0,2,1:T(4,128)S(1)} %get-tuple-element.16), channel_id=1, source_target_pairs={{8,0},{16,8},{24,16},{32,24},{40,32},{48,40},{56,48},{9,1},{17,9},... | collective-permute-start | bytes 98312 | tf_op jit(solution)/shard_map/ppermute | solution.py:29
  40.9 68.0 %all-to-all-start.1 = ((f32[64,8,512]{2,1,0:T(8,128)}), f32[64,8,512]{2,1,0:T(8,128)S(1)}, u32[]{:S(2)}, u32[]{:S(2)}) async-start(f32[64,8,512]{2,1,0:T(8,128)} %bitcast.18), calls=%async_computation.1 | async-start | bytes 2097152 | tf_op jit(solution)/shard_map/all_to_all | solution.py:80
  49.8 25.9 %collective-permute-start.4 = (s32[64,8]{1,0:T(8,128)S(1)}, s32[64,8]{1,0:T(8,128)S(1)}, u32[]{:S(2)}, u32[]{:S(2)}) collective-permute-start(s32[64,8]{1,0:T(8,128)S(1)} %bitcast.104), channel_id=1, source_target_pairs={{0,64},{64,0},{1,65},{65,1},{2,66},{66,2},{3,67},{67,3},{4,68},{68... | collective-permute-start | bytes 6152 | tf_op jit(solution)/shard_map/ppermute | solution.py:16
  61.0 14.7 %copy-start.6 = (s32[1,128,128]{2,1,0:T(8,128)S(1)}, s32[1,128,128]{2,1,0:T(8,128)}, u32[]{:S(2)}) copy-start(s32[1,128,128]{2,1,0:T(8,128)} %param.12) | copy-start | bytes 196612
  71.1 12.3 %collective-permute-start.3 = (f32[4,16,130,1]{2,1,3,0:T(8,128)S(1)}, f32[4,16,130,1]{2,1,3,0:T(8,128)S(1)}, u32[]{:S(2)}, u32[]{:S(2)}) collective-permute-start(f32[4,16,130,1]{2,1,3,0:T(8,128)S(1)} %copy.23), channel_id=1, source_target_pairs={{0,1},{1,2},{2,3},{3,4},{4,5},{5,6},{6,7},{8,9},{9,10},{10,11},{11... | collective-permute-start | bytes 99848 | tf_op jit(solution)/shard_map/ppermute | solution.py:27
  74.4 5.0 %collective-permute-start.2 = (f32[4,16,130,1]{2,1,3,0:T(8,128)S(1)}, f32[4,16,130,1]{2,1,3,0:T(8,128)S(1)}, u32[]{:S(2)}, u32[]{:S(2)}) collective-permute-start(f32[4,16,130,1]{2,1,3,0:T(8,128)S(1)} %copy.21), channel_id=1, source_target_pairs={{1,0},{2,1},{3,2},{4,3},{5,4},{6,5},{7,6},{9,8},{10,9},{11,10},{12... | collective-permute-start | bytes 99848 | tf_op jit(solution)/shard_map/ppermute | solution.py:29
  75.8 11.6 %copy-start.7 = (f32[1,4]{1,0:T(1,128)S(1)}, f32[1,4]{1,0:T(1,128)}, u32[]{:S(2)}) copy-start(f32[1,4]{1,0:T(1,128)} %param.9) | copy-start | bytes 52
  105.1 4.3 %copy-start.5 = (f32[1,128,128]{2,1,0:T(8,128)S(1)}, f32[1,128,128]{2,1,0:T(8,128)}, u32[]{:S(2)}) copy-start(f32[1,128,128]{2,1,0:T(8,128)} %param.10) | copy-start | bytes 196612
  108.9 24.1 %collective-permute-start.5 = (f32[64,8,512]{2,1,0:T(8,128)S(1)}, f32[64,8,512]{2,1,0:T(8,128)S(1)}, u32[]{:S(2)}, u32[]{:S(2)}) collective-permute-start(f32[64,8,512]{2,1,0:T(8,128)S(1)} %all-to-all-done.1), channel_id=1, source_target_pairs={{0,64},{64,0},{1,65},{65,1},{2,66},{66,2},{3,67},{67,3},{4,68},{68... | collective-permute-start | bytes 3145736 | tf_op jit(solution)/shard_map/ppermute | solution.py:16
  126.6 2.0 copy-start.4
  128.6 5.4 %copy-start.8 = (f32[1,4]{1,0:T(1,128)S(1)}, f32[1,4]{1,0:T(1,128)}, u32[]{:S(2)}) copy-start(f32[1,4]{1,0:T(1,128)} %param.11) | copy-start | bytes 52
  133.3 14.3 %copy-start = (f32[4,15,128,128]{3,0,2,1:T(4,128)S(1)}, f32[4,15,128,128]{3,0,2,1:T(4,128)}, u32[]{:S(2)}) copy-start(f32[4,15,128,128]{3,0,2,1:T(4,128)} %slice.126) | copy-start | bytes 11796484
  136.4 7.9 %collective-permute-start.7 = (f32[4,16,1,128]{3,0,2,1:T(4,128)S(1)}, f32[4,16,1,128]{3,0,2,1:T(4,128)S(1)}, u32[]{:S(2)}, u32[]{:S(2)}) collective-permute-start(f32[4,16,1,128]{3,0,2,1:T(4,128)S(1)} %get-tuple-element.11), channel_id=1, source_target_pairs={{0,8},{8,16},{16,24},{24,32},{32,40},{40,48},{48,56},{1,9},{9,17},... | collective-permute-start | bytes 98312 | tf_op jit(solution)/shard_map/ppermute | solution.py:27
  142.4 5.2 %collective-permute-start.6 = (f32[4,16,1,128]{3,0,2,1:T(4,128)S(1)}, f32[4,16,1,128]{3,0,2,1:T(4,128)S(1)}, u32[]{:S(2)}, u32[]{:S(2)}) collective-permute-start(f32[4,16,1,128]{3,0,2,1:T(4,128)S(1)} %get-tuple-element.12), channel_id=1, source_target_pairs={{8,0},{16,8},{24,16},{32,24},{40,32},{48,40},{56,48},{9,1},{17,9},... | collective-permute-start | bytes 98312 | tf_op jit(solution)/shard_map/ppermute | solution.py:29
  159.9 10.6 %collective-permute-start.8 = (f32[4,16,130,1]{2,1,3,0:T(8,128)S(1)}, f32[4,16,130,1]{2,1,3,0:T(8,128)S(1)}, u32[]{:S(2)}, u32[]{:S(2)}) collective-permute-start(f32[4,16,130,1]{2,1,3,0:T(8,128)S(1)} %copy.32), channel_id=1, source_target_pairs={{1,0},{2,1},{3,2},{4,3},{5,4},{6,5},{7,6},{9,8},{10,9},{11,10},{12... | collective-permute-start | bytes 99848 | tf_op jit(solution)/shard_map/ppermute | solution.py:29
  166.2 8.3 %collective-permute-start.9 = (f32[4,16,130,1]{2,1,3,0:T(8,128)S(1)}, f32[4,16,130,1]{2,1,3,0:T(8,128)S(1)}, u32[]{:S(2)}, u32[]{:S(2)}) collective-permute-start(f32[4,16,130,1]{2,1,3,0:T(8,128)S(1)} %copy.34), channel_id=1, source_target_pairs={{0,1},{1,2},{2,3},{3,4},{4,5},{5,6},{6,7},{8,9},{9,10},{10,11},{11... | collective-permute-start | bytes 99848 | tf_op jit(solution)/shard_map/ppermute | solution.py:27
  174.5 22.9 %slice-start = ((s8[4259840]{0:T(1024)(128)(4,1)}), s8[65536]{0:T(1024)(128)(4,1)S(1)}, s32[]{:S(2)}) async-start(s8[4259840]{0:T(1024)(128)(4,1)} %bitcast.97), calls=%async_computation.2 | async-start | bytes 131072
  178.5 18.9 %slice-start.1 = ((s8[4259840]{0:T(1024)(128)(4,1)}), s8[4194304]{0:T(1024)(128)(4,1)S(1)}, s32[]{:S(2)}) async-start(s8[4259840]{0:T(1024)(128)(4,1)} %bitcast.97), calls=%async_computation.3 | async-start | bytes 8388608
  195.1 2.3 %copy-start.1 = (f32[4,15,128,128]{3,0,2,1:T(4,128)S(1)}, f32[4,15,128,128]{3,0,2,1:T(4,128)}, u32[]{:S(2)}) copy-start(f32[4,15,128,128]{3,0,2,1:T(4,128)} %slice.126) | copy-start | bytes 11796484
  195.1 3.4 %copy-start.3 = (f32[4,16,130,1]{3,0,2,1:T(4,128)S(1)}, f32[4,16,130,1]{3,0,2,1:T(4,128)}, u32[]{:S(2)}) copy-start(f32[4,16,130,1]{3,0,2,1:T(4,128)} %copy.35) | copy-start | bytes 99844
where the time goes:
time: 218 us; the launch traced here: 215 us
  other arithmetic  80.9 us (37%)
  local copies, waits for them, and re-layouts  70.3 us (32%)
  starting transfers between devices  46.6 us (21%)
  waiting for transfers between devices  9.09 us (4%)
  matrix products  7.68 us (4%)
    add x2, other arithmetic, local(): values = values + horiz_rate * laplace  34.3 us
    add x2, other arithmetic, mix_levels(): return values + coef * (from_above + from_below)  29.3 us
    slice x4, local copies, waits for them, and re-layouts, extended(): head = lax.slice_in_dim(cells, 0, width, axis=dim)  21.6 us
    ppermute x4, starting transfers between devices, extended(): lax.ppermute(tail, axis, [(i, (i + 1) % count) for i in range(ends)])  17.1 us
    all_to_all x1, starting transfers between devices, local(): lax.all_to_all(labels, ('gx', 'gy'), split_axis=0, concat_axis=0, tiled=T...  10.9 us
    slice x3, local copies, waits for them, and re-layouts, extended(): lax.slice_in_dim(cells, cells.shape[dim] - width, cells.shape[dim], axis=...  10.1 us
    unnamed x25, local copies, waits for them, and re-layouts  9.42 us
    all_to_all x1, starting transfers between devices, local(): lax.all_to_all(packed, ('gx', 'gy'), split_axis=0, concat_axis=0, tiled=T...  8.9 us
  transfers between devices with their start and end apart: 12, of which 3 were waited for; matrix products, arithmetic and copies ran while one was open for 43% of the time, Pallas kernels for 0%

commit v1 on v0

v1 whole, which is shorter than its diff:
```python
import jax
import jax.numpy as jnp
from jax import lax
from jax.experimental import pallas as pl
from jax.experimental.pallas import tpu as pltpu
from jax.sharding import PartitionSpec as P

NV = 4
LEV = 16
T = 128
FAN = 4
CAP = 8
PEERS = 64
SLOTS = CAP + 1
HALF = 64
VMEM = 40 * 1024 * 1024
WIDE = 58 * 1024 * 1024

f32 = jnp.float32
i32 = jnp.int32


def params(limit=VMEM):
    return pltpu.CompilerParams(vmem_limit_bytes=limit)


def lanes(rows):
    return lax.broadcasted_iota(i32, (rows, T), 1)


def subl(rows):
    return lax.broadcasted_iota(i32, (rows, T), 0)


def unshift(v):
    return lax.rem((NV - v) * 32, T)


def cut(flags, column=None):
    if column is None:
        return flags[0], flags[1]
    return jnp.where((column & 1) == 0, flags[2], flags[3])


def edge_kernel(flags, mask, state, first, last, cols, surf, tile, sea_int, sems):
    loads = [pltpu.make_async_copy(state.at[0, v], tile.at[v], sems.at[v]) for v in range(NV)]
    loads.append(pltpu.make_async_copy(mask.at[0], sea_int, sems.at[NV]))
    for load in loads:
        load.start()
    up, down = cut(flags)
    lane = lanes(HALF)
    keep = cut(flags, lane)
    for v in range(NV):
        loads[v].wait()
        surf[pl.ds(v, T, stride=NV), :] = tile[v, 0]
        for l in range(LEV):
            first[v, l : l + 1, :] = tile[v, l, 0:1, :] * up
            last[v, l : l + 1, :] = tile[v, l, T - 1 : T, :] * down
        for lo in range(0, T, HALF):
            acc = jnp.zeros((HALF, T), f32) if v == 0 else cols[0, lo : lo + HALF, :]
            for l in range(LEV):
                p = v * LEV + l
                turned = pltpu.roll(tile[v, l, lo : lo + HALF, :], (2 * p + 1) % T, 1)
                acc = jnp.where((lane >> 1) == p, turned, acc)
            cols[0, lo : lo + HALF, :] = acc * keep if v == NV - 1 else acc
    loads[NV].wait()
    sea = sea_int[...].astype(f32)
    first[NV] = jnp.broadcast_to(sea[0:1, :] * up, (LEV, T))
    last[NV] = jnp.broadcast_to(sea[T - 1 : T, :] * down, (LEV, T))
    cols[1] = pltpu.roll(sea, 1, 1) * cut(flags, lanes(T))


def edges(flags, mask, state):
    vmem = pl.BlockSpec(memory_space=pltpu.VMEM)
    hbm = pl.BlockSpec(memory_space=pltpu.HBM)
    return pl.pallas_call(
        edge_kernel,
        in_specs=[pl.BlockSpec(memory_space=pltpu.SMEM), hbm, hbm],
        out_specs=[vmem] * 4,
        out_shape=[
            jax.ShapeDtypeStruct((NV + 1, LEV, T), f32),
            jax.ShapeDtypeStruct((NV + 1, LEV, T), f32),
            jax.ShapeDtypeStruct((2, T, T), f32),
            jax.ShapeDtypeStruct((T * NV, T), f32),
        ],
        scratch_shapes=[
            pltpu.VMEM((NV, LEV, T, T), f32),
            pltpu.VMEM((T, T), i32),
            pltpu.SemaphoreType.DMA((NV + 1,)),
        ],
        compiler_params=params(WIDE),
        cost_estimate=pl.CostEstimate(flops=4 << 20, bytes_accessed=5 << 20, transcendentals=0),
        name="edges",
    )(flags, mask, state)


CHUNKS = 16


def remap_kernel(dest, count, me, surf, weight, out, blocks, used, label, sems):
    rows = T // CHUNKS

    def fetch(c):
        piece = pl.ds(c * rows, rows)
        return pltpu.make_async_copy(weight.at[0, piece, 0], blocks.at[piece], sems.at[c])

    for c in range(CHUNKS):
        fetch(c).start()
    out[...] = jnp.zeros_like(out)

    def clear(i, _):
        used[i] = 0
        for k in range(CAP):
            label[i * CAP + k] = 0
        return 0

    lax.fori_loop(0, PEERS, clear, 0)

    def chunk(c, _):
        fetch(c).wait()
        for r in range(rows):
            row = c * rows + r
            at_pair = pl.multiple_of(c * rows * NV + (r // 2) * 8, 8)
            pair = surf[pl.ds(at_pair, 8), :].astype(jnp.bfloat16)
            live_count = count[row]
            for f in range(FAN):
                target = dest[row * FAN + f]
                peer = lax.shift_right_logical(target, 7) & (PEERS - 1)
                live = f < live_count
                at = used[peer]
                used[peer] = at + jnp.where(live, 1, 0)
                label[jnp.where(live, peer * CAP + at, PEERS * CAP)] = (target & (T - 1)) + 1
                slot = jnp.where(live, peer * SLOTS + at, CAP)
                product = jnp.dot(pair, blocks[row, f], preferred_element_type=f32)
                half = (r % 2) * NV
                out[slot] = product[half : half + NV, :]
        return 0

    lax.fori_loop(0, CHUNKS, chunk, 0)
    place = lax.broadcasted_iota(i32, (NV, T), 0) * T + lax.broadcasted_iota(i32, (NV, T), 1)
    place = place - me[0] * CAP

    def write(i, _):
        block = jnp.zeros((NV, T), i32)
        for k in range(CAP):
            block = jnp.where(place == k, label[i * CAP + k], block)
        out[i * SLOTS + CAP] = block.astype(f32)
        return 0

    lax.fori_loop(0, PEERS, write, 0)


def remap(dest, count, me, surf, weight):
    smem = pl.BlockSpec(memory_space=pltpu.SMEM)
    vmem = pl.BlockSpec(memory_space=pltpu.VMEM)
    hbm = pl.BlockSpec(memory_space=pltpu.HBM)
    return pl.pallas_call(
        remap_kernel,
        in_specs=[smem, smem, smem, vmem, hbm],
        out_specs=vmem,
        out_shape=jax.ShapeDtypeStruct((PEERS * SLOTS, NV, T), f32),
        scratch_shapes=[
            pltpu.VMEM((T, FAN, T, T), jnp.bfloat16),
            pltpu.SMEM((PEERS,), i32),
            pltpu.SMEM((PEERS * CAP + 8,), i32),
            pltpu.SemaphoreType.DMA((CHUNKS,)),
        ],
        compiler_params=params(),
        cost_estimate=pl.CostEstimate(flops=67 << 20, bytes_accessed=22 << 20, transcendentals=0),
        name="remap",
    )(dest, count, me, surf, weight)


def sealed(block, *after):
    anywhere = pl.BlockSpec(memory_space=pl.ANY)

    def kernel(*refs):
        del refs

    return pl.pallas_call(
        kernel,
        in_specs=[anywhere] * (1 + len(after)),
        out_specs=anywhere,
        out_shape=jax.ShapeDtypeStruct(block.shape, block.dtype),
        input_output_aliases={0: 0},
        name="sealed",
    )(block, *after)


def merged(left, right):
    return jnp.where((lanes(T) & 1) == 0, left, pltpu.roll(right, T - 2, 1))


def diffuse(u, up, down, side, rate):
    rows = u.shape[0]
    lane, sub = lanes(rows), subl(rows)
    north = jnp.where(sub == 0, up, pltpu.roll(u, 1, 0))
    south = jnp.where(sub == rows - 1, down, pltpu.roll(u, rows - 1, 0))
    west = jnp.where(lane == 0, side, pltpu.roll(u, 1, 1))
    east = jnp.where(lane == T - 1, side, pltpu.roll(u, T - 1, 1))
    return u + rate * ((north + south) + (west + east) - 4.0 * u)


def level_diffuse(u, top, bottom, side, rate, l, part):
    lo = part * HALF
    up = top[0, l : l + 1, :] if part == 0 else u[0, 0, l, lo - 1 : lo, :]
    down = bottom[0, l : l + 1, :] if lo + HALF == T else u[0, 0, l, lo + HALF : lo + HALF + 1, :]
    spin = side[lo : lo + HALF, :]
    if l:
        spin = pltpu.roll(spin, T - 2 * l, 1)
    return diffuse(u[0, 0, l, lo : lo + HALF, :], up, down, spin, rate)


def first_kernel(rate_ref, flags, u, vert, top, bottom, left, right, out, first, last, cols, side):
    v = pl.program_id(0)
    rate = rate_ref[v]
    side[...] = pltpu.roll(merged(left[0], right[0]), unshift(v), 1)
    for part in range(T // HALF):
        lo = part * HALF
        coef = vert[0, lo : lo + HALF, :]
        before = None
        here = level_diffuse(u, top, bottom, side, rate, 0, part)
        for l in range(LEV):
            after = level_diffuse(u, top, bottom, side, rate, l + 1, part) if l + 1 < LEV else None
            if before is None:
                term = after - here
            elif after is None:
                term = before - here
            else:
                term = (after - here) + (before - here)
            out[0, 0, l, lo : lo + HALF, :] = here + coef * term
            before, here = here, after
    lane = lanes(HALF)
    for lo in range(0, T, HALF):
        acc = jnp.zeros((HALF, T), f32)
        for l in range(LEV):
            turned = pltpu.roll(out[0, 0, l, lo : lo + HALF, :], 2 * l + 1, 1)
            acc = jnp.where((lane >> 1) == l, turned, acc)
        spot = pltpu.roll(acc, v * 32, 1)
        spot = spot * cut(flags, lane)
        cols[lo : lo + HALF, :] = jnp.where((lane >> 5) == v, spot, cols[lo : lo + HALF, :])
    up, down = cut(flags)
    for l in range(LEV):
        first[0, l : l + 1, :] = out[0, 0, l, 0:1, :] * up
        last[0, l : l + 1, :] = out[0, 0, l, T - 1 : T, :] * down


def second_kernel(rate_ref, flags, u, vert, top, bottom, left, right, out, side):
    v = pl.program_id(0)
    rate = rate_ref[v]
    side[...] = pltpu.roll(merged(left[...], right[...]), unshift(v), 1)
    for part in range(T // HALF):
        lo = part * HALF
        coef = vert[0, lo : lo + HALF, :]
        before = level_diffuse(u, top, bottom, side, rate, 1, part)
        here = level_diffuse(u, top, bottom, side, rate, 2, part)
        out[0, 0, 0, lo : lo + HALF, :] = before
        out[0, 0, 1, lo : lo + HALF, :] = before + coef * ((here - before) - before)
        for l in range(2, LEV):
            after = level_diffuse(u, top, bottom, side, rate, l + 1, part) if l + 1 < LEV else None
            term = before - here
            if after is not None:
                term = (after - here) + term
            out[0, 0, l, lo : lo + HALF, :] = here + coef * term
            before, here = here, after


def step_call(kernel, rate, flags, u, vert, top, bottom, left, right, emit, name):
    whole = lambda *n: pl.BlockSpec(n, lambda v: (0,) * len(n))
    rows = pl.BlockSpec((1, LEV, T), lambda v: (v, 0, 0))
    tile = pl.BlockSpec((1, 1, LEV, T, T), lambda v: (0, v, 0, 0, 0))
    side = whole(*left.shape)
    out_specs, out_shape = [tile], [jax.ShapeDtypeStruct(u.shape, f32)]
    if emit:
        out_specs += [rows, rows, whole(T, T)]
        out_shape += [jax.ShapeDtypeStruct((NV, LEV, T), f32)] * 2
        out_shape += [jax.ShapeDtypeStruct((T, T), f32)]
    return pl.pallas_call(
        kernel,
        grid=(NV,),
        in_specs=[
            pl.BlockSpec(memory_space=pltpu.SMEM),
            pl.BlockSpec(memory_space=pltpu.SMEM),
            tile,
            whole(1, T, T),
            rows,
            rows,
            side,
            side,
        ],
        out_specs=out_specs,
        out_shape=out_shape,
        scratch_shapes=[pltpu.VMEM((T, T), f32)],
        compiler_params=params(),
        cost_estimate=pl.CostEstimate(flops=24 << 20, bytes_accessed=9 << 20, transcendentals=0),
        name=name,
    )(rate, flags, u, vert, top, bottom, left, right)


def unpack_kernel(flags, data, after, imp, first, last, cols):
    del after
    size = SLOTS * NV
    sub = subl(T).astype(f32) + 1.0
    picks = []
    for j in range(NV):
        table = jnp.sum(data[pl.ds(CAP * NV + j, PEERS, stride=size), :], axis=0, keepdims=True)
        picks.append((sub == table).astype(jnp.bfloat16))
    pick = jnp.concatenate(picks, axis=1)
    lane = lanes(T)
    acc = jnp.zeros((T, T), f32)
    for v in range(NV):
        block = jnp.concatenate(
            [data[pl.ds(s * size + v, CAP, stride=NV), :] for s in range(PEERS)], axis=0
        )
        high = block.astype(jnp.bfloat16)
        low = (block - high.astype(f32)).astype(jnp.bfloat16)
        total = jnp.dot(pick, high, preferred_element_type=f32)
        total = total + jnp.dot(pick, low, preferred_element_type=f32)
        imp[v] = total
        first[v] = jnp.broadcast_to(total[0:1, :] * flags[0], (8, T))
        last[v] = jnp.broadcast_to(total[T - 1 : T, :] * flags[1], (8, T))
        acc = jnp.where((lane >> 1) == v * LEV, pltpu.roll(total, (32 * v + 1) % T, 1), acc)
    cols[...] = acc * cut(flags, lane)


def unpack(flags, data, after):
    return pl.pallas_call(
        unpack_kernel,
        in_specs=[
            pl.BlockSpec(memory_space=pltpu.SMEM),
            pl.BlockSpec(memory_space=pltpu.VMEM),
            pl.BlockSpec(memory_space=pl.ANY),
        ],
        out_shape=[
            jax.ShapeDtypeStruct((NV, T, T), f32),
            jax.ShapeDtypeStruct((NV, 8, T), f32),
            jax.ShapeDtypeStruct((NV, 8, T), f32),
            jax.ShapeDtypeStruct((T, T), f32),
        ],
        compiler_params=params(),
        cost_estimate=pl.CostEstimate(flops=200 << 20, bytes_accessed=2 << 20, transcendentals=0),
        name="unpack",
    )(flags, data, after)


def final_kernel(
    horiz, relax, prior, mid, vert, mask, top, bottom, left, right, sea_top, sea_bottom, sea_left, sea_right,
    imp, imp_top, imp_bottom, imp_left, imp_right, out,
):
    v = pl.program_id(0)
    pull = relax[v]
    spin = unshift(v)

    def relaxed(base, sea, new):
        return base + pull * sea * (new - base)

    sea = mask[0].astype(f32)
    new = imp[0]
    u = relaxed(prior[0, 0, 0], sea, new)
    up = relaxed(top[0, 0:1, :], sea_top[0, 0:1, :], imp_top[0, 0:1, :])
    down = relaxed(bottom[0, 0:1, :], sea_bottom[0, 0:1, :], imp_bottom[0, 0:1, :])
    side = relaxed(
        pltpu.roll(merged(left[...], right[...]), spin, 1),
        merged(sea_left[0], sea_right[0]),
        pltpu.roll(merged(imp_left[...], imp_right[...]), spin, 1),
    )
    h = diffuse(u, up, down, side, horiz[v])
    coef = vert[0]
    value = h + coef * (mid[0, 0, 0] - h)
    out[0, 0, 0] = relaxed(value, sea, new)
    out[0, 0, 1] = mid[0, 0, 1] + coef * h


def final(horiz, relax, prior, mid, vert, mask, rows2, cols2, rows1, cols1, imp, imp_rows, imp_cols):
    whole = lambda *n: pl.BlockSpec(n, lambda v: (0,) * len(n))
    smem = pl.BlockSpec(memory_space=pltpu.SMEM)
    row2 = pl.BlockSpec((1, LEV, T), lambda v: (v, 0, 0))
    row1 = pl.BlockSpec((1, LEV, T), lambda v: (NV, 0, 0))
    rowi = pl.BlockSpec((1, 8, T), lambda v: (v, 0, 0))
    sea_col = pl.BlockSpec((1, T, T), lambda v: (1, 0, 0))
    pairs = pl.BlockSpec((1, 1, 2, T, T), lambda v: (0, v, 0, 0, 0))
    return pl.pallas_call(
        final_kernel,
        grid=(NV,),
        in_specs=[
            smem,
            smem,
            pl.BlockSpec((1, 1, 1, T, T), lambda v: (0, v, 0, 0, 0)),
            pairs,
            whole(1, T, T),
            whole(1, T, T),
            row2,
            row2,
            whole(T, T),
            whole(T, T),
            row1,
            row1,
            sea_col,
            sea_col,
            pl.BlockSpec((1, T, T), lambda v: (v, 0, 0)),
            rowi,
            rowi,
            whole(T, T),
            whole(T, T),
        ],
        out_specs=pairs,
        out_shape=jax.ShapeDtypeStruct(mid.shape, f32),
        input_output_aliases={3: 0},
        compiler_params=params(),
        cost_estimate=pl.CostEstimate(flops=2 << 20, bytes_accessed=3 << 20, transcendentals=0),
        name="final",
    )(
        horiz, relax, prior, mid, vert, mask, *rows2, *cols2, *rows1, *cols1, imp, *imp_rows, *imp_cols
    )


def shifted(block, axis, by, across):
    count = lax.axis_size(axis)
    if not across:
        return lax.ppermute(
            block, axis, [(i, (i + by) % count) for i in range(count)]
        )
    return lax.ppermute(
        block,
        ("comp", axis),
        [
            (c * count + i, (1 - c) * count + (i + by) % count)
            for c in range(2)
            for i in range(count)
        ],
    )


def neighbours(first, last, cols, across=False):
    rows = shifted(last, "gx", 1, across), shifted(first, "gx", -1, across)
    sides = shifted(cols, "gy", 1, across), shifted(cols, "gy", -1, across)
    return rows, sides


def local(
    state, horiz_coef, vert_coef, couple_rate, sea_mask, dest_block, entry_count, remap_weight
):
    horiz, relax = horiz_coef[0], couple_rate[0]
    gx, gy = lax.axis_index("gx"), lax.axis_index("gy")
    ends = lax.axis_size("gx") - 1, lax.axis_size("gy") - 1
    me = (gx * (ends[1] + 1) + gy).astype(i32)
    flags = jnp.stack([gx > 0, gx < ends[0], gy < ends[1], gy > 0]).astype(f32)
    first, last, cols, surf = edges(flags, sea_mask, state)
    rows1, cols1 = neighbours(first, last, cols)
    packed = remap(
        dest_block.reshape(T * FAN), entry_count.reshape(T), me.reshape(1), surf, remap_weight
    )
    packed = sealed(packed, *rows1, *cols1).reshape(PEERS, SLOTS, NV, T)
    packed = lax.all_to_all(packed, ("gx", "gy"), split_axis=0, concat_axis=0, tiled=True)
    prior, first, last, cols = step_call(
        first_kernel, horiz, flags, state, vert_coef, *rows1, *cols1, True, "first_step"
    )
    rows2, cols2 = neighbours(first, last, cols)
    imp, first, last, cols = unpack(flags, packed.reshape(PEERS * SLOTS * NV, T), cols)
    imp = lax.ppermute(imp, "comp", [(0, 1), (1, 0)])
    imp_rows, imp_cols = neighbours(first, last, cols, across=True)
    (mid,) = step_call(
        second_kernel, horiz, flags, prior, vert_coef, *rows2, *cols2, False, "second_step"
    )
    return final(
        horiz, relax, prior, mid, vert_coef, sea_mask, rows2, cols2, rows1, cols1, imp, imp_rows, imp_cols
    )


def solution(mesh):
    in_specs = (
        P("comp", None, None, "gx", "gy"),
        P("comp", None),
        P("comp", "gx", "gy"),
        P("comp", None),
        P("comp", "gx", "gy"),
        P("comp", "gx", "gy", None),
        P("comp", "gx", "gy"),
        P("comp", "gx", "gy", None, None, None),
    )
    out_specs = P("comp", None, None, "gx", "gy")
    return jax.shard_map(local, mesh=mesh, in_specs=in_specs, out_specs=out_specs, check_vma=False)
```

time: 218 us -> 83.5 us (0.38)
  the two profiles are of different devices: /device:TPU:1 before, /device:TPU:24 now
where the time goes in v1:
time: 83.5 us; the launch traced here: 83 us
  starting transfers between devices  36 us (43%)
  Pallas kernels  29.3 us (35%)
  local copies, waits for them, and re-layouts  13.2 us (16%)
  waiting for transfers between devices  3.5 us (4%)
    ppermute x8, starting transfers between devices, shifted(): lax.ppermute(block, axis, [(i, (i + by) % count) for i in range(count)])  14.3 us
    unnamed x51, local copies, waits for them, and re-layouts  13.1 us
    pallas_call x2, Pallas kernels, step_call(): pl.pallas_call(kernel, grid=(NV,), in_specs=[pl.BlockSpec(memory_space=pl...  11.4 us
    ppermute x4, starting transfers between devices, shifted(): lax.ppermute(block, ('comp', axis), [(c * count + i, (1 - c) * count + (i...  10.7 us
    pallas_call x1, Pallas kernels, remap(): pl.pallas_call(remap_kernel, in_specs=[smem, smem, smem, vmem, hbm], out_...  9.09 us
    all_to_all x1, starting transfers between devices, local(): lax.all_to_all(packed, ('gx', 'gy'), split_axis=0, concat_axis=0, tiled=T...  8.26 us
    pallas_call x1, Pallas kernels, edges(): pl.pallas_call(edge_kernel, in_specs=[pl.BlockSpec(memory_space=pltpu.SME...  4.08 us
    pallas_call x1, Pallas kernels, final(): pl.pallas_call(final_kernel, grid=(NV,), in_specs=[smem, smem, pl.BlockSp...  3.64 us
  transfers between devices with their start and end apart: 14, of which 1 were waited for; matrix products, arithmetic and copies ran while one was open for 0% of the time, Pallas kernels for 25%

profile of v1, /device:TPU:24, one launch (start us, length us, event | category | flops | bytes accessed | tf_op | source)
XLA Modules:
  0.0 83.0 jit_solution(7756683937927247666)
XLA Ops:
  0.7 4.1 %edges.1 = (f32[5,16,128]{2,1,0:T(8,128)}, f32[5,16,128]{2,1,0:T(8,128)}, f32[2,128,128]{2,1,0:T(8,128)}, f32[512,128]{1,0:T(8,128)}) custom-call(f32[4]{0:T(128)} %add_convert_fusion.flags, s32[1,128,128]{2,1,0:T(8,128)} %mask.3, f32[1,4,16,128,128]{4,3,2,1,0:T(8,128)} %u.1), custom_call_target="tpu_custom_call" | custom-call | flops 4194304 | bytes 5242880 | tf_op jit(solution)/shard_map/edges/pallas_call | solution.py:76
  4.7 0.8 collective-permute-start.3
  5.6 3.4 %collective-permute-start.2 = (f32[2,128,128]{2,1,0:T(8,128)}, f32[2,128,128]{2,1,0:T(8,128)S(1)}, u32[]{:S(2)}, u32[]{:S(2)}) collective-permute-start(f32[2,128,128]{2,1,0:T(8,128)} %get-tuple-element.19), channel_id=1, source_target_pairs={{0,1},{1,2},{2,3},{3,4},{4,5},{5,6},{6,7},{7,0},{8,9},{9,10},{10,1... | collective-permute-start | bytes 393224 | tf_op jit(solution)/shard_map/ppermute | solution.py:420
  9.0 3.0 %collective-permute-start.1 = (f32[5,16,128]{2,1,0:T(8,128)}, f32[5,16,128]{2,1,0:T(8,128)S(1)}, u32[]{:S(2)}, u32[]{:S(2)}) collective-permute-start(f32[5,16,128]{2,1,0:T(8,128)} %get-tuple-element.18), channel_id=1, source_target_pairs={{0,56},{8,0},{16,8},{24,16},{32,24},{40,32},{48,40},{56,48},{1,57}... | collective-permute-start | bytes 122888 | tf_op jit(solution)/shard_map/ppermute | solution.py:420
  12.2 0.9 %copy-done.18 = f32[512,128]{1,0:T(8,128)S(1)} copy-done((f32[512,128]{1,0:T(8,128)S(1)}, f32[512,128]{1,0:T(8,128)}, u32[]{:S(2)}) %copy-start.18) | copy-done | bytes 262168
  13.1 9.1 %remap.1.refs_0_ = f32[576,4,128]{2,1,0:T(4,128)S(1)} custom-call(s32[512]{0:T(512)S(1)} %reshape.15.dest, s32[128]{0:T(128)S(1)} %bitcast.19, s32[1]{0:T(128)} %bitcast.7.me, f32[512,128]{1,0:T(8,128)S(1)} %copy-done.18, bf16[1,128,1,4,128,128]{5,4,3,2,1,0:T(8,128)(2,1)} %weight.1), custom_call_target="tpu_custom_call" | custom-call | flops 70254592 | bytes 23068672 | tf_op jit(solution)/shard_map/remap/pallas_call | solution.py:157
  22.2 1.0 %copy-done.4 = f32[576,4,128]{2,1,0:T(4,128)} copy-done((f32[576,4,128]{2,1,0:T(4,128)}, f32[576,4,128]{2,1,0:T(4,128)S(1)}, u32[]{:S(2)}) %copy-start.4) | copy-done | bytes 1179672
  24.6 8.3 %all-to-all-start = ((f32[64,9,4,128]{3,2,1,0:T(4,128)}), f32[64,9,4,128]{3,2,1,0:T(4,128)S(1)}, u32[]{:S(2)}, u32[]{:S(2)}) async-start(f32[64,9,4,128]{3,2,1,0:T(4,128)} %bitcast.14), calls=%async_computation | async-start | bytes 2359296 | tf_op jit(solution)/shard_map/all_to_all | solution.py:454
  32.9 2.2 %copy-done = f32[1,4,16,128,128]{4,3,2,1,0:T(8,128)S(1)} copy-done((f32[1,4,16,128,128]{4,3,2,1,0:T(8,128)S(1)}, f32[1,4,16,128,128]{4,3,2,1,0:T(8,128)}, u32[]{:S(2)}) %copy-start) | copy-done | bytes 4194328
  35.1 0.9 %copy-done.6 = f32[2,128,128]{2,1,0:T(8,128)S(1)} copy-done((f32[2,128,128]{2,1,0:T(8,128)S(1)}, f32[2,128,128]{2,1,0:T(8,128)}, u32[]{:S(2)}) %copy-start.6) | copy-done | bytes 131096
  36.0 0.9 %copy-done.9 = f32[2,128,128]{2,1,0:T(8,128)S(1)} copy-done((f32[2,128,128]{2,1,0:T(8,128)S(1)}, f32[2,128,128]{2,1,0:T(8,128)}, u32[]{:S(2)}) %copy-start.9) | copy-done | bytes 131096
  38.4 6.1 %first_step.1 = (f32[1,4,16,128,128]{4,3,2,1,0:T(8,128)S(1)}, f32[4,16,128]{2,1,0:T(8,128)S(1)}, f32[4,16,128]{2,1,0:T(8,128)S(1)}, f32[128,128]{1,0:T(8,128)S(1)}) custom-call(f32[4]{0:T(128)S(1)} %bitcast.16, f32[4]{0:T(128)S(1)} %copy-done.20, f32[1,4,16,128,128]{4,3,2,1,0:T(8,128)S(1)} %copy-done, f32[1,128,128]{2,1,0:T(8,128)S(1)} %copy-done.11, ...), custom_call_target="tpu_custom_call" | custom-call | flops 25165824 | bytes 9437184 | tf_op jit(solution)/shard_map/first_step/pallas_call | solution.py:278
  44.6 2.0 %copy-done.1 = f32[1,4,16,128,128]{4,3,2,1,0:T(8,128)} copy-done((f32[1,4,16,128,128]{4,3,2,1,0:T(8,128)}, f32[1,4,16,128,128]{4,3,2,1,0:T(8,128)S(1)}, u32[]{:S(2)}) %copy-start.1) | copy-done | bytes 4194328
  46.6 3.5 %all-to-all-done = f32[64,9,4,128]{3,2,1,0:T(4,128)S(1)} async-done(((f32[64,9,4,128]{3,2,1,0:T(4,128)}), f32[64,9,4,128]{3,2,1,0:T(4,128)S(1)}, u32[]{:S(2)}, u32[]{:S(2)}) %all-to-all-start) | async-done | bytes 1179680 | tf_op jit(solution)/shard_map/all_to_all | solution.py:454
  50.0 1.1 %unpack.1 = (f32[4,128,128]{2,1,0:T(8,128)S(1)}, f32[4,8,128]{2,1,0:T(8,128)S(1)}, f32[4,8,128]{2,1,0:T(8,128)S(1)}, f32[128,128]{1,0:T(8,128)S(1)}) custom-call(f32[4]{0:T(128)S(1)} %copy-done.20, f32[2304,128]{1,0:T(8,128)S(1)} %bitcast.15, f32[128,128]{1,0:T(8,128)S(1)} %get-tuple-element.23.after), custom_call_target="tpu_custom_call" | custom-call | flops 209715200 | bytes 2097152 | tf_op jit(solution)/shard_map/unpack/pallas_call | solution.py:327
  51.1 2.8 %collective-permute-start.8 = (f32[4,128,128]{2,1,0:T(8,128)S(1)}, f32[4,128,128]{2,1,0:T(8,128)S(1)}, u32[]{:S(2)}, u32[]{:S(2)}) collective-permute-start(f32[4,128,128]{2,1,0:T(8,128)S(1)} %get-tuple-element.25), channel_id=1, source_target_pairs={{0,64},{64,0},{1,65},{65,1},{2,66},{66,2},{3,67},{67,3},{4,68},{68... | collective-permute-start | bytes 786440 | tf_op jit(solution)/shard_map/ppermute | solution.py:460
  53.9 3.0 %collective-permute-start.5 = (f32[4,16,128]{2,1,0:T(8,128)S(1)}, f32[4,16,128]{2,1,0:T(8,128)S(1)}, u32[]{:S(2)}, u32[]{:S(2)}) collective-permute-start(f32[4,16,128]{2,1,0:T(8,128)S(1)} %get-tuple-element.22), channel_id=1, source_target_pairs={{0,56},{8,0},{16,8},{24,16},{32,24},{40,32},{48,40},{56,48},{1,57}... | collective-permute-start | bytes 98312 | tf_op jit(solution)/shard_map/ppermute | solution.py:420
  56.9 1.0 %collective-permute-start.7 = (f32[128,128]{1,0:T(8,128)S(1)}, f32[128,128]{1,0:T(8,128)S(1)}, u32[]{:S(2)}, u32[]{:S(2)}) collective-permute-start(f32[128,128]{1,0:T(8,128)S(1)} %get-tuple-element.23.after), channel_id=1, source_target_pairs={{0,7},{1,0},{2,1},{3,2},{4,3},{5,4},{6,5},{7,6},{8,15},{9,8},{10,9... | collective-permute-start | bytes 196616 | tf_op jit(solution)/shard_map/ppermute | solution.py:420
  57.8 3.2 %collective-permute-start.6 = (f32[128,128]{1,0:T(8,128)S(1)}, f32[128,128]{1,0:T(8,128)S(1)}, u32[]{:S(2)}, u32[]{:S(2)}) collective-permute-start(f32[128,128]{1,0:T(8,128)S(1)} %get-tuple-element.23.after), channel_id=1, source_target_pairs={{0,1},{1,2},{2,3},{3,4},{4,5},{5,6},{6,7},{7,0},{8,9},{9,10},{10,1... | collective-permute-start | bytes 196616 | tf_op jit(solution)/shard_map/ppermute | solution.py:420
  61.0 5.3 %collective-permute-start.11 = (f32[128,128]{1,0:T(8,128)S(1)}, f32[128,128]{1,0:T(8,128)S(1)}, u32[]{:S(2)}, u32[]{:S(2)}) collective-permute-start(f32[128,128]{1,0:T(8,128)S(1)} %get-tuple-element.28), channel_id=1, source_target_pairs={{0,65},{1,66},{2,67},{3,68},{4,69},{5,70},{6,71},{7,64},{64,1},{65... | collective-permute-start | bytes 196616 | tf_op jit(solution)/shard_map/ppermute | solution.py:423
  66.4 5.4 %collective-permute-start.10 = (f32[4,8,128]{2,1,0:T(8,128)S(1)}, f32[4,8,128]{2,1,0:T(8,128)S(1)}, u32[]{:S(2)}, u32[]{:S(2)}) collective-permute-start(f32[4,8,128]{2,1,0:T(8,128)S(1)} %get-tuple-element.27), channel_id=1, source_target_pairs={{0,120},{8,64},{16,72},{24,80},{32,88},{40,96},{48,104},{56,112},{... | collective-permute-start | bytes 49160 | tf_op jit(solution)/shard_map/ppermute | solution.py:423
  71.7 2.2 %copy-done.2 = f32[1,4,16,128,128]{4,3,2,1,0:T(8,128)S(1)} copy-done((f32[1,4,16,128,128]{4,3,2,1,0:T(8,128)S(1)}, f32[1,4,16,128,128]{4,3,2,1,0:T(8,128)}, u32[]{:S(2)}) %copy-start.2) | copy-done | bytes 4194328
  74.0 5.3 %second_step.1.mid = f32[1,4,16,128,128]{4,3,2,1,0:T(8,128)} custom-call(f32[4]{0:T(128)S(1)} %bitcast.17, f32[4]{0:T(128)S(1)} %copy-done.20, f32[1,4,16,128,128]{4,3,2,1,0:T(8,128)S(1)} %copy-done.2, f32[1,128,128]{2,1,0:T(8,128)S(1)} %copy-done.11, f32[4,16,128]{2,1,0:T(8,128)S(1)} %collective-permute-done.4.top, ...), custom_call_target="tpu_custom_call" | custom-call | flops 25165824 | bytes 9437184 | tf_op jit(solution)/shard_map/second_step/pallas_call | solution.py:278
  79.4 3.6 %final.1 = f32[1,4,16,128,128]{4,3,2,1,0:T(8,128)} custom-call(f32[4]{0:T(128)S(1)} %bitcast.18, f32[4]{0:T(128)S(1)} %bitcast.20, f32[1,4,16,128,128]{4,3,2,1,0:T(8,128)S(1)} %copy-done.3, f32[1,4,16,128,128]{4,3,2,1,0:T(8,128)} %second_step.1.mid, f32[1,128,128]{2,1,0:T(8,128)S(1)} %copy-done.11, ...), custom_call_target="tpu_custom_call", output_to_operand_aliasing={{}: (3, {})} | custom-call | flops 2097152 | bytes 3145728 | tf_op jit(solution)/shard_map/final/pallas_call | solution.py:382
  (64 shorter events, 3.8 us)
Async XLA Ops:
  0.0 11.9 %copy-start.24 = (s32[1,128,1,4]{1,3,2,0:T(4,128)S(1)}, s32[1,128,1,4]{1,3,2,0:T(4,128)}, u32[]{:S(2)}) copy-start(s32[1,128,1,4]{1,3,2,0:T(4,128)} %param.13) | copy-start | bytes 6148
  0.0 12.1 %copy-start.22 = (s32[1,128,1]{1,2,0:T(1,128)S(1)}, s32[1,128,1]{1,2,0:T(1,128)}, u32[]{:S(2)}) copy-start(s32[1,128,1]{1,2,0:T(1,128)} %param.14) | copy-start | bytes 1540
  4.7 18.5 %collective-permute-start.3 = (f32[2,128,128]{2,1,0:T(8,128)}, f32[2,128,128]{2,1,0:T(8,128)S(1)}, u32[]{:S(2)}, u32[]{:S(2)}) collective-permute-start(f32[2,128,128]{2,1,0:T(8,128)} %get-tuple-element.19), channel_id=1, source_target_pairs={{0,7},{1,0},{2,1},{3,2},{4,3},{5,4},{6,5},{7,6},{8,15},{9,8},{10,9... | collective-permute-start | bytes 393224 | tf_op jit(solution)/shard_map/ppermute | solution.py:420
  5.6 17.7 %collective-permute-start.2 = (f32[2,128,128]{2,1,0:T(8,128)}, f32[2,128,128]{2,1,0:T(8,128)S(1)}, u32[]{:S(2)}, u32[]{:S(2)}) collective-permute-start(f32[2,128,128]{2,1,0:T(8,128)} %get-tuple-element.19), channel_id=1, source_target_pairs={{0,1},{1,2},{2,3},{3,4},{4,5},{5,6},{6,7},{7,0},{8,9},{9,10},{10,1... | collective-permute-start | bytes 393224 | tf_op jit(solution)/shard_map/ppermute | solution.py:420
  8.9 14.3 %collective-permute-start = (f32[5,16,128]{2,1,0:T(8,128)}, f32[5,16,128]{2,1,0:T(8,128)S(1)}, u32[]{:S(2)}, u32[]{:S(2)}) collective-permute-start(f32[5,16,128]{2,1,0:T(8,128)} %get-tuple-element.17), channel_id=1, source_target_pairs={{0,8},{8,16},{16,24},{24,32},{32,40},{40,48},{48,56},{56,0},{1,9},... | collective-permute-start | bytes 122888 | tf_op jit(solution)/shard_map/ppermute | solution.py:420
  9.0 14.3 %collective-permute-start.1 = (f32[5,16,128]{2,1,0:T(8,128)}, f32[5,16,128]{2,1,0:T(8,128)S(1)}, u32[]{:S(2)}, u32[]{:S(2)}) collective-permute-start(f32[5,16,128]{2,1,0:T(8,128)} %get-tuple-element.18), channel_id=1, source_target_pairs={{0,56},{8,0},{16,8},{24,16},{32,24},{40,32},{48,40},{56,48},{1,57}... | collective-permute-start | bytes 122888 | tf_op jit(solution)/shard_map/ppermute | solution.py:420
  23.2 9.6 %copy-start.11 = (f32[1,128,128]{2,1,0:T(8,128)S(1)}, f32[1,128,128]{2,1,0:T(8,128)}, u32[]{:S(2)}) copy-start(f32[1,128,128]{2,1,0:T(8,128)} %vert.5) | copy-start | bytes 196612
  23.2 9.7 %copy-start.20 = (f32[4]{0:T(128)S(1)}, f32[4]{0:T(128)}, u32[]{:S(2)}) copy-start(f32[4]{0:T(128)} %add_convert_fusion.flags) | copy-start | bytes 52
  23.2 9.7 %copy-start.21 = (f32[1,4]{1,0:T(1,128)S(1)}, f32[1,4]{1,0:T(1,128)}, u32[]{:S(2)}) copy-start(f32[1,4]{1,0:T(1,128)} %param.9) | copy-start | bytes 52
  24.6 25.4 %all-to-all-start = ((f32[64,9,4,128]{3,2,1,0:T(4,128)}), f32[64,9,4,128]{3,2,1,0:T(4,128)S(1)}, u32[]{:S(2)}, u32[]{:S(2)}) async-start(f32[64,9,4,128]{3,2,1,0:T(4,128)} %bitcast.14), calls=%async_computation | async-start | bytes 2359296 | tf_op jit(solution)/shard_map/all_to_all | solution.py:454
  51.1 28.2 %collective-permute-start.8 = (f32[4,128,128]{2,1,0:T(8,128)S(1)}, f32[4,128,128]{2,1,0:T(8,128)S(1)}, u32[]{:S(2)}, u32[]{:S(2)}) collective-permute-start(f32[4,128,128]{2,1,0:T(8,128)S(1)} %get-tuple-element.25), channel_id=1, source_target_pairs={{0,64},{64,0},{1,65},{65,1},{2,66},{66,2},{3,67},{67,3},{4,68},{68... | collective-permute-start | bytes 786440 | tf_op jit(solution)/shard_map/ppermute | solution.py:460
  53.9 7.1 %collective-permute-start.4 = (f32[4,16,128]{2,1,0:T(8,128)S(1)}, f32[4,16,128]{2,1,0:T(8,128)S(1)}, u32[]{:S(2)}, u32[]{:S(2)}) collective-permute-start(f32[4,16,128]{2,1,0:T(8,128)S(1)} %get-tuple-element.21), channel_id=1, source_target_pairs={{0,8},{8,16},{16,24},{24,32},{32,40},{40,48},{48,56},{56,0},{1,9},... | collective-permute-start | bytes 98312 | tf_op jit(solution)/shard_map/ppermute | solution.py:420
  53.9 7.1 %collective-permute-start.5 = (f32[4,16,128]{2,1,0:T(8,128)S(1)}, f32[4,16,128]{2,1,0:T(8,128)S(1)}, u32[]{:S(2)}, u32[]{:S(2)}) collective-permute-start(f32[4,16,128]{2,1,0:T(8,128)S(1)} %get-tuple-element.22), channel_id=1, source_target_pairs={{0,56},{8,0},{16,8},{24,16},{32,24},{40,32},{48,40},{56,48},{1,57}... | collective-permute-start | bytes 98312 | tf_op jit(solution)/shard_map/ppermute | solution.py:420
  56.9 9.5 %collective-permute-start.7 = (f32[128,128]{1,0:T(8,128)S(1)}, f32[128,128]{1,0:T(8,128)S(1)}, u32[]{:S(2)}, u32[]{:S(2)}) collective-permute-start(f32[128,128]{1,0:T(8,128)S(1)} %get-tuple-element.23.after), channel_id=1, source_target_pairs={{0,7},{1,0},{2,1},{3,2},{4,3},{5,4},{6,5},{7,6},{8,15},{9,8},{10,9... | collective-permute-start | bytes 196616 | tf_op jit(solution)/shard_map/ppermute | solution.py:420
  57.8 8.5 %collective-permute-start.6 = (f32[128,128]{1,0:T(8,128)S(1)}, f32[128,128]{1,0:T(8,128)S(1)}, u32[]{:S(2)}, u32[]{:S(2)}) collective-permute-start(f32[128,128]{1,0:T(8,128)S(1)} %get-tuple-element.23.after), channel_id=1, source_target_pairs={{0,1},{1,2},{2,3},{3,4},{4,5},{5,6},{6,7},{7,0},{8,9},{9,10},{10,1... | collective-permute-start | bytes 196616 | tf_op jit(solution)/shard_map/ppermute | solution.py:420
  61.0 18.3 %collective-permute-start.12 = (f32[128,128]{1,0:T(8,128)S(1)}, f32[128,128]{1,0:T(8,128)S(1)}, u32[]{:S(2)}, u32[]{:S(2)}) collective-permute-start(f32[128,128]{1,0:T(8,128)S(1)} %get-tuple-element.28), channel_id=1, source_target_pairs={{0,71},{1,64},{2,65},{3,66},{4,67},{5,68},{6,69},{7,70},{64,7},{65... | collective-permute-start | bytes 196616 | tf_op jit(solution)/shard_map/ppermute | solution.py:423
  61.0 18.3 %collective-permute-start.11 = (f32[128,128]{1,0:T(8,128)S(1)}, f32[128,128]{1,0:T(8,128)S(1)}, u32[]{:S(2)}, u32[]{:S(2)}) collective-permute-start(f32[128,128]{1,0:T(8,128)S(1)} %get-tuple-element.28), channel_id=1, source_target_pairs={{0,65},{1,66},{2,67},{3,68},{4,69},{5,70},{6,71},{7,64},{64,1},{65... | collective-permute-start | bytes 196616 | tf_op jit(solution)/shard_map/ppermute | solution.py:423
  66.4 12.9 %collective-permute-start.9 = (f32[4,8,128]{2,1,0:T(8,128)S(1)}, f32[4,8,128]{2,1,0:T(8,128)S(1)}, u32[]{:S(2)}, u32[]{:S(2)}) collective-permute-start(f32[4,8,128]{2,1,0:T(8,128)S(1)} %get-tuple-element.26), channel_id=1, source_target_pairs={{0,72},{8,80},{16,88},{24,96},{32,104},{40,112},{48,120},{56,64},{... | collective-permute-start | bytes 49160 | tf_op jit(solution)/shard_map/ppermute | solution.py:423
  66.4 12.9 %collective-permute-start.10 = (f32[4,8,128]{2,1,0:T(8,128)S(1)}, f32[4,8,128]{2,1,0:T(8,128)S(1)}, u32[]{:S(2)}, u32[]{:S(2)}) collective-permute-start(f32[4,8,128]{2,1,0:T(8,128)S(1)} %get-tuple-element.27), channel_id=1, source_target_pairs={{0,120},{8,64},{16,72},{24,80},{32,88},{40,96},{48,104},{56,112},{... | collective-permute-start | bytes 49160 | tf_op jit(solution)/shard_map/ppermute | solution.py:423
  73.9 5.4 %copy-start.10 = (f32[2,128,128]{2,1,0:T(8,128)S(1)}, f32[2,128,128]{2,1,0:T(8,128)}, u32[]{:S(2)}) copy-start(f32[2,128,128]{2,1,0:T(8,128)} %copy-done.8) | copy-start | bytes 393220
  73.9 5.4 %copy-start.14 = (f32[5,16,128]{2,1,0:T(8,128)S(1)}, f32[5,16,128]{2,1,0:T(8,128)}, u32[]{:S(2)}) copy-start(f32[5,16,128]{2,1,0:T(8,128)} %copy-done.12) | copy-start | bytes 122884
  73.9 5.4 %copy-start.17 = (f32[5,16,128]{2,1,0:T(8,128)S(1)}, f32[5,16,128]{2,1,0:T(8,128)}, u32[]{:S(2)}) copy-start(f32[5,16,128]{2,1,0:T(8,128)} %copy-done.15) | copy-start | bytes 122884
  73.9 5.4 %copy-start.19 = (s32[1,128,128]{2,1,0:T(8,128)S(1)}, s32[1,128,128]{2,1,0:T(8,128)}, u32[]{:S(2)}) copy-start(s32[1,128,128]{2,1,0:T(8,128)} %mask.3) | copy-start | bytes 196612
  73.9 5.4 %copy-start.23 = (f32[1,4]{1,0:T(1,128)S(1)}, f32[1,4]{1,0:T(1,128)}, u32[]{:S(2)}) copy-start(f32[1,4]{1,0:T(1,128)} %param.11) | copy-start | bytes 52
  (15 other events, 25.0 us)

commit v2 on v0

v2 whole, which is shorter than its diff:
```python
import jax
import jax.numpy as jnp
from jax import lax
from jax.experimental import pallas as pl
from jax.experimental.pallas import tpu as pltpu
from jax.sharding import PartitionSpec as P

NV = 4
LEV = 16
PLANES = NV * LEV
T = 128
FAN = 4
CAP = 8
PEERS = 64
SLOTS = CAP + 1
HALF = 64
CHUNKS = 16
MIB = 1024 * 1024
LIMIT = 58 * MIB
ROW_VERT = 2 * PLANES
ROW_SEA = ROW_VERT + 8
ROW_SIZE = ROW_SEA + 8
COL_NEXT = T
COL_COEF = 2 * T
COL_TOP = 3 * T
COL_BOTTOM = COL_TOP + 8
COL_SIZE = COL_BOTTOM + 8
KEEP_BASE = 0
KEEP_ONE = NV * T
KEEP_PART = 2 * NV * T
KEEP_VERT = 3 * NV * T
KEEP_SEA = KEEP_VERT + T
KEEP_SIDE = KEEP_SEA + T
KEEP_SEA_SIDE = KEEP_SIDE + T
KEEP_ENDS = KEEP_SEA_SIDE + T
KEEP_SIZE = KEEP_ENDS + 16

f32 = jnp.float32
i32 = jnp.int32
bf16 = jnp.bfloat16

SMEM = pl.BlockSpec(memory_space=pltpu.SMEM)
VMEM = pl.BlockSpec(memory_space=pltpu.VMEM)
HBM = pl.BlockSpec(memory_space=pl.ANY)


def params(limit=LIMIT):
    return pltpu.CompilerParams(vmem_limit_bytes=limit)


def cost(flops, size):
    return pl.CostEstimate(flops=flops, bytes_accessed=size, transcendentals=0)


def lanes(rows):
    return lax.broadcasted_iota(i32, (rows, T), 1)


def subl(rows):
    return lax.broadcasted_iota(i32, (rows, T), 0)


def inside():
    gx, gy = lax.axis_index("gx"), lax.axis_index("gy")
    one = lambda test: jnp.where(test, 1.0, 0.0).astype(f32)
    return (
        one(gx > 0),
        one(gx < lax.axis_size("gx") - 1),
        one(gy > 0),
        one(gy < lax.axis_size("gy") - 1),
    )


def column_keep(rows):
    _, _, before, after = inside()
    return jnp.where((lanes(rows) & 1) == 0, after, before)


def run(copies):
    for copy in copies:
        copy.start()
    for copy in copies:
        copy.wait()


def row_kernel(state, vert, mask, head, tail, high, low, coef, sea, sems):
    ends = pl.ds(0, 8), pl.ds(T - 8, 8)
    copies = []
    for k, buffer in enumerate((high, low)):
        copies.append(pltpu.make_async_copy(state.at[0, :, :, ends[k]], buffer, sems.at[3 * k]))
        copies.append(pltpu.make_async_copy(vert.at[0, ends[k]], coef.at[k], sems.at[3 * k + 1]))
        copies.append(pltpu.make_async_copy(mask.at[0, ends[k]], sea.at[k], sems.at[3 * k + 2]))
    run(copies)
    up, down, _, _ = inside()
    for k, (out, buffer, keep) in enumerate(((head, high, up), (tail, low, down))):
        outer, following = (0, 1) if k == 0 else (7, 6)
        for p in range(PLANES):
            v, l = divmod(p, LEV)
            out[p : p + 1, :] = buffer[v, l, outer : outer + 1, :] * keep
            out[PLANES + p : PLANES + p + 1, :] = buffer[v, l, following : following + 1, :] * keep
        line = coef[k, outer : outer + 1, :] * keep
        out[ROW_VERT : ROW_VERT + 8, :] = jnp.broadcast_to(line, (8, T))
        line = sea[k, outer : outer + 1, :].astype(f32) * keep
        out[ROW_SEA : ROW_SEA + 8, :] = jnp.broadcast_to(line, (8, T))


def outer_rows(state, vert, mask):
    return pl.pallas_call(
        row_kernel,
        in_specs=[HBM, HBM, HBM],
        out_specs=[VMEM, VMEM],
        out_shape=[jax.ShapeDtypeStruct((ROW_SIZE, T), f32)] * 2,
        scratch_shapes=[
            pltpu.VMEM((NV, LEV, 8, T), f32),
            pltpu.VMEM((NV, LEV, 8, T), f32),
            pltpu.VMEM((2, 8, T), f32),
            pltpu.VMEM((2, 8, T), i32),
            pltpu.SemaphoreType.DMA((6,)),
        ],
        compiler_params=params(),
        cost_estimate=cost(1 << 16, 1 << 19),
        name="outer_rows",
    )(state, vert, mask)


def column_kernel(state, vert, mask, cols, surf, tile, coef, wet, sea, sems):
    loads = [pltpu.make_async_copy(state.at[0, v], tile.at[v], sems.at[v]) for v in range(NV)]
    loads.append(pltpu.make_async_copy(vert.at[0], coef, sems.at[NV]))
    loads.append(pltpu.make_async_copy(mask.at[0], sea, sems.at[NV + 1]))
    for load in loads:
        load.start()
    lane = lanes(HALF)
    keep = column_keep(HALF)
    for v in range(NV):
        loads[v].wait()
        surf[pl.ds(v, T, stride=NV), :] = tile[v, 0]
        for lo in range(0, T, HALF):
            outer, following = pl.ds(lo, HALF), pl.ds(COL_NEXT + lo, HALF)
            acc = jnp.zeros((HALF, T), f32) if v == 0 else cols[outer, :]
            acc2 = jnp.zeros((HALF, T), f32) if v == 0 else cols[following, :]
            for l in range(LEV):
                p = v * LEV + l
                plane = tile[v, l, lo : lo + HALF, :]
                acc = jnp.where((lane >> 1) == p, pltpu.roll(plane, (2 * p + 1) % T, 1), acc)
                hit = (lane == 2 * p) | (lane == (2 * p + 3) % T)
                acc2 = jnp.where(hit, pltpu.roll(plane, (2 * p + 2) % T, 1), acc2)
            last = v == NV - 1
            cols[outer, :] = acc * keep if last else acc
            cols[following, :] = acc2 * keep if last else acc2
    loads[NV].wait()
    loads[NV + 1].wait()
    lane = lanes(T)
    wet[...] = sea[...].astype(f32)
    pair = jnp.where(lane < 2, pltpu.roll(coef[...], 1, 1), pltpu.roll(wet[...], 3, 1))
    cols[COL_COEF : COL_COEF + T, :] = pair * column_keep(T)


def outer_columns(state, vert, mask):
    square = jax.ShapeDtypeStruct((T, T), f32)
    return pl.pallas_call(
        column_kernel,
        in_specs=[HBM, HBM, HBM],
        out_specs=[VMEM] * 5,
        out_shape=[
            jax.ShapeDtypeStruct((COL_TOP, T), f32),
            jax.ShapeDtypeStruct((T * NV, T), f32),
            jax.ShapeDtypeStruct((NV, LEV, T, T), f32),
            square,
            square,
        ],
        scratch_shapes=[pltpu.VMEM((T, T), i32), pltpu.SemaphoreType.DMA((NV + 2,))],
        compiler_params=params(47 * MIB),
        cost_estimate=cost(6 << 20, 9 << 20),
        name="outer_columns",
    )(state, vert, mask)


def corner_kernel(cols, top, bottom, out):
    out[0:COL_COEF, :] = cols[0:COL_COEF, :]
    lane, sub = lanes(PLANES), subl(PLANES)
    keep = column_keep(PLANES)
    for k, rows in enumerate((top, bottom)):
        line = rows[0:PLANES, :]
        at = COL_COEF + k * PLANES
        out[at : at + PLANES, :] = jnp.where(
            (lane == 4) | (lane == 5), pltpu.roll(line, 5, 1) * keep, cols[at : at + PLANES, :]
        )
        first = jnp.broadcast_to(line[:, 0:1], (PLANES, T))
        last = jnp.broadcast_to(line[:, T - 1 : T], (PLANES, T))
        spread = jnp.where(lane == 2 * sub, last, jnp.where(lane == 2 * sub + 1, first, 0.0))
        total = jnp.sum(spread * keep, axis=0, keepdims=True)
        at = COL_TOP + 8 * k
        out[at : at + 8, :] = jnp.broadcast_to(total, (8, T))


def with_corners(cols, top, bottom):
    return pl.pallas_call(
        corner_kernel,
        in_specs=[VMEM] * 3,
        out_specs=VMEM,
        out_shape=jax.ShapeDtypeStruct((COL_SIZE, T), f32),
        compiler_params=params(4 * MIB),
        cost_estimate=cost(1 << 16, 1 << 18),
        name="with_corners",
    )(cols, top, bottom)


def remap_kernel(dest_in, count_in, surf, weight, after, out, blocks, dest, count, used, label, sems):
    del after
    rows = T // CHUNKS
    lists = [
        pltpu.make_async_copy(dest_in, dest, sems.at[CHUNKS]),
        pltpu.make_async_copy(count_in, count, sems.at[CHUNKS + 1]),
    ]
    for copy in lists:
        copy.start()

    def fetch(c):
        piece = pl.ds(c * rows, rows)
        return pltpu.make_async_copy(weight.at[0, piece, 0], blocks.at[piece], sems.at[c])

    for c in range(CHUNKS):
        fetch(c).start()
    out[...] = jnp.zeros_like(out)

    def clear(i, _):
        used[i] = 0
        for k in range(CAP):
            label[i * CAP + k] = 0
        return 0

    lax.fori_loop(0, PEERS, clear, 0)
    for copy in lists:
        copy.wait()
    sub = subl(8)

    def slot_of(row, f):
        target = dest[f, row]
        peer = lax.shift_right_logical(target, 7) & (PEERS - 1)
        live = f < count[0, row]
        at = used[peer]
        used[peer] = at + jnp.where(live, 1, 0)
        label[jnp.where(live, peer * CAP + at, PEERS * CAP)] = (target & (T - 1)) + 1
        return jnp.where(live, peer * SLOTS + at, CAP)

    def chunk(c, _):
        fetch(c).wait()
        for r in range(0, rows, 2):
            row = c * rows + r
            slots = [[slot_of(row + q, f) for f in range(FAN)] for q in range(2)]
            pair = surf[pl.ds(pl.multiple_of(row * NV, 8), 8), :]
            pair = jnp.concatenate(
                [jnp.where(sub < NV, pair, 0.0), jnp.where(sub >= NV, pair, 0.0)], axis=1
            ).astype(bf16)
            for f in range(0, FAN, 2):
                block = jnp.concatenate(
                    [
                        jnp.concatenate([blocks[row + q, f], blocks[row + q, f + 1]], axis=1)
                        for q in range(2)
                    ],
                    axis=0,
                )
                product = jnp.dot(pair, block, preferred_element_type=f32)
                for q in range(2):
                    for g in range(2):
                        part = product[q * NV : (q + 1) * NV, g * T : (g + 1) * T]
                        out[slots[q][f + g]] = part
        return 0

    lax.fori_loop(0, CHUNKS, chunk, 0)
    me = lax.axis_index("gx") * lax.axis_size("gy") + lax.axis_index("gy")
    place = lax.broadcasted_iota(i32, (NV, T), 0) * T + lax.broadcasted_iota(i32, (NV, T), 1)
    place = place - me * CAP

    def write(i, _):
        block = jnp.zeros((NV, T), i32)
        for k in range(CAP):
            block = jnp.where(place == k, label[i * CAP + k], block)
        out[i * SLOTS + CAP] = block.astype(f32)
        return 0

    lax.fori_loop(0, PEERS, write, 0)


def remap(dest, count, surf, weight, after):
    return pl.pallas_call(
        remap_kernel,
        in_specs=[HBM, HBM, VMEM, HBM, HBM],
        out_specs=VMEM,
        out_shape=jax.ShapeDtypeStruct((PEERS * SLOTS, NV, T), f32),
        scratch_shapes=[
            pltpu.VMEM((T, FAN, T, T), bf16),
            pltpu.SMEM((FAN, T), i32),
            pltpu.SMEM((1, T), i32),
            pltpu.SMEM((PEERS,), i32),
            pltpu.SMEM((PEERS * CAP + 8,), i32),
            pltpu.SemaphoreType.DMA((CHUNKS + 2,)),
        ],
        compiler_params=params(44 * MIB),
        cost_estimate=cost(67 << 20, 20 << 20),
        name="remap",
    )(dest, count, surf, weight, after)


def sealed(block, *after):
    def kernel(*refs):
        del refs

    return pl.pallas_call(
        kernel,
        in_specs=[HBM] * (1 + len(after)),
        out_specs=HBM,
        out_shape=jax.ShapeDtypeStruct(block.shape, block.dtype),
        input_output_aliases={0: 0},
        name="sealed",
    )(block, *after)


def merged(left, right, back=2):
    return jnp.where((lanes(left.shape[0]) & 1) == 0, left, pltpu.roll(right, T - back, 1))


def diffuse(u, up, down, side, rate):
    rows = u.shape[0]
    lane, sub = lanes(rows), subl(rows)
    north = jnp.where(sub == 0, up, pltpu.roll(u, 1, 0))
    south = jnp.where(sub == rows - 1, down, pltpu.roll(u, rows - 1, 0))
    west = jnp.where(lane == 0, side, pltpu.roll(u, 1, 1))
    east = jnp.where(lane == T - 1, side, pltpu.roll(u, T - 1, 1))
    return u + rate * ((north + south) + (west + east) - 4.0 * u)


def level_diffuse(u, top, bottom, side, rate, l, lo):
    up = top[l : l + 1, :] if lo == 0 else u[l, lo - 1 : lo, :]
    down = bottom[l : l + 1, :] if lo + HALF == T else u[l, lo + HALF : lo + HALF + 1, :]
    spin = side[lo : lo + HALF, :]
    if l:
        spin = pltpu.roll(spin, T - 2 * l, 1)
    return diffuse(u[l, lo : lo + HALF, :], up, down, spin, rate)


def halo_columns(rate, left, right, own):
    lane, sub = lanes(T), subl(T)
    here = merged(left[0:T, :], right[0:T, :])
    outer = merged(left[COL_NEXT : COL_NEXT + T, :], right[COL_NEXT : COL_NEXT + T, :], 4)
    inner = pltpu.roll(own[0:T, :], T - 1, 1)
    ends = [merged(left[at : at + 8, :], right[at : at + 8, :])[0:1, :] for at in (COL_TOP, COL_BOTTOM)]
    north = jnp.where(sub == 0, ends[0], pltpu.roll(here, 1, 0))
    south = jnp.where(sub == T - 1, ends[1], pltpu.roll(here, T - 1, 0))
    plane = ((lane + 1) >> 1) & (PLANES - 1)
    number = jnp.full((T, T), rate[0, 0], f32)
    for v in range(1, NV):
        number = jnp.where(plane // LEV == v, rate[0, v], number)
    h = here + number * ((north + south) + (outer + inner) - 4.0 * here)
    coef = jnp.where(
        (lane & 1) == 0,
        jnp.broadcast_to(left[COL_COEF : COL_COEF + T, 0:1], (T, T)),
        jnp.broadcast_to(right[COL_COEF : COL_COEF + T, 1:2], (T, T)),
    )
    level = plane % LEV
    above = jnp.where(level < LEV - 1, pltpu.roll(h, T - 2, 1) - h, 0.0)
    below = jnp.where(level > 0, pltpu.roll(h, 2, 1) - h, 0.0)
    return here, h + coef * (above + below)


def halo_rows(rate, rows, own, left, right, k, v):
    at = v * LEV
    lane, level = lanes(LEV), subl(LEV)
    here = rows[at : at + LEV, :]
    corner = COL_COEF + k * PLANES + at
    west = jnp.where(
        lane == 0, pltpu.roll(left[corner : corner + LEV, :], T - 4, 1), pltpu.roll(here, 1, 1)
    )
    east = jnp.where(
        lane == T - 1,
        pltpu.roll(right[corner : corner + LEV, :], T - 6, 1),
        pltpu.roll(here, T - 1, 1),
    )
    outer = rows[PLANES + at : PLANES + at + LEV, :]
    inner = own[at : at + LEV, :]
    h = here + rate[0, v] * ((outer + inner) + (west + east) - 4.0 * here)
    above = jnp.where(level < LEV - 1, pltpu.roll(h, LEV - 1, 0) - h, 0.0)
    below = jnp.where(level > 0, pltpu.roll(h, 1, 0) - h, 0.0)
    return h + rows[ROW_VERT : ROW_VERT + 1, :] * (above + below)


def step_kernel(
    rate, u, coef, sea, own, top, bottom, near, far,
    out, keep, w, stage, inner, top1, bottom1, top2, bottom2, side1, side2, turned, sems,
):
    def emit(v):
        levels = pl.ds(2, LEV - 2)
        return pltpu.make_async_copy(stage.at[v], out.at[0, v, levels], sems.at[v])

    up, down, _, _ = inside()
    side1[...], side2[...] = halo_columns(rate, near, far, own)
    for v in range(NV):
        at = v * LEV
        for l in range(LEV):
            inner[0, at + l : at + l + 1, :] = u[v, l, 0:1, :] * up
            inner[1, at + l : at + l + 1, :] = u[v, l, T - 1 : T, :] * down
    for v in range(NV):
        at = v * LEV
        top1[v] = top[at : at + LEV, :]
        bottom1[v] = bottom[at : at + LEV, :]
        top2[v] = halo_rows(rate, top, inner.at[0], near, far, 0, v)
        bottom2[v] = halo_rows(rate, bottom, inner.at[1], near, far, 1, v)

    def first(v, _):
        number = rate[0, v]
        turned[...] = pltpu.roll(side1[...], lax.rem((NV - v) * 32, T), 1)
        source, result = u.at[v], w.at[v]
        for lo in range(0, T, HALF):
            mix = coef[lo : lo + HALF, :]
            at = lambda l: level_diffuse(source, top1.at[v], bottom1.at[v], turned, number, l, lo)
            before, here = None, at(0)
            for l in range(LEV):
                after = at(l + 1) if l + 1 < LEV else None
                if before is None:
                    term = after - here
                elif after is None:
                    term = before - here
                else:
                    term = (after - here) + (before - here)
                result[l, lo : lo + HALF, :] = here + mix * term
                before, here = here, after
        return 0

    lax.fori_loop(0, NV, first, 0)

    def second(v, _):
        number = rate[0, v]
        turned[...] = pltpu.roll(side2[...], lax.rem((NV - v) * 32, T), 1)
        source, result = w.at[v], stage.at[v]
        for lo in range(0, T, HALF):
            mix = coef[lo : lo + HALF, :]
            at = lambda l: level_diffuse(source, top2.at[v], bottom2.at[v], turned, number, l, lo)
            before, here = at(1), at(2)
            row = pl.multiple_of(v * T + lo, 8)
            keep[pl.ds(KEEP_BASE + row, HALF), :] = source[0, lo : lo + HALF, :]
            keep[pl.ds(KEEP_ONE + row, HALF), :] = before
            keep[pl.ds(KEEP_PART + row, HALF), :] = before + mix * ((here - before) - before)
            for l in range(2, LEV):
                after = at(l + 1) if l + 1 < LEV else None
                term = before - here
                if after is not None:
                    term = (after - here) + term
                result[l - 2, lo : lo + HALF, :] = here + mix * term
                before, here = here, after
        emit(v).start()
        return 0

    lax.fori_loop(0, NV, second, 0)
    keep[KEEP_VERT : KEEP_VERT + T, :] = coef[...]
    keep[KEEP_SEA : KEEP_SEA + T, :] = sea[...]
    keep[KEEP_SIDE : KEEP_SIDE + T, :] = side2[...]
    coefs = pl.ds(COL_COEF, T)
    keep[KEEP_SEA_SIDE : KEEP_SEA_SIDE + T, :] = jnp.where(
        lanes(T) == 0, pltpu.roll(near[coefs, :], T - 2, 1), pltpu.roll(far[coefs, :], T - 4, 1)
    )
    for k, (rows, line) in enumerate(((top2, top), (bottom2, bottom))):
        for v in range(NV):
            keep[KEEP_ENDS + 8 * k + v : KEEP_ENDS + 8 * k + v + 1, :] = rows[v, 0:1, :]
        keep[KEEP_ENDS + 8 * k + NV : KEEP_ENDS + 8 * k + 8, :] = line[ROW_SEA : ROW_SEA + NV, :]
    for v in range(NV):
        emit(v).wait()


def two_steps(rate, u, coef, sea, own, top, bottom, left, right):
    rows = pltpu.VMEM((NV, LEV, T), f32)
    square = pltpu.VMEM((T, T), f32)
    return pl.pallas_call(
        step_kernel,
        in_specs=[SMEM] + [VMEM] * 8,
        out_specs=[HBM, VMEM],
        out_shape=[
            jax.ShapeDtypeStruct((1,) + u.shape, f32),
            jax.ShapeDtypeStruct((KEEP_SIZE, T), f32),
        ],
        scratch_shapes=[
            pltpu.VMEM((NV, LEV, T, T), f32),
            pltpu.VMEM((NV, LEV - 2, T, T), f32),
            pltpu.VMEM((2, PLANES, T), f32),
            rows,
            rows,
            rows,
            rows,
            square,
            square,
            square,
            pltpu.SemaphoreType.DMA((NV,)),
        ],
        compiler_params=params(16 * MIB),
        cost_estimate=cost(48 << 20, 10 << 20),
        name="two_steps",
    )(rate, u, coef, sea, own, top, bottom, left, right)


def unpack_kernel(data, after, imp, first, last, cols):
    del after
    size = SLOTS * NV
    sub = subl(T).astype(f32) + 1.0
    picks = []
    for j in range(NV):
        table = jnp.sum(data[pl.ds(CAP * NV + j, PEERS, stride=size), :], axis=0, keepdims=True)
        picks.append((sub == table).astype(bf16))
    pick = jnp.concatenate(picks, axis=1)
    lane = lanes(T)
    up, down, _, _ = inside()
    acc = jnp.zeros((T, T), f32)
    for v in range(NV):
        block = jnp.concatenate(
            [data[pl.ds(s * size + v, CAP, stride=NV), :] for s in range(PEERS)], axis=0
        )
        high = block.astype(bf16)
        low = (block - high.astype(f32)).astype(bf16)
        total = jnp.dot(pick, high, preferred_element_type=f32)
        total = total + jnp.dot(pick, low, preferred_element_type=f32)
        imp[v] = total
        for out, row, keep in ((first, 0, up), (last, T - 1, down)):
            out[v : v + 1, :] = total[row : row + 1, :] * keep
            out[NV + v : NV + v + 1, :] = total[row : row + 1, :] * keep
        acc = jnp.where((lane >> 1) == v, pltpu.roll(total, 2 * v + 1, 1), acc)
    cols[...] = jnp.transpose(acc * column_keep(T))[0 : 2 * NV, :]


def unpack(data, after):
    return pl.pallas_call(
        unpack_kernel,
        in_specs=[VMEM, HBM],
        out_specs=[VMEM] * 4,
        out_shape=[
            jax.ShapeDtypeStruct((NV, T, T), f32),
            jax.ShapeDtypeStruct((2 * NV, T), f32),
            jax.ShapeDtypeStruct((2 * NV, T), f32),
            jax.ShapeDtypeStruct((2 * NV, T), f32),
        ],
        compiler_params=params(12 * MIB),
        cost_estimate=cost(200 << 20, 2 << 20),
        name="unpack",
    )(data, after)


def final_kernel(
    horiz, relax, mid, near, imp, imp_top, imp_bottom, imp_left, imp_right, out, stage, sems
):
    del mid
    odd = (subl(2 * NV) & 1) == 1
    ends = jnp.where(odd, imp_right[...], imp_left[...])
    ends = jnp.concatenate([ends, jnp.zeros((T - 2 * NV, T), f32)], axis=0)
    side_new = jnp.transpose(ends)
    sea, sea_side = near[KEEP_SEA : KEEP_SEA + T, :], near[KEEP_SEA_SIDE : KEEP_SEA_SIDE + T, :]
    coef = near[KEEP_VERT : KEEP_VERT + T, :]
    side_base = near[KEEP_SIDE : KEEP_SIDE + T, :]
    lane = lanes(T)
    copies = []
    for v in range(NV):
        pull = relax[0, v]

        def relaxed(base, wet, new, pull=pull):
            return base + pull * wet * (new - base)

        ends = []
        for k, new in enumerate((imp_top, imp_bottom)):
            at = KEEP_ENDS + 8 * k
            ends.append(
                relaxed(near[at + v : at + v + 1, :], near[at + NV : at + NV + 1, :], new[v : v + 1, :])
            )
        turn = (T - 32 * v) % T
        base = pltpu.roll(side_base, turn, 1) if turn else side_base
        new = pltpu.roll(side_new, T - 2 * v, 1) if v else side_new
        new = jnp.where(lane == 0, new, pltpu.roll(side_new, T - 2 - 2 * v, 1))
        u = relaxed(near[KEEP_BASE + v * T : KEEP_BASE + (v + 1) * T, :], sea, imp[v])
        h = diffuse(u, ends[0], ends[1], relaxed(base, sea_side, new), horiz[0, v])
        one = near[KEEP_ONE + v * T : KEEP_ONE + (v + 1) * T, :]
        stage[v, 0] = relaxed(h + coef * (one - h), sea, imp[v])
        stage[v, 1] = near[KEEP_PART + v * T : KEEP_PART + (v + 1) * T, :] + coef * h
        copies.append(
            pltpu.make_async_copy(stage.at[v], out.at[0, v, pl.ds(0, 2)], sems.at[v])
        )
        copies[-1].start()
    for copy in copies:
        copy.wait()


def final(horiz, relax, mid, keep, imp, imp_rows, imp_cols):
    return pl.pallas_call(
        final_kernel,
        in_specs=[SMEM, SMEM, HBM] + [VMEM] * 6,
        out_specs=HBM,
        out_shape=jax.ShapeDtypeStruct(mid.shape, f32),
        input_output_aliases={2: 0},
        scratch_shapes=[
            pltpu.VMEM((NV, 2, T, T), f32),
            pltpu.SemaphoreType.DMA((NV,)),
        ],
        compiler_params=params(6 * MIB),
        cost_estimate=cost(2 << 20, 3 << 20),
        name="final",
    )(horiz, relax, mid, keep, imp, *imp_rows, *imp_cols)


def shifted(block, axis, by, across=False):
    count = lax.axis_size(axis)
    if not across:
        return lax.ppermute(block, axis, [(i, (i + by) % count) for i in range(count)])
    return lax.ppermute(
        block,
        ("comp", axis),
        [
            (c * count + i, (1 - c) * count + (i + by) % count)
            for c in range(2)
            for i in range(count)
        ],
    )


def local(
    state, horiz_coef, vert_coef, couple_rate, sea_mask, dest_block, entry_count, remap_weight
):
    head, tail = outer_rows(state, vert_coef, sea_mask)
    top, bottom = shifted(tail, "gx", 1), shifted(head, "gx", -1)
    cols, surf, tile, coef, sea = outer_columns(state, vert_coef, sea_mask)
    cols = with_corners(cols, top, bottom)
    left, right = shifted(cols, "gy", 1), shifted(cols, "gy", -1)
    dest = dest_block.reshape(T, FAN).T
    packed = remap(dest, entry_count.reshape(1, T), surf, remap_weight, cols)
    packed = sealed(packed, left, right).reshape(PEERS, SLOTS, NV, T)
    packed = lax.all_to_all(packed, ("gx", "gy"), split_axis=0, concat_axis=0, tiled=True)
    mid, keep = two_steps(horiz_coef, tile, coef, sea, cols, top, bottom, left, right)
    imp, first, last, cols = unpack(packed.reshape(PEERS * SLOTS * NV, T), keep)
    imp = lax.ppermute(imp, "comp", [(0, 1), (1, 0)])
    imp_rows = shifted(last, "gx", 1, True), shifted(first, "gx", -1, True)
    imp_cols = shifted(cols, "gy", 1, True), shifted(cols, "gy", -1, True)
    return final(horiz_coef, couple_rate, mid, keep, imp, imp_rows, imp_cols)


def solution(mesh):
    in_specs = (
        P("comp", None, None, "gx", "gy"),
        P("comp", None),
        P("comp", "gx", "gy"),
        P("comp", None),
        P("comp", "gx", "gy"),
        P("comp", "gx", "gy", None),
        P("comp", "gx", "gy"),
        P("comp", "gx", "gy", None, None, None),
    )
    out_specs = P("comp", None, None, "gx", "gy")
    return jax.shard_map(local, mesh=mesh, in_specs=in_specs, out_specs=out_specs, check_vma=False)
```

time: 218 us -> 70.1 us (0.32)
  the two profiles are of different devices: /device:TPU:1 before, /device:TPU:0 now
where the time goes in v2:
time: 70.1 us; the launch traced here: 69.8 us
  starting transfers between devices  28.3 us (40%)
  Pallas kernels  24.8 us (35%)
  waiting for transfers between devices  10 us (14%)
  local copies, waits for them, and re-layouts  6.48 us (9%)
    ppermute x4, starting transfers between devices, shifted(): lax.ppermute(block, ('comp', axis), [(c * count + i, (1 - c) * count + (i...  9.79 us
    pallas_call x1, Pallas kernels, two_steps(): pl.pallas_call(step_kernel, in_specs=[SMEM] + [VMEM] * 8, out_specs=[HBM,...  8.96 us
    all_to_all x1, starting transfers between devices, local(): lax.all_to_all(packed, ('gx', 'gy'), split_axis=0, concat_axis=0, tiled=T...  8.13 us
    pallas_call x1, Pallas kernels, remap(): pl.pallas_call(remap_kernel, in_specs=[HBM, HBM, VMEM, HBM, HBM], out_spe...  7.73 us
    ppermute x4, starting transfers between devices, shifted(): lax.ppermute(block, axis, [(i, (i + by) % count) for i in range(count)])  7.62 us
    unnamed x26, local copies, waits for them, and re-layouts  6.48 us
    all_to_all x1, waiting for transfers between devices, local(): lax.all_to_all(packed, ('gx', 'gy'), split_axis=0, concat_axis=0, tiled=T...  5.74 us
    ppermute x4, waiting for transfers between devices, shifted(): lax.ppermute(block, ('comp', axis), [(c * count + i, (1 - c) * count + (i...  4.26 us
  transfers between devices with their start and end apart: 10, of which 3 were waited for; matrix products, arithmetic and copies ran while one was open for 0% of the time, Pallas kernels for 29%

profile of v2, /device:TPU:0, one launch (start us, length us, event | category | flops | bytes accessed | tf_op | source)
XLA Modules:
  0.0 69.8 jit_solution(9958588955951019055)
XLA Ops:
  0.0 1.9 %outer_rows.1 = (f32[144,128]{1,0:T(8,128)}, f32[144,128]{1,0:T(8,128)}) custom-call(f32[1,4,16,128,128]{4,3,2,1,0:T(8,128)} %state.3, f32[1,128,128]{2,1,0:T(8,128)} %vert.3, s32[1,128,128]{2,1,0:T(8,128)} %mask.3), custom_call_target="tpu_custom_call" | custom-call | flops 65536 | bytes 524288 | tf_op jit(solution)/shard_map/outer_rows/pallas_call | solution.py:108
  2.0 3.6 %collective-permute-start.1 = (f32[144,128]{1,0:T(8,128)}, f32[144,128]{1,0:T(8,128)S(1)}, u32[]{:S(2)}, u32[]{:S(2)}) collective-permute-start(f32[144,128]{1,0:T(8,128)} %get-tuple-element.23), channel_id=1, source_target_pairs={{0,56},{8,0},{16,8},{24,16},{32,24},{40,32},{48,40},{56,48},{1,57}... | collective-permute-start | bytes 221192 | tf_op jit(solution)/shard_map/ppermute | solution.py:606
  5.5 3.9 %outer_columns.1 = (f32[384,128]{1,0:T(8,128)S(1)}, f32[512,128]{1,0:T(8,128)S(1)}, f32[4,16,128,128]{3,2,1,0:T(8,128)S(1)}, f32[128,128]{1,0:T(8,128)S(1)}, f32[128,128]{1,0:T(8,128)S(1)}) custom-call(f32[1,4,16,128,128]{4,3,2,1,0:T(8,128)} %state.3, f32[1,128,128]{2,1,0:T(8,128)S(1)} %copy-done.7, s32[1,128,128]{2,1,0:T(8,128)S(1)} %copy-done.8), custom_call_target="tpu_custom_call" | custom-call | flops 6291456 | bytes 9437184 | tf_op jit(solution)/shard_map/outer_columns/pallas_call | solution.py:160
  9.5 0.1 with_corners.1.own.after
  9.6 4.0 %collective-permute-start.3 = (f32[400,128]{1,0:T(8,128)S(1)}, f32[400,128]{1,0:T(8,128)S(1)}, u32[]{:S(2)}, u32[]{:S(2)}) collective-permute-start(f32[400,128]{1,0:T(8,128)S(1)} %with_corners.1.own.after), channel_id=1, source_target_pairs={{0,7},{1,0},{2,1},{3,2},{4,3},{5,4},{6,5},{7,6},{8,15},{9,8},{10,9... | collective-permute-start | bytes 614408 | tf_op jit(solution)/shard_map/ppermute | solution.py:606
  13.6 7.7 %remap.1.refs_0_ = f32[576,4,128]{2,1,0:T(4,128)S(1)} custom-call(s32[4,128]{1,0:T(4,128)S(1)} %bitcast.8, s32[1,128]{1,0:T(1,128)S(1)} %bitcast.9, f32[512,128]{1,0:T(8,128)S(1)} %get-tuple-element.26.surf, bf16[1,128,1,4,128,128]{5,4,3,2,1,0:T(8,128)(2,1)} %weight.1, f32[400,128]{1,0:T(8,128)S(1)} %with_corners.1.own.after), custom_call_target="tpu_custom_call" | custom-call | flops 70254592 | bytes 20971520 | tf_op jit(solution)/shard_map/remap/pallas_call | solution.py:286
  21.4 1.0 %copy-done = f32[576,4,128]{2,1,0:T(4,128)} copy-done((f32[576,4,128]{2,1,0:T(4,128)}, f32[576,4,128]{2,1,0:T(4,128)S(1)}, u32[]{:S(2)}) %copy-start) | copy-done | bytes 1179672
  22.4 0.7 copy-done.3
  23.1 0.7 copy-done.5
  23.8 8.1 %all-to-all-start = ((f32[64,9,4,128]{3,2,1,0:T(4,128)}), f32[64,9,4,128]{3,2,1,0:T(4,128)S(1)}, u32[]{:S(2)}, u32[]{:S(2)}) async-start(f32[64,9,4,128]{3,2,1,0:T(4,128)} %bitcast.6), calls=%async_computation | async-start | bytes 2359296 | tf_op jit(solution)/shard_map/all_to_all | solution.py:629
  32.0 2.2 %copy-done.2 = f32[4,16,128,128]{3,2,1,0:T(8,128)S(1)} copy-done((f32[4,16,128,128]{3,2,1,0:T(8,128)S(1)}, f32[4,16,128,128]{3,2,1,0:T(8,128)}, u32[]{:S(2)}) %copy-start.2) | copy-done | bytes 4194328
  34.1 0.9 %copy-done.4 = f32[400,128]{1,0:T(8,128)S(1)} copy-done((f32[400,128]{1,0:T(8,128)S(1)}, f32[400,128]{1,0:T(8,128)}, u32[]{:S(2)}) %copy-start.4) | copy-done | bytes 204824
  35.1 0.9 %copy-done.6 = f32[400,128]{1,0:T(8,128)S(1)} copy-done((f32[400,128]{1,0:T(8,128)S(1)}, f32[400,128]{1,0:T(8,128)}, u32[]{:S(2)}) %copy-start.6) | copy-done | bytes 204824
  36.0 9.0 %two_steps.1 = (f32[1,4,16,128,128]{4,3,2,1,0:T(8,128)}, f32[2064,128]{1,0:T(8,128)S(1)}) custom-call(f32[1,4]{1,0:T(1,128)S(1)} %copy-done.9, f32[4,16,128,128]{3,2,1,0:T(8,128)S(1)} %copy-done.2, f32[128,128]{1,0:T(8,128)S(1)} %get-tuple-element.19.coef, f32[128,128]{1,0:T(8,128)S(1)} %get-tuple-element.20.sea, f32[400,128]{1,0:T(8,128)S(1)} %with_corners.1.own.after, ...), custom_call_target="tpu_custom_call" | custom-call | flops 50331648 | bytes 10485760 | tf_op jit(solution)/shard_map/two_steps/pallas_call | solution.py:472
  45.0 5.7 %all-to-all-done = f32[64,9,4,128]{3,2,1,0:T(4,128)S(1)} async-done(((f32[64,9,4,128]{3,2,1,0:T(4,128)}), f32[64,9,4,128]{3,2,1,0:T(4,128)S(1)}, u32[]{:S(2)}, u32[]{:S(2)}) %all-to-all-start) | async-done | bytes 1179680 | tf_op jit(solution)/shard_map/all_to_all | solution.py:629
  50.7 0.6 unpack.1
  51.3 2.8 %collective-permute-start.4 = (f32[4,128,128]{2,1,0:T(8,128)S(1)}, f32[4,128,128]{2,1,0:T(8,128)S(1)}, u32[]{:S(2)}, u32[]{:S(2)}) collective-permute-start(f32[4,128,128]{2,1,0:T(8,128)S(1)} %get-tuple-element.27), channel_id=1, source_target_pairs={{0,64},{64,0},{1,65},{65,1},{2,66},{66,2},{3,67},{67,3},{4,68},{68... | collective-permute-start | bytes 786440 | tf_op jit(solution)/shard_map/ppermute | solution.py:632
  54.1 0.7 collective-permute-start.5
  54.7 4.7 %collective-permute-start.6 = (f32[8,128]{1,0:T(8,128)S(1)}, f32[8,128]{1,0:T(8,128)S(1)}, u32[]{:S(2)}, u32[]{:S(2)}) collective-permute-start(f32[8,128]{1,0:T(8,128)S(1)} %get-tuple-element.29), channel_id=1, source_target_pairs={{0,120},{8,64},{16,72},{24,80},{32,88},{40,96},{48,104},{56,112},{... | collective-permute-start | bytes 12296 | tf_op jit(solution)/shard_map/ppermute | solution.py:607
  59.4 1.8 %collective-permute-start.8 = (f32[8,128]{1,0:T(8,128)S(1)}, f32[8,128]{1,0:T(8,128)S(1)}, u32[]{:S(2)}, u32[]{:S(2)}) collective-permute-start(f32[8,128]{1,0:T(8,128)S(1)} %get-tuple-element.30), channel_id=1, source_target_pairs={{0,71},{1,64},{2,65},{3,66},{4,67},{5,68},{6,69},{7,70},{64,7},{65... | collective-permute-start | bytes 12296 | tf_op jit(solution)/shard_map/ppermute | solution.py:607
  61.2 2.7 %collective-permute-start.7 = (f32[8,128]{1,0:T(8,128)S(1)}, f32[8,128]{1,0:T(8,128)S(1)}, u32[]{:S(2)}, u32[]{:S(2)}) collective-permute-start(f32[8,128]{1,0:T(8,128)S(1)} %get-tuple-element.30), channel_id=1, source_target_pairs={{0,65},{1,66},{2,67},{3,68},{4,69},{5,70},{6,71},{7,64},{64,1},{65... | collective-permute-start | bytes 12296 | tf_op jit(solution)/shard_map/ppermute | solution.py:607
  63.9 1.6 %collective-permute-done.8.imp_right = f32[8,128]{1,0:T(8,128)S(1)} collective-permute-done((f32[8,128]{1,0:T(8,128)S(1)}, f32[8,128]{1,0:T(8,128)S(1)}, u32[]{:S(2)}, u32[]{:S(2)}) %collective-permute-start.8) | collective-permute-done | bytes 4128 | tf_op jit(solution)/shard_map/ppermute | solution.py:607
  65.4 2.7 %collective-permute-done.7.imp_left = f32[8,128]{1,0:T(8,128)S(1)} collective-permute-done((f32[8,128]{1,0:T(8,128)S(1)}, f32[8,128]{1,0:T(8,128)S(1)}, u32[]{:S(2)}, u32[]{:S(2)}) %collective-permute-start.7) | collective-permute-done | bytes 4128 | tf_op jit(solution)/shard_map/ppermute | solution.py:607
  68.1 1.7 %final.1 = f32[1,4,16,128,128]{4,3,2,1,0:T(8,128)} custom-call(f32[1,4]{1,0:T(1,128)S(1)} %copy-done.9, f32[1,4]{1,0:T(1,128)S(1)} %copy-done.12, f32[1,4,16,128,128]{4,3,2,1,0:T(8,128)} %get-tuple-element.24.mid, f32[2064,128]{1,0:T(8,128)S(1)} %get-tuple-element.25.after.near, ...), custom_call_target="tpu_custom_call", output_to_operand_aliasing={{}: (2, {})} | custom-call | flops 2097152 | bytes 3145728 | tf_op jit(solution)/shard_map/final/pallas_call | solution.py:587
  (30 shorter events, 0.1 us)
Async XLA Ops:
  0.0 5.5 %copy-start.8 = (s32[1,128,128]{2,1,0:T(8,128)S(1)}, s32[1,128,128]{2,1,0:T(8,128)}, u32[]{:S(2)}) copy-start(s32[1,128,128]{2,1,0:T(8,128)} %mask.3) | copy-start | bytes 196612
  0.0 5.5 %copy-start.7 = (f32[1,128,128]{2,1,0:T(8,128)S(1)}, f32[1,128,128]{2,1,0:T(8,128)}, u32[]{:S(2)}) copy-start(f32[1,128,128]{2,1,0:T(8,128)} %vert.3) | copy-start | bytes 196612
  0.0 13.6 %copy-start.11 = (s32[1,128,1]{1,2,0:T(1,128)S(1)}, s32[1,128,1]{1,2,0:T(1,128)}, u32[]{:S(2)}) copy-start(s32[1,128,1]{1,2,0:T(1,128)} %param.14) | copy-start | bytes 1540
  0.0 13.6 %copy-start.10 = (s32[1,128,1,4]{1,3,2,0:T(4,128)S(1)}, s32[1,128,1,4]{1,3,2,0:T(4,128)}, u32[]{:S(2)}) copy-start(s32[1,128,1,4]{1,3,2,0:T(4,128)} %param.13) | copy-start | bytes 6148
  1.9 7.5 %collective-permute-start = (f32[144,128]{1,0:T(8,128)}, f32[144,128]{1,0:T(8,128)S(1)}, u32[]{:S(2)}, u32[]{:S(2)}) collective-permute-start(f32[144,128]{1,0:T(8,128)} %get-tuple-element.22), channel_id=1, source_target_pairs={{0,8},{8,16},{16,24},{24,32},{32,40},{40,48},{48,56},{56,0},{1,9},... | collective-permute-start | bytes 221192 | tf_op jit(solution)/shard_map/ppermute | solution.py:606
  2.0 7.5 %collective-permute-start.1 = (f32[144,128]{1,0:T(8,128)}, f32[144,128]{1,0:T(8,128)S(1)}, u32[]{:S(2)}, u32[]{:S(2)}) collective-permute-start(f32[144,128]{1,0:T(8,128)} %get-tuple-element.23), channel_id=1, source_target_pairs={{0,56},{8,0},{16,8},{24,16},{32,24},{40,32},{48,40},{56,48},{1,57}... | collective-permute-start | bytes 221192 | tf_op jit(solution)/shard_map/ppermute | solution.py:606
  9.4 11.9 %copy-start.1 = (f32[4,16,128,128]{3,2,1,0:T(8,128)}, f32[4,16,128,128]{3,2,1,0:T(8,128)S(1)}, u32[]{:S(2)}) copy-start(f32[4,16,128,128]{3,2,1,0:T(8,128)S(1)} %get-tuple-element.18.u) | copy-start | bytes 12582916
  9.6 12.8 %collective-permute-start.3 = (f32[400,128]{1,0:T(8,128)S(1)}, f32[400,128]{1,0:T(8,128)S(1)}, u32[]{:S(2)}, u32[]{:S(2)}) collective-permute-start(f32[400,128]{1,0:T(8,128)S(1)} %with_corners.1.own.after), channel_id=1, source_target_pairs={{0,7},{1,0},{2,1},{3,2},{4,3},{5,4},{6,5},{7,6},{8,15},{9,8},{10,9... | collective-permute-start | bytes 614408 | tf_op jit(solution)/shard_map/ppermute | solution.py:606
  13.6 8.8 %collective-permute-start.2 = (f32[400,128]{1,0:T(8,128)S(1)}, f32[400,128]{1,0:T(8,128)S(1)}, u32[]{:S(2)}, u32[]{:S(2)}) collective-permute-start(f32[400,128]{1,0:T(8,128)S(1)} %with_corners.1.own.after), channel_id=1, source_target_pairs={{0,1},{1,2},{2,3},{3,4},{4,5},{5,6},{6,7},{7,0},{8,9},{9,10},{10,1... | collective-permute-start | bytes 614408 | tf_op jit(solution)/shard_map/ppermute | solution.py:606
  21.4 1.0 %copy-start = (f32[576,4,128]{2,1,0:T(4,128)}, f32[576,4,128]{2,1,0:T(4,128)S(1)}, u32[]{:S(2)}) copy-start(f32[576,4,128]{2,1,0:T(4,128)S(1)} %remap.1.refs_0_) | copy-start | bytes 3538948
  22.4 9.5 %copy-start.9 = (f32[1,4]{1,0:T(1,128)S(1)}, f32[1,4]{1,0:T(1,128)}, u32[]{:S(2)}) copy-start(f32[1,4]{1,0:T(1,128)} %horiz.1) | copy-start | bytes 52
  22.4 0.7 copy-start.3
  23.1 0.7 copy-start.5
  23.8 26.9 %all-to-all-start = ((f32[64,9,4,128]{3,2,1,0:T(4,128)}), f32[64,9,4,128]{3,2,1,0:T(4,128)S(1)}, u32[]{:S(2)}, u32[]{:S(2)}) async-start(f32[64,9,4,128]{3,2,1,0:T(4,128)} %bitcast.6), calls=%async_computation | async-start | bytes 2359296 | tf_op jit(solution)/shard_map/all_to_all | solution.py:629
  31.9 36.2 %copy-start.12 = (f32[1,4]{1,0:T(1,128)S(1)}, f32[1,4]{1,0:T(1,128)}, u32[]{:S(2)}) copy-start(f32[1,4]{1,0:T(1,128)} %relax.1) | copy-start | bytes 52
  32.0 2.2 %copy-start.2 = (f32[4,16,128,128]{3,2,1,0:T(8,128)S(1)}, f32[4,16,128,128]{3,2,1,0:T(8,128)}, u32[]{:S(2)}) copy-start(f32[4,16,128,128]{3,2,1,0:T(8,128)} %copy-done.1) | copy-start | bytes 12582916
  34.1 0.9 %copy-start.4 = (f32[400,128]{1,0:T(8,128)S(1)}, f32[400,128]{1,0:T(8,128)}, u32[]{:S(2)}) copy-start(f32[400,128]{1,0:T(8,128)} %copy-done.3) | copy-start | bytes 614404
  35.1 0.9 %copy-start.6 = (f32[400,128]{1,0:T(8,128)S(1)}, f32[400,128]{1,0:T(8,128)}, u32[]{:S(2)}) copy-start(f32[400,128]{1,0:T(8,128)} %copy-done.5) | copy-start | bytes 614404
  51.3 16.8 %collective-permute-start.4 = (f32[4,128,128]{2,1,0:T(8,128)S(1)}, f32[4,128,128]{2,1,0:T(8,128)S(1)}, u32[]{:S(2)}, u32[]{:S(2)}) collective-permute-start(f32[4,128,128]{2,1,0:T(8,128)S(1)} %get-tuple-element.27), channel_id=1, source_target_pairs={{0,64},{64,0},{1,65},{65,1},{2,66},{66,2},{3,67},{67,3},{4,68},{68... | collective-permute-start | bytes 786440 | tf_op jit(solution)/shard_map/ppermute | solution.py:632
  54.1 9.8 %collective-permute-start.5 = (f32[8,128]{1,0:T(8,128)S(1)}, f32[8,128]{1,0:T(8,128)S(1)}, u32[]{:S(2)}, u32[]{:S(2)}) collective-permute-start(f32[8,128]{1,0:T(8,128)S(1)} %get-tuple-element.28), channel_id=1, source_target_pairs={{0,72},{8,80},{16,88},{24,96},{32,104},{40,112},{48,120},{56,64},{... | collective-permute-start | bytes 12296 | tf_op jit(solution)/shard_map/ppermute | solution.py:607
  54.7 9.1 %collective-permute-start.6 = (f32[8,128]{1,0:T(8,128)S(1)}, f32[8,128]{1,0:T(8,128)S(1)}, u32[]{:S(2)}, u32[]{:S(2)}) collective-permute-start(f32[8,128]{1,0:T(8,128)S(1)} %get-tuple-element.29), channel_id=1, source_target_pairs={{0,120},{8,64},{16,72},{24,80},{32,88},{40,96},{48,104},{56,112},{... | collective-permute-start | bytes 12296 | tf_op jit(solution)/shard_map/ppermute | solution.py:607
  59.4 6.0 %collective-permute-start.8 = (f32[8,128]{1,0:T(8,128)S(1)}, f32[8,128]{1,0:T(8,128)S(1)}, u32[]{:S(2)}, u32[]{:S(2)}) collective-permute-start(f32[8,128]{1,0:T(8,128)S(1)} %get-tuple-element.30), channel_id=1, source_target_pairs={{0,71},{1,64},{2,65},{3,66},{4,67},{5,68},{6,69},{7,70},{64,7},{65... | collective-permute-start | bytes 12296 | tf_op jit(solution)/shard_map/ppermute | solution.py:607
  61.2 6.9 %collective-permute-start.7 = (f32[8,128]{1,0:T(8,128)S(1)}, f32[8,128]{1,0:T(8,128)S(1)}, u32[]{:S(2)}, u32[]{:S(2)}) collective-permute-start(f32[8,128]{1,0:T(8,128)S(1)} %get-tuple-element.30), channel_id=1, source_target_pairs={{0,65},{1,66},{2,67},{3,68},{4,69},{5,70},{6,71},{7,64},{64,1},{65... | collective-permute-start | bytes 12296 | tf_op jit(solution)/shard_map/ppermute | solution.py:607

commit v3 on v2

--- a/solution.py
+++ b/solution.py
@@ -16,7 +16,6 @@
 HALF = 64
 CHUNKS = 16
 MIB = 1024 * 1024
-LIMIT = 58 * MIB
 ROW_VERT = 2 * PLANES
 ROW_SEA = ROW_VERT + 8
 ROW_SIZE = ROW_SEA + 8
@@ -44,7 +43,7 @@
 HBM = pl.BlockSpec(memory_space=pl.ANY)
 
 
-def params(limit=LIMIT):
+def params(limit):
     return pltpu.CompilerParams(vmem_limit_bytes=limit)
 
 
@@ -83,7 +82,8 @@
         copy.wait()
 
 
-def row_kernel(state, vert, mask, head, tail, high, low, coef, sea, sems):
+def row_kernel(state, vert, mask, after, head, tail, high, low, coef, sea, sems):
+    del after
     ends = pl.ds(0, 8), pl.ds(T - 8, 8)
     copies = []
     for k, buffer in enumerate((high, low)):
@@ -104,10 +104,10 @@
         out[ROW_SEA : ROW_SEA + 8, :] = jnp.broadcast_to(line, (8, T))
 
 
-def outer_rows(state, vert, mask):
+def outer_rows(state, vert, mask, after):
     return pl.pallas_call(
         row_kernel,
-        in_specs=[HBM, HBM, HBM],
+        in_specs=[HBM] * 4,
         out_specs=[VMEM, VMEM],
         out_shape=[jax.ShapeDtypeStruct((ROW_SIZE, T), f32)] * 2,
         scratch_shapes=[
@@ -117,13 +117,14 @@
             pltpu.VMEM((2, 8, T), i32),
             pltpu.SemaphoreType.DMA((6,)),
         ],
-        compiler_params=params(),
+        compiler_params=params(51 * MIB),
         cost_estimate=cost(1 << 16, 1 << 19),
         name="outer_rows",
-    )(state, vert, mask)
-
-
-def column_kernel(state, vert, mask, cols, surf, tile, coef, wet, sea, sems):
+    )(state, vert, mask, after)
+
+
+def column_kernel(state, vert, mask, after, cols, tile, coef, wet, sea, sems):
+    del after
     loads = [pltpu.make_async_copy(state.at[0, v], tile.at[v], sems.at[v]) for v in range(NV)]
     loads.append(pltpu.make_async_copy(vert.at[0], coef, sems.at[NV]))
     loads.append(pltpu.make_async_copy(mask.at[0], sea, sems.at[NV + 1]))
@@ -133,7 +134,6 @@
     keep = column_keep(HALF)
     for v in range(NV):
         loads[v].wait()
-        surf[pl.ds(v, T, stride=NV), :] = tile[v, 0]
         for lo in range(0, T, HALF):
             outer, following = pl.ds(lo, HALF), pl.ds(COL_NEXT + lo, HALF)
             acc = jnp.zeros((HALF, T), f32) if v == 0 else cols[outer, :]
@@ -155,24 +155,23 @@
     cols[COL_COEF : COL_COEF + T, :] = pair * column_keep(T)
 
 
-def outer_columns(state, vert, mask):
+def outer_columns(state, vert, mask, after):
     square = jax.ShapeDtypeStruct((T, T), f32)
     return pl.pallas_call(
         column_kernel,
-        in_specs=[HBM, HBM, HBM],
-        out_specs=[VMEM] * 5,
+        in_specs=[HBM] * 4,
+        out_specs=[VMEM] * 4,
         out_shape=[
             jax.ShapeDtypeStruct((COL_TOP, T), f32),
-            jax.ShapeDtypeStruct((T * NV, T), f32),
             jax.ShapeDtypeStruct((NV, LEV, T, T), f32),
             square,
             square,
         ],
         scratch_shapes=[pltpu.VMEM((T, T), i32), pltpu.SemaphoreType.DMA((NV + 2,))],
-        compiler_params=params(47 * MIB),
+        compiler_params=params(46 * MIB),
         cost_estimate=cost(6 << 20, 9 << 20),
         name="outer_columns",
-    )(state, vert, mask)
+    )(state, vert, mask, after)
 
 
 def corner_kernel(cols, top, bottom, out):
@@ -205,13 +204,16 @@
     )(cols, top, bottom)
 
 
-def remap_kernel(dest_in, count_in, surf, weight, after, out, blocks, dest, count, used, label, sems):
-    del after
+def remap_kernel(
+    dest_in, count_in, state, weight, out, blocks, planes, surf, dest, count, used, label, sems
+):
     rows = T // CHUNKS
     lists = [
         pltpu.make_async_copy(dest_in, dest, sems.at[CHUNKS]),
         pltpu.make_async_copy(count_in, count, sems.at[CHUNKS + 1]),
     ]
+    for v in range(NV):
+        lists.append(pltpu.make_async_copy(state.at[0, v, 0], planes.at[v], sems.at[CHUNKS + 2 + v]))
     for copy in lists:
         copy.start()
 
@@ -232,6 +234,8 @@
     lax.fori_loop(0, PEERS, clear, 0)
     for copy in lists:
         copy.wait()
+    for v in range(NV):
+        surf[pl.ds(v, T, stride=NV), :] = planes[v]
     sub = subl(8)
 
     def slot_of(row, f):
@@ -282,38 +286,26 @@
     lax.fori_loop(0, PEERS, write, 0)
 
 
-def remap(dest, count, surf, weight, after):
+def remap(dest, count, state, weight):
     return pl.pallas_call(
         remap_kernel,
-        in_specs=[HBM, HBM, VMEM, HBM, HBM],
+        in_specs=[HBM] * 4,
         out_specs=VMEM,
         out_shape=jax.ShapeDtypeStruct((PEERS * SLOTS, NV, T), f32),
         scratch_shapes=[
             pltpu.VMEM((T, FAN, T, T), bf16),
+            pltpu.VMEM((NV, T, T), f32),
+            pltpu.VMEM((T * NV, T), f32),
             pltpu.SMEM((FAN, T), i32),
             pltpu.SMEM((1, T), i32),
             pltpu.SMEM((PEERS,), i32),
             pltpu.SMEM((PEERS * CAP + 8,), i32),
-            pltpu.SemaphoreType.DMA((CHUNKS + 2,)),
-        ],
-        compiler_params=params(44 * MIB),
+            pltpu.SemaphoreType.DMA((CHUNKS + 2 + NV,)),
+        ],
+        compiler_params=params(51 * MIB),
         cost_estimate=cost(67 << 20, 20 << 20),
         name="remap",
-    )(dest, count, surf, weight, after)
-
-
-def sealed(block, *after):
-    def kernel(*refs):
-        del refs
-
-    return pl.pallas_call(
-        kernel,
-        in_specs=[HBM] * (1 + len(after)),
-        out_specs=HBM,
-        out_shape=jax.ShapeDtypeStruct(block.shape, block.dtype),
-        input_output_aliases={0: 0},
-        name="sealed",
-    )(block, *after)
+    )(dest, count, state, weight)
 
 
 def merged(left, right, back=2):
@@ -385,9 +377,11 @@
 
 
 def step_kernel(
-    rate, u, coef, sea, own, top, bottom, near, far,
+    rate, u, coef, sea, own, top, bottom, near, far, after,
     out, keep, w, stage, inner, top1, bottom1, top2, bottom2, side1, side2, turned, sems,
 ):
+    del after
+
     def emit(v):
         levels = pl.ds(2, LEV - 2)
         return pltpu.make_async_copy(stage.at[v], out.at[0, v, levels], sems.at[v])
@@ -466,12 +460,12 @@
         emit(v).wait()
 
 
-def two_steps(rate, u, coef, sea, own, top, bottom, left, right):
+def two_steps(rate, u, coef, sea, own, top, bottom, left, right, after):
     rows = pltpu.VMEM((NV, LEV, T), f32)
     square = pltpu.VMEM((T, T), f32)
     return pl.pallas_call(
         step_kernel,
-        in_specs=[SMEM] + [VMEM] * 8,
+        in_specs=[SMEM] + [VMEM] * 8 + [HBM],
         out_specs=[HBM, VMEM],
         out_shape=[
             jax.ShapeDtypeStruct((1,) + u.shape, f32),
@@ -493,7 +487,7 @@
         compiler_params=params(16 * MIB),
         cost_estimate=cost(48 << 20, 10 << 20),
         name="two_steps",
-    )(rate, u, coef, sea, own, top, bottom, left, right)
+    )(rate, u, coef, sea, own, top, bottom, left, right, after)
 
 
 def unpack_kernel(data, after, imp, first, last, cols):
@@ -618,20 +612,21 @@
 def local(
     state, horiz_coef, vert_coef, couple_rate, sea_mask, dest_block, entry_count, remap_weight
 ):
-    head, tail = outer_rows(state, vert_coef, sea_mask)
+    dest = dest_block.reshape(T, FAN).T
+    sent = remap(dest, entry_count.reshape(1, T), state, remap_weight)
+    packed = lax.all_to_all(
+        sent.reshape(PEERS, SLOTS, NV, T), ("gx", "gy"), split_axis=0, concat_axis=0, tiled=True
+    )
+    head, tail = outer_rows(state, vert_coef, sea_mask, sent)
     top, bottom = shifted(tail, "gx", 1), shifted(head, "gx", -1)
-    cols, surf, tile, coef, sea = outer_columns(state, vert_coef, sea_mask)
+    cols, tile, coef, sea = outer_columns(state, vert_coef, sea_mask, head)
     cols = with_corners(cols, top, bottom)
     left, right = shifted(cols, "gy", 1), shifted(cols, "gy", -1)
-    dest = dest_block.reshape(T, FAN).T
-    packed = remap(dest, entry_count.reshape(1, T), surf, remap_weight, cols)
-    packed = sealed(packed, left, right).reshape(PEERS, SLOTS, NV, T)
-    packed = lax.all_to_all(packed, ("gx", "gy"), split_axis=0, concat_axis=0, tiled=True)
-    mid, keep = two_steps(horiz_coef, tile, coef, sea, cols, top, bottom, left, right)
-    imp, first, last, cols = unpack(packed.reshape(PEERS * SLOTS * NV, T), keep)
-    imp = lax.ppermute(imp, "comp", [(0, 1), (1, 0)])
+    new, first, last, sides = unpack(packed.reshape(PEERS * SLOTS * NV, T), cols)
+    imp = lax.ppermute(new, "comp", [(0, 1), (1, 0)])
     imp_rows = shifted(last, "gx", 1, True), shifted(first, "gx", -1, True)
-    imp_cols = shifted(cols, "gy", 1, True), shifted(cols, "gy", -1, True)
+    imp_cols = shifted(sides, "gy", 1, True), shifted(sides, "gy", -1, True)
+    mid, keep = two_steps(horiz_coef, tile, coef, sea, cols, top, bottom, left, right, new)
     return final(horiz_coef, couple_rate, mid, keep, imp, imp_rows, imp_cols)
 
 

time: 70.1 us -> 72.4 us (1.033)
  starting transfers between devices: 28.3 us -> 30.4 us
  local copies, waits for them, and re-layouts: 6.48 us -> 5.55 us
    ppermute x4, waiting for transfers between devices: 0.01 us -> 9.51 us  [shifted(): lax.ppermute(block, axis, [(i, (i + by) % count) for i in range(count)])]
    all_to_all x1, waiting for transfers between devices: 5.74 us -> 1.05 us  [local(): lax.all_to_all(sent.reshape(PEERS, SLOTS, NV, T), ('gx', 'gy'), split_axi...]
    ppermute x4, waiting for transfers between devices: 4.26 us -> 0.01 us  [shifted(): lax.ppermute(block, ('comp', axis), [(c * count + i, (1 - c) * count + (i...]
    all_to_all x1, starting transfers between devices: 8.13 us -> 9.98 us  [local(): lax.all_to_all(sent.reshape(PEERS, SLOTS, NV, T), ('gx', 'gy'), split_axi...]
    unnamed x26 -> x16, local copies, waits for them, and re-layouts: 6.48 us -> 5.55 us
    ppermute x4, starting transfers between devices: 9.79 us -> 10.7 us  [shifted(): lax.ppermute(block, ('comp', axis), [(c * count + i, (1 - c) * count + (i...]
    pallas_call x5 -> x4, Pallas kernels: 22.5 us -> 23.1 us  [the longest x1 9.02 us: two_steps(): pl.pallas_call(step_kernel, in_specs=[SMEM] + [VMEM] * 8 + [HBM], out_spe...]
  transfers between devices with their start and end apart: 10 -> 10, of which waited for: 3 -> 3; matrix products, arithmetic and copies ran while one was open for 0% -> 0% of each run, Pallas kernels for 29% -> 20%
where the time goes in v3:
time: 72.4 us; the launch traced here: 72.1 us
  starting transfers between devices  30.4 us (42%)
  Pallas kernels  25.5 us (35%)
  waiting for transfers between devices  10.6 us (15%)
  local copies, waits for them, and re-layouts  5.55 us (8%)
    ppermute x4, starting transfers between devices, shifted(): lax.ppermute(block, ('comp', axis), [(c * count + i, (1 - c) * count + (i...  10.7 us
    all_to_all x1, starting transfers between devices, local(): lax.all_to_all(sent.reshape(PEERS, SLOTS, NV, T), ('gx', 'gy'), split_axi...  9.98 us
    ppermute x4, waiting for transfers between devices, shifted(): lax.ppermute(block, axis, [(i, (i + by) % count) for i in range(count)])  9.51 us
    pallas_call x1, Pallas kernels, two_steps(): pl.pallas_call(step_kernel, in_specs=[SMEM] + [VMEM] * 8 + [HBM], out_spe...  9.02 us
    pallas_call x1, Pallas kernels, remap(): pl.pallas_call(remap_kernel, in_specs=[HBM] * 4, out_specs=VMEM, out_shap...  9.01 us
    ppermute x4, starting transfers between devices, shifted(): lax.ppermute(block, axis, [(i, (i + by) % count) for i in range(count)])  6.92 us
    unnamed x16, local copies, waits for them, and re-layouts  5.55 us
    pallas_call x1, Pallas kernels, outer_columns(): pl.pallas_call(column_kernel, in_specs=[HBM] * 4, out_specs=[VMEM] * 4, o...  3.88 us
  transfers between devices with their start and end apart: 10, of which 3 were waited for; matrix products, arithmetic and copies ran while one was open for 0% of the time, Pallas kernels for 20%

profile of v3, /device:TPU:0, one launch (start us, length us, event | category | flops | bytes accessed | tf_op | source)
XLA Modules:
  0.0 72.1 jit_solution(3769840169030612376)
XLA Ops:
  0.0 0.7 copy-done.4
  0.7 0.7 copy-done.6
  1.3 9.0 %remap.1.after = f32[576,4,128]{2,1,0:T(4,128)} custom-call(s32[4,128]{1,0:T(4,128)S(1)} %bitcast.7, s32[1,128]{1,0:T(1,128)S(1)} %bitcast.8, f32[1,4,16,128,128]{4,3,2,1,0:T(8,128)} %state.5, bf16[1,128,1,4,128,128]{5,4,3,2,1,0:T(8,128)(2,1)} %weight.1), custom_call_target="tpu_custom_call" | custom-call | flops 70254592 | bytes 20971520 | tf_op jit(solution)/shard_map/remap/pallas_call | solution.py:290
  10.4 10.0 %all-to-all-start = ((f32[64,9,4,128]{3,2,1,0:T(4,128)}), f32[64,9,4,128]{3,2,1,0:T(4,128)S(1)}, u32[]{:S(2)}, u32[]{:S(2)}) async-start(f32[64,9,4,128]{3,2,1,0:T(4,128)} %bitcast.3), calls=%async_computation | async-start | bytes 2359296 | tf_op jit(solution)/shard_map/all_to_all | solution.py:617
  20.4 1.2 %outer_rows.1 = (f32[144,128]{1,0:T(8,128)S(1)}, f32[144,128]{1,0:T(8,128)S(1)}) custom-call(f32[1,4,16,128,128]{4,3,2,1,0:T(8,128)} %state.5, f32[1,128,128]{2,1,0:T(8,128)S(1)} %copy-done.2, s32[1,128,128]{2,1,0:T(8,128)S(1)} %copy-done.3, f32[576,4,128]{2,1,0:T(4,128)} %remap.1.after), custom_call_target="tpu_custom_call" | custom-call | flops 65536 | bytes 524288 | tf_op jit(solution)/shard_map/outer_rows/pallas_call | solution.py:108
  21.6 0.0 copy-start.5
  21.6 2.8 %collective-permute-start.1 = (f32[144,128]{1,0:T(8,128)S(1)}, f32[144,128]{1,0:T(8,128)S(1)}, u32[]{:S(2)}, u32[]{:S(2)}) collective-permute-start(f32[144,128]{1,0:T(8,128)S(1)} %get-tuple-element.17.after), channel_id=1, source_target_pairs={{0,56},{8,0},{16,8},{24,16},{32,24},{40,32},{48,40},{56,48},{1,57}... | collective-permute-start | bytes 221192 | tf_op jit(solution)/shard_map/ppermute | solution.py:600
  24.4 3.9 %outer_columns.1 = (f32[384,128]{1,0:T(8,128)S(1)}, f32[4,16,128,128]{3,2,1,0:T(8,128)S(1)}, f32[128,128]{1,0:T(8,128)S(1)}, f32[128,128]{1,0:T(8,128)S(1)}) custom-call(f32[1,4,16,128,128]{4,3,2,1,0:T(8,128)} %state.5, f32[1,128,128]{2,1,0:T(8,128)S(1)} %copy-done.2, s32[1,128,128]{2,1,0:T(8,128)S(1)} %copy-done.3, f32[144,128]{1,0:T(8,128)S(1)} %get-tuple-element.17.after), custom_call_target="tpu_custom_call" | custom-call | flops 6291456 | bytes 9437184 | tf_op jit(solution)/shard_map/outer_columns/pallas_call | solution.py:160
  28.2 0.0 copy-start
  28.3 2.0 %copy-done = f32[4,16,128,128]{3,2,1,0:T(8,128)} copy-done((f32[4,16,128,128]{3,2,1,0:T(8,128)}, f32[4,16,128,128]{3,2,1,0:T(8,128)S(1)}, u32[]{:S(2)}) %copy-start) | copy-done | bytes 4194328
  30.3 7.7 %collective-permute-done.top = f32[144,128]{1,0:T(8,128)S(1)} collective-permute-done((f32[144,128]{1,0:T(8,128)S(1)}, f32[144,128]{1,0:T(8,128)S(1)}, u32[]{:S(2)}, u32[]{:S(2)}) %collective-permute-start) | collective-permute-done | bytes 73760 | tf_op jit(solution)/shard_map/ppermute | solution.py:600
  38.0 0.1 with_corners.1.after.own
  38.1 1.1 %all-to-all-done = f32[64,9,4,128]{3,2,1,0:T(4,128)S(1)} async-done(((f32[64,9,4,128]{3,2,1,0:T(4,128)}), f32[64,9,4,128]{3,2,1,0:T(4,128)S(1)}, u32[]{:S(2)}, u32[]{:S(2)}) %all-to-all-start) | async-done | bytes 1179680 | tf_op jit(solution)/shard_map/all_to_all | solution.py:617
  39.1 0.6 unpack.1
  39.7 2.8 %collective-permute-start.4 = (f32[4,128,128]{2,1,0:T(8,128)S(1)}, f32[4,128,128]{2,1,0:T(8,128)S(1)}, u32[]{:S(2)}, u32[]{:S(2)}) collective-permute-start(f32[4,128,128]{2,1,0:T(8,128)S(1)} %get-tuple-element.23.after), channel_id=1, source_target_pairs={{0,64},{64,0},{1,65},{65,1},{2,66},{66,2},{3,67},{67,3},{4,68},{68... | collective-permute-start | bytes 786440 | tf_op jit(solution)/shard_map/ppermute | solution.py:626
  42.5 0.7 %collective-permute-start.2 = (f32[400,128]{1,0:T(8,128)S(1)}, f32[400,128]{1,0:T(8,128)S(1)}, u32[]{:S(2)}, u32[]{:S(2)}) collective-permute-start(f32[400,128]{1,0:T(8,128)S(1)} %with_corners.1.after.own), channel_id=1, source_target_pairs={{0,1},{1,2},{2,3},{3,4},{4,5},{5,6},{6,7},{7,0},{8,9},{9,10},{10,1... | collective-permute-start | bytes 614408 | tf_op jit(solution)/shard_map/ppermute | solution.py:600
  43.2 3.4 %collective-permute-start.3 = (f32[400,128]{1,0:T(8,128)S(1)}, f32[400,128]{1,0:T(8,128)S(1)}, u32[]{:S(2)}, u32[]{:S(2)}) collective-permute-start(f32[400,128]{1,0:T(8,128)S(1)} %with_corners.1.after.own), channel_id=1, source_target_pairs={{0,7},{1,0},{2,1},{3,2},{4,3},{5,4},{6,5},{7,6},{8,15},{9,8},{10,9... | collective-permute-start | bytes 614408 | tf_op jit(solution)/shard_map/ppermute | solution.py:600
  46.6 0.0 collective-permute-start.7
  46.6 5.3 %collective-permute-start.8 = (f32[8,128]{1,0:T(8,128)S(1)}, f32[8,128]{1,0:T(8,128)S(1)}, u32[]{:S(2)}, u32[]{:S(2)}) collective-permute-start(f32[8,128]{1,0:T(8,128)S(1)} %get-tuple-element.28), channel_id=1, source_target_pairs={{0,71},{1,64},{2,65},{3,66},{4,67},{5,68},{6,69},{7,70},{64,7},{65... | collective-permute-start | bytes 12296 | tf_op jit(solution)/shard_map/ppermute | solution.py:601
  52.0 1.8 %collective-permute-done.2.near = f32[400,128]{1,0:T(8,128)S(1)} collective-permute-done((f32[400,128]{1,0:T(8,128)S(1)}, f32[400,128]{1,0:T(8,128)S(1)}, u32[]{:S(2)}, u32[]{:S(2)}) %collective-permute-start.2) | collective-permute-done | bytes 204832 | tf_op jit(solution)/shard_map/ppermute | solution.py:600
  53.8 5.4 %collective-permute-start.6 = (f32[8,128]{1,0:T(8,128)S(1)}, f32[8,128]{1,0:T(8,128)S(1)}, u32[]{:S(2)}, u32[]{:S(2)}) collective-permute-start(f32[8,128]{1,0:T(8,128)S(1)} %get-tuple-element.27), channel_id=1, source_target_pairs={{0,120},{8,64},{16,72},{24,80},{32,88},{40,96},{48,104},{56,112},{... | collective-permute-start | bytes 12296 | tf_op jit(solution)/shard_map/ppermute | solution.py:601
  59.2 2.2 %copy-done.1 = f32[4,16,128,128]{3,2,1,0:T(8,128)S(1)} copy-done((f32[4,16,128,128]{3,2,1,0:T(8,128)S(1)}, f32[4,16,128,128]{3,2,1,0:T(8,128)}, u32[]{:S(2)}) %copy-start.1) | copy-done | bytes 4194328
  61.3 9.0 %two_steps.1 = (f32[1,4,16,128,128]{4,3,2,1,0:T(8,128)}, f32[2064,128]{1,0:T(8,128)S(1)}) custom-call(f32[1,4]{1,0:T(1,128)S(1)} %copy-done.5, f32[4,16,128,128]{3,2,1,0:T(8,128)S(1)} %copy-done.1, f32[128,128]{1,0:T(8,128)S(1)} %get-tuple-element.19.coef, f32[128,128]{1,0:T(8,128)S(1)} %get-tuple-element.20.sea, f32[400,128]{1,0:T(8,128)S(1)} %with_corners.1.after.own, ...), custom_call_target="tpu_custom_call" | custom-call | flops 50331648 | bytes 10485760 | tf_op jit(solution)/shard_map/two_steps/pallas_call | solution.py:466
  70.4 1.7 %final.1 = f32[1,4,16,128,128]{4,3,2,1,0:T(8,128)} custom-call(f32[1,4]{1,0:T(1,128)S(1)} %copy-done.5, f32[1,4]{1,0:T(1,128)S(1)} %copy-done.7, f32[1,4,16,128,128]{4,3,2,1,0:T(8,128)} %get-tuple-element.24.mid, f32[2064,128]{1,0:T(8,128)S(1)} %get-tuple-element.25.near, ...), custom_call_target="tpu_custom_call", output_to_operand_aliasing={{}: (2, {})} | custom-call | flops 2097152 | bytes 3145728 | tf_op jit(solution)/shard_map/final/pallas_call | solution.py:581
  (19 shorter events, 0.0 us)
Async XLA Ops:
  0.0 0.7 copy-start.4
  0.7 0.7 copy-start.6
  1.3 19.0 %copy-start.2 = (f32[1,128,128]{2,1,0:T(8,128)S(1)}, f32[1,128,128]{2,1,0:T(8,128)}, u32[]{:S(2)}) copy-start(f32[1,128,128]{2,1,0:T(8,128)} %vert.3) | copy-start | bytes 196612
  1.3 19.0 %copy-start.3 = (s32[1,128,128]{2,1,0:T(8,128)S(1)}, s32[1,128,128]{2,1,0:T(8,128)}, u32[]{:S(2)}) copy-start(s32[1,128,128]{2,1,0:T(8,128)} %mask.3) | copy-start | bytes 196612
  10.4 28.8 %all-to-all-start = ((f32[64,9,4,128]{3,2,1,0:T(4,128)}), f32[64,9,4,128]{3,2,1,0:T(4,128)S(1)}, u32[]{:S(2)}, u32[]{:S(2)}) async-start(f32[64,9,4,128]{3,2,1,0:T(4,128)} %bitcast.3), calls=%async_computation | async-start | bytes 2359296 | tf_op jit(solution)/shard_map/all_to_all | solution.py:617
  21.6 37.6 %copy-start.5 = (f32[1,4]{1,0:T(1,128)S(1)}, f32[1,4]{1,0:T(1,128)}, u32[]{:S(2)}) copy-start(f32[1,4]{1,0:T(1,128)} %horiz.1) | copy-start | bytes 52
  21.6 8.7 %collective-permute-start.1 = (f32[144,128]{1,0:T(8,128)S(1)}, f32[144,128]{1,0:T(8,128)S(1)}, u32[]{:S(2)}, u32[]{:S(2)}) collective-permute-start(f32[144,128]{1,0:T(8,128)S(1)} %get-tuple-element.17.after), channel_id=1, source_target_pairs={{0,56},{8,0},{16,8},{24,16},{32,24},{40,32},{48,40},{56,48},{1,57}... | collective-permute-start | bytes 221192 | tf_op jit(solution)/shard_map/ppermute | solution.py:600
  24.4 13.6 %collective-permute-start = (f32[144,128]{1,0:T(8,128)S(1)}, f32[144,128]{1,0:T(8,128)S(1)}, u32[]{:S(2)}, u32[]{:S(2)}) collective-permute-start(f32[144,128]{1,0:T(8,128)S(1)} %get-tuple-element.22), channel_id=1, source_target_pairs={{0,8},{8,16},{16,24},{24,32},{32,40},{40,48},{48,56},{56,0},{1,9},... | collective-permute-start | bytes 221192 | tf_op jit(solution)/shard_map/ppermute | solution.py:600
  28.2 2.0 %copy-start = (f32[4,16,128,128]{3,2,1,0:T(8,128)}, f32[4,16,128,128]{3,2,1,0:T(8,128)S(1)}, u32[]{:S(2)}) copy-start(f32[4,16,128,128]{3,2,1,0:T(8,128)S(1)} %get-tuple-element.18.u) | copy-start | bytes 12582916
  30.3 40.2 %copy-start.7 = (f32[1,4]{1,0:T(1,128)S(1)}, f32[1,4]{1,0:T(1,128)}, u32[]{:S(2)}) copy-start(f32[1,4]{1,0:T(1,128)} %relax.1) | copy-start | bytes 52
  39.7 30.7 %collective-permute-start.4 = (f32[4,128,128]{2,1,0:T(8,128)S(1)}, f32[4,128,128]{2,1,0:T(8,128)S(1)}, u32[]{:S(2)}, u32[]{:S(2)}) collective-permute-start(f32[4,128,128]{2,1,0:T(8,128)S(1)} %get-tuple-element.23.after), channel_id=1, source_target_pairs={{0,64},{64,0},{1,65},{65,1},{2,66},{66,2},{3,67},{67,3},{4,68},{68... | collective-permute-start | bytes 786440 | tf_op jit(solution)/shard_map/ppermute | solution.py:626
  42.5 11.3 %collective-permute-start.2 = (f32[400,128]{1,0:T(8,128)S(1)}, f32[400,128]{1,0:T(8,128)S(1)}, u32[]{:S(2)}, u32[]{:S(2)}) collective-permute-start(f32[400,128]{1,0:T(8,128)S(1)} %with_corners.1.after.own), channel_id=1, source_target_pairs={{0,1},{1,2},{2,3},{3,4},{4,5},{5,6},{6,7},{7,0},{8,9},{9,10},{10,1... | collective-permute-start | bytes 614408 | tf_op jit(solution)/shard_map/ppermute | solution.py:600
  43.2 10.6 %collective-permute-start.3 = (f32[400,128]{1,0:T(8,128)S(1)}, f32[400,128]{1,0:T(8,128)S(1)}, u32[]{:S(2)}, u32[]{:S(2)}) collective-permute-start(f32[400,128]{1,0:T(8,128)S(1)} %with_corners.1.after.own), channel_id=1, source_target_pairs={{0,7},{1,0},{2,1},{3,2},{4,3},{5,4},{6,5},{7,6},{8,15},{9,8},{10,9... | collective-permute-start | bytes 614408 | tf_op jit(solution)/shard_map/ppermute | solution.py:600
  46.6 23.8 %collective-permute-start.7 = (f32[8,128]{1,0:T(8,128)S(1)}, f32[8,128]{1,0:T(8,128)S(1)}, u32[]{:S(2)}, u32[]{:S(2)}) collective-permute-start(f32[8,128]{1,0:T(8,128)S(1)} %get-tuple-element.28), channel_id=1, source_target_pairs={{0,65},{1,66},{2,67},{3,68},{4,69},{5,70},{6,71},{7,64},{64,1},{65... | collective-permute-start | bytes 12296 | tf_op jit(solution)/shard_map/ppermute | solution.py:601
  46.6 23.8 %collective-permute-start.8 = (f32[8,128]{1,0:T(8,128)S(1)}, f32[8,128]{1,0:T(8,128)S(1)}, u32[]{:S(2)}, u32[]{:S(2)}) collective-permute-start(f32[8,128]{1,0:T(8,128)S(1)} %get-tuple-element.28), channel_id=1, source_target_pairs={{0,71},{1,64},{2,65},{3,66},{4,67},{5,68},{6,69},{7,70},{64,7},{65... | collective-permute-start | bytes 12296 | tf_op jit(solution)/shard_map/ppermute | solution.py:601
  53.8 16.6 %collective-permute-start.5 = (f32[8,128]{1,0:T(8,128)S(1)}, f32[8,128]{1,0:T(8,128)S(1)}, u32[]{:S(2)}, u32[]{:S(2)}) collective-permute-start(f32[8,128]{1,0:T(8,128)S(1)} %get-tuple-element.26), channel_id=1, source_target_pairs={{0,72},{8,80},{16,88},{24,96},{32,104},{40,112},{48,120},{56,64},{... | collective-permute-start | bytes 12296 | tf_op jit(solution)/shard_map/ppermute | solution.py:601
  53.8 16.6 %collective-permute-start.6 = (f32[8,128]{1,0:T(8,128)S(1)}, f32[8,128]{1,0:T(8,128)S(1)}, u32[]{:S(2)}, u32[]{:S(2)}) collective-permute-start(f32[8,128]{1,0:T(8,128)S(1)} %get-tuple-element.27), channel_id=1, source_target_pairs={{0,120},{8,64},{16,72},{24,80},{32,88},{40,96},{48,104},{56,112},{... | collective-permute-start | bytes 12296 | tf_op jit(solution)/shard_map/ppermute | solution.py:601
  59.2 2.2 %copy-start.1 = (f32[4,16,128,128]{3,2,1,0:T(8,128)S(1)}, f32[4,16,128,128]{3,2,1,0:T(8,128)}, u32[]{:S(2)}) copy-start(f32[4,16,128,128]{3,2,1,0:T(8,128)} %copy-done) | copy-start | bytes 12582916

commit v4 on v3

--- a/solution.py
+++ b/solution.py
@@ -15,6 +15,7 @@
 SLOTS = CAP + 1
 HALF = 64
 CHUNKS = 16
+MIRROR = 4
 MIB = 1024 * 1024
 ROW_VERT = 2 * PLANES
 ROW_SEA = ROW_VERT + 8
@@ -59,8 +60,8 @@
     return lax.broadcasted_iota(i32, (rows, T), 0)
 
 
-def inside():
-    gx, gy = lax.axis_index("gx"), lax.axis_index("gy")
+def inside(flip=0):
+    gx, gy = lax.axis_index("gx"), lax.axis_index("gy") ^ flip
     one = lambda test: jnp.where(test, 1.0, 0.0).astype(f32)
     return (
         one(gx > 0),
@@ -70,8 +71,8 @@
     )
 
 
-def column_keep(rows):
-    _, _, before, after = inside()
+def column_keep(rows, flip=0):
+    _, _, before, after = inside(flip)
     return jnp.where((lanes(rows) & 1) == 0, after, before)
 
 
@@ -82,8 +83,7 @@
         copy.wait()
 
 
-def row_kernel(state, vert, mask, after, head, tail, high, low, coef, sea, sems):
-    del after
+def row_kernel(state, vert, mask, head, tail, high, low, coef, sea, sems):
     ends = pl.ds(0, 8), pl.ds(T - 8, 8)
     copies = []
     for k, buffer in enumerate((high, low)):
@@ -104,10 +104,10 @@
         out[ROW_SEA : ROW_SEA + 8, :] = jnp.broadcast_to(line, (8, T))
 
 
-def outer_rows(state, vert, mask, after):
+def outer_rows(state, vert, mask):
     return pl.pallas_call(
         row_kernel,
-        in_specs=[HBM] * 4,
+        in_specs=[HBM] * 3,
         out_specs=[VMEM, VMEM],
         out_shape=[jax.ShapeDtypeStruct((ROW_SIZE, T), f32)] * 2,
         scratch_shapes=[
@@ -117,10 +117,10 @@
             pltpu.VMEM((2, 8, T), i32),
             pltpu.SemaphoreType.DMA((6,)),
         ],
-        compiler_params=params(51 * MIB),
+        compiler_params=params(58 * MIB),
         cost_estimate=cost(1 << 16, 1 << 19),
         name="outer_rows",
-    )(state, vert, mask, after)
+    )(state, vert, mask)
 
 
 def column_kernel(state, vert, mask, after, cols, tile, coef, wet, sea, sems):
@@ -205,8 +205,9 @@
 
 
 def remap_kernel(
-    dest_in, count_in, state, weight, out, blocks, planes, surf, dest, count, used, label, sems
+    dest_in, count_in, state, weight, after, out, blocks, planes, surf, dest, count, used, label, sems
 ):
+    del after
     rows = T // CHUNKS
     lists = [
         pltpu.make_async_copy(dest_in, dest, sems.at[CHUNKS]),
@@ -240,7 +241,7 @@
 
     def slot_of(row, f):
         target = dest[f, row]
-        peer = lax.shift_right_logical(target, 7) & (PEERS - 1)
+        peer = (lax.shift_right_logical(target, 7) & (PEERS - 1)) ^ MIRROR
         live = f < count[0, row]
         at = used[peer]
         used[peer] = at + jnp.where(live, 1, 0)
@@ -286,10 +287,10 @@
     lax.fori_loop(0, PEERS, write, 0)
 
 
-def remap(dest, count, state, weight):
+def remap(dest, count, state, weight, after):
     return pl.pallas_call(
         remap_kernel,
-        in_specs=[HBM] * 4,
+        in_specs=[HBM] * 5,
         out_specs=VMEM,
         out_shape=jax.ShapeDtypeStruct((PEERS * SLOTS, NV, T), f32),
         scratch_shapes=[
@@ -305,7 +306,7 @@
         compiler_params=params(51 * MIB),
         cost_estimate=cost(67 << 20, 20 << 20),
         name="remap",
-    )(dest, count, state, weight)
+    )(dest, count, state, weight, after)
 
 
 def merged(left, right, back=2):
@@ -322,6 +323,49 @@
     return u + rate * ((north + south) + (west + east) - 4.0 * u)
 
 
+def level_inner(u, rate, l, lo):
+    nothing = jnp.zeros((1, T), f32)
+    up = nothing if lo == 0 else u[l, lo - 1 : lo, :]
+    down = nothing if lo + HALF == T else u[l, lo + HALF : lo + HALF + 1, :]
+    return diffuse(u[l, lo : lo + HALF, :], up, down, 0.0, rate)
+
+
+def inner_kernel(rate, u, coef, after, out):
+    del after
+
+    def body(v, _):
+        number = rate[0, v]
+        source, result = u.at[v], out.at[v]
+        for lo in range(0, T, HALF):
+            mix = coef[lo : lo + HALF, :]
+            before, here = None, level_inner(source, number, 0, lo)
+            for l in range(LEV):
+                after = level_inner(source, number, l + 1, lo) if l + 1 < LEV else None
+                if before is None:
+                    term = after - here
+                elif after is None:
+                    term = before - here
+                else:
+                    term = (after - here) + (before - here)
+                result[l, lo : lo + HALF, :] = here + mix * term
+                before, here = here, after
+        return 0
+
+    lax.fori_loop(0, NV, body, 0)
+
+
+def inner_step(rate, u, coef, after):
+    return pl.pallas_call(
+        inner_kernel,
+        in_specs=[SMEM, VMEM, VMEM, HBM],
+        out_specs=VMEM,
+        out_shape=jax.ShapeDtypeStruct(u.shape, f32),
+        compiler_params=params(10 * MIB),
+        cost_estimate=cost(24 << 20, 9 << 20),
+        name="inner_step",
+    )(rate, u, coef, after)
+
+
 def level_diffuse(u, top, bottom, side, rate, l, lo):
     up = top[l : l + 1, :] if lo == 0 else u[l, lo - 1 : lo, :]
     down = bottom[l : l + 1, :] if lo + HALF == T else u[l, lo + HALF : lo + HALF + 1, :]
@@ -331,7 +375,7 @@
     return diffuse(u[l, lo : lo + HALF, :], up, down, spin, rate)
 
 
-def halo_columns(rate, left, right, own):
+def halo_columns(rate, vert, left, right, own):
     lane, sub = lanes(T), subl(T)
     here = merged(left[0:T, :], right[0:T, :])
     outer = merged(left[COL_NEXT : COL_NEXT + T, :], right[COL_NEXT : COL_NEXT + T, :], 4)
@@ -350,12 +394,21 @@
         jnp.broadcast_to(right[COL_COEF : COL_COEF + T, 1:2], (T, T)),
     )
     level = plane % LEV
-    above = jnp.where(level < LEV - 1, pltpu.roll(h, T - 2, 1) - h, 0.0)
-    below = jnp.where(level > 0, pltpu.roll(h, 2, 1) - h, 0.0)
-    return here, h + coef * (above + below)
-
-
-def halo_rows(rate, rows, own, left, right, k, v):
+
+    def mixed(h, coef):
+        above = jnp.where(level < LEV - 1, pltpu.roll(h, T - 2, 1) - h, 0.0)
+        below = jnp.where(level > 0, pltpu.roll(h, 2, 1) - h, 0.0)
+        return h + coef * (above + below)
+
+    mine = jnp.where(
+        (lane & 1) == 0,
+        jnp.broadcast_to(vert[:, 0:1], (T, T)),
+        jnp.broadcast_to(vert[:, T - 1 : T], (T, T)),
+    )
+    return mixed(number * here, mine), mixed(h, coef)
+
+
+def halo_rows(rate, vert, rows, own, left, right, k, v):
     at = v * LEV
     lane, level = lanes(LEV), subl(LEV)
     here = rows[at : at + LEV, :]
@@ -371,56 +424,57 @@
     outer = rows[PLANES + at : PLANES + at + LEV, :]
     inner = own[at : at + LEV, :]
     h = here + rate[0, v] * ((outer + inner) + (west + east) - 4.0 * here)
-    above = jnp.where(level < LEV - 1, pltpu.roll(h, LEV - 1, 0) - h, 0.0)
-    below = jnp.where(level > 0, pltpu.roll(h, 1, 0) - h, 0.0)
-    return h + rows[ROW_VERT : ROW_VERT + 1, :] * (above + below)
+
+    def mixed(h, coef):
+        above = jnp.where(level < LEV - 1, pltpu.roll(h, LEV - 1, 0) - h, 0.0)
+        below = jnp.where(level > 0, pltpu.roll(h, 1, 0) - h, 0.0)
+        return h + coef * (above + below)
+
+    edge = k * (T - 1)
+    return (
+        mixed(rate[0, v] * here, vert[edge : edge + 1, :]),
+        mixed(h, rows[ROW_VERT : ROW_VERT + 1, :]),
+    )
 
 
 def step_kernel(
-    rate, u, coef, sea, own, top, bottom, near, far, after,
-    out, keep, w, stage, inner, top1, bottom1, top2, bottom2, side1, side2, turned, sems,
+    rate, inner, coef, sea, head, tail, own, top, bottom, near, far, after,
+    out, keep, w, stage, ends, top1, bottom1, top2, bottom2, side1, side2, turned, sems,
 ):
     del after
+    loads = [
+        pltpu.make_async_copy(rows.at[pl.ds(0, PLANES)], ends.at[k], sems.at[k])
+        for k, rows in enumerate((head, tail))
+    ]
+    for load in loads:
+        load.start()
 
     def emit(v):
         levels = pl.ds(2, LEV - 2)
         return pltpu.make_async_copy(stage.at[v], out.at[0, v, levels], sems.at[v])
 
-    up, down, _, _ = inside()
-    side1[...], side2[...] = halo_columns(rate, near, far, own)
+    side1[...], side2[...] = halo_columns(rate, coef, near, far, own)
+    for load in loads:
+        load.wait()
     for v in range(NV):
-        at = v * LEV
+        top1[v], top2[v] = halo_rows(rate, coef, top, ends.at[0], near, far, 0, v)
+        bottom1[v], bottom2[v] = halo_rows(rate, coef, bottom, ends.at[1], near, far, 1, v)
+    lane = lanes(HALF)
+    rim = (lane == 0) | (lane == T - 1)
+
+    def complete(v, _):
+        turned[...] = pltpu.roll(side1[...], lax.rem((NV - v) * 32, T), 1)
         for l in range(LEV):
-            inner[0, at + l : at + l + 1, :] = u[v, l, 0:1, :] * up
-            inner[1, at + l : at + l + 1, :] = u[v, l, T - 1 : T, :] * down
-    for v in range(NV):
-        at = v * LEV
-        top1[v] = top[at : at + LEV, :]
-        bottom1[v] = bottom[at : at + LEV, :]
-        top2[v] = halo_rows(rate, top, inner.at[0], near, far, 0, v)
-        bottom2[v] = halo_rows(rate, bottom, inner.at[1], near, far, 1, v)
-
-    def first(v, _):
-        number = rate[0, v]
-        turned[...] = pltpu.roll(side1[...], lax.rem((NV - v) * 32, T), 1)
-        source, result = u.at[v], w.at[v]
-        for lo in range(0, T, HALF):
-            mix = coef[lo : lo + HALF, :]
-            at = lambda l: level_diffuse(source, top1.at[v], bottom1.at[v], turned, number, l, lo)
-            before, here = None, at(0)
-            for l in range(LEV):
-                after = at(l + 1) if l + 1 < LEV else None
-                if before is None:
-                    term = after - here
-                elif after is None:
-                    term = before - here
-                else:
-                    term = (after - here) + (before - here)
-                result[l, lo : lo + HALF, :] = here + mix * term
-                before, here = here, after
+            for lo in range(0, T, HALF):
+                add = turned[lo : lo + HALF, :]
+                if l:
+                    add = pltpu.roll(add, T - 2 * l, 1)
+                w[v, l, lo : lo + HALF, :] = inner[v, l, lo : lo + HALF, :] + jnp.where(rim, add, 0.0)
+            w[v, l, 0:1, :] = w[v, l, 0:1, :] + top1[v, l : l + 1, :]
+            w[v, l, T - 1 : T, :] = w[v, l, T - 1 : T, :] + bottom1[v, l : l + 1, :]
         return 0
 
-    lax.fori_loop(0, NV, first, 0)
+    lax.fori_loop(0, NV, complete, 0)
 
     def second(v, _):
         number = rate[0, v]
@@ -460,15 +514,15 @@
         emit(v).wait()
 
 
-def two_steps(rate, u, coef, sea, own, top, bottom, left, right, after):
+def second_step(rate, inner, coef, sea, head, tail, own, top, bottom, left, right, after):
     rows = pltpu.VMEM((NV, LEV, T), f32)
     square = pltpu.VMEM((T, T), f32)
     return pl.pallas_call(
         step_kernel,
-        in_specs=[SMEM] + [VMEM] * 8 + [HBM],
+        in_specs=[SMEM] + [VMEM] * 3 + [HBM] * 2 + [VMEM] * 5 + [HBM],
         out_specs=[HBM, VMEM],
         out_shape=[
-            jax.ShapeDtypeStruct((1,) + u.shape, f32),
+            jax.ShapeDtypeStruct((1,) + inner.shape, f32),
             jax.ShapeDtypeStruct((KEEP_SIZE, T), f32),
         ],
         scratch_shapes=[
@@ -486,12 +540,12 @@
         ],
         compiler_params=params(16 * MIB),
         cost_estimate=cost(48 << 20, 10 << 20),
-        name="two_steps",
-    )(rate, u, coef, sea, own, top, bottom, left, right, after)
-
-
-def unpack_kernel(data, after, imp, first, last, cols):
-    del after
+        name="second_step",
+    )(rate, inner, coef, sea, head, tail, own, top, bottom, left, right, after)
+
+
+def unpack_kernel(data, left, right, step, imp, first, last, cols):
+    del left, right, step
     size = SLOTS * NV
     sub = subl(T).astype(f32) + 1.0
     picks = []
@@ -515,13 +569,13 @@
             out[v : v + 1, :] = total[row : row + 1, :] * keep
             out[NV + v : NV + v + 1, :] = total[row : row + 1, :] * keep
         acc = jnp.where((lane >> 1) == v, pltpu.roll(total, 2 * v + 1, 1), acc)
-    cols[...] = jnp.transpose(acc * column_keep(T))[0 : 2 * NV, :]
-
-
-def unpack(data, after):
+    cols[...] = jnp.transpose(acc * column_keep(T, MIRROR))[0 : 2 * NV, :]
+
+
+def unpack(data, *after):
     return pl.pallas_call(
         unpack_kernel,
-        in_specs=[VMEM, HBM],
+        in_specs=[VMEM] + [HBM] * len(after),
         out_specs=[VMEM] * 4,
         out_shape=[
             jax.ShapeDtypeStruct((NV, T, T), f32),
@@ -532,7 +586,7 @@
         compiler_params=params(12 * MIB),
         cost_estimate=cost(200 << 20, 2 << 20),
         name="unpack",
-    )(data, after)
+    )(data, *after)
 
 
 def final_kernel(
@@ -594,39 +648,45 @@
     )(horiz, relax, mid, keep, imp, *imp_rows, *imp_cols)
 
 
-def shifted(block, axis, by, across=False):
+def shifted(block, axis, by):
     count = lax.axis_size(axis)
-    if not across:
-        return lax.ppermute(block, axis, [(i, (i + by) % count) for i in range(count)])
-    return lax.ppermute(
-        block,
-        ("comp", axis),
-        [
-            (c * count + i, (1 - c) * count + (i + by) % count)
-            for c in range(2)
-            for i in range(count)
-        ],
-    )
+    return lax.ppermute(block, axis, [(i, (i + by) % count) for i in range(count)])
+
+
+def crossed(block, gx_by=0, gy_by=0):
+    size = lax.axis_size("gx"), lax.axis_size("gy")
+    route = []
+    for c in range(2):
+        for i in range(size[0]):
+            for j in range(size[1]):
+                to = (i + gx_by) % size[0], ((j ^ MIRROR) + gy_by) % size[1]
+                route.append(((c * size[0] + i) * size[1] + j, ((1 - c) * size[0] + to[0]) * size[1] + to[1]))
+    return lax.ppermute(block, ("comp", "gx", "gy"), route)
 
 
 def local(
     state, horiz_coef, vert_coef, couple_rate, sea_mask, dest_block, entry_count, remap_weight
 ):
+    head, tail = outer_rows(state, vert_coef, sea_mask)
+    top, bottom = shifted(tail, "gx", 1), shifted(head, "gx", -1)
     dest = dest_block.reshape(T, FAN).T
-    sent = remap(dest, entry_count.reshape(1, T), state, remap_weight)
+    sent = remap(dest, entry_count.reshape(1, T), state, remap_weight, head)
     packed = lax.all_to_all(
         sent.reshape(PEERS, SLOTS, NV, T), ("gx", "gy"), split_axis=0, concat_axis=0, tiled=True
     )
-    head, tail = outer_rows(state, vert_coef, sea_mask, sent)
-    top, bottom = shifted(tail, "gx", 1), shifted(head, "gx", -1)
-    cols, tile, coef, sea = outer_columns(state, vert_coef, sea_mask, head)
+    cols, tile, coef, sea = outer_columns(state, vert_coef, sea_mask, sent)
     cols = with_corners(cols, top, bottom)
     left, right = shifted(cols, "gy", 1), shifted(cols, "gy", -1)
-    new, first, last, sides = unpack(packed.reshape(PEERS * SLOTS * NV, T), cols)
-    imp = lax.ppermute(new, "comp", [(0, 1), (1, 0)])
-    imp_rows = shifted(last, "gx", 1, True), shifted(first, "gx", -1, True)
-    imp_cols = shifted(sides, "gy", 1, True), shifted(sides, "gy", -1, True)
-    mid, keep = two_steps(horiz_coef, tile, coef, sea, cols, top, bottom, left, right, new)
+    inner = inner_step(horiz_coef, tile, coef, cols)
+    new, first, last, sides = unpack(
+        packed.reshape(PEERS * SLOTS * NV, T), left, right, inner
+    )
+    imp = crossed(new)
+    imp_rows = crossed(last, gx_by=1), crossed(first, gx_by=-1)
+    imp_cols = crossed(sides, gy_by=1), crossed(sides, gy_by=-1)
+    mid, keep = second_step(
+        horiz_coef, inner, coef, sea, head, tail, cols, top, bottom, left, right, new
+    )
     return final(horiz_coef, couple_rate, mid, keep, imp, imp_rows, imp_cols)
 
 

time: 72.4 us -> 73.2 us (1.011)
  waiting for transfers between devices: 10.6 us -> 1.6 us
  starting transfers between devices: 30.4 us -> 38.1 us
  Pallas kernels: 25.5 us -> 27.9 us
    ppermute x4, starting transfers between devices: 6.92 us -> 15.5 us  [shifted(): lax.ppermute(block, axis, [(i, (i + by) % count) for i in range(count)])]
    ppermute x4, waiting for transfers between devices: 9.51 us -> 1.59 us  [shifted(): lax.ppermute(block, axis, [(i, (i + by) % count) for i in range(count)])]
    pallas_call x4 -> x5, Pallas kernels: 19.8 us -> 22.2 us  [the longest x1 9.13 us: remap(): pl.pallas_call(remap_kernel, in_specs=[HBM] * 5, out_specs=VMEM, out_shap...]
    all_to_all x1, waiting for transfers between devices: 1.05 us -> 0.01 us  [local(): lax.all_to_all(sent.reshape(PEERS, SLOTS, NV, T), ('gx', 'gy'), split_axi...]
    ppermute x5, starting transfers between devices: 13.5 us -> 12.6 us  [crossed(): return lax.ppermute(block, ('comp', 'gx', 'gy'), route)]
    unnamed x16 -> x24, local copies, waits for them, and re-layouts: 5.55 us -> 5.1 us
  transfers between devices with their start and end apart: 10 -> 10, of which waited for: 3 -> 2; matrix products, arithmetic and copies ran while one was open for 0% -> 0% of each run, Pallas kernels for 20% -> 20%
where the time goes in v4:
time: 73.2 us; the launch traced here: 72.9 us
  starting transfers between devices  38.1 us (52%)
  Pallas kernels  27.9 us (38%)
  local copies, waits for them, and re-layouts  5.1 us (7%)
  waiting for transfers between devices  1.6 us (2%)
    ppermute x4, starting transfers between devices, shifted(): lax.ppermute(block, axis, [(i, (i + by) % count) for i in range(count)])  15.5 us
    ppermute x5, starting transfers between devices, crossed(): return lax.ppermute(block, ('comp', 'gx', 'gy'), route)  12.6 us
    all_to_all x1, starting transfers between devices, local(): lax.all_to_all(sent.reshape(PEERS, SLOTS, NV, T), ('gx', 'gy'), split_axi...  9.98 us
    pallas_call x1, Pallas kernels, remap(): pl.pallas_call(remap_kernel, in_specs=[HBM] * 5, out_specs=VMEM, out_shap...  9.13 us
    pallas_call x1, Pallas kernels, second_step(): pl.pallas_call(step_kernel, in_specs=[SMEM] + [VMEM] * 3 + [HBM] * 2 + [V...  7.23 us
    unnamed x24, local copies, waits for them, and re-layouts  5.1 us
    pallas_call x1, Pallas kernels, outer_columns(): pl.pallas_call(column_kernel, in_specs=[HBM] * 4, out_specs=[VMEM] * 4, o...  3.86 us
    pallas_call x1, Pallas kernels, inner_step(): pl.pallas_call(inner_kernel, in_specs=[SMEM, VMEM, VMEM, HBM], out_specs=...  3.37 us
  transfers between devices with their start and end apart: 10, of which 2 were waited for; matrix products, arithmetic and copies ran while one was open for 0% of the time, Pallas kernels for 20%

profile of v4, /device:TPU:0, one launch (start us, length us, event | category | flops | bytes accessed | tf_op | source)
XLA Modules:
  0.0 72.9 jit_solution(7292483629122459736)
XLA Ops:
  0.0 1.9 %outer_rows.1 = (f32[144,128]{1,0:T(8,128)}, f32[144,128]{1,0:T(8,128)}) custom-call(f32[1,4,16,128,128]{4,3,2,1,0:T(8,128)} %state.5, f32[1,128,128]{2,1,0:T(8,128)} %vert.3, s32[1,128,128]{2,1,0:T(8,128)} %mask.3), custom_call_target="tpu_custom_call" | custom-call | flops 65536 | bytes 524288 | tf_op jit(solution)/shard_map/outer_rows/pallas_call | solution.py:108
  1.9 0.0 copy-start.3
  1.9 0.9 %copy-done.3 = f32[144,128]{1,0:T(8,128)S(1)} copy-done((f32[144,128]{1,0:T(8,128)S(1)}, f32[144,128]{1,0:T(8,128)}, u32[]{:S(2)}) %copy-start.3) | copy-done | bytes 73752
  2.8 9.1 %remap.1.after = f32[576,4,128]{2,1,0:T(4,128)} custom-call(s32[4,128]{1,0:T(4,128)S(1)} %bitcast.7, s32[1,128]{1,0:T(1,128)S(1)} %bitcast.8, f32[1,4,16,128,128]{4,3,2,1,0:T(8,128)} %state.5, bf16[1,128,1,4,128,128]{5,4,3,2,1,0:T(8,128)(2,1)} %weight.1, f32[144,128]{1,0:T(8,128)S(1)} %copy-done.3), custom_call_target="tpu_custom_call" | custom-call | flops 70254592 | bytes 20971520 | tf_op jit(solution)/shard_map/remap/pallas_call | solution.py:291
  12.0 0.0 copy-start.8
  12.0 10.0 %all-to-all-start = ((f32[64,9,4,128]{3,2,1,0:T(4,128)}), f32[64,9,4,128]{3,2,1,0:T(4,128)S(1)}, u32[]{:S(2)}, u32[]{:S(2)}) async-start(f32[64,9,4,128]{3,2,1,0:T(4,128)} %bitcast.3), calls=%async_computation | async-start | bytes 2359296 | tf_op jit(solution)/shard_map/all_to_all | solution.py:674
  22.0 2.8 %collective-permute-start.1 = (f32[144,128]{1,0:T(8,128)S(1)}, f32[144,128]{1,0:T(8,128)S(1)}, u32[]{:S(2)}, u32[]{:S(2)}) collective-permute-start(f32[144,128]{1,0:T(8,128)S(1)} %copy-done.4), channel_id=1, source_target_pairs={{0,56},{8,0},{16,8},{24,16},{32,24},{40,32},{48,40},{56,48},{1,57}... | collective-permute-start | bytes 221192 | tf_op jit(solution)/shard_map/ppermute | solution.py:653
  24.8 3.9 %outer_columns.1 = (f32[384,128]{1,0:T(8,128)S(1)}, f32[4,16,128,128]{3,2,1,0:T(8,128)S(1)}, f32[128,128]{1,0:T(8,128)S(1)}, f32[128,128]{1,0:T(8,128)S(1)}) custom-call(f32[1,4,16,128,128]{4,3,2,1,0:T(8,128)} %state.5, f32[1,128,128]{2,1,0:T(8,128)S(1)} %copy-done.5, s32[1,128,128]{2,1,0:T(8,128)S(1)} %copy-done.6, f32[576,4,128]{2,1,0:T(4,128)} %remap.1.after), custom_call_target="tpu_custom_call" | custom-call | flops 6291456 | bytes 9437184 | tf_op jit(solution)/shard_map/outer_columns/pallas_call | solution.py:160
  28.6 0.3 collective-permute-done.1.bottom
  28.9 1.3 %collective-permute-done.top = f32[144,128]{1,0:T(8,128)S(1)} collective-permute-done((f32[144,128]{1,0:T(8,128)S(1)}, f32[144,128]{1,0:T(8,128)S(1)}, u32[]{:S(2)}, u32[]{:S(2)}) %collective-permute-start) | collective-permute-done | bytes 73760 | tf_op jit(solution)/shard_map/ppermute | solution.py:653
  30.2 0.1 with_corners.1.after.own
  30.3 9.8 %collective-permute-start.2 = (f32[400,128]{1,0:T(8,128)S(1)}, f32[400,128]{1,0:T(8,128)S(1)}, u32[]{:S(2)}, u32[]{:S(2)}) collective-permute-start(f32[400,128]{1,0:T(8,128)S(1)} %with_corners.1.after.own), channel_id=1, source_target_pairs={{0,1},{1,2},{2,3},{3,4},{4,5},{5,6},{6,7},{7,0},{8,9},{9,10},{10,1... | collective-permute-start | bytes 614408 | tf_op jit(solution)/shard_map/ppermute | solution.py:653
  40.1 3.0 %collective-permute-start.3 = (f32[400,128]{1,0:T(8,128)S(1)}, f32[400,128]{1,0:T(8,128)S(1)}, u32[]{:S(2)}, u32[]{:S(2)}) collective-permute-start(f32[400,128]{1,0:T(8,128)S(1)} %with_corners.1.after.own), channel_id=1, source_target_pairs={{0,7},{1,0},{2,1},{3,2},{4,3},{5,4},{6,5},{7,6},{8,15},{9,8},{10,9... | collective-permute-start | bytes 614408 | tf_op jit(solution)/shard_map/ppermute | solution.py:653
  43.1 3.4 %inner_step.1.step.inner = f32[4,16,128,128]{3,2,1,0:T(8,128)S(1)} custom-call(f32[1,4]{1,0:T(1,128)S(1)} %copy-done.8, f32[4,16,128,128]{3,2,1,0:T(8,128)S(1)} %get-tuple-element.18.u, f32[128,128]{1,0:T(8,128)S(1)} %get-tuple-element.19.coef, f32[400,128]{1,0:T(8,128)S(1)} %with_corners.1.after.own), custom_call_target="tpu_custom_call" | custom-call | flops 25165824 | bytes 9437184 | tf_op jit(solution)/shard_map/inner_step/pallas_call | solution.py:358
  46.5 0.0 copy-start
  46.5 2.0 %copy-done = f32[4,16,128,128]{3,2,1,0:T(8,128)} copy-done((f32[4,16,128,128]{3,2,1,0:T(8,128)}, f32[4,16,128,128]{3,2,1,0:T(8,128)S(1)}, u32[]{:S(2)}) %copy-start) | copy-done | bytes 4194328
  48.5 2.2 %copy-done.1 = f32[4,16,128,128]{3,2,1,0:T(8,128)S(1)} copy-done((f32[4,16,128,128]{3,2,1,0:T(8,128)S(1)}, f32[4,16,128,128]{3,2,1,0:T(8,128)}, u32[]{:S(2)}) %copy-start.1) | copy-done | bytes 4194328
  50.7 0.6 unpack.1
  51.3 1.9 %collective-permute-start.4 = (f32[4,128,128]{2,1,0:T(8,128)S(1)}, f32[4,128,128]{2,1,0:T(8,128)S(1)}, u32[]{:S(2)}, u32[]{:S(2)}) collective-permute-start(f32[4,128,128]{2,1,0:T(8,128)S(1)} %get-tuple-element.23.after), channel_id=1, source_target_pairs={{0,68},{1,69},{2,70},{3,71},{4,64},{5,65},{6,66},{7,67},{8,76},{9,... | collective-permute-start | bytes 786440 | tf_op jit(solution)/shard_map/ppermute | solution.py:664
  53.2 0.1 collective-permute-start.7
  53.3 5.6 %collective-permute-start.8 = (f32[8,128]{1,0:T(8,128)S(1)}, f32[8,128]{1,0:T(8,128)S(1)}, u32[]{:S(2)}, u32[]{:S(2)}) collective-permute-start(f32[8,128]{1,0:T(8,128)S(1)} %get-tuple-element.28), channel_id=1, source_target_pairs={{0,67},{1,68},{2,69},{3,70},{4,71},{5,64},{6,65},{7,66},{8,75},{9,... | collective-permute-start | bytes 12296 | tf_op jit(solution)/shard_map/ppermute | solution.py:664
  58.8 5.1 %collective-permute-start.6 = (f32[8,128]{1,0:T(8,128)S(1)}, f32[8,128]{1,0:T(8,128)S(1)}, u32[]{:S(2)}, u32[]{:S(2)}) collective-permute-start(f32[8,128]{1,0:T(8,128)S(1)} %get-tuple-element.27), channel_id=1, source_target_pairs={{0,124},{1,125},{2,126},{3,127},{4,120},{5,121},{6,122},{7,123},{8... | collective-permute-start | bytes 12296 | tf_op jit(solution)/shard_map/ppermute | solution.py:664
  63.9 7.2 %second_step.1 = (f32[1,4,16,128,128]{4,3,2,1,0:T(8,128)}, f32[2064,128]{1,0:T(8,128)S(1)}) custom-call(f32[1,4]{1,0:T(1,128)S(1)} %copy-done.8, f32[4,16,128,128]{3,2,1,0:T(8,128)S(1)} %copy-done.2, f32[128,128]{1,0:T(8,128)S(1)} %get-tuple-element.19.coef, f32[128,128]{1,0:T(8,128)S(1)} %get-tuple-element.22.sea, f32[144,128]{1,0:T(8,128)S(1)} %copy-done.4, ...), custom_call_target="tpu_custom_call" | custom-call | flops 50331648 | bytes 10485760 | tf_op jit(solution)/shard_map/second_step/pallas_call | solution.py:520
  71.2 1.7 %final.1 = f32[1,4,16,128,128]{4,3,2,1,0:T(8,128)} custom-call(f32[1,4]{1,0:T(1,128)S(1)} %copy-done.8, f32[1,4]{1,0:T(1,128)S(1)} %copy-done.11, f32[1,4,16,128,128]{4,3,2,1,0:T(8,128)} %get-tuple-element.24.mid, f32[2064,128]{1,0:T(8,128)S(1)} %get-tuple-element.25.near, ...), custom_call_target="tpu_custom_call", output_to_operand_aliasing={{}: (2, {})} | custom-call | flops 2097152 | bytes 3145728 | tf_op jit(solution)/shard_map/final/pallas_call | solution.py:635
  (28 shorter events, 0.1 us)
Async XLA Ops:
  0.0 1.9 %copy-start.9 = (s32[1,128,1,4]{1,3,2,0:T(4,128)S(1)}, s32[1,128,1,4]{1,3,2,0:T(4,128)}, u32[]{:S(2)}) copy-start(s32[1,128,1,4]{1,3,2,0:T(4,128)} %param.13) | copy-start | bytes 6148
  0.0 1.9 %copy-start.10 = (s32[1,128,1]{1,2,0:T(1,128)S(1)}, s32[1,128,1]{1,2,0:T(1,128)}, u32[]{:S(2)}) copy-start(s32[1,128,1]{1,2,0:T(1,128)} %param.14) | copy-start | bytes 1540
  1.9 0.9 %copy-start.3 = (f32[144,128]{1,0:T(8,128)S(1)}, f32[144,128]{1,0:T(8,128)}, u32[]{:S(2)}) copy-start(f32[144,128]{1,0:T(8,128)} %get-tuple-element.17.after.head) | copy-start | bytes 221188
  2.8 19.1 %copy-start.4 = (f32[144,128]{1,0:T(8,128)S(1)}, f32[144,128]{1,0:T(8,128)}, u32[]{:S(2)}) copy-start(f32[144,128]{1,0:T(8,128)} %get-tuple-element.17.after.head) | copy-start | bytes 221188
  2.8 21.9 %copy-start.7 = (f32[144,128]{1,0:T(8,128)S(1)}, f32[144,128]{1,0:T(8,128)}, u32[]{:S(2)}) copy-start(f32[144,128]{1,0:T(8,128)} %get-tuple-element.21.tail) | copy-start | bytes 221188
  2.8 21.9 %copy-start.5 = (f32[1,128,128]{2,1,0:T(8,128)S(1)}, f32[1,128,128]{2,1,0:T(8,128)}, u32[]{:S(2)}) copy-start(f32[1,128,128]{2,1,0:T(8,128)} %vert.3) | copy-start | bytes 196612
  2.8 21.9 %copy-start.6 = (s32[1,128,128]{2,1,0:T(8,128)S(1)}, s32[1,128,128]{2,1,0:T(8,128)}, u32[]{:S(2)}) copy-start(s32[1,128,128]{2,1,0:T(8,128)} %mask.3) | copy-start | bytes 196612
  12.0 31.2 %copy-start.8 = (f32[1,4]{1,0:T(1,128)S(1)}, f32[1,4]{1,0:T(1,128)}, u32[]{:S(2)}) copy-start(f32[1,4]{1,0:T(1,128)} %horiz.1) | copy-start | bytes 52
  12.0 36.5 %all-to-all-start = ((f32[64,9,4,128]{3,2,1,0:T(4,128)}), f32[64,9,4,128]{3,2,1,0:T(4,128)S(1)}, u32[]{:S(2)}, u32[]{:S(2)}) async-start(f32[64,9,4,128]{3,2,1,0:T(4,128)} %bitcast.3), calls=%async_computation | async-start | bytes 2359296 | tf_op jit(solution)/shard_map/all_to_all | solution.py:674
  22.0 7.0 %collective-permute-start.1 = (f32[144,128]{1,0:T(8,128)S(1)}, f32[144,128]{1,0:T(8,128)S(1)}, u32[]{:S(2)}, u32[]{:S(2)}) collective-permute-start(f32[144,128]{1,0:T(8,128)S(1)} %copy-done.4), channel_id=1, source_target_pairs={{0,56},{8,0},{16,8},{24,16},{32,24},{40,32},{48,40},{56,48},{1,57}... | collective-permute-start | bytes 221192 | tf_op jit(solution)/shard_map/ppermute | solution.py:653
  24.7 5.5 %collective-permute-start = (f32[144,128]{1,0:T(8,128)S(1)}, f32[144,128]{1,0:T(8,128)S(1)}, u32[]{:S(2)}, u32[]{:S(2)}) collective-permute-start(f32[144,128]{1,0:T(8,128)S(1)} %copy-done.7), channel_id=1, source_target_pairs={{0,8},{8,16},{16,24},{24,32},{32,40},{40,48},{48,56},{56,0},{1,9},... | collective-permute-start | bytes 221192 | tf_op jit(solution)/shard_map/ppermute | solution.py:653
  30.3 18.2 %collective-permute-start.2 = (f32[400,128]{1,0:T(8,128)S(1)}, f32[400,128]{1,0:T(8,128)S(1)}, u32[]{:S(2)}, u32[]{:S(2)}) collective-permute-start(f32[400,128]{1,0:T(8,128)S(1)} %with_corners.1.after.own), channel_id=1, source_target_pairs={{0,1},{1,2},{2,3},{3,4},{4,5},{5,6},{6,7},{7,0},{8,9},{9,10},{10,1... | collective-permute-start | bytes 614408 | tf_op jit(solution)/shard_map/ppermute | solution.py:653
  40.1 8.4 %collective-permute-start.3 = (f32[400,128]{1,0:T(8,128)S(1)}, f32[400,128]{1,0:T(8,128)S(1)}, u32[]{:S(2)}, u32[]{:S(2)}) collective-permute-start(f32[400,128]{1,0:T(8,128)S(1)} %with_corners.1.after.own), channel_id=1, source_target_pairs={{0,7},{1,0},{2,1},{3,2},{4,3},{5,4},{6,5},{7,6},{8,15},{9,8},{10,9... | collective-permute-start | bytes 614408 | tf_op jit(solution)/shard_map/ppermute | solution.py:653
  46.5 2.0 %copy-start = (f32[4,16,128,128]{3,2,1,0:T(8,128)}, f32[4,16,128,128]{3,2,1,0:T(8,128)S(1)}, u32[]{:S(2)}) copy-start(f32[4,16,128,128]{3,2,1,0:T(8,128)S(1)} %inner_step.1.step.inner) | copy-start | bytes 12582916
  48.5 2.2 %copy-start.1 = (f32[4,16,128,128]{3,2,1,0:T(8,128)S(1)}, f32[4,16,128,128]{3,2,1,0:T(8,128)}, u32[]{:S(2)}) copy-start(f32[4,16,128,128]{3,2,1,0:T(8,128)} %copy-done) | copy-start | bytes 12582916
  50.7 13.2 %copy-start.2 = (f32[4,16,128,128]{3,2,1,0:T(8,128)S(1)}, f32[4,16,128,128]{3,2,1,0:T(8,128)}, u32[]{:S(2)}) copy-start(f32[4,16,128,128]{3,2,1,0:T(8,128)} %copy-done) | copy-start | bytes 12582916
  51.3 19.9 %copy-start.11 = (f32[1,4]{1,0:T(1,128)S(1)}, f32[1,4]{1,0:T(1,128)}, u32[]{:S(2)}) copy-start(f32[1,4]{1,0:T(1,128)} %relax.1) | copy-start | bytes 52
  51.3 19.9 %collective-permute-start.4 = (f32[4,128,128]{2,1,0:T(8,128)S(1)}, f32[4,128,128]{2,1,0:T(8,128)S(1)}, u32[]{:S(2)}, u32[]{:S(2)}) collective-permute-start(f32[4,128,128]{2,1,0:T(8,128)S(1)} %get-tuple-element.23.after), channel_id=1, source_target_pairs={{0,68},{1,69},{2,70},{3,71},{4,64},{5,65},{6,66},{7,67},{8,76},{9,... | collective-permute-start | bytes 786440 | tf_op jit(solution)/shard_map/ppermute | solution.py:664
  53.2 18.0 %collective-permute-start.7 = (f32[8,128]{1,0:T(8,128)S(1)}, f32[8,128]{1,0:T(8,128)S(1)}, u32[]{:S(2)}, u32[]{:S(2)}) collective-permute-start(f32[8,128]{1,0:T(8,128)S(1)} %get-tuple-element.28), channel_id=1, source_target_pairs={{0,69},{1,70},{2,71},{3,64},{4,65},{5,66},{6,67},{7,68},{8,77},{9,... | collective-permute-start | bytes 12296 | tf_op jit(solution)/shard_map/ppermute | solution.py:664
  53.3 17.9 %collective-permute-start.8 = (f32[8,128]{1,0:T(8,128)S(1)}, f32[8,128]{1,0:T(8,128)S(1)}, u32[]{:S(2)}, u32[]{:S(2)}) collective-permute-start(f32[8,128]{1,0:T(8,128)S(1)} %get-tuple-element.28), channel_id=1, source_target_pairs={{0,67},{1,68},{2,69},{3,70},{4,71},{5,64},{6,65},{7,66},{8,75},{9,... | collective-permute-start | bytes 12296 | tf_op jit(solution)/shard_map/ppermute | solution.py:664
  58.8 12.3 %collective-permute-start.5 = (f32[8,128]{1,0:T(8,128)S(1)}, f32[8,128]{1,0:T(8,128)S(1)}, u32[]{:S(2)}, u32[]{:S(2)}) collective-permute-start(f32[8,128]{1,0:T(8,128)S(1)} %get-tuple-element.26), channel_id=1, source_target_pairs={{0,76},{1,77},{2,78},{3,79},{4,72},{5,73},{6,74},{7,75},{8,84},{9,... | collective-permute-start | bytes 12296 | tf_op jit(solution)/shard_map/ppermute | solution.py:664
  58.8 12.3 %collective-permute-start.6 = (f32[8,128]{1,0:T(8,128)S(1)}, f32[8,128]{1,0:T(8,128)S(1)}, u32[]{:S(2)}, u32[]{:S(2)}) collective-permute-start(f32[8,128]{1,0:T(8,128)S(1)} %get-tuple-element.27), channel_id=1, source_target_pairs={{0,124},{1,125},{2,126},{3,127},{4,120},{5,121},{6,122},{7,123},{8... | collective-permute-start | bytes 12296 | tf_op jit(solution)/shard_map/ppermute | solution.py:664

commit v5 on v2

--- a/solution.py
+++ b/solution.py
@@ -15,6 +15,7 @@
 SLOTS = CAP + 1
 HALF = 64
 CHUNKS = 16
+MIRROR = 4
 MIB = 1024 * 1024
 LIMIT = 58 * MIB
 ROW_VERT = 2 * PLANES
@@ -60,8 +61,8 @@
     return lax.broadcasted_iota(i32, (rows, T), 0)
 
 
-def inside():
-    gx, gy = lax.axis_index("gx"), lax.axis_index("gy")
+def inside(flip=0):
+    gx, gy = lax.axis_index("gx"), lax.axis_index("gy") ^ flip
     one = lambda test: jnp.where(test, 1.0, 0.0).astype(f32)
     return (
         one(gx > 0),
@@ -71,8 +72,8 @@
     )
 
 
-def column_keep(rows):
-    _, _, before, after = inside()
+def column_keep(rows, flip=0):
+    _, _, before, after = inside(flip)
     return jnp.where((lanes(rows) & 1) == 0, after, before)
 
 
@@ -236,7 +237,7 @@
 
     def slot_of(row, f):
         target = dest[f, row]
-        peer = lax.shift_right_logical(target, 7) & (PEERS - 1)
+        peer = (lax.shift_right_logical(target, 7) & (PEERS - 1)) ^ MIRROR
         live = f < count[0, row]
         at = used[peer]
         used[peer] = at + jnp.where(live, 1, 0)
@@ -312,6 +313,7 @@
         out_specs=HBM,
         out_shape=jax.ShapeDtypeStruct(block.shape, block.dtype),
         input_output_aliases={0: 0},
+        compiler_params=params(MIB),
         name="sealed",
     )(block, *after)
 
@@ -521,7 +523,7 @@
             out[v : v + 1, :] = total[row : row + 1, :] * keep
             out[NV + v : NV + v + 1, :] = total[row : row + 1, :] * keep
         acc = jnp.where((lane >> 1) == v, pltpu.roll(total, 2 * v + 1, 1), acc)
-    cols[...] = jnp.transpose(acc * column_keep(T))[0 : 2 * NV, :]
+    cols[...] = jnp.transpose(acc * column_keep(T, MIRROR))[0 : 2 * NV, :]
 
 
 def unpack(data, after):
@@ -600,19 +602,20 @@
     )(horiz, relax, mid, keep, imp, *imp_rows, *imp_cols)
 
 
-def shifted(block, axis, by, across=False):
+def shifted(block, axis, by):
     count = lax.axis_size(axis)
-    if not across:
-        return lax.ppermute(block, axis, [(i, (i + by) % count) for i in range(count)])
-    return lax.ppermute(
-        block,
-        ("comp", axis),
-        [
-            (c * count + i, (1 - c) * count + (i + by) % count)
-            for c in range(2)
-            for i in range(count)
-        ],
-    )
+    return lax.ppermute(block, axis, [(i, (i + by) % count) for i in range(count)])
+
+
+def crossed(block, gx_by=0, gy_by=0):
+    size = lax.axis_size("gx"), lax.axis_size("gy")
+    route = []
+    for c in range(2):
+        for i in range(size[0]):
+            for j in range(size[1]):
+                to = (i + gx_by) % size[0], ((j ^ MIRROR) + gy_by) % size[1]
+                route.append(((c * size[0] + i) * size[1] + j, ((1 - c) * size[0] + to[0]) * size[1] + to[1]))
+    return lax.ppermute(block, ("comp", "gx", "gy"), route)
 
 
 def local(
@@ -628,10 +631,10 @@
     packed = sealed(packed, left, right).reshape(PEERS, SLOTS, NV, T)
     packed = lax.all_to_all(packed, ("gx", "gy"), split_axis=0, concat_axis=0, tiled=True)
     mid, keep = two_steps(horiz_coef, tile, coef, sea, cols, top, bottom, left, right)
-    imp, first, last, cols = unpack(packed.reshape(PEERS * SLOTS * NV, T), keep)
-    imp = lax.ppermute(imp, "comp", [(0, 1), (1, 0)])
-    imp_rows = shifted(last, "gx", 1, True), shifted(first, "gx", -1, True)
-    imp_cols = shifted(cols, "gy", 1, True), shifted(cols, "gy", -1, True)
+    new, first, last, sides = unpack(packed.reshape(PEERS * SLOTS * NV, T), keep)
+    imp = crossed(new)
+    imp_rows = crossed(last, gx_by=1), crossed(first, gx_by=-1)
+    imp_cols = crossed(sides, gy_by=1), crossed(sides, gy_by=-1)
     return final(horiz_coef, couple_rate, mid, keep, imp, imp_rows, imp_cols)
 
 

time: 70.1 us -> 67.8 us (0.967)
  the two profiles are of different devices: /device:TPU:0 before, /device:TPU:4 now
where the time goes in v5:
time: 67.8 us; the launch traced here: 67.6 us
  Pallas kernels  26 us (38%)
  starting transfers between devices  24.4 us (36%)
  waiting for transfers between devices  14.8 us (22%)
  local copies, waits for them, and re-layouts  2.22 us (3%)
    ppermute x5, starting transfers between devices, crossed(): return lax.ppermute(block, ('comp', 'gx', 'gy'), route)  9.01 us
    pallas_call x1, Pallas kernels, two_steps(): pl.pallas_call(step_kernel, in_specs=[SMEM] + [VMEM] * 8, out_specs=[HBM,...  8.96 us
    pallas_call x1, Pallas kernels, remap(): pl.pallas_call(remap_kernel, in_specs=[HBM, HBM, VMEM, HBM, HBM], out_spe...  8.9 us
    all_to_all x1, starting transfers between devices, local(): lax.all_to_all(packed, ('gx', 'gy'), split_axis=0, concat_axis=0, tiled=T...  8.14 us
    all_to_all x1, waiting for transfers between devices, local(): lax.all_to_all(packed, ('gx', 'gy'), split_axis=0, concat_axis=0, tiled=T...  7.6 us
    ppermute x4, starting transfers between devices, shifted(): lax.ppermute(block, axis, [(i, (i + by) % count) for i in range(count)])  7.23 us
    ppermute x5, waiting for transfers between devices, crossed(): return lax.ppermute(block, ('comp', 'gx', 'gy'), route)  7.22 us
    pallas_call x1, Pallas kernels, outer_columns(): pl.pallas_call(column_kernel, in_specs=[HBM, HBM, HBM], out_specs=[VMEM]...  3.87 us
  transfers between devices with their start and end apart: 10, of which 3 were waited for; matrix products, arithmetic and copies ran while one was open for 0% of the time, Pallas kernels for 32%

profile of v5, /device:TPU:4, one launch (start us, length us, event | category | flops | bytes accessed | tf_op | source)
XLA Modules:
  0.0 67.6 jit_solution(4787390477442812349)
XLA Ops:
  0.0 1.9 %outer_rows.1 = (f32[144,128]{1,0:T(8,128)}, f32[144,128]{1,0:T(8,128)}) custom-call(f32[1,4,16,128,128]{4,3,2,1,0:T(8,128)} %state.3, f32[1,128,128]{2,1,0:T(8,128)} %vert.3, s32[1,128,128]{2,1,0:T(8,128)} %mask.3), custom_call_target="tpu_custom_call" | custom-call | flops 65536 | bytes 524288 | tf_op jit(solution)/shard_map/outer_rows/pallas_call | solution.py:109
  1.9 0.0 collective-permute-start
  2.0 3.5 %collective-permute-start.1 = (f32[144,128]{1,0:T(8,128)}, f32[144,128]{1,0:T(8,128)S(1)}, u32[]{:S(2)}, u32[]{:S(2)}) collective-permute-start(f32[144,128]{1,0:T(8,128)} %get-tuple-element.23), channel_id=1, source_target_pairs={{0,56},{8,0},{16,8},{24,16},{32,24},{40,32},{48,40},{56,48},{1,57}... | collective-permute-start | bytes 221192 | tf_op jit(solution)/shard_map/ppermute | solution.py:607
  5.5 3.9 %outer_columns.1 = (f32[384,128]{1,0:T(8,128)S(1)}, f32[512,128]{1,0:T(8,128)S(1)}, f32[4,16,128,128]{3,2,1,0:T(8,128)S(1)}, f32[128,128]{1,0:T(8,128)S(1)}, f32[128,128]{1,0:T(8,128)S(1)}) custom-call(f32[1,4,16,128,128]{4,3,2,1,0:T(8,128)} %state.3, f32[1,128,128]{2,1,0:T(8,128)S(1)} %copy-done.2, s32[1,128,128]{2,1,0:T(8,128)S(1)} %copy-done.3), custom_call_target="tpu_custom_call" | custom-call | flops 6291456 | bytes 9437184 | tf_op jit(solution)/shard_map/outer_columns/pallas_call | solution.py:161
  9.3 0.0 copy-start
  9.3 0.0 collective-permute-done.top
  9.4 0.1 with_corners.1.own.after
  9.5 3.7 %collective-permute-start.3 = (f32[400,128]{1,0:T(8,128)S(1)}, f32[400,128]{1,0:T(8,128)S(1)}, u32[]{:S(2)}, u32[]{:S(2)}) collective-permute-start(f32[400,128]{1,0:T(8,128)S(1)} %with_corners.1.own.after), channel_id=1, source_target_pairs={{0,7},{1,0},{2,1},{3,2},{4,3},{5,4},{6,5},{7,6},{8,15},{9,8},{10,9... | collective-permute-start | bytes 614408 | tf_op jit(solution)/shard_map/ppermute | solution.py:607
  13.2 8.9 %remap.1.refs_0_ = f32[576,4,128]{2,1,0:T(4,128)} custom-call(s32[4,128]{1,0:T(4,128)S(1)} %bitcast.7, s32[1,128]{1,0:T(1,128)S(1)} %bitcast.8, f32[512,128]{1,0:T(8,128)S(1)} %get-tuple-element.26.surf, bf16[1,128,1,4,128,128]{5,4,3,2,1,0:T(8,128)(2,1)} %weight.1, f32[400,128]{1,0:T(8,128)S(1)} %with_corners.1.own.after), custom_call_target="tpu_custom_call" | custom-call | flops 70254592 | bytes 20971520 | tf_op jit(solution)/shard_map/remap/pallas_call | solution.py:287
  22.1 0.0 copy-start.4
  22.2 8.1 %all-to-all-start = ((f32[64,9,4,128]{3,2,1,0:T(4,128)}), f32[64,9,4,128]{3,2,1,0:T(4,128)S(1)}, u32[]{:S(2)}, u32[]{:S(2)}) async-start(f32[64,9,4,128]{3,2,1,0:T(4,128)} %bitcast.3), calls=%async_computation | async-start | bytes 2359296 | tf_op jit(solution)/shard_map/all_to_all | solution.py:632
  30.3 0.0 copy-start.7
  30.4 0.0 copy-start.1
  30.4 2.2 %copy-done.1 = f32[4,16,128,128]{3,2,1,0:T(8,128)S(1)} copy-done((f32[4,16,128,128]{3,2,1,0:T(8,128)S(1)}, f32[4,16,128,128]{3,2,1,0:T(8,128)}, u32[]{:S(2)}) %copy-start.1) | copy-done | bytes 4194328
  32.5 9.0 %two_steps.1 = (f32[1,4,16,128,128]{4,3,2,1,0:T(8,128)}, f32[2064,128]{1,0:T(8,128)S(1)}) custom-call(f32[1,4]{1,0:T(1,128)S(1)} %copy-done.4, f32[4,16,128,128]{3,2,1,0:T(8,128)S(1)} %copy-done.1, f32[128,128]{1,0:T(8,128)S(1)} %get-tuple-element.19.coef, f32[128,128]{1,0:T(8,128)S(1)} %get-tuple-element.20.sea, f32[400,128]{1,0:T(8,128)S(1)} %with_corners.1.own.after, ...), custom_call_target="tpu_custom_call" | custom-call | flops 50331648 | bytes 10485760 | tf_op jit(solution)/shard_map/two_steps/pallas_call | solution.py:474
  41.5 7.6 %all-to-all-done = f32[64,9,4,128]{3,2,1,0:T(4,128)S(1)} async-done(((f32[64,9,4,128]{3,2,1,0:T(4,128)}), f32[64,9,4,128]{3,2,1,0:T(4,128)S(1)}, u32[]{:S(2)}, u32[]{:S(2)}) %all-to-all-start) | async-done | bytes 1179680 | tf_op jit(solution)/shard_map/all_to_all | solution.py:632
  49.1 0.6 unpack.1
  49.7 1.0 %collective-permute-start.4 = (f32[4,128,128]{2,1,0:T(8,128)S(1)}, f32[4,128,128]{2,1,0:T(8,128)S(1)}, u32[]{:S(2)}, u32[]{:S(2)}) collective-permute-start(f32[4,128,128]{2,1,0:T(8,128)S(1)} %get-tuple-element.27), channel_id=1, source_target_pairs={{0,68},{1,69},{2,70},{3,71},{4,64},{5,65},{6,66},{7,67},{8,76},{9,... | collective-permute-start | bytes 786440 | tf_op jit(solution)/shard_map/ppermute | solution.py:618
  50.6 1.0 %collective-permute-start.5 = (f32[8,128]{1,0:T(8,128)S(1)}, f32[8,128]{1,0:T(8,128)S(1)}, u32[]{:S(2)}, u32[]{:S(2)}) collective-permute-start(f32[8,128]{1,0:T(8,128)S(1)} %get-tuple-element.28), channel_id=1, source_target_pairs={{0,76},{1,77},{2,78},{3,79},{4,72},{5,73},{6,74},{7,75},{8,84},{9,... | collective-permute-start | bytes 12296 | tf_op jit(solution)/shard_map/ppermute | solution.py:618
  51.6 2.9 %collective-permute-start.6 = (f32[8,128]{1,0:T(8,128)S(1)}, f32[8,128]{1,0:T(8,128)S(1)}, u32[]{:S(2)}, u32[]{:S(2)}) collective-permute-start(f32[8,128]{1,0:T(8,128)S(1)} %get-tuple-element.29), channel_id=1, source_target_pairs={{0,124},{1,125},{2,126},{3,127},{4,120},{5,121},{6,122},{7,123},{8... | collective-permute-start | bytes 12296 | tf_op jit(solution)/shard_map/ppermute | solution.py:618
  54.5 4.2 %collective-permute-start.8 = (f32[8,128]{1,0:T(8,128)S(1)}, f32[8,128]{1,0:T(8,128)S(1)}, u32[]{:S(2)}, u32[]{:S(2)}) collective-permute-start(f32[8,128]{1,0:T(8,128)S(1)} %get-tuple-element.30), channel_id=1, source_target_pairs={{0,67},{1,68},{2,69},{3,70},{4,71},{5,64},{6,65},{7,66},{8,75},{9,... | collective-permute-start | bytes 12296 | tf_op jit(solution)/shard_map/ppermute | solution.py:618
  58.7 1.3 %collective-permute-done.8.imp_right = f32[8,128]{1,0:T(8,128)S(1)} collective-permute-done((f32[8,128]{1,0:T(8,128)S(1)}, f32[8,128]{1,0:T(8,128)S(1)}, u32[]{:S(2)}, u32[]{:S(2)}) %collective-permute-start.8) | collective-permute-done | bytes 4128 | tf_op jit(solution)/shard_map/ppermute | solution.py:618
  60.0 5.9 %collective-permute-done.7.imp_left = f32[8,128]{1,0:T(8,128)S(1)} collective-permute-done((f32[8,128]{1,0:T(8,128)S(1)}, f32[8,128]{1,0:T(8,128)S(1)}, u32[]{:S(2)}, u32[]{:S(2)}) %collective-permute-start.7) | collective-permute-done | bytes 4128 | tf_op jit(solution)/shard_map/ppermute | solution.py:618
  65.9 1.7 %final.1 = f32[1,4,16,128,128]{4,3,2,1,0:T(8,128)} custom-call(f32[1,4]{1,0:T(1,128)S(1)} %copy-done.4, f32[1,4]{1,0:T(1,128)S(1)} %copy-done.7, f32[1,4,16,128,128]{4,3,2,1,0:T(8,128)} %get-tuple-element.24.mid, f32[2064,128]{1,0:T(8,128)S(1)} %get-tuple-element.25.after.near, ...), custom_call_target="tpu_custom_call", output_to_operand_aliasing={{}: (2, {})} | custom-call | flops 2097152 | bytes 3145728 | tf_op jit(solution)/shard_map/final/pallas_call | solution.py:589
  (20 shorter events, 0.0 us)
Async XLA Ops:
  0.0 5.5 %copy-start.3 = (s32[1,128,128]{2,1,0:T(8,128)S(1)}, s32[1,128,128]{2,1,0:T(8,128)}, u32[]{:S(2)}) copy-start(s32[1,128,128]{2,1,0:T(8,128)} %mask.3) | copy-start | bytes 196612
  0.0 5.5 %copy-start.2 = (f32[1,128,128]{2,1,0:T(8,128)S(1)}, f32[1,128,128]{2,1,0:T(8,128)}, u32[]{:S(2)}) copy-start(f32[1,128,128]{2,1,0:T(8,128)} %vert.3) | copy-start | bytes 196612
  0.0 13.2 %copy-start.6 = (s32[1,128,1]{1,2,0:T(1,128)S(1)}, s32[1,128,1]{1,2,0:T(1,128)}, u32[]{:S(2)}) copy-start(s32[1,128,1]{1,2,0:T(1,128)} %param.14) | copy-start | bytes 1540
  0.0 13.2 %copy-start.5 = (s32[1,128,1,4]{1,3,2,0:T(4,128)S(1)}, s32[1,128,1,4]{1,3,2,0:T(4,128)}, u32[]{:S(2)}) copy-start(s32[1,128,1,4]{1,3,2,0:T(4,128)} %param.13) | copy-start | bytes 6148
  1.9 7.4 %collective-permute-start = (f32[144,128]{1,0:T(8,128)}, f32[144,128]{1,0:T(8,128)S(1)}, u32[]{:S(2)}, u32[]{:S(2)}) collective-permute-start(f32[144,128]{1,0:T(8,128)} %get-tuple-element.22), channel_id=1, source_target_pairs={{0,8},{8,16},{16,24},{24,32},{32,40},{40,48},{48,56},{56,0},{1,9},... | collective-permute-start | bytes 221192 | tf_op jit(solution)/shard_map/ppermute | solution.py:607
  2.0 7.4 %collective-permute-start.1 = (f32[144,128]{1,0:T(8,128)}, f32[144,128]{1,0:T(8,128)S(1)}, u32[]{:S(2)}, u32[]{:S(2)}) collective-permute-start(f32[144,128]{1,0:T(8,128)} %get-tuple-element.23), channel_id=1, source_target_pairs={{0,56},{8,0},{16,8},{24,16},{32,24},{40,32},{48,40},{56,48},{1,57}... | collective-permute-start | bytes 221192 | tf_op jit(solution)/shard_map/ppermute | solution.py:607
  9.3 12.8 %copy-start = (f32[4,16,128,128]{3,2,1,0:T(8,128)}, f32[4,16,128,128]{3,2,1,0:T(8,128)S(1)}, u32[]{:S(2)}) copy-start(f32[4,16,128,128]{3,2,1,0:T(8,128)S(1)} %get-tuple-element.18.u) | copy-start | bytes 12582916
  9.5 12.7 %collective-permute-start.3 = (f32[400,128]{1,0:T(8,128)S(1)}, f32[400,128]{1,0:T(8,128)S(1)}, u32[]{:S(2)}, u32[]{:S(2)}) collective-permute-start(f32[400,128]{1,0:T(8,128)S(1)} %with_corners.1.own.after), channel_id=1, source_target_pairs={{0,7},{1,0},{2,1},{3,2},{4,3},{5,4},{6,5},{7,6},{8,15},{9,8},{10,9... | collective-permute-start | bytes 614408 | tf_op jit(solution)/shard_map/ppermute | solution.py:607
  13.2 8.9 %collective-permute-start.2 = (f32[400,128]{1,0:T(8,128)S(1)}, f32[400,128]{1,0:T(8,128)S(1)}, u32[]{:S(2)}, u32[]{:S(2)}) collective-permute-start(f32[400,128]{1,0:T(8,128)S(1)} %with_corners.1.own.after), channel_id=1, source_target_pairs={{0,1},{1,2},{2,3},{3,4},{4,5},{5,6},{6,7},{7,0},{8,9},{9,10},{10,1... | collective-permute-start | bytes 614408 | tf_op jit(solution)/shard_map/ppermute | solution.py:607
  22.1 8.2 %copy-start.4 = (f32[1,4]{1,0:T(1,128)S(1)}, f32[1,4]{1,0:T(1,128)}, u32[]{:S(2)}) copy-start(f32[1,4]{1,0:T(1,128)} %horiz.1) | copy-start | bytes 52
  22.2 26.9 %all-to-all-start = ((f32[64,9,4,128]{3,2,1,0:T(4,128)}), f32[64,9,4,128]{3,2,1,0:T(4,128)S(1)}, u32[]{:S(2)}, u32[]{:S(2)}) async-start(f32[64,9,4,128]{3,2,1,0:T(4,128)} %bitcast.3), calls=%async_computation | async-start | bytes 2359296 | tf_op jit(solution)/shard_map/all_to_all | solution.py:632
  30.3 35.6 %copy-start.7 = (f32[1,4]{1,0:T(1,128)S(1)}, f32[1,4]{1,0:T(1,128)}, u32[]{:S(2)}) copy-start(f32[1,4]{1,0:T(1,128)} %relax.1) | copy-start | bytes 52
  30.4 2.2 %copy-start.1 = (f32[4,16,128,128]{3,2,1,0:T(8,128)S(1)}, f32[4,16,128,128]{3,2,1,0:T(8,128)}, u32[]{:S(2)}) copy-start(f32[4,16,128,128]{3,2,1,0:T(8,128)} %copy-done) | copy-start | bytes 12582916
  49.7 16.2 %collective-permute-start.4 = (f32[4,128,128]{2,1,0:T(8,128)S(1)}, f32[4,128,128]{2,1,0:T(8,128)S(1)}, u32[]{:S(2)}, u32[]{:S(2)}) collective-permute-start(f32[4,128,128]{2,1,0:T(8,128)S(1)} %get-tuple-element.27), channel_id=1, source_target_pairs={{0,68},{1,69},{2,70},{3,71},{4,64},{5,65},{6,66},{7,67},{8,76},{9,... | collective-permute-start | bytes 786440 | tf_op jit(solution)/shard_map/ppermute | solution.py:618
  50.6 8.1 %collective-permute-start.5 = (f32[8,128]{1,0:T(8,128)S(1)}, f32[8,128]{1,0:T(8,128)S(1)}, u32[]{:S(2)}, u32[]{:S(2)}) collective-permute-start(f32[8,128]{1,0:T(8,128)S(1)} %get-tuple-element.28), channel_id=1, source_target_pairs={{0,76},{1,77},{2,78},{3,79},{4,72},{5,73},{6,74},{7,75},{8,84},{9,... | collective-permute-start | bytes 12296 | tf_op jit(solution)/shard_map/ppermute | solution.py:618
  51.6 7.1 %collective-permute-start.6 = (f32[8,128]{1,0:T(8,128)S(1)}, f32[8,128]{1,0:T(8,128)S(1)}, u32[]{:S(2)}, u32[]{:S(2)}) collective-permute-start(f32[8,128]{1,0:T(8,128)S(1)} %get-tuple-element.29), channel_id=1, source_target_pairs={{0,124},{1,125},{2,126},{3,127},{4,120},{5,121},{6,122},{7,123},{8... | collective-permute-start | bytes 12296 | tf_op jit(solution)/shard_map/ppermute | solution.py:618
  54.5 5.5 %collective-permute-start.8 = (f32[8,128]{1,0:T(8,128)S(1)}, f32[8,128]{1,0:T(8,128)S(1)}, u32[]{:S(2)}, u32[]{:S(2)}) collective-permute-start(f32[8,128]{1,0:T(8,128)S(1)} %get-tuple-element.30), channel_id=1, source_target_pairs={{0,67},{1,68},{2,69},{3,70},{4,71},{5,64},{6,65},{7,66},{8,75},{9,... | collective-permute-start | bytes 12296 | tf_op jit(solution)/shard_map/ppermute | solution.py:618
  58.7 7.2 %collective-permute-start.7 = (f32[8,128]{1,0:T(8,128)S(1)}, f32[8,128]{1,0:T(8,128)S(1)}, u32[]{:S(2)}, u32[]{:S(2)}) collective-permute-start(f32[8,128]{1,0:T(8,128)S(1)} %get-tuple-element.30), channel_id=1, source_target_pairs={{0,69},{1,70},{2,71},{3,64},{4,65},{5,66},{6,67},{7,68},{8,77},{9,... | collective-permute-start | bytes 12296 | tf_op jit(solution)/shard_map/ppermute | solution.py:618

commit v6 on v5

--- a/solution.py
+++ b/solution.py
@@ -124,7 +124,7 @@
     )(state, vert, mask)
 
 
-def column_kernel(state, vert, mask, cols, surf, tile, coef, wet, sea, sems):
+def column_kernel(state, vert, mask, cols, surf, coef, wet, tile, sea, sems):
     loads = [pltpu.make_async_copy(state.at[0, v], tile.at[v], sems.at[v]) for v in range(NV)]
     loads.append(pltpu.make_async_copy(vert.at[0], coef, sems.at[NV]))
     loads.append(pltpu.make_async_copy(mask.at[0], sea, sems.at[NV + 1]))
@@ -161,16 +161,19 @@
     return pl.pallas_call(
         column_kernel,
         in_specs=[HBM, HBM, HBM],
-        out_specs=[VMEM] * 5,
+        out_specs=[VMEM] * 4,
         out_shape=[
             jax.ShapeDtypeStruct((COL_TOP, T), f32),
             jax.ShapeDtypeStruct((T * NV, T), f32),
-            jax.ShapeDtypeStruct((NV, LEV, T, T), f32),
             square,
             square,
         ],
-        scratch_shapes=[pltpu.VMEM((T, T), i32), pltpu.SemaphoreType.DMA((NV + 2,))],
-        compiler_params=params(47 * MIB),
+        scratch_shapes=[
+            pltpu.VMEM((NV, LEV, T, T), f32),
+            pltpu.VMEM((T, T), i32),
+            pltpu.SemaphoreType.DMA((NV + 2,)),
+        ],
+        compiler_params=params(51 * MIB),
         cost_estimate=cost(6 << 20, 9 << 20),
         name="outer_columns",
     )(state, vert, mask)
@@ -237,7 +240,8 @@
 
     def slot_of(row, f):
         target = dest[f, row]
-        peer = (lax.shift_right_logical(target, 7) & (PEERS - 1)) ^ MIRROR
+        device = (lax.shift_right_logical(target, 7) & (PEERS - 1)) ^ MIRROR
+        peer = (device & 7) * 8 + (device >> 3)
         live = f < count[0, row]
         at = used[peer]
         used[peer] = at + jnp.where(live, 1, 0)
@@ -269,7 +273,7 @@
         return 0
 
     lax.fori_loop(0, CHUNKS, chunk, 0)
-    me = lax.axis_index("gx") * lax.axis_size("gy") + lax.axis_index("gy")
+    me = lax.axis_index("gy") * lax.axis_size("gx") + lax.axis_index("gx")
     place = lax.broadcasted_iota(i32, (NV, T), 0) * T + lax.broadcasted_iota(i32, (NV, T), 1)
     place = place - me * CAP
 
@@ -387,16 +391,20 @@
 
 
 def step_kernel(
-    rate, u, coef, sea, own, top, bottom, near, far,
-    out, keep, w, stage, inner, top1, bottom1, top2, bottom2, side1, side2, turned, sems,
+    rate, state, coef, sea, own, top, bottom, near, far,
+    out, keep, u, w, stage, inner, top1, bottom1, top2, bottom2, side1, side2, turned, sems,
 ):
     def emit(v):
         levels = pl.ds(2, LEV - 2)
         return pltpu.make_async_copy(stage.at[v], out.at[0, v, levels], sems.at[v])
 
+    loads = [pltpu.make_async_copy(state.at[0, v], u.at[v], sems.at[v]) for v in range(NV)]
+    for load in loads:
+        load.start()
     up, down, _, _ = inside()
     side1[...], side2[...] = halo_columns(rate, near, far, own)
     for v in range(NV):
+        loads[v].wait()
         at = v * LEV
         for l in range(LEV):
             inner[0, at + l : at + l + 1, :] = u[v, l, 0:1, :] * up
@@ -468,18 +476,19 @@
         emit(v).wait()
 
 
-def two_steps(rate, u, coef, sea, own, top, bottom, left, right):
+def two_steps(rate, state, coef, sea, own, top, bottom, left, right):
     rows = pltpu.VMEM((NV, LEV, T), f32)
     square = pltpu.VMEM((T, T), f32)
     return pl.pallas_call(
         step_kernel,
-        in_specs=[SMEM] + [VMEM] * 8,
+        in_specs=[SMEM, HBM] + [VMEM] * 7,
         out_specs=[HBM, VMEM],
         out_shape=[
-            jax.ShapeDtypeStruct((1,) + u.shape, f32),
+            jax.ShapeDtypeStruct(state.shape, f32),
             jax.ShapeDtypeStruct((KEEP_SIZE, T), f32),
         ],
         scratch_shapes=[
+            pltpu.VMEM((NV, LEV, T, T), f32),
             pltpu.VMEM((NV, LEV, T, T), f32),
             pltpu.VMEM((NV, LEV - 2, T, T), f32),
             pltpu.VMEM((2, PLANES, T), f32),
@@ -492,10 +501,10 @@
             square,
             pltpu.SemaphoreType.DMA((NV,)),
         ],
-        compiler_params=params(16 * MIB),
+        compiler_params=params(20 * MIB),
         cost_estimate=cost(48 << 20, 10 << 20),
         name="two_steps",
-    )(rate, u, coef, sea, own, top, bottom, left, right)
+    )(rate, state, coef, sea, own, top, bottom, left, right)
 
 
 def unpack_kernel(data, after, imp, first, last, cols):
@@ -623,14 +632,14 @@
 ):
     head, tail = outer_rows(state, vert_coef, sea_mask)
     top, bottom = shifted(tail, "gx", 1), shifted(head, "gx", -1)
-    cols, surf, tile, coef, sea = outer_columns(state, vert_coef, sea_mask)
+    cols, surf, coef, sea = outer_columns(state, vert_coef, sea_mask)
     cols = with_corners(cols, top, bottom)
     left, right = shifted(cols, "gy", 1), shifted(cols, "gy", -1)
     dest = dest_block.reshape(T, FAN).T
     packed = remap(dest, entry_count.reshape(1, T), surf, remap_weight, cols)
     packed = sealed(packed, left, right).reshape(PEERS, SLOTS, NV, T)
-    packed = lax.all_to_all(packed, ("gx", "gy"), split_axis=0, concat_axis=0, tiled=True)
-    mid, keep = two_steps(horiz_coef, tile, coef, sea, cols, top, bottom, left, right)
+    packed = lax.all_to_all(packed, ("gy", "gx"), split_axis=0, concat_axis=0, tiled=True)
+    mid, keep = two_steps(horiz_coef, state, coef, sea, cols, top, bottom, left, right)
     new, first, last, sides = unpack(packed.reshape(PEERS * SLOTS * NV, T), keep)
     imp = crossed(new)
     imp_rows = crossed(last, gx_by=1), crossed(first, gx_by=-1)

time: 67.8 us -> 68.9 us (1.016)
  the two profiles are of different devices: /device:TPU:4 before, /device:TPU:2 now
where the time goes in v6:
time: 68.9 us; the launch traced here: 68.7 us
  Pallas kernels  26.8 us (39%)
  starting transfers between devices  24.8 us (36%)
  waiting for transfers between devices  14.6 us (21%)
  local copies, waits for them, and re-layouts  2.21 us (3%)
    pallas_call x1, Pallas kernels, two_steps(): pl.pallas_call(step_kernel, in_specs=[SMEM, HBM] + [VMEM] * 7, out_specs=...  9.36 us
    pallas_call x1, Pallas kernels, remap(): pl.pallas_call(remap_kernel, in_specs=[HBM, HBM, VMEM, HBM, HBM], out_spe...  9.32 us
    all_to_all x1, starting transfers between devices, local(): lax.all_to_all(packed, ('gy', 'gx'), split_axis=0, concat_axis=0, tiled=T...  9.28 us
    ppermute x5, starting transfers between devices, crossed(): return lax.ppermute(block, ('comp', 'gx', 'gy'), route)  9 us
    all_to_all x1, waiting for transfers between devices, local(): lax.all_to_all(packed, ('gy', 'gx'), split_axis=0, concat_axis=0, tiled=T...  7.4 us
    ppermute x5, waiting for transfers between devices, crossed(): return lax.ppermute(block, ('comp', 'gx', 'gy'), route)  7.22 us
    ppermute x4, starting transfers between devices, shifted(): lax.ppermute(block, axis, [(i, (i + by) % count) for i in range(count)])  6.56 us
    pallas_call x1, Pallas kernels, outer_columns(): pl.pallas_call(column_kernel, in_specs=[HBM, HBM, HBM], out_specs=[VMEM]...  3.86 us
  transfers between devices with their start and end apart: 10, of which 3 were waited for; matrix products, arithmetic and copies ran while one was open for 0% of the time, Pallas kernels for 33%

profile of v6, /device:TPU:2, one launch (start us, length us, event | category | flops | bytes accessed | tf_op | source)
XLA Modules:
  0.0 68.7 jit_solution(12318878180530018400)
XLA Ops:
  0.0 1.9 %outer_rows.1 = (f32[144,128]{1,0:T(8,128)}, f32[144,128]{1,0:T(8,128)}) custom-call(f32[1,4,16,128,128]{4,3,2,1,0:T(8,128)} %state.5, f32[1,128,128]{2,1,0:T(8,128)} %vert.3, s32[1,128,128]{2,1,0:T(8,128)} %mask.3), custom_call_target="tpu_custom_call" | custom-call | flops 65536 | bytes 524288 | tf_op jit(solution)/shard_map/outer_rows/pallas_call | solution.py:109
  1.9 0.0 collective-permute-start
  2.0 3.5 %collective-permute-start.1 = (f32[144,128]{1,0:T(8,128)}, f32[144,128]{1,0:T(8,128)S(1)}, u32[]{:S(2)}, u32[]{:S(2)}) collective-permute-start(f32[144,128]{1,0:T(8,128)} %get-tuple-element.21), channel_id=1, source_target_pairs={{0,56},{8,0},{16,8},{24,16},{32,24},{40,32},{48,40},{56,48},{1,57}... | collective-permute-start | bytes 221192 | tf_op jit(solution)/shard_map/ppermute | solution.py:616
  5.5 3.9 %outer_columns.1 = (f32[384,128]{1,0:T(8,128)S(1)}, f32[512,128]{1,0:T(8,128)S(1)}, f32[128,128]{1,0:T(8,128)S(1)}, f32[128,128]{1,0:T(8,128)S(1)}) custom-call(f32[1,4,16,128,128]{4,3,2,1,0:T(8,128)} %state.5, f32[1,128,128]{2,1,0:T(8,128)S(1)} %copy-done.1, s32[1,128,128]{2,1,0:T(8,128)S(1)} %copy-done.2), custom_call_target="tpu_custom_call" | custom-call | flops 6291456 | bytes 9437184 | tf_op jit(solution)/shard_map/outer_columns/pallas_call | solution.py:161
  9.3 0.0 collective-permute-done.top
  9.3 0.0 collective-permute-done.1.bottom
  9.3 0.1 with_corners.1.own.after
  9.5 3.1 %collective-permute-start.3 = (f32[400,128]{1,0:T(8,128)S(1)}, f32[400,128]{1,0:T(8,128)S(1)}, u32[]{:S(2)}, u32[]{:S(2)}) collective-permute-start(f32[400,128]{1,0:T(8,128)S(1)} %with_corners.1.own.after), channel_id=1, source_target_pairs={{0,7},{1,0},{2,1},{3,2},{4,3},{5,4},{6,5},{7,6},{8,15},{9,8},{10,9... | collective-permute-start | bytes 614408 | tf_op jit(solution)/shard_map/ppermute | solution.py:616
  12.5 0.0 collective-permute-start.2
  12.5 9.3 %remap.1.refs_0_ = f32[576,4,128]{2,1,0:T(4,128)} custom-call(s32[4,128]{1,0:T(4,128)S(1)} %bitcast.7, s32[1,128]{1,0:T(1,128)S(1)} %bitcast.8, f32[512,128]{1,0:T(8,128)S(1)} %get-tuple-element.24.surf, bf16[1,128,1,4,128,128]{5,4,3,2,1,0:T(8,128)(2,1)} %weight.1, f32[400,128]{1,0:T(8,128)S(1)} %with_corners.1.own.after), custom_call_target="tpu_custom_call" | custom-call | flops 70254592 | bytes 20971520 | tf_op jit(solution)/shard_map/remap/pallas_call | solution.py:291
  21.9 0.0 copy-start.3
  21.9 9.3 %all-to-all-start = ((f32[64,9,4,128]{3,2,1,0:T(4,128)}), f32[64,9,4,128]{3,2,1,0:T(4,128)S(1)}, u32[]{:S(2)}, u32[]{:S(2)}) async-start(f32[64,9,4,128]{3,2,1,0:T(4,128)} %bitcast.3), calls=%async_computation | async-start | bytes 2359296 | tf_op jit(solution)/shard_map/all_to_all | solution.py:641
  31.2 0.0 copy-start.6
  31.2 0.0 copy-start
  31.2 2.2 %copy-done = f32[1,4,16,128,128]{4,3,2,1,0:T(8,128)S(1)} copy-done((f32[1,4,16,128,128]{4,3,2,1,0:T(8,128)S(1)}, f32[1,4,16,128,128]{4,3,2,1,0:T(8,128)}, u32[]{:S(2)}) %copy-start) | copy-done | bytes 4194328
  33.4 9.4 %two_steps.1 = (f32[1,4,16,128,128]{4,3,2,1,0:T(8,128)}, f32[2064,128]{1,0:T(8,128)S(1)}) custom-call(f32[1,4]{1,0:T(1,128)S(1)} %copy-done.3, f32[1,4,16,128,128]{4,3,2,1,0:T(8,128)S(1)} %copy-done, f32[128,128]{1,0:T(8,128)S(1)} %get-tuple-element.17.coef, f32[128,128]{1,0:T(8,128)S(1)} %get-tuple-element.18.sea, f32[400,128]{1,0:T(8,128)S(1)} %with_corners.1.own.after, ...), custom_call_target="tpu_custom_call" | custom-call | flops 50331648 | bytes 10485760 | tf_op jit(solution)/shard_map/two_steps/pallas_call | solution.py:482
  42.8 7.4 %all-to-all-done = f32[64,9,4,128]{3,2,1,0:T(4,128)S(1)} async-done(((f32[64,9,4,128]{3,2,1,0:T(4,128)}), f32[64,9,4,128]{3,2,1,0:T(4,128)S(1)}, u32[]{:S(2)}, u32[]{:S(2)}) %all-to-all-start) | async-done | bytes 1179680 | tf_op jit(solution)/shard_map/all_to_all | solution.py:641
  50.2 0.6 unpack.1
  50.8 0.7 collective-permute-start.4
  51.4 3.9 %collective-permute-start.6 = (f32[8,128]{1,0:T(8,128)S(1)}, f32[8,128]{1,0:T(8,128)S(1)}, u32[]{:S(2)}, u32[]{:S(2)}) collective-permute-start(f32[8,128]{1,0:T(8,128)S(1)} %get-tuple-element.27), channel_id=1, source_target_pairs={{0,124},{1,125},{2,126},{3,127},{4,120},{5,121},{6,122},{7,123},{8... | collective-permute-start | bytes 12296 | tf_op jit(solution)/shard_map/ppermute | solution.py:627
  55.3 4.5 %collective-permute-start.8 = (f32[8,128]{1,0:T(8,128)S(1)}, f32[8,128]{1,0:T(8,128)S(1)}, u32[]{:S(2)}, u32[]{:S(2)}) collective-permute-start(f32[8,128]{1,0:T(8,128)S(1)} %get-tuple-element.28), channel_id=1, source_target_pairs={{0,67},{1,68},{2,69},{3,70},{4,71},{5,64},{6,65},{7,66},{8,75},{9,... | collective-permute-start | bytes 12296 | tf_op jit(solution)/shard_map/ppermute | solution.py:627
  59.8 1.3 %collective-permute-done.8.imp_right = f32[8,128]{1,0:T(8,128)S(1)} collective-permute-done((f32[8,128]{1,0:T(8,128)S(1)}, f32[8,128]{1,0:T(8,128)S(1)}, u32[]{:S(2)}, u32[]{:S(2)}) %collective-permute-start.8) | collective-permute-done | bytes 4128 | tf_op jit(solution)/shard_map/ppermute | solution.py:627
  61.1 5.9 %collective-permute-done.7.imp_left = f32[8,128]{1,0:T(8,128)S(1)} collective-permute-done((f32[8,128]{1,0:T(8,128)S(1)}, f32[8,128]{1,0:T(8,128)S(1)}, u32[]{:S(2)}, u32[]{:S(2)}) %collective-permute-start.7) | collective-permute-done | bytes 4128 | tf_op jit(solution)/shard_map/ppermute | solution.py:627
  67.0 1.7 %final.1 = f32[1,4,16,128,128]{4,3,2,1,0:T(8,128)} custom-call(f32[1,4]{1,0:T(1,128)S(1)} %copy-done.3, f32[1,4]{1,0:T(1,128)S(1)} %copy-done.6, f32[1,4,16,128,128]{4,3,2,1,0:T(8,128)} %get-tuple-element.22.mid, f32[2064,128]{1,0:T(8,128)S(1)} %get-tuple-element.23.after.near, ...), custom_call_target="tpu_custom_call", output_to_operand_aliasing={{}: (2, {})} | custom-call | flops 2097152 | bytes 3145728 | tf_op jit(solution)/shard_map/final/pallas_call | solution.py:598
  (18 shorter events, 0.0 us)
Async XLA Ops:
  0.0 5.5 %copy-start.2 = (s32[1,128,128]{2,1,0:T(8,128)S(1)}, s32[1,128,128]{2,1,0:T(8,128)}, u32[]{:S(2)}) copy-start(s32[1,128,128]{2,1,0:T(8,128)} %mask.3) | copy-start | bytes 196612
  0.0 5.5 %copy-start.1 = (f32[1,128,128]{2,1,0:T(8,128)S(1)}, f32[1,128,128]{2,1,0:T(8,128)}, u32[]{:S(2)}) copy-start(f32[1,128,128]{2,1,0:T(8,128)} %vert.3) | copy-start | bytes 196612
  0.0 12.5 %copy-start.5 = (s32[1,128,1]{1,2,0:T(1,128)S(1)}, s32[1,128,1]{1,2,0:T(1,128)}, u32[]{:S(2)}) copy-start(s32[1,128,1]{1,2,0:T(1,128)} %param.14) | copy-start | bytes 1540
  0.0 12.5 %copy-start.4 = (s32[1,128,1,4]{1,3,2,0:T(4,128)S(1)}, s32[1,128,1,4]{1,3,2,0:T(4,128)}, u32[]{:S(2)}) copy-start(s32[1,128,1,4]{1,3,2,0:T(4,128)} %param.13) | copy-start | bytes 6148
  1.9 7.4 %collective-permute-start = (f32[144,128]{1,0:T(8,128)}, f32[144,128]{1,0:T(8,128)S(1)}, u32[]{:S(2)}, u32[]{:S(2)}) collective-permute-start(f32[144,128]{1,0:T(8,128)} %get-tuple-element.20), channel_id=1, source_target_pairs={{0,8},{8,16},{16,24},{24,32},{32,40},{40,48},{48,56},{56,0},{1,9},... | collective-permute-start | bytes 221192 | tf_op jit(solution)/shard_map/ppermute | solution.py:616
  2.0 7.4 %collective-permute-start.1 = (f32[144,128]{1,0:T(8,128)}, f32[144,128]{1,0:T(8,128)S(1)}, u32[]{:S(2)}, u32[]{:S(2)}) collective-permute-start(f32[144,128]{1,0:T(8,128)} %get-tuple-element.21), channel_id=1, source_target_pairs={{0,56},{8,0},{16,8},{24,16},{32,24},{40,32},{48,40},{56,48},{1,57}... | collective-permute-start | bytes 221192 | tf_op jit(solution)/shard_map/ppermute | solution.py:616
  9.5 12.4 %collective-permute-start.3 = (f32[400,128]{1,0:T(8,128)S(1)}, f32[400,128]{1,0:T(8,128)S(1)}, u32[]{:S(2)}, u32[]{:S(2)}) collective-permute-start(f32[400,128]{1,0:T(8,128)S(1)} %with_corners.1.own.after), channel_id=1, source_target_pairs={{0,7},{1,0},{2,1},{3,2},{4,3},{5,4},{6,5},{7,6},{8,15},{9,8},{10,9... | collective-permute-start | bytes 614408 | tf_op jit(solution)/shard_map/ppermute | solution.py:616
  12.5 9.4 %collective-permute-start.2 = (f32[400,128]{1,0:T(8,128)S(1)}, f32[400,128]{1,0:T(8,128)S(1)}, u32[]{:S(2)}, u32[]{:S(2)}) collective-permute-start(f32[400,128]{1,0:T(8,128)S(1)} %with_corners.1.own.after), channel_id=1, source_target_pairs={{0,1},{1,2},{2,3},{3,4},{4,5},{5,6},{6,7},{7,0},{8,9},{9,10},{10,1... | collective-permute-start | bytes 614408 | tf_op jit(solution)/shard_map/ppermute | solution.py:616
  21.9 9.3 %copy-start.3 = (f32[1,4]{1,0:T(1,128)S(1)}, f32[1,4]{1,0:T(1,128)}, u32[]{:S(2)}) copy-start(f32[1,4]{1,0:T(1,128)} %horiz.1) | copy-start | bytes 52
  21.9 28.3 %all-to-all-start = ((f32[64,9,4,128]{3,2,1,0:T(4,128)}), f32[64,9,4,128]{3,2,1,0:T(4,128)S(1)}, u32[]{:S(2)}, u32[]{:S(2)}) async-start(f32[64,9,4,128]{3,2,1,0:T(4,128)} %bitcast.3), calls=%async_computation | async-start | bytes 2359296 | tf_op jit(solution)/shard_map/all_to_all | solution.py:641
  31.2 35.8 %copy-start.6 = (f32[1,4]{1,0:T(1,128)S(1)}, f32[1,4]{1,0:T(1,128)}, u32[]{:S(2)}) copy-start(f32[1,4]{1,0:T(1,128)} %relax.1) | copy-start | bytes 52
  31.2 2.2 %copy-start = (f32[1,4,16,128,128]{4,3,2,1,0:T(8,128)S(1)}, f32[1,4,16,128,128]{4,3,2,1,0:T(8,128)}, u32[]{:S(2)}) copy-start(f32[1,4,16,128,128]{4,3,2,1,0:T(8,128)} %state.5) | copy-start | bytes 12582916
  50.8 16.2 %collective-permute-start.4 = (f32[4,128,128]{2,1,0:T(8,128)S(1)}, f32[4,128,128]{2,1,0:T(8,128)S(1)}, u32[]{:S(2)}, u32[]{:S(2)}) collective-permute-start(f32[4,128,128]{2,1,0:T(8,128)S(1)} %get-tuple-element.25), channel_id=1, source_target_pairs={{0,68},{1,69},{2,70},{3,71},{4,64},{5,65},{6,66},{7,67},{8,76},{9,... | collective-permute-start | bytes 786440 | tf_op jit(solution)/shard_map/ppermute | solution.py:627
  51.4 8.3 %collective-permute-start.5 = (f32[8,128]{1,0:T(8,128)S(1)}, f32[8,128]{1,0:T(8,128)S(1)}, u32[]{:S(2)}, u32[]{:S(2)}) collective-permute-start(f32[8,128]{1,0:T(8,128)S(1)} %get-tuple-element.26), channel_id=1, source_target_pairs={{0,76},{1,77},{2,78},{3,79},{4,72},{5,73},{6,74},{7,75},{8,84},{9,... | collective-permute-start | bytes 12296 | tf_op jit(solution)/shard_map/ppermute | solution.py:627
  51.4 8.3 %collective-permute-start.6 = (f32[8,128]{1,0:T(8,128)S(1)}, f32[8,128]{1,0:T(8,128)S(1)}, u32[]{:S(2)}, u32[]{:S(2)}) collective-permute-start(f32[8,128]{1,0:T(8,128)S(1)} %get-tuple-element.27), channel_id=1, source_target_pairs={{0,124},{1,125},{2,126},{3,127},{4,120},{5,121},{6,122},{7,123},{8... | collective-permute-start | bytes 12296 | tf_op jit(solution)/shard_map/ppermute | solution.py:627
  55.3 5.8 %collective-permute-start.8 = (f32[8,128]{1,0:T(8,128)S(1)}, f32[8,128]{1,0:T(8,128)S(1)}, u32[]{:S(2)}, u32[]{:S(2)}) collective-permute-start(f32[8,128]{1,0:T(8,128)S(1)} %get-tuple-element.28), channel_id=1, source_target_pairs={{0,67},{1,68},{2,69},{3,70},{4,71},{5,64},{6,65},{7,66},{8,75},{9,... | collective-permute-start | bytes 12296 | tf_op jit(solution)/shard_map/ppermute | solution.py:627
  59.8 7.2 %collective-permute-start.7 = (f32[8,128]{1,0:T(8,128)S(1)}, f32[8,128]{1,0:T(8,128)S(1)}, u32[]{:S(2)}, u32[]{:S(2)}) collective-permute-start(f32[8,128]{1,0:T(8,128)S(1)} %get-tuple-element.28), channel_id=1, source_target_pairs={{0,69},{1,70},{2,71},{3,64},{4,65},{5,66},{6,67},{7,68},{8,77},{9,... | collective-permute-start | bytes 12296 | tf_op jit(solution)/shard_map/ppermute | solution.py:627

commit v7 on v6

--- a/solution.py
+++ b/solution.py
@@ -12,7 +12,8 @@
 FAN = 4
 CAP = 8
 PEERS = 64
-SLOTS = CAP + 1
+SIZE = CAP * NV + 1
+EDGE = 32
 HALF = 64
 CHUNKS = 16
 MIRROR = 4
@@ -61,8 +62,8 @@
     return lax.broadcasted_iota(i32, (rows, T), 0)
 
 
-def inside(flip=0):
-    gx, gy = lax.axis_index("gx"), lax.axis_index("gy") ^ flip
+def inside():
+    gx, gy = lax.axis_index("gx"), lax.axis_index("gy")
     one = lambda test: jnp.where(test, 1.0, 0.0).astype(f32)
     return (
         one(gx > 0),
@@ -72,8 +73,8 @@
     )
 
 
-def column_keep(rows, flip=0):
-    _, _, before, after = inside(flip)
+def column_keep(rows):
+    _, _, before, after = inside()
     return jnp.where((lanes(rows) & 1) == 0, after, before)
 
 
@@ -209,7 +210,9 @@
     )(cols, top, bottom)
 
 
-def remap_kernel(dest_in, count_in, surf, weight, after, out, blocks, dest, count, used, label, sems):
+def remap_kernel(
+    dest_in, count_in, surf, weight, after, out, blocks, buffer, names, dest, count, used, label, sems
+):
     del after
     rows = T // CHUNKS
     lists = [
@@ -225,7 +228,7 @@
 
     for c in range(CHUNKS):
         fetch(c).start()
-    out[...] = jnp.zeros_like(out)
+    buffer[...] = jnp.zeros_like(buffer)
 
     def clear(i, _):
         used[i] = 0
@@ -238,21 +241,20 @@
         copy.wait()
     sub = subl(8)
 
-    def slot_of(row, f):
+    def place_of(row, f):
         target = dest[f, row]
-        device = (lax.shift_right_logical(target, 7) & (PEERS - 1)) ^ MIRROR
-        peer = (device & 7) * 8 + (device >> 3)
+        peer = (lax.shift_right_logical(target, 7) & (PEERS - 1)) ^ MIRROR
         live = f < count[0, row]
         at = used[peer]
         used[peer] = at + jnp.where(live, 1, 0)
         label[jnp.where(live, peer * CAP + at, PEERS * CAP)] = (target & (T - 1)) + 1
-        return jnp.where(live, peer * SLOTS + at, CAP)
+        return jnp.where(live, peer * SIZE + at * NV, PEERS * SIZE)
 
     def chunk(c, _):
         fetch(c).wait()
         for r in range(0, rows, 2):
             row = c * rows + r
-            slots = [[slot_of(row + q, f) for f in range(FAN)] for q in range(2)]
+            places = [[place_of(row + q, f) for f in range(FAN)] for q in range(2)]
             pair = surf[pl.ds(pl.multiple_of(row * NV, 8), 8), :]
             pair = jnp.concatenate(
                 [jnp.where(sub < NV, pair, 0.0), jnp.where(sub >= NV, pair, 0.0)], axis=1
@@ -269,32 +271,48 @@
                 for q in range(2):
                     for g in range(2):
                         part = product[q * NV : (q + 1) * NV, g * T : (g + 1) * T]
-                        out[slots[q][f + g]] = part
+                        buffer[pl.ds(places[q][f + g], NV), :] = part
         return 0
 
     lax.fori_loop(0, CHUNKS, chunk, 0)
-    me = lax.axis_index("gy") * lax.axis_size("gx") + lax.axis_index("gx")
-    place = lax.broadcasted_iota(i32, (NV, T), 0) * T + lax.broadcasted_iota(i32, (NV, T), 1)
-    place = place - me * CAP
-
-    def write(i, _):
-        block = jnp.zeros((NV, T), i32)
+    lane = lanes(1)
+
+    def name(i, _):
+        line = jnp.zeros((1, T), i32)
         for k in range(CAP):
-            block = jnp.where(place == k, label[i * CAP + k], block)
-        out[i * SLOTS + CAP] = block.astype(f32)
+            line = jnp.where(lane == k, label[i * CAP + k], line)
+        names[pl.ds(i, 1), :] = line.astype(f32)
         return 0
 
-    lax.fori_loop(0, PEERS, write, 0)
+    lax.fori_loop(0, PEERS, name, 0)
+    lane = lanes(PEERS)
+    rims = jnp.zeros((PEERS, T), f32)
+    for j in range(CAP * NV):
+        column = EDGE + 2 * j
+        turned = pltpu.roll(buffer[pl.ds(j, PEERS, stride=SIZE), :], (column + 1) % T, 1)
+        rims = jnp.where((lane >> 1) == column >> 1, turned, rims)
+    lane, sub = lanes(8), subl(8)
+    left_end, right_end = sub == MIRROR, sub == MIRROR - 1
+    for b in range(PEERS // 8):
+        own, rim = names[b * 8 : b * 8 + 8, :], rims[b * 8 : b * 8 + 8, :]
+        left_name, left_rim = (jnp.where(left_end, 0.0, pltpu.roll(x, 1, 0)) for x in (own, rim))
+        right_name, right_rim = (jnp.where(right_end, 0.0, pltpu.roll(x, 7, 0)) for x in (own, rim))
+        line = own + pltpu.roll(left_name, CAP, 1) + pltpu.roll(right_name, 2 * CAP, 1)
+        line = line + jnp.where((lane & 1) == 0, left_rim, right_rim)
+        buffer[pl.ds(b * 8 * SIZE + SIZE - 1, 8, stride=SIZE), :] = line
+    run([pltpu.make_async_copy(buffer.at[pl.ds(0, PEERS * SIZE)], out, sems.at[0])])
 
 
 def remap(dest, count, surf, weight, after):
     return pl.pallas_call(
         remap_kernel,
         in_specs=[HBM, HBM, VMEM, HBM, HBM],
-        out_specs=VMEM,
-        out_shape=jax.ShapeDtypeStruct((PEERS * SLOTS, NV, T), f32),
+        out_specs=HBM,
+        out_shape=jax.ShapeDtypeStruct((PEERS * SIZE, T), f32),
         scratch_shapes=[
             pltpu.VMEM((T, FAN, T, T), bf16),
+            pltpu.VMEM((PEERS * SIZE + 8, T), f32),
+            pltpu.VMEM((PEERS, T), f32),
             pltpu.SMEM((FAN, T), i32),
             pltpu.SMEM((1, T), i32),
             pltpu.SMEM((PEERS,), i32),
@@ -507,42 +525,56 @@
     )(rate, state, coef, sea, own, top, bottom, left, right)
 
 
-def unpack_kernel(data, after, imp, first, last, cols):
+def unpack_kernel(data, after, imp, first, last):
     del after
-    size = SLOTS * NV
     sub = subl(T).astype(f32) + 1.0
-    picks = []
-    for j in range(NV):
-        table = jnp.sum(data[pl.ds(CAP * NV + j, PEERS, stride=size), :], axis=0, keepdims=True)
-        picks.append((sub == table).astype(bf16))
-    pick = jnp.concatenate(picks, axis=1)
-    lane = lanes(T)
+    line = data[pl.ds(SIZE - 1, PEERS, stride=SIZE), :]
+    fields = jnp.transpose(jnp.concatenate([line, jnp.zeros((T - PEERS, T), f32)], axis=0))
+
+    def two(at, size):
+        return fields[at : at + size, :] + pltpu.roll(fields[at + size : at + 2 * size, :], PEERS, 1)
+
+    def split(x):
+        high = x.astype(bf16)
+        return high, (x - high.astype(f32)).astype(bf16)
+
+    def picks(at):
+        return jnp.concatenate(
+            [(sub == two(at + k, 1)).astype(bf16) for k in range(0, CAP, 2)], axis=1
+        )
+
+    pick = picks(0)
     up, down, _, _ = inside()
-    acc = jnp.zeros((T, T), f32)
     for v in range(NV):
         block = jnp.concatenate(
-            [data[pl.ds(s * size + v, CAP, stride=NV), :] for s in range(PEERS)], axis=0
+            [data[pl.ds(k * NV + v, PEERS, stride=SIZE), :] for k in range(CAP)], axis=0
         )
-        high = block.astype(bf16)
-        low = (block - high.astype(f32)).astype(bf16)
+        high, low = split(block)
         total = jnp.dot(pick, high, preferred_element_type=f32)
         total = total + jnp.dot(pick, low, preferred_element_type=f32)
-        imp[v] = total
+        imp[v * T : (v + 1) * T, :] = total
         for out, row, keep in ((first, 0, up), (last, T - 1, down)):
             out[v : v + 1, :] = total[row : row + 1, :] * keep
             out[NV + v : NV + v + 1, :] = total[row : row + 1, :] * keep
-        acc = jnp.where((lane >> 1) == v, pltpu.roll(total, 2 * v + 1, 1), acc)
-    cols[...] = jnp.transpose(acc * column_keep(T, MIRROR))[0 : 2 * NV, :]
+    rims = jnp.concatenate([two(EDGE + 8 * k, 8) for k in range(0, CAP, 2)], axis=1)
+    sides = []
+    for at in (CAP, 2 * CAP):
+        pick = picks(at)
+        high, low = (
+            lax.dot_general(part, pick, (((1,), (1,)), ((), ())), preferred_element_type=f32)
+            for part in split(rims)
+        )
+        sides.append(high + low)
+    imp[NV * T : NV * T + 8, :] = jnp.where((subl(8) & 1) == 0, sides[0], sides[1])
 
 
 def unpack(data, after):
     return pl.pallas_call(
         unpack_kernel,
         in_specs=[VMEM, HBM],
-        out_specs=[VMEM] * 4,
+        out_specs=[VMEM] * 3,
         out_shape=[
-            jax.ShapeDtypeStruct((NV, T, T), f32),
-            jax.ShapeDtypeStruct((2 * NV, T), f32),
+            jax.ShapeDtypeStruct((NV * T + 8, T), f32),
             jax.ShapeDtypeStruct((2 * NV, T), f32),
             jax.ShapeDtypeStruct((2 * NV, T), f32),
         ],
@@ -553,12 +585,10 @@
 
 
 def final_kernel(
-    horiz, relax, mid, near, imp, imp_top, imp_bottom, imp_left, imp_right, out, stage, sems
+    horiz, relax, mid, near, imp, imp_top, imp_bottom, out, stage, sems
 ):
     del mid
-    odd = (subl(2 * NV) & 1) == 1
-    ends = jnp.where(odd, imp_right[...], imp_left[...])
-    ends = jnp.concatenate([ends, jnp.zeros((T - 2 * NV, T), f32)], axis=0)
+    ends = jnp.concatenate([imp[NV * T : NV * T + 8, :], jnp.zeros((T - 8, T), f32)], axis=0)
     side_new = jnp.transpose(ends)
     sea, sea_side = near[KEEP_SEA : KEEP_SEA + T, :], near[KEEP_SEA_SIDE : KEEP_SEA_SIDE + T, :]
     coef = near[KEEP_VERT : KEEP_VERT + T, :]
@@ -581,10 +611,11 @@
         base = pltpu.roll(side_base, turn, 1) if turn else side_base
         new = pltpu.roll(side_new, T - 2 * v, 1) if v else side_new
         new = jnp.where(lane == 0, new, pltpu.roll(side_new, T - 2 - 2 * v, 1))
-        u = relaxed(near[KEEP_BASE + v * T : KEEP_BASE + (v + 1) * T, :], sea, imp[v])
+        mine = imp[v * T : (v + 1) * T, :]
+        u = relaxed(near[KEEP_BASE + v * T : KEEP_BASE + (v + 1) * T, :], sea, mine)
         h = diffuse(u, ends[0], ends[1], relaxed(base, sea_side, new), horiz[0, v])
         one = near[KEEP_ONE + v * T : KEEP_ONE + (v + 1) * T, :]
-        stage[v, 0] = relaxed(h + coef * (one - h), sea, imp[v])
+        stage[v, 0] = relaxed(h + coef * (one - h), sea, mine)
         stage[v, 1] = near[KEEP_PART + v * T : KEEP_PART + (v + 1) * T, :] + coef * h
         copies.append(
             pltpu.make_async_copy(stage.at[v], out.at[0, v, pl.ds(0, 2)], sems.at[v])
@@ -594,10 +625,10 @@
         copy.wait()
 
 
-def final(horiz, relax, mid, keep, imp, imp_rows, imp_cols):
+def final(horiz, relax, mid, keep, imp, imp_rows):
     return pl.pallas_call(
         final_kernel,
-        in_specs=[SMEM, SMEM, HBM] + [VMEM] * 6,
+        in_specs=[SMEM, SMEM, HBM] + [VMEM] * 4,
         out_specs=HBM,
         out_shape=jax.ShapeDtypeStruct(mid.shape, f32),
         input_output_aliases={2: 0},
@@ -608,7 +639,7 @@
         compiler_params=params(6 * MIB),
         cost_estimate=cost(2 << 20, 3 << 20),
         name="final",
-    )(horiz, relax, mid, keep, imp, *imp_rows, *imp_cols)
+    )(horiz, relax, mid, keep, imp, *imp_rows)
 
 
 def shifted(block, axis, by):
@@ -616,14 +647,14 @@
     return lax.ppermute(block, axis, [(i, (i + by) % count) for i in range(count)])
 
 
-def crossed(block, gx_by=0, gy_by=0):
+def crossed(block, gx_by=0):
     size = lax.axis_size("gx"), lax.axis_size("gy")
     route = []
     for c in range(2):
         for i in range(size[0]):
             for j in range(size[1]):
-                to = (i + gx_by) % size[0], ((j ^ MIRROR) + gy_by) % size[1]
-                route.append(((c * size[0] + i) * size[1] + j, ((1 - c) * size[0] + to[0]) * size[1] + to[1]))
+                to = (1 - c) * size[0] + (i + gx_by) % size[0]
+                route.append(((c * size[0] + i) * size[1] + j, to * size[1] + (j ^ MIRROR)))
     return lax.ppermute(block, ("comp", "gx", "gy"), route)
 
 
@@ -637,14 +668,13 @@
     left, right = shifted(cols, "gy", 1), shifted(cols, "gy", -1)
     dest = dest_block.reshape(T, FAN).T
     packed = remap(dest, entry_count.reshape(1, T), surf, remap_weight, cols)
-    packed = sealed(packed, left, right).reshape(PEERS, SLOTS, NV, T)
-    packed = lax.all_to_all(packed, ("gy", "gx"), split_axis=0, concat_axis=0, tiled=True)
+    packed = sealed(packed, left, right).reshape(PEERS, SIZE, 1, T)
+    packed = lax.all_to_all(packed, ("gx", "gy"), split_axis=0, concat_axis=0, tiled=True)
     mid, keep = two_steps(horiz_coef, state, coef, sea, cols, top, bottom, left, right)
-    new, first, last, sides = unpack(packed.reshape(PEERS * SLOTS * NV, T), keep)
+    new, first, last = unpack(packed.reshape(PEERS * SIZE, T), keep)
     imp = crossed(new)
-    imp_rows = crossed(last, gx_by=1), crossed(first, gx_by=-1)
-    imp_cols = crossed(sides, gy_by=1), crossed(sides, gy_by=-1)
-    return final(horiz_coef, couple_rate, mid, keep, imp, imp_rows, imp_cols)
+    imp_rows = crossed(last, 1), crossed(first, -1)
+    return final(horiz_coef, couple_rate, mid, keep, imp, imp_rows)
 
 
 def solution(mesh):

time: 68.9 us -> 62.5 us (0.907)
  the two profiles are of different devices: /device:TPU:2 before, /device:TPU:1 now
where the time goes in v7:
time: 62.5 us; the launch traced here: 62.3 us
  Pallas kernels  26.8 us (43%)
  starting transfers between devices  20.7 us (33%)
  waiting for transfers between devices  12.4 us (20%)
  local copies, waits for them, and re-layouts  2.21 us (4%)
    all_to_all x1, starting transfers between devices, local(): lax.all_to_all(packed, ('gx', 'gy'), split_axis=0, concat_axis=0, tiled=T...  9.86 us
    pallas_call x1, Pallas kernels, two_steps(): pl.pallas_call(step_kernel, in_specs=[SMEM, HBM] + [VMEM] * 7, out_specs=...  9.36 us
    pallas_call x1, Pallas kernels, remap(): pl.pallas_call(remap_kernel, in_specs=[HBM, HBM, VMEM, HBM, HBM], out_spe...  9.18 us
    ppermute x4, starting transfers between devices, shifted(): lax.ppermute(block, axis, [(i, (i + by) % count) for i in range(count)])  6.78 us
    all_to_all x1, waiting for transfers between devices, local(): lax.all_to_all(packed, ('gx', 'gy'), split_axis=0, concat_axis=0, tiled=T...  6.7 us
    ppermute x3, waiting for transfers between devices, crossed(): return lax.ppermute(block, ('comp', 'gx', 'gy'), route)  5.62 us
    ppermute x3, starting transfers between devices, crossed(): return lax.ppermute(block, ('comp', 'gx', 'gy'), route)  4.1 us
    pallas_call x1, Pallas kernels, outer_columns(): pl.pallas_call(column_kernel, in_specs=[HBM, HBM, HBM], out_specs=[VMEM]...  3.86 us
  transfers between devices with their start and end apart: 8, of which 3 were waited for; matrix products, arithmetic and copies ran while one was open for 0% of the time, Pallas kernels for 36%

profile of v7, /device:TPU:1, one launch (start us, length us, event | category | flops | bytes accessed | tf_op | source)
XLA Modules:
  0.0 62.3 jit_solution(1481946072910974635)
XLA Ops:
  0.0 1.9 %outer_rows.1 = (f32[144,128]{1,0:T(8,128)}, f32[144,128]{1,0:T(8,128)}) custom-call(f32[1,4,16,128,128]{4,3,2,1,0:T(8,128)} %state.5, f32[1,128,128]{2,1,0:T(8,128)} %vert.3, s32[1,128,128]{2,1,0:T(8,128)} %mask.3), custom_call_target="tpu_custom_call" | custom-call | flops 65536 | bytes 524288 | tf_op jit(solution)/shard_map/outer_rows/pallas_call | solution.py:110
  1.9 3.0 %collective-permute-start = (f32[144,128]{1,0:T(8,128)}, f32[144,128]{1,0:T(8,128)S(1)}, u32[]{:S(2)}, u32[]{:S(2)}) collective-permute-start(f32[144,128]{1,0:T(8,128)} %get-tuple-element.19), channel_id=1, source_target_pairs={{0,8},{8,16},{16,24},{24,32},{32,40},{40,48},{48,56},{56,0},{1,9},... | collective-permute-start | bytes 221192 | tf_op jit(solution)/shard_map/ppermute | solution.py:647
  5.0 3.9 %outer_columns.1 = (f32[384,128]{1,0:T(8,128)S(1)}, f32[512,128]{1,0:T(8,128)S(1)}, f32[128,128]{1,0:T(8,128)S(1)}, f32[128,128]{1,0:T(8,128)S(1)}) custom-call(f32[1,4,16,128,128]{4,3,2,1,0:T(8,128)} %state.5, f32[1,128,128]{2,1,0:T(8,128)S(1)} %copy-done.1, s32[1,128,128]{2,1,0:T(8,128)S(1)} %copy-done.2), custom_call_target="tpu_custom_call" | custom-call | flops 6291456 | bytes 9437184 | tf_op jit(solution)/shard_map/outer_columns/pallas_call | solution.py:162
  8.9 0.0 collective-permute-done.top
  8.9 0.1 collective-permute-done.1.bottom
  9.0 0.1 with_corners.1.own.after
  9.1 3.7 %collective-permute-start.3 = (f32[400,128]{1,0:T(8,128)S(1)}, f32[400,128]{1,0:T(8,128)S(1)}, u32[]{:S(2)}, u32[]{:S(2)}) collective-permute-start(f32[400,128]{1,0:T(8,128)S(1)} %with_corners.1.own.after), channel_id=1, source_target_pairs={{0,7},{1,0},{2,1},{3,2},{4,3},{5,4},{6,5},{7,6},{8,15},{9,8},{10,9... | collective-permute-start | bytes 614408 | tf_op jit(solution)/shard_map/ppermute | solution.py:647
  12.8 9.2 %remap.1.refs_0_ = f32[2112,128]{1,0:T(8,128)} custom-call(s32[4,128]{1,0:T(4,128)S(1)} %bitcast.7, s32[1,128]{1,0:T(1,128)S(1)} %bitcast.8, f32[512,128]{1,0:T(8,128)S(1)} %get-tuple-element.23.surf, bf16[1,128,1,4,128,128]{5,4,3,2,1,0:T(8,128)(2,1)} %weight.1, f32[400,128]{1,0:T(8,128)S(1)} %with_corners.1.own.after), custom_call_target="tpu_custom_call" | custom-call | flops 70254592 | bytes 20971520 | tf_op jit(solution)/shard_map/remap/pallas_call | solution.py:307
  22.0 0.0 copy-start.3
  22.0 0.0 collective-permute-done.2.near.refs_1_
  22.1 0.0 copy-start.6
  22.1 9.9 %all-to-all-start = ((f32[64,33,1,128]{3,2,1,0:T(1,128)}), f32[64,33,1,128]{3,2,1,0:T(1,128)S(1)}, u32[]{:S(2)}, u32[]{:S(2)}) async-start(f32[64,33,1,128]{3,2,1,0:T(1,128)} %bitcast.3), calls=%async_computation | async-start | bytes 2162688 | tf_op jit(solution)/shard_map/all_to_all | solution.py:672
  31.9 0.0 copy-start
  32.0 2.2 %copy-done = f32[1,4,16,128,128]{4,3,2,1,0:T(8,128)S(1)} copy-done((f32[1,4,16,128,128]{4,3,2,1,0:T(8,128)S(1)}, f32[1,4,16,128,128]{4,3,2,1,0:T(8,128)}, u32[]{:S(2)}) %copy-start) | copy-done | bytes 4194328
  34.1 9.4 %two_steps.1 = (f32[1,4,16,128,128]{4,3,2,1,0:T(8,128)}, f32[2064,128]{1,0:T(8,128)S(1)}) custom-call(f32[1,4]{1,0:T(1,128)S(1)} %copy-done.3, f32[1,4,16,128,128]{4,3,2,1,0:T(8,128)S(1)} %copy-done, f32[128,128]{1,0:T(8,128)S(1)} %get-tuple-element.16.coef, f32[128,128]{1,0:T(8,128)S(1)} %get-tuple-element.17.sea, f32[400,128]{1,0:T(8,128)S(1)} %with_corners.1.own.after, ...), custom_call_target="tpu_custom_call" | custom-call | flops 50331648 | bytes 10485760 | tf_op jit(solution)/shard_map/two_steps/pallas_call | solution.py:500
  43.5 6.7 %all-to-all-done = f32[64,33,1,128]{3,2,1,0:T(1,128)S(1)} async-done(((f32[64,33,1,128]{3,2,1,0:T(1,128)}), f32[64,33,1,128]{3,2,1,0:T(1,128)S(1)}, u32[]{:S(2)}, u32[]{:S(2)}) %all-to-all-start) | async-done | bytes 1081376 | tf_op jit(solution)/shard_map/all_to_all | solution.py:672
  50.2 0.7 %unpack.1 = (f32[520,128]{1,0:T(8,128)S(1)}, f32[8,128]{1,0:T(8,128)S(1)}, f32[8,128]{1,0:T(8,128)S(1)}) custom-call(f32[2112,128]{1,0:T(8,128)S(1)} %bitcast.6, f32[2064,128]{1,0:T(8,128)S(1)} %get-tuple-element.22.after.near), custom_call_target="tpu_custom_call" | custom-call | flops 209715200 | bytes 2097152 | tf_op jit(solution)/shard_map/unpack/pallas_call | solution.py:572
  50.9 1.1 %collective-permute-start.4 = (f32[520,128]{1,0:T(8,128)S(1)}, f32[520,128]{1,0:T(8,128)S(1)}, u32[]{:S(2)}, u32[]{:S(2)}) collective-permute-start(f32[520,128]{1,0:T(8,128)S(1)} %get-tuple-element.24), channel_id=1, source_target_pairs={{0,68},{1,69},{2,70},{3,71},{4,64},{5,65},{6,66},{7,67},{8,76},{9,... | collective-permute-start | bytes 798728 | tf_op jit(solution)/shard_map/ppermute | solution.py:658
  52.0 1.8 %collective-permute-start.5 = (f32[8,128]{1,0:T(8,128)S(1)}, f32[8,128]{1,0:T(8,128)S(1)}, u32[]{:S(2)}, u32[]{:S(2)}) collective-permute-start(f32[8,128]{1,0:T(8,128)S(1)} %get-tuple-element.25), channel_id=1, source_target_pairs={{0,76},{1,77},{2,78},{3,79},{4,72},{5,73},{6,74},{7,75},{8,84},{9,... | collective-permute-start | bytes 12296 | tf_op jit(solution)/shard_map/ppermute | solution.py:658
  53.8 1.2 %collective-permute-start.6 = (f32[8,128]{1,0:T(8,128)S(1)}, f32[8,128]{1,0:T(8,128)S(1)}, u32[]{:S(2)}, u32[]{:S(2)}) collective-permute-start(f32[8,128]{1,0:T(8,128)S(1)} %get-tuple-element.26), channel_id=1, source_target_pairs={{0,124},{1,125},{2,126},{3,127},{4,120},{5,121},{6,122},{7,123},{8... | collective-permute-start | bytes 12296 | tf_op jit(solution)/shard_map/ppermute | solution.py:658
  55.0 5.6 %collective-permute-done.5.imp_top = f32[8,128]{1,0:T(8,128)S(1)} collective-permute-done((f32[8,128]{1,0:T(8,128)S(1)}, f32[8,128]{1,0:T(8,128)S(1)}, u32[]{:S(2)}, u32[]{:S(2)}) %collective-permute-start.5) | collective-permute-done | bytes 4128 | tf_op jit(solution)/shard_map/ppermute | solution.py:658
  60.6 0.0 collective-permute-done.6.imp_bottom
  60.6 0.0 collective-permute-done.4.imp
  60.6 1.7 %final.1 = f32[1,4,16,128,128]{4,3,2,1,0:T(8,128)} custom-call(f32[1,4]{1,0:T(1,128)S(1)} %copy-done.3, f32[1,4]{1,0:T(1,128)S(1)} %copy-done.6, f32[1,4,16,128,128]{4,3,2,1,0:T(8,128)} %get-tuple-element.21.mid, f32[2064,128]{1,0:T(8,128)S(1)} %get-tuple-element.22.after.near, ...), custom_call_target="tpu_custom_call", output_to_operand_aliasing={{}: (2, {})} | custom-call | flops 2097152 | bytes 3145728 | tf_op jit(solution)/shard_map/final/pallas_call | solution.py:629
  (14 shorter events, 0.0 us)
Async XLA Ops:
  0.0 5.0 %copy-start.2 = (s32[1,128,128]{2,1,0:T(8,128)S(1)}, s32[1,128,128]{2,1,0:T(8,128)}, u32[]{:S(2)}) copy-start(s32[1,128,128]{2,1,0:T(8,128)} %mask.3) | copy-start | bytes 196612
  0.0 5.0 %copy-start.1 = (f32[1,128,128]{2,1,0:T(8,128)S(1)}, f32[1,128,128]{2,1,0:T(8,128)}, u32[]{:S(2)}) copy-start(f32[1,128,128]{2,1,0:T(8,128)} %vert.3) | copy-start | bytes 196612
  0.0 12.8 %copy-start.5 = (s32[1,128,1]{1,2,0:T(1,128)S(1)}, s32[1,128,1]{1,2,0:T(1,128)}, u32[]{:S(2)}) copy-start(s32[1,128,1]{1,2,0:T(1,128)} %param.14) | copy-start | bytes 1540
  0.0 12.8 %copy-start.4 = (s32[1,128,1,4]{1,3,2,0:T(4,128)S(1)}, s32[1,128,1,4]{1,3,2,0:T(4,128)}, u32[]{:S(2)}) copy-start(s32[1,128,1,4]{1,3,2,0:T(4,128)} %param.13) | copy-start | bytes 6148
  1.9 6.9 %collective-permute-start = (f32[144,128]{1,0:T(8,128)}, f32[144,128]{1,0:T(8,128)S(1)}, u32[]{:S(2)}, u32[]{:S(2)}) collective-permute-start(f32[144,128]{1,0:T(8,128)} %get-tuple-element.19), channel_id=1, source_target_pairs={{0,8},{8,16},{16,24},{24,32},{32,40},{40,48},{48,56},{56,0},{1,9},... | collective-permute-start | bytes 221192 | tf_op jit(solution)/shard_map/ppermute | solution.py:647
  5.0 4.0 %collective-permute-start.1 = (f32[144,128]{1,0:T(8,128)}, f32[144,128]{1,0:T(8,128)S(1)}, u32[]{:S(2)}, u32[]{:S(2)}) collective-permute-start(f32[144,128]{1,0:T(8,128)} %get-tuple-element.20), channel_id=1, source_target_pairs={{0,56},{8,0},{16,8},{24,16},{32,24},{40,32},{48,40},{56,48},{1,57}... | collective-permute-start | bytes 221192 | tf_op jit(solution)/shard_map/ppermute | solution.py:647
  9.1 12.9 %collective-permute-start.3 = (f32[400,128]{1,0:T(8,128)S(1)}, f32[400,128]{1,0:T(8,128)S(1)}, u32[]{:S(2)}, u32[]{:S(2)}) collective-permute-start(f32[400,128]{1,0:T(8,128)S(1)} %with_corners.1.own.after), channel_id=1, source_target_pairs={{0,7},{1,0},{2,1},{3,2},{4,3},{5,4},{6,5},{7,6},{8,15},{9,8},{10,9... | collective-permute-start | bytes 614408 | tf_op jit(solution)/shard_map/ppermute | solution.py:647
  12.8 9.2 %collective-permute-start.2 = (f32[400,128]{1,0:T(8,128)S(1)}, f32[400,128]{1,0:T(8,128)S(1)}, u32[]{:S(2)}, u32[]{:S(2)}) collective-permute-start(f32[400,128]{1,0:T(8,128)S(1)} %with_corners.1.own.after), channel_id=1, source_target_pairs={{0,1},{1,2},{2,3},{3,4},{4,5},{5,6},{6,7},{7,0},{8,9},{9,10},{10,1... | collective-permute-start | bytes 614408 | tf_op jit(solution)/shard_map/ppermute | solution.py:647
  22.0 9.9 %copy-start.3 = (f32[1,4]{1,0:T(1,128)S(1)}, f32[1,4]{1,0:T(1,128)}, u32[]{:S(2)}) copy-start(f32[1,4]{1,0:T(1,128)} %horiz.1) | copy-start | bytes 52
  22.1 38.5 %copy-start.6 = (f32[1,4]{1,0:T(1,128)S(1)}, f32[1,4]{1,0:T(1,128)}, u32[]{:S(2)}) copy-start(f32[1,4]{1,0:T(1,128)} %relax.1) | copy-start | bytes 52
  22.1 28.1 %all-to-all-start = ((f32[64,33,1,128]{3,2,1,0:T(1,128)}), f32[64,33,1,128]{3,2,1,0:T(1,128)S(1)}, u32[]{:S(2)}, u32[]{:S(2)}) async-start(f32[64,33,1,128]{3,2,1,0:T(1,128)} %bitcast.3), calls=%async_computation | async-start | bytes 2162688 | tf_op jit(solution)/shard_map/all_to_all | solution.py:672
  31.9 2.2 %copy-start = (f32[1,4,16,128,128]{4,3,2,1,0:T(8,128)S(1)}, f32[1,4,16,128,128]{4,3,2,1,0:T(8,128)}, u32[]{:S(2)}) copy-start(f32[1,4,16,128,128]{4,3,2,1,0:T(8,128)} %state.5) | copy-start | bytes 12582916
  50.9 9.7 %collective-permute-start.4 = (f32[520,128]{1,0:T(8,128)S(1)}, f32[520,128]{1,0:T(8,128)S(1)}, u32[]{:S(2)}, u32[]{:S(2)}) collective-permute-start(f32[520,128]{1,0:T(8,128)S(1)} %get-tuple-element.24), channel_id=1, source_target_pairs={{0,68},{1,69},{2,70},{3,71},{4,64},{5,65},{6,66},{7,67},{8,76},{9,... | collective-permute-start | bytes 798728 | tf_op jit(solution)/shard_map/ppermute | solution.py:658
  52.0 8.6 %collective-permute-start.5 = (f32[8,128]{1,0:T(8,128)S(1)}, f32[8,128]{1,0:T(8,128)S(1)}, u32[]{:S(2)}, u32[]{:S(2)}) collective-permute-start(f32[8,128]{1,0:T(8,128)S(1)} %get-tuple-element.25), channel_id=1, source_target_pairs={{0,76},{1,77},{2,78},{3,79},{4,72},{5,73},{6,74},{7,75},{8,84},{9,... | collective-permute-start | bytes 12296 | tf_op jit(solution)/shard_map/ppermute | solution.py:658
  53.8 6.8 %collective-permute-start.6 = (f32[8,128]{1,0:T(8,128)S(1)}, f32[8,128]{1,0:T(8,128)S(1)}, u32[]{:S(2)}, u32[]{:S(2)}) collective-permute-start(f32[8,128]{1,0:T(8,128)S(1)} %get-tuple-element.26), channel_id=1, source_target_pairs={{0,124},{1,125},{2,126},{3,127},{4,120},{5,121},{6,122},{7,123},{8... | collective-permute-start | bytes 12296 | tf_op jit(solution)/shard_map/ppermute | solution.py:658

commit v8 on v7

--- a/solution.py
+++ b/solution.py
@@ -73,9 +73,9 @@
     )
 
 
-def column_keep(rows):
+def column_keep(rows, later=0):
     _, _, before, after = inside()
-    return jnp.where((lanes(rows) & 1) == 0, after, before)
+    return jnp.where((lanes(rows) & 1) == later, after, before)
 
 
 def run(copies):
@@ -96,10 +96,9 @@
     up, down, _, _ = inside()
     for k, (out, buffer, keep) in enumerate(((head, high, up), (tail, low, down))):
         outer, following = (0, 1) if k == 0 else (7, 6)
-        for p in range(PLANES):
-            v, l = divmod(p, LEV)
-            out[p : p + 1, :] = buffer[v, l, outer : outer + 1, :] * keep
-            out[PLANES + p : PLANES + p + 1, :] = buffer[v, l, following : following + 1, :] * keep
+        flat = buffer.reshape(PLANES * 8, T)
+        out[0:PLANES, :] = flat[pl.ds(outer, PLANES, stride=8), :] * keep
+        out[PLANES : 2 * PLANES, :] = flat[pl.ds(following, PLANES, stride=8), :] * keep
         line = coef[k, outer : outer + 1, :] * keep
         out[ROW_VERT : ROW_VERT + 8, :] = jnp.broadcast_to(line, (8, T))
         line = sea[k, outer : outer + 1, :].astype(f32) * keep
@@ -133,6 +132,7 @@
         load.start()
     lane = lanes(HALF)
     keep = column_keep(HALF)
+    keep2 = column_keep(HALF, 1)
     for v in range(NV):
         loads[v].wait()
         surf[pl.ds(v, T, stride=NV), :] = tile[v, 0]
@@ -143,12 +143,12 @@
             for l in range(LEV):
                 p = v * LEV + l
                 plane = tile[v, l, lo : lo + HALF, :]
-                acc = jnp.where((lane >> 1) == p, pltpu.roll(plane, (2 * p + 1) % T, 1), acc)
-                hit = (lane == 2 * p) | (lane == (2 * p + 3) % T)
-                acc2 = jnp.where(hit, pltpu.roll(plane, (2 * p + 2) % T, 1), acc2)
+                turned = pltpu.roll(plane, (2 * p + 1) % T, 1)
+                acc = jnp.where((lane >> 1) == p, turned, acc)
+                acc2 = jnp.where((lane == (2 * p - 1) % T) | (lane == (2 * p + 2) % T), turned, acc2)
             last = v == NV - 1
             cols[outer, :] = acc * keep if last else acc
-            cols[following, :] = acc2 * keep if last else acc2
+            cols[following, :] = acc2 * keep2 if last else acc2
     loads[NV].wait()
     loads[NV + 1].wait()
     lane = lanes(T)
@@ -284,7 +284,7 @@
         names[pl.ds(i, 1), :] = line.astype(f32)
         return 0
 
-    lax.fori_loop(0, PEERS, name, 0)
+    lax.fori_loop(0, PEERS, name, 0, unroll=8)
     lane = lanes(PEERS)
     rims = jnp.zeros((PEERS, T), f32)
     for j in range(CAP * NV):
@@ -366,7 +366,7 @@
 def halo_columns(rate, left, right, own):
     lane, sub = lanes(T), subl(T)
     here = merged(left[0:T, :], right[0:T, :])
-    outer = merged(left[COL_NEXT : COL_NEXT + T, :], right[COL_NEXT : COL_NEXT + T, :], 4)
+    outer = merged(pltpu.roll(left[COL_NEXT : COL_NEXT + T, :], 1, 1), right[COL_NEXT : COL_NEXT + T, :], 3)
     inner = pltpu.roll(own[0:T, :], T - 1, 1)
     ends = [merged(left[at : at + 8, :], right[at : at + 8, :])[0:1, :] for at in (COL_TOP, COL_BOTTOM)]
     north = jnp.where(sub == 0, ends[0], pltpu.roll(here, 1, 0))

time: 62.5 us -> 61.1 us (0.978)
  Pallas kernels: 26.8 us -> 25.3 us
  waiting for transfers between devices: 12.4 us -> 13.5 us
  starting transfers between devices: 20.7 us -> 19.7 us
    pallas_call x1, Pallas kernels: 3.86 us -> 2.77 us  [outer_columns(): pl.pallas_call(column_kernel, in_specs=[HBM, HBM, HBM], out_specs=[VMEM]...]
    ppermute x4, waiting for transfers between devices: 0.1 us -> 1.2 us  [shifted(): lax.ppermute(block, axis, [(i, (i + by) % count) for i in range(count)])]
    all_to_all x1, starting transfers between devices: 9.86 us -> 8.83 us  [local(): lax.all_to_all(packed, ('gx', 'gy'), split_axis=0, concat_axis=0, tiled=T...]
  transfers between devices with their start and end apart: 8 -> 8, of which waited for: 3 -> 3; matrix products, arithmetic and copies ran while one was open for 0% -> 0% of each run, Pallas kernels for 36% -> 35%
where the time goes in v8:
time: 61.1 us; the launch traced here: 60.8 us
  Pallas kernels  25.3 us (41%)
  starting transfers between devices  19.7 us (32%)
  waiting for transfers between devices  13.5 us (22%)
  local copies, waits for them, and re-layouts  2.21 us (4%)
    pallas_call x1, Pallas kernels, two_steps(): pl.pallas_call(step_kernel, in_specs=[SMEM, HBM] + [VMEM] * 7, out_specs=...  9.38 us
    all_to_all x1, starting transfers between devices, local(): lax.all_to_all(packed, ('gx', 'gy'), split_axis=0, concat_axis=0, tiled=T...  8.83 us
    pallas_call x1, Pallas kernels, remap(): pl.pallas_call(remap_kernel, in_specs=[HBM, HBM, VMEM, HBM, HBM], out_spe...  8.83 us
    ppermute x4, starting transfers between devices, shifted(): lax.ppermute(block, axis, [(i, (i + by) % count) for i in range(count)])  6.78 us
    all_to_all x1, waiting for transfers between devices, local(): lax.all_to_all(packed, ('gx', 'gy'), split_axis=0, concat_axis=0, tiled=T...  6.69 us
    ppermute x3, waiting for transfers between devices, crossed(): return lax.ppermute(block, ('comp', 'gx', 'gy'), route)  5.62 us
    ppermute x3, starting transfers between devices, crossed(): return lax.ppermute(block, ('comp', 'gx', 'gy'), route)  4.1 us
    pallas_call x1, Pallas kernels, outer_columns(): pl.pallas_call(column_kernel, in_specs=[HBM, HBM, HBM], out_specs=[VMEM]...  2.77 us
  transfers between devices with their start and end apart: 8, of which 3 were waited for; matrix products, arithmetic and copies ran while one was open for 0% of the time, Pallas kernels for 35%

profile of v8, /device:TPU:1, one launch (start us, length us, event | category | flops | bytes accessed | tf_op | source)
XLA Modules:
  0.0 60.8 jit_solution(660244926577815094)
XLA Ops:
  0.0 1.8 %outer_rows.1 = (f32[144,128]{1,0:T(8,128)}, f32[144,128]{1,0:T(8,128)}) custom-call(f32[1,4,16,128,128]{4,3,2,1,0:T(8,128)} %state.5, f32[1,128,128]{2,1,0:T(8,128)} %vert.3, s32[1,128,128]{2,1,0:T(8,128)} %mask.3), custom_call_target="tpu_custom_call" | custom-call | flops 65536 | bytes 524288 | tf_op jit(solution)/shard_map/outer_rows/pallas_call | solution.py:109
  1.9 3.0 %collective-permute-start = (f32[144,128]{1,0:T(8,128)}, f32[144,128]{1,0:T(8,128)S(1)}, u32[]{:S(2)}, u32[]{:S(2)}) collective-permute-start(f32[144,128]{1,0:T(8,128)} %get-tuple-element.19), channel_id=1, source_target_pairs={{0,8},{8,16},{16,24},{24,32},{32,40},{40,48},{48,56},{56,0},{1,9},... | collective-permute-start | bytes 221192 | tf_op jit(solution)/shard_map/ppermute | solution.py:647
  4.9 0.0 collective-permute-start.1
  4.9 2.8 %outer_columns.1 = (f32[384,128]{1,0:T(8,128)S(1)}, f32[512,128]{1,0:T(8,128)S(1)}, f32[128,128]{1,0:T(8,128)S(1)}, f32[128,128]{1,0:T(8,128)S(1)}) custom-call(f32[1,4,16,128,128]{4,3,2,1,0:T(8,128)} %state.5, f32[1,128,128]{2,1,0:T(8,128)S(1)} %copy-done.1, s32[1,128,128]{2,1,0:T(8,128)S(1)} %copy-done.2), custom_call_target="tpu_custom_call" | custom-call | flops 6291456 | bytes 9437184 | tf_op jit(solution)/shard_map/outer_columns/pallas_call | solution.py:162
  7.7 0.0 collective-permute-done.top
  7.7 1.2 %collective-permute-done.1.bottom = f32[144,128]{1,0:T(8,128)S(1)} collective-permute-done((f32[144,128]{1,0:T(8,128)}, f32[144,128]{1,0:T(8,128)S(1)}, u32[]{:S(2)}, u32[]{:S(2)}) %collective-permute-start.1) | collective-permute-done | bytes 73760 | tf_op jit(solution)/shard_map/ppermute | solution.py:647
  8.9 0.1 with_corners.1.own.after
  9.0 3.7 %collective-permute-start.3 = (f32[400,128]{1,0:T(8,128)S(1)}, f32[400,128]{1,0:T(8,128)S(1)}, u32[]{:S(2)}, u32[]{:S(2)}) collective-permute-start(f32[400,128]{1,0:T(8,128)S(1)} %with_corners.1.own.after), channel_id=1, source_target_pairs={{0,7},{1,0},{2,1},{3,2},{4,3},{5,4},{6,5},{7,6},{8,15},{9,8},{10,9... | collective-permute-start | bytes 614408 | tf_op jit(solution)/shard_map/ppermute | solution.py:647
  12.8 8.8 %remap.1.refs_0_ = f32[2112,128]{1,0:T(8,128)} custom-call(s32[4,128]{1,0:T(4,128)S(1)} %bitcast.7, s32[1,128]{1,0:T(1,128)S(1)} %bitcast.8, f32[512,128]{1,0:T(8,128)S(1)} %get-tuple-element.23.surf, bf16[1,128,1,4,128,128]{5,4,3,2,1,0:T(8,128)(2,1)} %weight.1, f32[400,128]{1,0:T(8,128)S(1)} %with_corners.1.own.after), custom_call_target="tpu_custom_call" | custom-call | flops 70254592 | bytes 20971520 | tf_op jit(solution)/shard_map/remap/pallas_call | solution.py:307
  21.6 0.0 copy-start.3
  21.6 0.0 collective-permute-done.2.near.refs_1_
  21.6 0.0 copy-start.6
  21.7 8.8 %all-to-all-start = ((f32[64,33,1,128]{3,2,1,0:T(1,128)}), f32[64,33,1,128]{3,2,1,0:T(1,128)S(1)}, u32[]{:S(2)}, u32[]{:S(2)}) async-start(f32[64,33,1,128]{3,2,1,0:T(1,128)} %bitcast.3), calls=%async_computation | async-start | bytes 2162688 | tf_op jit(solution)/shard_map/all_to_all | solution.py:672
  30.5 0.0 copy-start
  30.5 2.2 %copy-done = f32[1,4,16,128,128]{4,3,2,1,0:T(8,128)S(1)} copy-done((f32[1,4,16,128,128]{4,3,2,1,0:T(8,128)S(1)}, f32[1,4,16,128,128]{4,3,2,1,0:T(8,128)}, u32[]{:S(2)}) %copy-start) | copy-done | bytes 4194328
  32.7 9.4 %two_steps.1 = (f32[1,4,16,128,128]{4,3,2,1,0:T(8,128)}, f32[2064,128]{1,0:T(8,128)S(1)}) custom-call(f32[1,4]{1,0:T(1,128)S(1)} %copy-done.3, f32[1,4,16,128,128]{4,3,2,1,0:T(8,128)S(1)} %copy-done, f32[128,128]{1,0:T(8,128)S(1)} %get-tuple-element.16.coef, f32[128,128]{1,0:T(8,128)S(1)} %get-tuple-element.17.sea, f32[400,128]{1,0:T(8,128)S(1)} %with_corners.1.own.after, ...), custom_call_target="tpu_custom_call" | custom-call | flops 50331648 | bytes 10485760 | tf_op jit(solution)/shard_map/two_steps/pallas_call | solution.py:500
  42.1 6.7 %all-to-all-done = f32[64,33,1,128]{3,2,1,0:T(1,128)S(1)} async-done(((f32[64,33,1,128]{3,2,1,0:T(1,128)}), f32[64,33,1,128]{3,2,1,0:T(1,128)S(1)}, u32[]{:S(2)}, u32[]{:S(2)}) %all-to-all-start) | async-done | bytes 1081376 | tf_op jit(solution)/shard_map/all_to_all | solution.py:672
  48.8 0.7 %unpack.1 = (f32[520,128]{1,0:T(8,128)S(1)}, f32[8,128]{1,0:T(8,128)S(1)}, f32[8,128]{1,0:T(8,128)S(1)}) custom-call(f32[2112,128]{1,0:T(8,128)S(1)} %bitcast.6, f32[2064,128]{1,0:T(8,128)S(1)} %get-tuple-element.22.after.near), custom_call_target="tpu_custom_call" | custom-call | flops 209715200 | bytes 2097152 | tf_op jit(solution)/shard_map/unpack/pallas_call | solution.py:572
  49.4 1.1 %collective-permute-start.4 = (f32[520,128]{1,0:T(8,128)S(1)}, f32[520,128]{1,0:T(8,128)S(1)}, u32[]{:S(2)}, u32[]{:S(2)}) collective-permute-start(f32[520,128]{1,0:T(8,128)S(1)} %get-tuple-element.24), channel_id=1, source_target_pairs={{0,68},{1,69},{2,70},{3,71},{4,64},{5,65},{6,66},{7,67},{8,76},{9,... | collective-permute-start | bytes 798728 | tf_op jit(solution)/shard_map/ppermute | solution.py:658
  50.6 1.8 %collective-permute-start.5 = (f32[8,128]{1,0:T(8,128)S(1)}, f32[8,128]{1,0:T(8,128)S(1)}, u32[]{:S(2)}, u32[]{:S(2)}) collective-permute-start(f32[8,128]{1,0:T(8,128)S(1)} %get-tuple-element.25), channel_id=1, source_target_pairs={{0,76},{1,77},{2,78},{3,79},{4,72},{5,73},{6,74},{7,75},{8,84},{9,... | collective-permute-start | bytes 12296 | tf_op jit(solution)/shard_map/ppermute | solution.py:658
  52.4 1.2 %collective-permute-start.6 = (f32[8,128]{1,0:T(8,128)S(1)}, f32[8,128]{1,0:T(8,128)S(1)}, u32[]{:S(2)}, u32[]{:S(2)}) collective-permute-start(f32[8,128]{1,0:T(8,128)S(1)} %get-tuple-element.26), channel_id=1, source_target_pairs={{0,124},{1,125},{2,126},{3,127},{4,120},{5,121},{6,122},{7,123},{8... | collective-permute-start | bytes 12296 | tf_op jit(solution)/shard_map/ppermute | solution.py:658
  53.5 5.6 %collective-permute-done.5.imp_top = f32[8,128]{1,0:T(8,128)S(1)} collective-permute-done((f32[8,128]{1,0:T(8,128)S(1)}, f32[8,128]{1,0:T(8,128)S(1)}, u32[]{:S(2)}, u32[]{:S(2)}) %collective-permute-start.5) | collective-permute-done | bytes 4128 | tf_op jit(solution)/shard_map/ppermute | solution.py:658
  59.2 0.0 collective-permute-done.6.imp_bottom
  59.2 1.7 %final.1 = f32[1,4,16,128,128]{4,3,2,1,0:T(8,128)} custom-call(f32[1,4]{1,0:T(1,128)S(1)} %copy-done.3, f32[1,4]{1,0:T(1,128)S(1)} %copy-done.6, f32[1,4,16,128,128]{4,3,2,1,0:T(8,128)} %get-tuple-element.21.mid, f32[2064,128]{1,0:T(8,128)S(1)} %get-tuple-element.22.after.near, ...), custom_call_target="tpu_custom_call", output_to_operand_aliasing={{}: (2, {})} | custom-call | flops 2097152 | bytes 3145728 | tf_op jit(solution)/shard_map/final/pallas_call | solution.py:629
  (14 shorter events, 0.0 us)
Async XLA Ops:
  0.0 4.9 %copy-start.2 = (s32[1,128,128]{2,1,0:T(8,128)S(1)}, s32[1,128,128]{2,1,0:T(8,128)}, u32[]{:S(2)}) copy-start(s32[1,128,128]{2,1,0:T(8,128)} %mask.3) | copy-start | bytes 196612
  0.0 4.9 %copy-start.1 = (f32[1,128,128]{2,1,0:T(8,128)S(1)}, f32[1,128,128]{2,1,0:T(8,128)}, u32[]{:S(2)}) copy-start(f32[1,128,128]{2,1,0:T(8,128)} %vert.3) | copy-start | bytes 196612
  0.0 12.8 %copy-start.5 = (s32[1,128,1]{1,2,0:T(1,128)S(1)}, s32[1,128,1]{1,2,0:T(1,128)}, u32[]{:S(2)}) copy-start(s32[1,128,1]{1,2,0:T(1,128)} %param.14) | copy-start | bytes 1540
  0.0 12.7 %copy-start.4 = (s32[1,128,1,4]{1,3,2,0:T(4,128)S(1)}, s32[1,128,1,4]{1,3,2,0:T(4,128)}, u32[]{:S(2)}) copy-start(s32[1,128,1,4]{1,3,2,0:T(4,128)} %param.13) | copy-start | bytes 6148
  1.9 5.8 %collective-permute-start = (f32[144,128]{1,0:T(8,128)}, f32[144,128]{1,0:T(8,128)S(1)}, u32[]{:S(2)}, u32[]{:S(2)}) collective-permute-start(f32[144,128]{1,0:T(8,128)} %get-tuple-element.19), channel_id=1, source_target_pairs={{0,8},{8,16},{16,24},{24,32},{32,40},{40,48},{48,56},{56,0},{1,9},... | collective-permute-start | bytes 221192 | tf_op jit(solution)/shard_map/ppermute | solution.py:647
  4.9 4.0 %collective-permute-start.1 = (f32[144,128]{1,0:T(8,128)}, f32[144,128]{1,0:T(8,128)S(1)}, u32[]{:S(2)}, u32[]{:S(2)}) collective-permute-start(f32[144,128]{1,0:T(8,128)} %get-tuple-element.20), channel_id=1, source_target_pairs={{0,56},{8,0},{16,8},{24,16},{32,24},{40,32},{48,40},{56,48},{1,57}... | collective-permute-start | bytes 221192 | tf_op jit(solution)/shard_map/ppermute | solution.py:647
  9.0 12.6 %collective-permute-start.3 = (f32[400,128]{1,0:T(8,128)S(1)}, f32[400,128]{1,0:T(8,128)S(1)}, u32[]{:S(2)}, u32[]{:S(2)}) collective-permute-start(f32[400,128]{1,0:T(8,128)S(1)} %with_corners.1.own.after), channel_id=1, source_target_pairs={{0,7},{1,0},{2,1},{3,2},{4,3},{5,4},{6,5},{7,6},{8,15},{9,8},{10,9... | collective-permute-start | bytes 614408 | tf_op jit(solution)/shard_map/ppermute | solution.py:647
  12.7 8.9 %collective-permute-start.2 = (f32[400,128]{1,0:T(8,128)S(1)}, f32[400,128]{1,0:T(8,128)S(1)}, u32[]{:S(2)}, u32[]{:S(2)}) collective-permute-start(f32[400,128]{1,0:T(8,128)S(1)} %with_corners.1.own.after), channel_id=1, source_target_pairs={{0,1},{1,2},{2,3},{3,4},{4,5},{5,6},{6,7},{7,0},{8,9},{9,10},{10,1... | collective-permute-start | bytes 614408 | tf_op jit(solution)/shard_map/ppermute | solution.py:647
  21.6 8.9 %copy-start.3 = (f32[1,4]{1,0:T(1,128)S(1)}, f32[1,4]{1,0:T(1,128)}, u32[]{:S(2)}) copy-start(f32[1,4]{1,0:T(1,128)} %horiz.1) | copy-start | bytes 52
  21.6 37.5 %copy-start.6 = (f32[1,4]{1,0:T(1,128)S(1)}, f32[1,4]{1,0:T(1,128)}, u32[]{:S(2)}) copy-start(f32[1,4]{1,0:T(1,128)} %relax.1) | copy-start | bytes 52
  21.7 27.1 %all-to-all-start = ((f32[64,33,1,128]{3,2,1,0:T(1,128)}), f32[64,33,1,128]{3,2,1,0:T(1,128)S(1)}, u32[]{:S(2)}, u32[]{:S(2)}) async-start(f32[64,33,1,128]{3,2,1,0:T(1,128)} %bitcast.3), calls=%async_computation | async-start | bytes 2162688 | tf_op jit(solution)/shard_map/all_to_all | solution.py:672
  30.5 2.2 %copy-start = (f32[1,4,16,128,128]{4,3,2,1,0:T(8,128)S(1)}, f32[1,4,16,128,128]{4,3,2,1,0:T(8,128)}, u32[]{:S(2)}) copy-start(f32[1,4,16,128,128]{4,3,2,1,0:T(8,128)} %state.5) | copy-start | bytes 12582916
  49.4 9.7 %collective-permute-start.4 = (f32[520,128]{1,0:T(8,128)S(1)}, f32[520,128]{1,0:T(8,128)S(1)}, u32[]{:S(2)}, u32[]{:S(2)}) collective-permute-start(f32[520,128]{1,0:T(8,128)S(1)} %get-tuple-element.24), channel_id=1, source_target_pairs={{0,68},{1,69},{2,70},{3,71},{4,64},{5,65},{6,66},{7,67},{8,76},{9,... | collective-permute-start | bytes 798728 | tf_op jit(solution)/shard_map/ppermute | solution.py:658
  50.6 8.6 %collective-permute-start.5 = (f32[8,128]{1,0:T(8,128)S(1)}, f32[8,128]{1,0:T(8,128)S(1)}, u32[]{:S(2)}, u32[]{:S(2)}) collective-permute-start(f32[8,128]{1,0:T(8,128)S(1)} %get-tuple-element.25), channel_id=1, source_target_pairs={{0,76},{1,77},{2,78},{3,79},{4,72},{5,73},{6,74},{7,75},{8,84},{9,... | collective-permute-start | bytes 12296 | tf_op jit(solution)/shard_map/ppermute | solution.py:658
  52.4 6.8 %collective-permute-start.6 = (f32[8,128]{1,0:T(8,128)S(1)}, f32[8,128]{1,0:T(8,128)S(1)}, u32[]{:S(2)}, u32[]{:S(2)}) collective-permute-start(f32[8,128]{1,0:T(8,128)S(1)} %get-tuple-element.26), channel_id=1, source_target_pairs={{0,124},{1,125},{2,126},{3,127},{4,120},{5,121},{6,122},{7,123},{8... | collective-permute-start | bytes 12296 | tf_op jit(solution)/shard_map/ppermute | solution.py:658

commit v9 on v8

--- a/solution.py
+++ b/solution.py
@@ -16,6 +16,7 @@
 EDGE = 32
 HALF = 64
 CHUNKS = 16
+EARLY = 32
 MIRROR = 4
 MIB = 1024 * 1024
 LIMIT = 58 * MIB
@@ -124,10 +125,11 @@
     )(state, vert, mask)
 
 
-def column_kernel(state, vert, mask, cols, surf, coef, wet, tile, sea, sems):
+def column_kernel(state, vert, mask, weight, cols, surf, coef, wet, early, tile, sea, sems):
     loads = [pltpu.make_async_copy(state.at[0, v], tile.at[v], sems.at[v]) for v in range(NV)]
     loads.append(pltpu.make_async_copy(vert.at[0], coef, sems.at[NV]))
     loads.append(pltpu.make_async_copy(mask.at[0], sea, sems.at[NV + 1]))
+    loads.append(pltpu.make_async_copy(weight.at[0, pl.ds(0, EARLY), 0], early, sems.at[NV + 2]))
     for load in loads:
         load.start()
     lane = lanes(HALF)
@@ -155,29 +157,31 @@
     wet[...] = sea[...].astype(f32)
     pair = jnp.where(lane < 2, pltpu.roll(coef[...], 1, 1), pltpu.roll(wet[...], 3, 1))
     cols[COL_COEF : COL_COEF + T, :] = pair * column_keep(T)
-
-
-def outer_columns(state, vert, mask):
+    loads[NV + 2].wait()
+
+
+def outer_columns(state, vert, mask, weight):
     square = jax.ShapeDtypeStruct((T, T), f32)
     return pl.pallas_call(
         column_kernel,
-        in_specs=[HBM, HBM, HBM],
-        out_specs=[VMEM] * 4,
+        in_specs=[HBM] * 4,
+        out_specs=[VMEM] * 5,
         out_shape=[
             jax.ShapeDtypeStruct((COL_TOP, T), f32),
             jax.ShapeDtypeStruct((T * NV, T), f32),
             square,
             square,
+            jax.ShapeDtypeStruct((EARLY, FAN, T, T), bf16),
         ],
         scratch_shapes=[
             pltpu.VMEM((NV, LEV, T, T), f32),
             pltpu.VMEM((T, T), i32),
-            pltpu.SemaphoreType.DMA((NV + 2,)),
+            pltpu.SemaphoreType.DMA((NV + 3,)),
         ],
-        compiler_params=params(51 * MIB),
+        compiler_params=params(46 * MIB),
         cost_estimate=cost(6 << 20, 9 << 20),
         name="outer_columns",
-    )(state, vert, mask)
+    )(state, vert, mask, weight)
 
 
 def corner_kernel(cols, top, bottom, out):
@@ -211,7 +215,7 @@
 
 
 def remap_kernel(
-    dest_in, count_in, surf, weight, after, out, blocks, buffer, names, dest, count, used, label, sems
+    dest_in, count_in, surf, weight, early, after, out, blocks, buffer, names, dest, count, used, label, sems
 ):
     del after
     rows = T // CHUNKS
@@ -224,9 +228,10 @@
 
     def fetch(c):
         piece = pl.ds(c * rows, rows)
-        return pltpu.make_async_copy(weight.at[0, piece, 0], blocks.at[piece], sems.at[c])
-
-    for c in range(CHUNKS):
+        there = pl.ds(c * rows - EARLY, rows)
+        return pltpu.make_async_copy(weight.at[0, piece, 0], blocks.at[there], sems.at[c])
+
+    for c in range(EARLY // rows, CHUNKS):
         fetch(c).start()
     buffer[...] = jnp.zeros_like(buffer)
 
@@ -250,8 +255,7 @@
         label[jnp.where(live, peer * CAP + at, PEERS * CAP)] = (target & (T - 1)) + 1
         return jnp.where(live, peer * SIZE + at * NV, PEERS * SIZE)
 
-    def chunk(c, _):
-        fetch(c).wait()
+    def chunk(c, given, skipped):
         for r in range(0, rows, 2):
             row = c * rows + r
             places = [[place_of(row + q, f) for f in range(FAN)] for q in range(2)]
@@ -262,7 +266,7 @@
             for f in range(0, FAN, 2):
                 block = jnp.concatenate(
                     [
-                        jnp.concatenate([blocks[row + q, f], blocks[row + q, f + 1]], axis=1)
+                        jnp.concatenate([given[row + q - skipped, f + g] for g in range(2)], axis=1)
                         for q in range(2)
                     ],
                     axis=0,
@@ -272,9 +276,18 @@
                     for g in range(2):
                         part = product[q * NV : (q + 1) * NV, g * T : (g + 1) * T]
                         buffer[pl.ds(places[q][f + g], NV), :] = part
+
+    def near(c, _):
+        chunk(c, early, 0)
         return 0
 
-    lax.fori_loop(0, CHUNKS, chunk, 0)
+    def far(c, _):
+        fetch(c).wait()
+        chunk(c, blocks, EARLY)
+        return 0
+
+    lax.fori_loop(0, EARLY // rows, near, 0)
+    lax.fori_loop(EARLY // rows, CHUNKS, far, 0)
     lane = lanes(1)
 
     def name(i, _):
@@ -303,14 +316,14 @@
     run([pltpu.make_async_copy(buffer.at[pl.ds(0, PEERS * SIZE)], out, sems.at[0])])
 
 
-def remap(dest, count, surf, weight, after):
+def remap(dest, count, surf, weight, early, after):
     return pl.pallas_call(
         remap_kernel,
-        in_specs=[HBM, HBM, VMEM, HBM, HBM],
+        in_specs=[HBM, HBM, VMEM, HBM, VMEM, HBM],
         out_specs=HBM,
         out_shape=jax.ShapeDtypeStruct((PEERS * SIZE, T), f32),
         scratch_shapes=[
-            pltpu.VMEM((T, FAN, T, T), bf16),
+            pltpu.VMEM((T - EARLY, FAN, T, T), bf16),
             pltpu.VMEM((PEERS * SIZE + 8, T), f32),
             pltpu.VMEM((PEERS, T), f32),
             pltpu.SMEM((FAN, T), i32),
@@ -322,7 +335,7 @@
         compiler_params=params(44 * MIB),
         cost_estimate=cost(67 << 20, 20 << 20),
         name="remap",
-    )(dest, count, surf, weight, after)
+    )(dest, count, surf, weight, early, after)
 
 
 def sealed(block, *after):
@@ -663,11 +676,11 @@
 ):
     head, tail = outer_rows(state, vert_coef, sea_mask)
     top, bottom = shifted(tail, "gx", 1), shifted(head, "gx", -1)
-    cols, surf, coef, sea = outer_columns(state, vert_coef, sea_mask)
+    cols, surf, coef, sea, early = outer_columns(state, vert_coef, sea_mask, remap_weight)
     cols = with_corners(cols, top, bottom)
     left, right = shifted(cols, "gy", 1), shifted(cols, "gy", -1)
     dest = dest_block.reshape(T, FAN).T
-    packed = remap(dest, entry_count.reshape(1, T), surf, remap_weight, cols)
+    packed = remap(dest, entry_count.reshape(1, T), surf, remap_weight, early, cols)
     packed = sealed(packed, left, right).reshape(PEERS, SIZE, 1, T)
     packed = lax.all_to_all(packed, ("gx", "gy"), split_axis=0, concat_axis=0, tiled=True)
     mid, keep = two_steps(horiz_coef, state, coef, sea, cols, top, bottom, left, right)

time: 61.1 us -> 61.4 us (level)
  waiting for transfers between devices: 13.5 us -> 12.7 us
  starting transfers between devices: 19.7 us -> 20.4 us
    ppermute x4, waiting for transfers between devices: 1.2 us -> 0.38 us  [shifted(): lax.ppermute(block, axis, [(i, (i + by) % count) for i in range(count)])]
    all_to_all x1, starting transfers between devices: 8.83 us -> 9.57 us  [local(): lax.all_to_all(packed, ('gx', 'gy'), split_axis=0, concat_axis=0, tiled=T...]
where the time goes in v9:
time: 61.4 us; the launch traced here: 61.2 us
  Pallas kernels  25.7 us (42%)
  starting transfers between devices  20.4 us (33%)
  waiting for transfers between devices  12.7 us (21%)
  local copies, waits for them, and re-layouts  2.21 us (4%)
    all_to_all x1, starting transfers between devices, local(): lax.all_to_all(packed, ('gx', 'gy'), split_axis=0, concat_axis=0, tiled=T...  9.57 us
    pallas_call x1, Pallas kernels, two_steps(): pl.pallas_call(step_kernel, in_specs=[SMEM, HBM] + [VMEM] * 7, out_specs=...  9.38 us
    pallas_call x1, Pallas kernels, remap(): pl.pallas_call(remap_kernel, in_specs=[HBM, HBM, VMEM, HBM, VMEM, HBM], o...  8.43 us
    ppermute x4, starting transfers between devices, shifted(): lax.ppermute(block, axis, [(i, (i + by) % count) for i in range(count)])  6.78 us
    all_to_all x1, waiting for transfers between devices, local(): lax.all_to_all(packed, ('gx', 'gy'), split_axis=0, concat_axis=0, tiled=T...  6.69 us
    ppermute x3, waiting for transfers between devices, crossed(): return lax.ppermute(block, ('comp', 'gx', 'gy'), route)  5.62 us
    ppermute x3, starting transfers between devices, crossed(): return lax.ppermute(block, ('comp', 'gx', 'gy'), route)  4.1 us
    pallas_call x1, Pallas kernels, outer_columns(): pl.pallas_call(column_kernel, in_specs=[HBM] * 4, out_specs=[VMEM] * 5, o...  3.58 us
  transfers between devices with their start and end apart: 8, of which 3 were waited for; matrix products, arithmetic and copies ran while one was open for 0% of the time, Pallas kernels for 35%

profile of v9, /device:TPU:1, one launch (start us, length us, event | category | flops | bytes accessed | tf_op | source)
XLA Modules:
  0.0 61.2 jit_solution(12975826310490110384)
XLA Ops:
  0.0 1.8 %outer_rows.1 = (f32[144,128]{1,0:T(8,128)}, f32[144,128]{1,0:T(8,128)}) custom-call(f32[1,4,16,128,128]{4,3,2,1,0:T(8,128)} %state.5, f32[1,128,128]{2,1,0:T(8,128)} %vert.3, s32[1,128,128]{2,1,0:T(8,128)} %mask.3), custom_call_target="tpu_custom_call" | custom-call | flops 65536 | bytes 524288 | tf_op jit(solution)/shard_map/outer_rows/pallas_call | solution.py:110
  1.8 3.0 %collective-permute-start = (f32[144,128]{1,0:T(8,128)}, f32[144,128]{1,0:T(8,128)S(1)}, u32[]{:S(2)}, u32[]{:S(2)}) collective-permute-start(f32[144,128]{1,0:T(8,128)} %get-tuple-element.20), channel_id=1, source_target_pairs={{0,8},{8,16},{16,24},{24,32},{32,40},{40,48},{48,56},{56,0},{1,9},... | collective-permute-start | bytes 221192 | tf_op jit(solution)/shard_map/ppermute | solution.py:660
  4.9 0.0 collective-permute-start.1
  4.9 3.6 %outer_columns.1 = (f32[384,128]{1,0:T(8,128)S(1)}, f32[512,128]{1,0:T(8,128)S(1)}, f32[128,128]{1,0:T(8,128)S(1)}, f32[128,128]{1,0:T(8,128)S(1)}, bf16[32,4,128,128]{3,2,1,0:T(8,128)(2,1)S(1)}) custom-call(f32[1,4,16,128,128]{4,3,2,1,0:T(8,128)} %state.5, f32[1,128,128]{2,1,0:T(8,128)S(1)} %copy-done.1, s32[1,128,128]{2,1,0:T(8,128)S(1)} %copy-done.2, ...), custom_call_target="tpu_custom_call" | custom-call | flops 6291456 | bytes 9437184 | tf_op jit(solution)/shard_map/outer_columns/pallas_call | solution.py:165
  8.5 0.0 collective-permute-done.top
  8.5 0.4 collective-permute-done.1.bottom
  8.9 0.1 with_corners.1.own.after
  9.0 3.7 %collective-permute-start.3 = (f32[400,128]{1,0:T(8,128)S(1)}, f32[400,128]{1,0:T(8,128)S(1)}, u32[]{:S(2)}, u32[]{:S(2)}) collective-permute-start(f32[400,128]{1,0:T(8,128)S(1)} %with_corners.1.own.after), channel_id=1, source_target_pairs={{0,7},{1,0},{2,1},{3,2},{4,3},{5,4},{6,5},{7,6},{8,15},{9,8},{10,9... | collective-permute-start | bytes 614408 | tf_op jit(solution)/shard_map/ppermute | solution.py:660
  12.7 8.4 %remap.1.refs_0_ = f32[2112,128]{1,0:T(8,128)} custom-call(s32[4,128]{1,0:T(4,128)S(1)} %bitcast.7, s32[1,128]{1,0:T(1,128)S(1)} %bitcast.8, f32[512,128]{1,0:T(8,128)S(1)} %get-tuple-element.24.surf, bf16[1,128,1,4,128,128]{5,4,3,2,1,0:T(8,128)(2,1)} %weight.3, bf16[32,4,128,128]{3,2,1,0:T(8,128)(2,1)S(1)} %get-tuple-element.25.early, ...), custom_call_target="tpu_custom_call" | custom-call | flops 70254592 | bytes 20971520 | tf_op jit(solution)/shard_map/remap/pallas_call | solution.py:320
  21.2 0.0 copy-start.4
  21.2 0.0 collective-permute-done.2.near.refs_1_
  21.2 0.0 copy-start.6
  21.2 9.6 %all-to-all-start = ((f32[64,33,1,128]{3,2,1,0:T(1,128)}), f32[64,33,1,128]{3,2,1,0:T(1,128)S(1)}, u32[]{:S(2)}, u32[]{:S(2)}) async-start(f32[64,33,1,128]{3,2,1,0:T(1,128)} %bitcast.3), calls=%async_computation | async-start | bytes 2162688 | tf_op jit(solution)/shard_map/all_to_all | solution.py:685
  30.8 0.0 copy-start
  30.8 2.2 %copy-done = f32[1,4,16,128,128]{4,3,2,1,0:T(8,128)S(1)} copy-done((f32[1,4,16,128,128]{4,3,2,1,0:T(8,128)S(1)}, f32[1,4,16,128,128]{4,3,2,1,0:T(8,128)}, u32[]{:S(2)}) %copy-start) | copy-done | bytes 4194328
  33.0 9.4 %two_steps.1 = (f32[1,4,16,128,128]{4,3,2,1,0:T(8,128)}, f32[2064,128]{1,0:T(8,128)S(1)}) custom-call(f32[1,4]{1,0:T(1,128)S(1)} %copy-done.4, f32[1,4,16,128,128]{4,3,2,1,0:T(8,128)S(1)} %copy-done, f32[128,128]{1,0:T(8,128)S(1)} %get-tuple-element.17.coef, f32[128,128]{1,0:T(8,128)S(1)} %get-tuple-element.18.sea, f32[400,128]{1,0:T(8,128)S(1)} %with_corners.1.own.after, ...), custom_call_target="tpu_custom_call" | custom-call | flops 50331648 | bytes 10485760 | tf_op jit(solution)/shard_map/two_steps/pallas_call | solution.py:513
  42.4 6.7 %all-to-all-done = f32[64,33,1,128]{3,2,1,0:T(1,128)S(1)} async-done(((f32[64,33,1,128]{3,2,1,0:T(1,128)}), f32[64,33,1,128]{3,2,1,0:T(1,128)S(1)}, u32[]{:S(2)}, u32[]{:S(2)}) %all-to-all-start) | async-done | bytes 1081376 | tf_op jit(solution)/shard_map/all_to_all | solution.py:685
  49.1 0.7 %unpack.1 = (f32[520,128]{1,0:T(8,128)S(1)}, f32[8,128]{1,0:T(8,128)S(1)}, f32[8,128]{1,0:T(8,128)S(1)}) custom-call(f32[2112,128]{1,0:T(8,128)S(1)} %bitcast.6, f32[2064,128]{1,0:T(8,128)S(1)} %get-tuple-element.23.after.near), custom_call_target="tpu_custom_call" | custom-call | flops 209715200 | bytes 2097152 | tf_op jit(solution)/shard_map/unpack/pallas_call | solution.py:585
  49.8 1.1 %collective-permute-start.4 = (f32[520,128]{1,0:T(8,128)S(1)}, f32[520,128]{1,0:T(8,128)S(1)}, u32[]{:S(2)}, u32[]{:S(2)}) collective-permute-start(f32[520,128]{1,0:T(8,128)S(1)} %get-tuple-element.26), channel_id=1, source_target_pairs={{0,68},{1,69},{2,70},{3,71},{4,64},{5,65},{6,66},{7,67},{8,76},{9,... | collective-permute-start | bytes 798728 | tf_op jit(solution)/shard_map/ppermute | solution.py:671
  50.9 1.8 %collective-permute-start.5 = (f32[8,128]{1,0:T(8,128)S(1)}, f32[8,128]{1,0:T(8,128)S(1)}, u32[]{:S(2)}, u32[]{:S(2)}) collective-permute-start(f32[8,128]{1,0:T(8,128)S(1)} %get-tuple-element.27), channel_id=1, source_target_pairs={{0,76},{1,77},{2,78},{3,79},{4,72},{5,73},{6,74},{7,75},{8,84},{9,... | collective-permute-start | bytes 12296 | tf_op jit(solution)/shard_map/ppermute | solution.py:671
  52.7 1.2 %collective-permute-start.6 = (f32[8,128]{1,0:T(8,128)S(1)}, f32[8,128]{1,0:T(8,128)S(1)}, u32[]{:S(2)}, u32[]{:S(2)}) collective-permute-start(f32[8,128]{1,0:T(8,128)S(1)} %get-tuple-element.28), channel_id=1, source_target_pairs={{0,124},{1,125},{2,126},{3,127},{4,120},{5,121},{6,122},{7,123},{8... | collective-permute-start | bytes 12296 | tf_op jit(solution)/shard_map/ppermute | solution.py:671
  53.9 5.6 %collective-permute-done.5.imp_top = f32[8,128]{1,0:T(8,128)S(1)} collective-permute-done((f32[8,128]{1,0:T(8,128)S(1)}, f32[8,128]{1,0:T(8,128)S(1)}, u32[]{:S(2)}, u32[]{:S(2)}) %collective-permute-start.5) | collective-permute-done | bytes 4128 | tf_op jit(solution)/shard_map/ppermute | solution.py:671
  59.5 0.0 collective-permute-done.6.imp_bottom
  59.5 1.7 %final.1 = f32[1,4,16,128,128]{4,3,2,1,0:T(8,128)} custom-call(f32[1,4]{1,0:T(1,128)S(1)} %copy-done.4, f32[1,4]{1,0:T(1,128)S(1)} %copy-done.6, f32[1,4,16,128,128]{4,3,2,1,0:T(8,128)} %get-tuple-element.22.mid, f32[2064,128]{1,0:T(8,128)S(1)} %get-tuple-element.23.after.near, ...), custom_call_target="tpu_custom_call", output_to_operand_aliasing={{}: (2, {})} | custom-call | flops 2097152 | bytes 3145728 | tf_op jit(solution)/shard_map/final/pallas_call | solution.py:642
  (14 shorter events, 0.0 us)
Async XLA Ops:
  0.0 4.9 %copy-start.2 = (s32[1,128,128]{2,1,0:T(8,128)S(1)}, s32[1,128,128]{2,1,0:T(8,128)}, u32[]{:S(2)}) copy-start(s32[1,128,128]{2,1,0:T(8,128)} %mask.3) | copy-start | bytes 196612
  0.0 4.9 %copy-start.1 = (f32[1,128,128]{2,1,0:T(8,128)S(1)}, f32[1,128,128]{2,1,0:T(8,128)}, u32[]{:S(2)}) copy-start(f32[1,128,128]{2,1,0:T(8,128)} %vert.3) | copy-start | bytes 196612
  1.8 6.7 %collective-permute-start = (f32[144,128]{1,0:T(8,128)}, f32[144,128]{1,0:T(8,128)S(1)}, u32[]{:S(2)}, u32[]{:S(2)}) collective-permute-start(f32[144,128]{1,0:T(8,128)} %get-tuple-element.20), channel_id=1, source_target_pairs={{0,8},{8,16},{16,24},{24,32},{32,40},{40,48},{48,56},{56,0},{1,9},... | collective-permute-start | bytes 221192 | tf_op jit(solution)/shard_map/ppermute | solution.py:660
  4.9 7.9 %copy-start.3 = (s32[1,128,1,4]{1,3,2,0:T(4,128)S(1)}, s32[1,128,1,4]{1,3,2,0:T(4,128)}, u32[]{:S(2)}) copy-start(s32[1,128,1,4]{1,3,2,0:T(4,128)} %param.13) | copy-start | bytes 6148
  4.9 7.9 %copy-start.5 = (s32[1,128,1]{1,2,0:T(1,128)S(1)}, s32[1,128,1]{1,2,0:T(1,128)}, u32[]{:S(2)}) copy-start(s32[1,128,1]{1,2,0:T(1,128)} %param.14) | copy-start | bytes 1540
  4.9 4.0 %collective-permute-start.1 = (f32[144,128]{1,0:T(8,128)}, f32[144,128]{1,0:T(8,128)S(1)}, u32[]{:S(2)}, u32[]{:S(2)}) collective-permute-start(f32[144,128]{1,0:T(8,128)} %get-tuple-element.21), channel_id=1, source_target_pairs={{0,56},{8,0},{16,8},{24,16},{32,24},{40,32},{48,40},{56,48},{1,57}... | collective-permute-start | bytes 221192 | tf_op jit(solution)/shard_map/ppermute | solution.py:660
  9.0 12.2 %collective-permute-start.3 = (f32[400,128]{1,0:T(8,128)S(1)}, f32[400,128]{1,0:T(8,128)S(1)}, u32[]{:S(2)}, u32[]{:S(2)}) collective-permute-start(f32[400,128]{1,0:T(8,128)S(1)} %with_corners.1.own.after), channel_id=1, source_target_pairs={{0,7},{1,0},{2,1},{3,2},{4,3},{5,4},{6,5},{7,6},{8,15},{9,8},{10,9... | collective-permute-start | bytes 614408 | tf_op jit(solution)/shard_map/ppermute | solution.py:660
  12.7 8.5 %collective-permute-start.2 = (f32[400,128]{1,0:T(8,128)S(1)}, f32[400,128]{1,0:T(8,128)S(1)}, u32[]{:S(2)}, u32[]{:S(2)}) collective-permute-start(f32[400,128]{1,0:T(8,128)S(1)} %with_corners.1.own.after), channel_id=1, source_target_pairs={{0,1},{1,2},{2,3},{3,4},{4,5},{5,6},{6,7},{7,0},{8,9},{9,10},{10,1... | collective-permute-start | bytes 614408 | tf_op jit(solution)/shard_map/ppermute | solution.py:660
  21.2 9.6 %copy-start.4 = (f32[1,4]{1,0:T(1,128)S(1)}, f32[1,4]{1,0:T(1,128)}, u32[]{:S(2)}) copy-start(f32[1,4]{1,0:T(1,128)} %horiz.1) | copy-start | bytes 52
  21.2 38.3 %copy-start.6 = (f32[1,4]{1,0:T(1,128)S(1)}, f32[1,4]{1,0:T(1,128)}, u32[]{:S(2)}) copy-start(f32[1,4]{1,0:T(1,128)} %relax.1) | copy-start | bytes 52
  21.2 27.8 %all-to-all-start = ((f32[64,33,1,128]{3,2,1,0:T(1,128)}), f32[64,33,1,128]{3,2,1,0:T(1,128)S(1)}, u32[]{:S(2)}, u32[]{:S(2)}) async-start(f32[64,33,1,128]{3,2,1,0:T(1,128)} %bitcast.3), calls=%async_computation | async-start | bytes 2162688 | tf_op jit(solution)/shard_map/all_to_all | solution.py:685
  30.8 2.2 %copy-start = (f32[1,4,16,128,128]{4,3,2,1,0:T(8,128)S(1)}, f32[1,4,16,128,128]{4,3,2,1,0:T(8,128)}, u32[]{:S(2)}) copy-start(f32[1,4,16,128,128]{4,3,2,1,0:T(8,128)} %state.5) | copy-start | bytes 12582916
  49.8 9.7 %collective-permute-start.4 = (f32[520,128]{1,0:T(8,128)S(1)}, f32[520,128]{1,0:T(8,128)S(1)}, u32[]{:S(2)}, u32[]{:S(2)}) collective-permute-start(f32[520,128]{1,0:T(8,128)S(1)} %get-tuple-element.26), channel_id=1, source_target_pairs={{0,68},{1,69},{2,70},{3,71},{4,64},{5,65},{6,66},{7,67},{8,76},{9,... | collective-permute-start | bytes 798728 | tf_op jit(solution)/shard_map/ppermute | solution.py:671
  50.9 8.6 %collective-permute-start.5 = (f32[8,128]{1,0:T(8,128)S(1)}, f32[8,128]{1,0:T(8,128)S(1)}, u32[]{:S(2)}, u32[]{:S(2)}) collective-permute-start(f32[8,128]{1,0:T(8,128)S(1)} %get-tuple-element.27), channel_id=1, source_target_pairs={{0,76},{1,77},{2,78},{3,79},{4,72},{5,73},{6,74},{7,75},{8,84},{9,... | collective-permute-start | bytes 12296 | tf_op jit(solution)/shard_map/ppermute | solution.py:671
  52.7 6.8 %collective-permute-start.6 = (f32[8,128]{1,0:T(8,128)S(1)}, f32[8,128]{1,0:T(8,128)S(1)}, u32[]{:S(2)}, u32[]{:S(2)}) collective-permute-start(f32[8,128]{1,0:T(8,128)S(1)} %get-tuple-element.28), channel_id=1, source_target_pairs={{0,124},{1,125},{2,126},{3,127},{4,120},{5,121},{6,122},{7,123},{8... | collective-permute-start | bytes 12296 | tf_op jit(solution)/shard_map/ppermute | solution.py:671

commit v10 on v8

--- a/solution.py
+++ b/solution.py
@@ -231,9 +231,10 @@
     buffer[...] = jnp.zeros_like(buffer)
 
     def clear(i, _):
-        used[i] = 0
+        row = (i ^ MIRROR) * SIZE
+        used[i] = row
         for k in range(CAP):
-            label[i * CAP + k] = 0
+            label[row + k * NV] = 0
         return 0
 
     lax.fori_loop(0, PEERS, clear, 0)
@@ -243,12 +244,13 @@
 
     def place_of(row, f):
         target = dest[f, row]
-        peer = (lax.shift_right_logical(target, 7) & (PEERS - 1)) ^ MIRROR
+        device = lax.shift_right_logical(target, 7) & (PEERS - 1)
         live = f < count[0, row]
-        at = used[peer]
-        used[peer] = at + jnp.where(live, 1, 0)
-        label[jnp.where(live, peer * CAP + at, PEERS * CAP)] = (target & (T - 1)) + 1
-        return jnp.where(live, peer * SIZE + at * NV, PEERS * SIZE)
+        at = used[device]
+        used[device] = jnp.where(live, at + NV, at)
+        place = jnp.where(live, at, PEERS * SIZE)
+        label[place] = (target & (T - 1)) + 1
+        return place
 
     def chunk(c, _):
         fetch(c).wait()
@@ -280,7 +282,7 @@
     def name(i, _):
         line = jnp.zeros((1, T), i32)
         for k in range(CAP):
-            line = jnp.where(lane == k, label[i * CAP + k], line)
+            line = jnp.where(lane == k, label[i * SIZE + k * NV], line)
         names[pl.ds(i, 1), :] = line.astype(f32)
         return 0
 
@@ -316,7 +318,7 @@
             pltpu.SMEM((FAN, T), i32),
             pltpu.SMEM((1, T), i32),
             pltpu.SMEM((PEERS,), i32),
-            pltpu.SMEM((PEERS * CAP + 8,), i32),
+            pltpu.SMEM((PEERS * SIZE + 8,), i32),
             pltpu.SemaphoreType.DMA((CHUNKS + 2,)),
         ],
         compiler_params=params(44 * MIB),

time: 61.1 us -> 60.1 us (0.984)
  Pallas kernels: 25.3 us -> 24.3 us
    pallas_call x1, Pallas kernels: 8.83 us -> 7.88 us  [remap(): pl.pallas_call(remap_kernel, in_specs=[HBM, HBM, VMEM, HBM, HBM], out_spe...]
  transfers between devices with their start and end apart: 8 -> 8, of which waited for: 3 -> 3; matrix products, arithmetic and copies ran while one was open for 0% -> 0% of each run, Pallas kernels for 35% -> 33%
where the time goes in v10:
time: 60.1 us; the launch traced here: 59.9 us
  Pallas kernels  24.3 us (40%)
  starting transfers between devices  19.7 us (33%)
  waiting for transfers between devices  13.5 us (22%)
  local copies, waits for them, and re-layouts  2.21 us (4%)
    pallas_call x1, Pallas kernels, two_steps(): pl.pallas_call(step_kernel, in_specs=[SMEM, HBM] + [VMEM] * 7, out_specs=...  9.38 us
    all_to_all x1, starting transfers between devices, local(): lax.all_to_all(packed, ('gx', 'gy'), split_axis=0, concat_axis=0, tiled=T...  8.83 us
    pallas_call x1, Pallas kernels, remap(): pl.pallas_call(remap_kernel, in_specs=[HBM, HBM, VMEM, HBM, HBM], out_spe...  7.88 us
    ppermute x4, starting transfers between devices, shifted(): lax.ppermute(block, axis, [(i, (i + by) % count) for i in range(count)])  6.78 us
    all_to_all x1, waiting for transfers between devices, local(): lax.all_to_all(packed, ('gx', 'gy'), split_axis=0, concat_axis=0, tiled=T...  6.69 us
    ppermute x3, waiting for transfers between devices, crossed(): return lax.ppermute(block, ('comp', 'gx', 'gy'), route)  5.62 us
    ppermute x3, starting transfers between devices, crossed(): return lax.ppermute(block, ('comp', 'gx', 'gy'), route)  4.1 us
    pallas_call x1, Pallas kernels, outer_columns(): pl.pallas_call(column_kernel, in_specs=[HBM, HBM, HBM], out_specs=[VMEM]...  2.77 us
  transfers between devices with their start and end apart: 8, of which 3 were waited for; matrix products, arithmetic and copies ran while one was open for 0% of the time, Pallas kernels for 33%

profile of v10, /device:TPU:1, one launch (start us, length us, event | category | flops | bytes accessed | tf_op | source)
XLA Modules:
  0.0 59.9 jit_solution(12577101682263056965)
XLA Ops:
  0.0 1.8 %outer_rows.1 = (f32[144,128]{1,0:T(8,128)}, f32[144,128]{1,0:T(8,128)}) custom-call(f32[1,4,16,128,128]{4,3,2,1,0:T(8,128)} %state.5, f32[1,128,128]{2,1,0:T(8,128)} %vert.3, s32[1,128,128]{2,1,0:T(8,128)} %mask.3), custom_call_target="tpu_custom_call" | custom-call | flops 65536 | bytes 524288 | tf_op jit(solution)/shard_map/outer_rows/pallas_call | solution.py:109
  1.9 3.0 %collective-permute-start = (f32[144,128]{1,0:T(8,128)}, f32[144,128]{1,0:T(8,128)S(1)}, u32[]{:S(2)}, u32[]{:S(2)}) collective-permute-start(f32[144,128]{1,0:T(8,128)} %get-tuple-element.19), channel_id=1, source_target_pairs={{0,8},{8,16},{16,24},{24,32},{32,40},{40,48},{48,56},{56,0},{1,9},... | collective-permute-start | bytes 221192 | tf_op jit(solution)/shard_map/ppermute | solution.py:649
  4.9 0.0 collective-permute-start.1
  4.9 2.8 %outer_columns.1 = (f32[384,128]{1,0:T(8,128)S(1)}, f32[512,128]{1,0:T(8,128)S(1)}, f32[128,128]{1,0:T(8,128)S(1)}, f32[128,128]{1,0:T(8,128)S(1)}) custom-call(f32[1,4,16,128,128]{4,3,2,1,0:T(8,128)} %state.5, f32[1,128,128]{2,1,0:T(8,128)S(1)} %copy-done.1, s32[1,128,128]{2,1,0:T(8,128)S(1)} %copy-done.2), custom_call_target="tpu_custom_call" | custom-call | flops 6291456 | bytes 9437184 | tf_op jit(solution)/shard_map/outer_columns/pallas_call | solution.py:162
  7.7 1.2 %collective-permute-done.1.bottom = f32[144,128]{1,0:T(8,128)S(1)} collective-permute-done((f32[144,128]{1,0:T(8,128)}, f32[144,128]{1,0:T(8,128)S(1)}, u32[]{:S(2)}, u32[]{:S(2)}) %collective-permute-start.1) | collective-permute-done | bytes 73760 | tf_op jit(solution)/shard_map/ppermute | solution.py:649
  8.9 0.1 with_corners.1.own.after
  9.0 3.7 %collective-permute-start.3 = (f32[400,128]{1,0:T(8,128)S(1)}, f32[400,128]{1,0:T(8,128)S(1)}, u32[]{:S(2)}, u32[]{:S(2)}) collective-permute-start(f32[400,128]{1,0:T(8,128)S(1)} %with_corners.1.own.after), channel_id=1, source_target_pairs={{0,7},{1,0},{2,1},{3,2},{4,3},{5,4},{6,5},{7,6},{8,15},{9,8},{10,9... | collective-permute-start | bytes 614408 | tf_op jit(solution)/shard_map/ppermute | solution.py:649
  12.7 0.0 collective-permute-start.2
  12.8 7.9 %remap.1.refs_0_ = f32[2112,128]{1,0:T(8,128)} custom-call(s32[4,128]{1,0:T(4,128)S(1)} %bitcast.7, s32[1,128]{1,0:T(1,128)S(1)} %bitcast.8, f32[512,128]{1,0:T(8,128)S(1)} %get-tuple-element.23.surf, bf16[1,128,1,4,128,128]{5,4,3,2,1,0:T(8,128)(2,1)} %weight.1, f32[400,128]{1,0:T(8,128)S(1)} %with_corners.1.own.after), custom_call_target="tpu_custom_call" | custom-call | flops 70254592 | bytes 20971520 | tf_op jit(solution)/shard_map/remap/pallas_call | solution.py:309
  20.6 0.0 copy-start.3
  20.7 0.0 collective-permute-done.3.far.refs_2_
  20.7 0.0 copy-start.6
  20.7 8.8 %all-to-all-start = ((f32[64,33,1,128]{3,2,1,0:T(1,128)}), f32[64,33,1,128]{3,2,1,0:T(1,128)S(1)}, u32[]{:S(2)}, u32[]{:S(2)}) async-start(f32[64,33,1,128]{3,2,1,0:T(1,128)} %bitcast.3), calls=%async_computation | async-start | bytes 2162688 | tf_op jit(solution)/shard_map/all_to_all | solution.py:674
  29.6 0.0 copy-start
  29.6 2.2 %copy-done = f32[1,4,16,128,128]{4,3,2,1,0:T(8,128)S(1)} copy-done((f32[1,4,16,128,128]{4,3,2,1,0:T(8,128)S(1)}, f32[1,4,16,128,128]{4,3,2,1,0:T(8,128)}, u32[]{:S(2)}) %copy-start) | copy-done | bytes 4194328
  31.7 9.4 %two_steps.1 = (f32[1,4,16,128,128]{4,3,2,1,0:T(8,128)}, f32[2064,128]{1,0:T(8,128)S(1)}) custom-call(f32[1,4]{1,0:T(1,128)S(1)} %copy-done.3, f32[1,4,16,128,128]{4,3,2,1,0:T(8,128)S(1)} %copy-done, f32[128,128]{1,0:T(8,128)S(1)} %get-tuple-element.16.coef, f32[128,128]{1,0:T(8,128)S(1)} %get-tuple-element.17.sea, f32[400,128]{1,0:T(8,128)S(1)} %with_corners.1.own.after, ...), custom_call_target="tpu_custom_call" | custom-call | flops 50331648 | bytes 10485760 | tf_op jit(solution)/shard_map/two_steps/pallas_call | solution.py:502
  41.1 6.7 %all-to-all-done = f32[64,33,1,128]{3,2,1,0:T(1,128)S(1)} async-done(((f32[64,33,1,128]{3,2,1,0:T(1,128)}), f32[64,33,1,128]{3,2,1,0:T(1,128)S(1)}, u32[]{:S(2)}, u32[]{:S(2)}) %all-to-all-start) | async-done | bytes 1081376 | tf_op jit(solution)/shard_map/all_to_all | solution.py:674
  47.8 0.7 %unpack.1 = (f32[520,128]{1,0:T(8,128)S(1)}, f32[8,128]{1,0:T(8,128)S(1)}, f32[8,128]{1,0:T(8,128)S(1)}) custom-call(f32[2112,128]{1,0:T(8,128)S(1)} %bitcast.6, f32[2064,128]{1,0:T(8,128)S(1)} %get-tuple-element.22.after.near), custom_call_target="tpu_custom_call" | custom-call | flops 209715200 | bytes 2097152 | tf_op jit(solution)/shard_map/unpack/pallas_call | solution.py:574
  48.5 1.1 %collective-permute-start.4 = (f32[520,128]{1,0:T(8,128)S(1)}, f32[520,128]{1,0:T(8,128)S(1)}, u32[]{:S(2)}, u32[]{:S(2)}) collective-permute-start(f32[520,128]{1,0:T(8,128)S(1)} %get-tuple-element.24), channel_id=1, source_target_pairs={{0,68},{1,69},{2,70},{3,71},{4,64},{5,65},{6,66},{7,67},{8,76},{9,... | collective-permute-start | bytes 798728 | tf_op jit(solution)/shard_map/ppermute | solution.py:660
  49.6 1.8 %collective-permute-start.5 = (f32[8,128]{1,0:T(8,128)S(1)}, f32[8,128]{1,0:T(8,128)S(1)}, u32[]{:S(2)}, u32[]{:S(2)}) collective-permute-start(f32[8,128]{1,0:T(8,128)S(1)} %get-tuple-element.25), channel_id=1, source_target_pairs={{0,76},{1,77},{2,78},{3,79},{4,72},{5,73},{6,74},{7,75},{8,84},{9,... | collective-permute-start | bytes 12296 | tf_op jit(solution)/shard_map/ppermute | solution.py:660
  51.4 1.2 %collective-permute-start.6 = (f32[8,128]{1,0:T(8,128)S(1)}, f32[8,128]{1,0:T(8,128)S(1)}, u32[]{:S(2)}, u32[]{:S(2)}) collective-permute-start(f32[8,128]{1,0:T(8,128)S(1)} %get-tuple-element.26), channel_id=1, source_target_pairs={{0,124},{1,125},{2,126},{3,127},{4,120},{5,121},{6,122},{7,123},{8... | collective-permute-start | bytes 12296 | tf_op jit(solution)/shard_map/ppermute | solution.py:660
  52.6 5.6 %collective-permute-done.5.imp_top = f32[8,128]{1,0:T(8,128)S(1)} collective-permute-done((f32[8,128]{1,0:T(8,128)S(1)}, f32[8,128]{1,0:T(8,128)S(1)}, u32[]{:S(2)}, u32[]{:S(2)}) %collective-permute-start.5) | collective-permute-done | bytes 4128 | tf_op jit(solution)/shard_map/ppermute | solution.py:660
  58.2 0.0 collective-permute-done.6.imp_bottom
  58.2 1.7 %final.1 = f32[1,4,16,128,128]{4,3,2,1,0:T(8,128)} custom-call(f32[1,4]{1,0:T(1,128)S(1)} %copy-done.3, f32[1,4]{1,0:T(1,128)S(1)} %copy-done.6, f32[1,4,16,128,128]{4,3,2,1,0:T(8,128)} %get-tuple-element.21.mid, f32[2064,128]{1,0:T(8,128)S(1)} %get-tuple-element.22.after.near, ...), custom_call_target="tpu_custom_call", output_to_operand_aliasing={{}: (2, {})} | custom-call | flops 2097152 | bytes 3145728 | tf_op jit(solution)/shard_map/final/pallas_call | solution.py:631
  (14 shorter events, 0.0 us)
Async XLA Ops:
  0.0 4.9 %copy-start.2 = (s32[1,128,128]{2,1,0:T(8,128)S(1)}, s32[1,128,128]{2,1,0:T(8,128)}, u32[]{:S(2)}) copy-start(s32[1,128,128]{2,1,0:T(8,128)} %mask.3) | copy-start | bytes 196612
  0.0 4.9 %copy-start.1 = (f32[1,128,128]{2,1,0:T(8,128)S(1)}, f32[1,128,128]{2,1,0:T(8,128)}, u32[]{:S(2)}) copy-start(f32[1,128,128]{2,1,0:T(8,128)} %vert.3) | copy-start | bytes 196612
  0.0 12.8 %copy-start.5 = (s32[1,128,1]{1,2,0:T(1,128)S(1)}, s32[1,128,1]{1,2,0:T(1,128)}, u32[]{:S(2)}) copy-start(s32[1,128,1]{1,2,0:T(1,128)} %param.14) | copy-start | bytes 1540
  0.0 12.7 %copy-start.4 = (s32[1,128,1,4]{1,3,2,0:T(4,128)S(1)}, s32[1,128,1,4]{1,3,2,0:T(4,128)}, u32[]{:S(2)}) copy-start(s32[1,128,1,4]{1,3,2,0:T(4,128)} %param.13) | copy-start | bytes 6148
  1.9 5.8 %collective-permute-start = (f32[144,128]{1,0:T(8,128)}, f32[144,128]{1,0:T(8,128)S(1)}, u32[]{:S(2)}, u32[]{:S(2)}) collective-permute-start(f32[144,128]{1,0:T(8,128)} %get-tuple-element.19), channel_id=1, source_target_pairs={{0,8},{8,16},{16,24},{24,32},{32,40},{40,48},{48,56},{56,0},{1,9},... | collective-permute-start | bytes 221192 | tf_op jit(solution)/shard_map/ppermute | solution.py:649
  4.9 4.0 %collective-permute-start.1 = (f32[144,128]{1,0:T(8,128)}, f32[144,128]{1,0:T(8,128)S(1)}, u32[]{:S(2)}, u32[]{:S(2)}) collective-permute-start(f32[144,128]{1,0:T(8,128)} %get-tuple-element.20), channel_id=1, source_target_pairs={{0,56},{8,0},{16,8},{24,16},{32,24},{40,32},{48,40},{56,48},{1,57}... | collective-permute-start | bytes 221192 | tf_op jit(solution)/shard_map/ppermute | solution.py:649
  9.0 11.6 %collective-permute-start.3 = (f32[400,128]{1,0:T(8,128)S(1)}, f32[400,128]{1,0:T(8,128)S(1)}, u32[]{:S(2)}, u32[]{:S(2)}) collective-permute-start(f32[400,128]{1,0:T(8,128)S(1)} %with_corners.1.own.after), channel_id=1, source_target_pairs={{0,7},{1,0},{2,1},{3,2},{4,3},{5,4},{6,5},{7,6},{8,15},{9,8},{10,9... | collective-permute-start | bytes 614408 | tf_op jit(solution)/shard_map/ppermute | solution.py:649
  12.7 7.9 %collective-permute-start.2 = (f32[400,128]{1,0:T(8,128)S(1)}, f32[400,128]{1,0:T(8,128)S(1)}, u32[]{:S(2)}, u32[]{:S(2)}) collective-permute-start(f32[400,128]{1,0:T(8,128)S(1)} %with_corners.1.own.after), channel_id=1, source_target_pairs={{0,1},{1,2},{2,3},{3,4},{4,5},{5,6},{6,7},{7,0},{8,9},{9,10},{10,1... | collective-permute-start | bytes 614408 | tf_op jit(solution)/shard_map/ppermute | solution.py:649
  20.6 8.9 %copy-start.3 = (f32[1,4]{1,0:T(1,128)S(1)}, f32[1,4]{1,0:T(1,128)}, u32[]{:S(2)}) copy-start(f32[1,4]{1,0:T(1,128)} %horiz.1) | copy-start | bytes 52
  20.7 37.5 %copy-start.6 = (f32[1,4]{1,0:T(1,128)S(1)}, f32[1,4]{1,0:T(1,128)}, u32[]{:S(2)}) copy-start(f32[1,4]{1,0:T(1,128)} %relax.1) | copy-start | bytes 52
  20.7 27.1 %all-to-all-start = ((f32[64,33,1,128]{3,2,1,0:T(1,128)}), f32[64,33,1,128]{3,2,1,0:T(1,128)S(1)}, u32[]{:S(2)}, u32[]{:S(2)}) async-start(f32[64,33,1,128]{3,2,1,0:T(1,128)} %bitcast.3), calls=%async_computation | async-start | bytes 2162688 | tf_op jit(solution)/shard_map/all_to_all | solution.py:674
  29.6 2.2 %copy-start = (f32[1,4,16,128,128]{4,3,2,1,0:T(8,128)S(1)}, f32[1,4,16,128,128]{4,3,2,1,0:T(8,128)}, u32[]{:S(2)}) copy-start(f32[1,4,16,128,128]{4,3,2,1,0:T(8,128)} %state.5) | copy-start | bytes 12582916
  48.5 9.7 %collective-permute-start.4 = (f32[520,128]{1,0:T(8,128)S(1)}, f32[520,128]{1,0:T(8,128)S(1)}, u32[]{:S(2)}, u32[]{:S(2)}) collective-permute-start(f32[520,128]{1,0:T(8,128)S(1)} %get-tuple-element.24), channel_id=1, source_target_pairs={{0,68},{1,69},{2,70},{3,71},{4,64},{5,65},{6,66},{7,67},{8,76},{9,... | collective-permute-start | bytes 798728 | tf_op jit(solution)/shard_map/ppermute | solution.py:660
  49.6 8.6 %collective-permute-start.5 = (f32[8,128]{1,0:T(8,128)S(1)}, f32[8,128]{1,0:T(8,128)S(1)}, u32[]{:S(2)}, u32[]{:S(2)}) collective-permute-start(f32[8,128]{1,0:T(8,128)S(1)} %get-tuple-element.25), channel_id=1, source_target_pairs={{0,76},{1,77},{2,78},{3,79},{4,72},{5,73},{6,74},{7,75},{8,84},{9,... | collective-permute-start | bytes 12296 | tf_op jit(solution)/shard_map/ppermute | solution.py:660
  51.4 6.8 %collective-permute-start.6 = (f32[8,128]{1,0:T(8,128)S(1)}, f32[8,128]{1,0:T(8,128)S(1)}, u32[]{:S(2)}, u32[]{:S(2)}) collective-permute-start(f32[8,128]{1,0:T(8,128)S(1)} %get-tuple-element.26), channel_id=1, source_target_pairs={{0,124},{1,125},{2,126},{3,127},{4,120},{5,121},{6,122},{7,123},{8... | collective-permute-start | bytes 12296 | tf_op jit(solution)/shard_map/ppermute | solution.py:660

commit v11 on v10

--- a/solution.py
+++ b/solution.py
@@ -24,7 +24,7 @@
 ROW_SIZE = ROW_SEA + 8
 COL_NEXT = T
 COL_COEF = 2 * T
-COL_TOP = 3 * T
+COL_TOP = COL_COEF + 8
 COL_BOTTOM = COL_TOP + 8
 COL_SIZE = COL_BOTTOM + 8
 KEEP_BASE = 0
@@ -154,7 +154,7 @@
     lane = lanes(T)
     wet[...] = sea[...].astype(f32)
     pair = jnp.where(lane < 2, pltpu.roll(coef[...], 1, 1), pltpu.roll(wet[...], 3, 1))
-    cols[COL_COEF : COL_COEF + T, :] = pair * column_keep(T)
+    cols[COL_COEF : COL_COEF + 8, :] = jnp.transpose(pair * column_keep(T))[0:8, :]
 
 
 def outer_columns(state, vert, mask):
@@ -181,15 +181,11 @@
 
 
 def corner_kernel(cols, top, bottom, out):
-    out[0:COL_COEF, :] = cols[0:COL_COEF, :]
+    out[0:COL_TOP, :] = cols[...]
     lane, sub = lanes(PLANES), subl(PLANES)
     keep = column_keep(PLANES)
     for k, rows in enumerate((top, bottom)):
         line = rows[0:PLANES, :]
-        at = COL_COEF + k * PLANES
-        out[at : at + PLANES, :] = jnp.where(
-            (lane == 4) | (lane == 5), pltpu.roll(line, 5, 1) * keep, cols[at : at + PLANES, :]
-        )
         first = jnp.broadcast_to(line[:, 0:1], (PLANES, T))
         last = jnp.broadcast_to(line[:, T - 1 : T], (PLANES, T))
         spread = jnp.where(lane == 2 * sub, last, jnp.where(lane == 2 * sub + 1, first, 0.0))
@@ -365,7 +361,7 @@
     return diffuse(u[l, lo : lo + HALF, :], up, down, spin, rate)
 
 
-def halo_columns(rate, left, right, own):
+def halo_columns(rate, left, right, sides, own):
     lane, sub = lanes(T), subl(T)
     here = merged(left[0:T, :], right[0:T, :])
     outer = merged(pltpu.roll(left[COL_NEXT : COL_NEXT + T, :], 1, 1), right[COL_NEXT : COL_NEXT + T, :], 3)
@@ -380,8 +376,8 @@
     h = here + number * ((north + south) + (outer + inner) - 4.0 * here)
     coef = jnp.where(
         (lane & 1) == 0,
-        jnp.broadcast_to(left[COL_COEF : COL_COEF + T, 0:1], (T, T)),
-        jnp.broadcast_to(right[COL_COEF : COL_COEF + T, 1:2], (T, T)),
+        jnp.broadcast_to(sides[0][:, 0:1], (T, T)),
+        jnp.broadcast_to(sides[1][:, 1:2], (T, T)),
     )
     level = plane % LEV
     above = jnp.where(level < LEV - 1, pltpu.roll(h, T - 2, 1) - h, 0.0)
@@ -393,15 +389,14 @@
     at = v * LEV
     lane, level = lanes(LEV), subl(LEV)
     here = rows[at : at + LEV, :]
-    corner = COL_COEF + k * PLANES + at
-    west = jnp.where(
-        lane == 0, pltpu.roll(left[corner : corner + LEV, :], T - 4, 1), pltpu.roll(here, 1, 1)
-    )
-    east = jnp.where(
-        lane == T - 1,
-        pltpu.roll(right[corner : corner + LEV, :], T - 6, 1),
-        pltpu.roll(here, T - 1, 1),
-    )
+    edge = COL_TOP + 8 * k
+
+    def corner(message, later):
+        line = jnp.broadcast_to(message[edge : edge + 1, :], (LEV, T))
+        return jnp.sum(jnp.where(lane == 2 * (at + level) + later, line, 0.0), axis=1, keepdims=True)
+
+    west = jnp.where(lane == 0, corner(left, 0), pltpu.roll(here, 1, 1))
+    east = jnp.where(lane == T - 1, corner(right, 1), pltpu.roll(here, T - 1, 1))
     outer = rows[PLANES + at : PLANES + at + LEV, :]
     inner = own[at : at + LEV, :]
     h = here + rate[0, v] * ((outer + inner) + (west + east) - 4.0 * here)
@@ -422,7 +417,15 @@
     for load in loads:
         load.start()
     up, down, _, _ = inside()
-    side1[...], side2[...] = halo_columns(rate, near, far, own)
+    rest = jnp.zeros((T - 8, T), f32)
+    sides = [
+        jnp.transpose(jnp.concatenate([x[COL_COEF : COL_COEF + 8, :], rest], axis=0))
+        for x in (near, far)
+    ]
+    side1[...], side2[...] = halo_columns(rate, near, far, sides, own)
+    keep[KEEP_SEA_SIDE : KEEP_SEA_SIDE + T, :] = jnp.where(
+        lanes(T) == 0, pltpu.roll(sides[0], T - 2, 1), pltpu.roll(sides[1], T - 4, 1)
+    )
     for v in range(NV):
         loads[v].wait()
         at = v * LEV
@@ -484,10 +487,6 @@
     keep[KEEP_VERT : KEEP_VERT + T, :] = coef[...]
     keep[KEEP_SEA : KEEP_SEA + T, :] = sea[...]
     keep[KEEP_SIDE : KEEP_SIDE + T, :] = side2[...]
-    coefs = pl.ds(COL_COEF, T)
-    keep[KEEP_SEA_SIDE : KEEP_SEA_SIDE + T, :] = jnp.where(
-        lanes(T) == 0, pltpu.roll(near[coefs, :], T - 2, 1), pltpu.roll(far[coefs, :], T - 4, 1)
-    )
     for k, (rows, line) in enumerate(((top2, top), (bottom2, bottom))):
         for v in range(NV):
             keep[KEEP_ENDS + 8 * k + v : KEEP_ENDS + 8 * k + v + 1, :] = rows[v, 0:1, :]

time: 60.1 us -> 60.1 us (level)
  transfers between devices with their start and end apart: 8 -> 8, of which waited for: 3 -> 3; matrix products, arithmetic and copies ran while one was open for 0% -> 0% of each run, Pallas kernels for 33% -> 34%
where the time goes in v11:
time: 60.1 us; the launch traced here: 59.9 us
  Pallas kernels  24.7 us (41%)
  starting transfers between devices  19.7 us (33%)
  waiting for transfers between devices  13.1 us (22%)
  local copies, waits for them, and re-layouts  2.21 us (4%)
    pallas_call x1, Pallas kernels, two_steps(): pl.pallas_call(step_kernel, in_specs=[SMEM, HBM] + [VMEM] * 7, out_specs=...  9.71 us
    all_to_all x1, starting transfers between devices, local(): lax.all_to_all(packed, ('gx', 'gy'), split_axis=0, concat_axis=0, tiled=T...  8.83 us
    pallas_call x1, Pallas kernels, remap(): pl.pallas_call(remap_kernel, in_specs=[HBM, HBM, VMEM, HBM, HBM], out_spe...  7.88 us
    ppermute x4, starting transfers between devices, shifted(): lax.ppermute(block, axis, [(i, (i + by) % count) for i in range(count)])  6.78 us
    all_to_all x1, waiting for transfers between devices, local(): lax.all_to_all(packed, ('gx', 'gy'), split_axis=0, concat_axis=0, tiled=T...  6.36 us
    ppermute x3, waiting for transfers between devices, crossed(): return lax.ppermute(block, ('comp', 'gx', 'gy'), route)  5.62 us
    ppermute x3, starting transfers between devices, crossed(): return lax.ppermute(block, ('comp', 'gx', 'gy'), route)  4.1 us
    pallas_call x1, Pallas kernels, outer_columns(): pl.pallas_call(column_kernel, in_specs=[HBM, HBM, HBM], out_specs=[VMEM]...  2.82 us
  transfers between devices with their start and end apart: 8, of which 3 were waited for; matrix products, arithmetic and copies ran while one was open for 0% of the time, Pallas kernels for 34%

profile of v11, /device:TPU:1, one launch (start us, length us, event | category | flops | bytes accessed | tf_op | source)
XLA Modules:
  0.0 59.9 jit_solution(2365271383526592798)
XLA Ops:
  0.0 1.8 %outer_rows.1 = (f32[144,128]{1,0:T(8,128)}, f32[144,128]{1,0:T(8,128)}) custom-call(f32[1,4,16,128,128]{4,3,2,1,0:T(8,128)} %state.5, f32[1,128,128]{2,1,0:T(8,128)} %vert.3, s32[1,128,128]{2,1,0:T(8,128)} %mask.3), custom_call_target="tpu_custom_call" | custom-call | flops 65536 | bytes 524288 | tf_op jit(solution)/shard_map/outer_rows/pallas_call | solution.py:109
  1.9 3.0 %collective-permute-start = (f32[144,128]{1,0:T(8,128)}, f32[144,128]{1,0:T(8,128)S(1)}, u32[]{:S(2)}, u32[]{:S(2)}) collective-permute-start(f32[144,128]{1,0:T(8,128)} %get-tuple-element.19), channel_id=1, source_target_pairs={{0,8},{8,16},{16,24},{24,32},{32,40},{40,48},{48,56},{56,0},{1,9},... | collective-permute-start | bytes 221192 | tf_op jit(solution)/shard_map/ppermute | solution.py:648
  4.9 0.0 collective-permute-start.1
  4.9 2.8 %outer_columns.1 = (f32[264,128]{1,0:T(8,128)S(1)}, f32[512,128]{1,0:T(8,128)S(1)}, f32[128,128]{1,0:T(8,128)S(1)}, f32[128,128]{1,0:T(8,128)S(1)}) custom-call(f32[1,4,16,128,128]{4,3,2,1,0:T(8,128)} %state.5, f32[1,128,128]{2,1,0:T(8,128)S(1)} %copy-done.1, s32[1,128,128]{2,1,0:T(8,128)S(1)} %copy-done.2), custom_call_target="tpu_custom_call" | custom-call | flops 6291456 | bytes 9437184 | tf_op jit(solution)/shard_map/outer_columns/pallas_call | solution.py:162
  7.7 0.0 collective-permute-done.top
  7.7 1.1 %collective-permute-done.1.bottom = f32[144,128]{1,0:T(8,128)S(1)} collective-permute-done((f32[144,128]{1,0:T(8,128)}, f32[144,128]{1,0:T(8,128)S(1)}, u32[]{:S(2)}, u32[]{:S(2)}) %collective-permute-start.1) | collective-permute-done | bytes 73760 | tf_op jit(solution)/shard_map/ppermute | solution.py:648
  8.9 0.1 with_corners.1.own.after
  9.0 3.7 %collective-permute-start.3 = (f32[280,128]{1,0:T(8,128)S(1)}, f32[280,128]{1,0:T(8,128)S(1)}, u32[]{:S(2)}, u32[]{:S(2)}) collective-permute-start(f32[280,128]{1,0:T(8,128)S(1)} %with_corners.1.own.after), channel_id=1, source_target_pairs={{0,7},{1,0},{2,1},{3,2},{4,3},{5,4},{6,5},{7,6},{8,15},{9,8},{10,9... | collective-permute-start | bytes 430088 | tf_op jit(solution)/shard_map/ppermute | solution.py:648
  12.7 0.0 collective-permute-start.2
  12.7 7.9 %remap.1.refs_0_ = f32[2112,128]{1,0:T(8,128)} custom-call(s32[4,128]{1,0:T(4,128)S(1)} %bitcast.7, s32[1,128]{1,0:T(1,128)S(1)} %bitcast.8, f32[512,128]{1,0:T(8,128)S(1)} %get-tuple-element.23.surf, bf16[1,128,1,4,128,128]{5,4,3,2,1,0:T(8,128)(2,1)} %weight.1, f32[280,128]{1,0:T(8,128)S(1)} %with_corners.1.own.after), custom_call_target="tpu_custom_call" | custom-call | flops 70254592 | bytes 20971520 | tf_op jit(solution)/shard_map/remap/pallas_call | solution.py:305
  20.6 0.0 copy-start.4
  20.6 0.0 collective-permute-done.3.far.refs_2_
  20.7 0.0 copy-start.6
  20.7 8.8 %all-to-all-start = ((f32[64,33,1,128]{3,2,1,0:T(1,128)}), f32[64,33,1,128]{3,2,1,0:T(1,128)S(1)}, u32[]{:S(2)}, u32[]{:S(2)}) async-start(f32[64,33,1,128]{3,2,1,0:T(1,128)} %bitcast.3), calls=%async_computation | async-start | bytes 2162688 | tf_op jit(solution)/shard_map/all_to_all | solution.py:673
  29.5 0.0 copy-start
  29.5 2.2 %copy-done = f32[1,4,16,128,128]{4,3,2,1,0:T(8,128)S(1)} copy-done((f32[1,4,16,128,128]{4,3,2,1,0:T(8,128)S(1)}, f32[1,4,16,128,128]{4,3,2,1,0:T(8,128)}, u32[]{:S(2)}) %copy-start) | copy-done | bytes 4194328
  31.7 9.7 %two_steps.1 = (f32[1,4,16,128,128]{4,3,2,1,0:T(8,128)}, f32[2064,128]{1,0:T(8,128)S(1)}) custom-call(f32[1,4]{1,0:T(1,128)S(1)} %copy-done.4, f32[1,4,16,128,128]{4,3,2,1,0:T(8,128)S(1)} %copy-done, f32[128,128]{1,0:T(8,128)S(1)} %get-tuple-element.16.coef, f32[128,128]{1,0:T(8,128)S(1)} %get-tuple-element.17.sea, f32[280,128]{1,0:T(8,128)S(1)} %with_corners.1.own.after, ...), custom_call_target="tpu_custom_call" | custom-call | flops 50331648 | bytes 10485760 | tf_op jit(solution)/shard_map/two_steps/pallas_call | solution.py:501
  41.4 6.4 %all-to-all-done = f32[64,33,1,128]{3,2,1,0:T(1,128)S(1)} async-done(((f32[64,33,1,128]{3,2,1,0:T(1,128)}), f32[64,33,1,128]{3,2,1,0:T(1,128)S(1)}, u32[]{:S(2)}, u32[]{:S(2)}) %all-to-all-start) | async-done | bytes 1081376 | tf_op jit(solution)/shard_map/all_to_all | solution.py:673
  47.8 0.7 %unpack.1 = (f32[520,128]{1,0:T(8,128)S(1)}, f32[8,128]{1,0:T(8,128)S(1)}, f32[8,128]{1,0:T(8,128)S(1)}) custom-call(f32[2112,128]{1,0:T(8,128)S(1)} %bitcast.6, f32[2064,128]{1,0:T(8,128)S(1)} %get-tuple-element.22.after.near), custom_call_target="tpu_custom_call" | custom-call | flops 209715200 | bytes 2097152 | tf_op jit(solution)/shard_map/unpack/pallas_call | solution.py:573
  48.5 1.1 %collective-permute-start.4 = (f32[520,128]{1,0:T(8,128)S(1)}, f32[520,128]{1,0:T(8,128)S(1)}, u32[]{:S(2)}, u32[]{:S(2)}) collective-permute-start(f32[520,128]{1,0:T(8,128)S(1)} %get-tuple-element.24), channel_id=1, source_target_pairs={{0,68},{1,69},{2,70},{3,71},{4,64},{5,65},{6,66},{7,67},{8,76},{9,... | collective-permute-start | bytes 798728 | tf_op jit(solution)/shard_map/ppermute | solution.py:659
  49.6 1.8 %collective-permute-start.5 = (f32[8,128]{1,0:T(8,128)S(1)}, f32[8,128]{1,0:T(8,128)S(1)}, u32[]{:S(2)}, u32[]{:S(2)}) collective-permute-start(f32[8,128]{1,0:T(8,128)S(1)} %get-tuple-element.25), channel_id=1, source_target_pairs={{0,76},{1,77},{2,78},{3,79},{4,72},{5,73},{6,74},{7,75},{8,84},{9,... | collective-permute-start | bytes 12296 | tf_op jit(solution)/shard_map/ppermute | solution.py:659
  51.4 1.2 %collective-permute-start.6 = (f32[8,128]{1,0:T(8,128)S(1)}, f32[8,128]{1,0:T(8,128)S(1)}, u32[]{:S(2)}, u32[]{:S(2)}) collective-permute-start(f32[8,128]{1,0:T(8,128)S(1)} %get-tuple-element.26), channel_id=1, source_target_pairs={{0,124},{1,125},{2,126},{3,127},{4,120},{5,121},{6,122},{7,123},{8... | collective-permute-start | bytes 12296 | tf_op jit(solution)/shard_map/ppermute | solution.py:659
  52.6 5.6 %collective-permute-done.5.imp_top = f32[8,128]{1,0:T(8,128)S(1)} collective-permute-done((f32[8,128]{1,0:T(8,128)S(1)}, f32[8,128]{1,0:T(8,128)S(1)}, u32[]{:S(2)}, u32[]{:S(2)}) %collective-permute-start.5) | collective-permute-done | bytes 4128 | tf_op jit(solution)/shard_map/ppermute | solution.py:659
  58.2 1.7 %final.1 = f32[1,4,16,128,128]{4,3,2,1,0:T(8,128)} custom-call(f32[1,4]{1,0:T(1,128)S(1)} %copy-done.4, f32[1,4]{1,0:T(1,128)S(1)} %copy-done.6, f32[1,4,16,128,128]{4,3,2,1,0:T(8,128)} %get-tuple-element.21.mid, f32[2064,128]{1,0:T(8,128)S(1)} %get-tuple-element.22.after.near, ...), custom_call_target="tpu_custom_call", output_to_operand_aliasing={{}: (2, {})} | custom-call | flops 2097152 | bytes 3145728 | tf_op jit(solution)/shard_map/final/pallas_call | solution.py:630
  (14 shorter events, 0.0 us)
Async XLA Ops:
  0.0 4.9 %copy-start.2 = (s32[1,128,128]{2,1,0:T(8,128)S(1)}, s32[1,128,128]{2,1,0:T(8,128)}, u32[]{:S(2)}) copy-start(s32[1,128,128]{2,1,0:T(8,128)} %mask.3) | copy-start | bytes 196612
  0.0 4.9 %copy-start.1 = (f32[1,128,128]{2,1,0:T(8,128)S(1)}, f32[1,128,128]{2,1,0:T(8,128)}, u32[]{:S(2)}) copy-start(f32[1,128,128]{2,1,0:T(8,128)} %vert.3) | copy-start | bytes 196612
  0.0 12.7 %copy-start.5 = (s32[1,128,1]{1,2,0:T(1,128)S(1)}, s32[1,128,1]{1,2,0:T(1,128)}, u32[]{:S(2)}) copy-start(s32[1,128,1]{1,2,0:T(1,128)} %param.14) | copy-start | bytes 1540
  0.0 12.7 %copy-start.3 = (s32[1,128,1,4]{1,3,2,0:T(4,128)S(1)}, s32[1,128,1,4]{1,3,2,0:T(4,128)}, u32[]{:S(2)}) copy-start(s32[1,128,1,4]{1,3,2,0:T(4,128)} %param.13) | copy-start | bytes 6148
  1.9 5.9 %collective-permute-start = (f32[144,128]{1,0:T(8,128)}, f32[144,128]{1,0:T(8,128)S(1)}, u32[]{:S(2)}, u32[]{:S(2)}) collective-permute-start(f32[144,128]{1,0:T(8,128)} %get-tuple-element.19), channel_id=1, source_target_pairs={{0,8},{8,16},{16,24},{24,32},{32,40},{40,48},{48,56},{56,0},{1,9},... | collective-permute-start | bytes 221192 | tf_op jit(solution)/shard_map/ppermute | solution.py:648
  4.9 4.0 %collective-permute-start.1 = (f32[144,128]{1,0:T(8,128)}, f32[144,128]{1,0:T(8,128)S(1)}, u32[]{:S(2)}, u32[]{:S(2)}) collective-permute-start(f32[144,128]{1,0:T(8,128)} %get-tuple-element.20), channel_id=1, source_target_pairs={{0,56},{8,0},{16,8},{24,16},{32,24},{40,32},{48,40},{56,48},{1,57}... | collective-permute-start | bytes 221192 | tf_op jit(solution)/shard_map/ppermute | solution.py:648
  9.0 11.6 %collective-permute-start.3 = (f32[280,128]{1,0:T(8,128)S(1)}, f32[280,128]{1,0:T(8,128)S(1)}, u32[]{:S(2)}, u32[]{:S(2)}) collective-permute-start(f32[280,128]{1,0:T(8,128)S(1)} %with_corners.1.own.after), channel_id=1, source_target_pairs={{0,7},{1,0},{2,1},{3,2},{4,3},{5,4},{6,5},{7,6},{8,15},{9,8},{10,9... | collective-permute-start | bytes 430088 | tf_op jit(solution)/shard_map/ppermute | solution.py:648
  12.7 7.9 %collective-permute-start.2 = (f32[280,128]{1,0:T(8,128)S(1)}, f32[280,128]{1,0:T(8,128)S(1)}, u32[]{:S(2)}, u32[]{:S(2)}) collective-permute-start(f32[280,128]{1,0:T(8,128)S(1)} %with_corners.1.own.after), channel_id=1, source_target_pairs={{0,1},{1,2},{2,3},{3,4},{4,5},{5,6},{6,7},{7,0},{8,9},{9,10},{10,1... | collective-permute-start | bytes 430088 | tf_op jit(solution)/shard_map/ppermute | solution.py:648
  20.6 8.9 %copy-start.4 = (f32[1,4]{1,0:T(1,128)S(1)}, f32[1,4]{1,0:T(1,128)}, u32[]{:S(2)}) copy-start(f32[1,4]{1,0:T(1,128)} %horiz.1) | copy-start | bytes 52
  20.7 37.5 %copy-start.6 = (f32[1,4]{1,0:T(1,128)S(1)}, f32[1,4]{1,0:T(1,128)}, u32[]{:S(2)}) copy-start(f32[1,4]{1,0:T(1,128)} %relax.1) | copy-start | bytes 52
  20.7 27.1 %all-to-all-start = ((f32[64,33,1,128]{3,2,1,0:T(1,128)}), f32[64,33,1,128]{3,2,1,0:T(1,128)S(1)}, u32[]{:S(2)}, u32[]{:S(2)}) async-start(f32[64,33,1,128]{3,2,1,0:T(1,128)} %bitcast.3), calls=%async_computation | async-start | bytes 2162688 | tf_op jit(solution)/shard_map/all_to_all | solution.py:673
  29.5 2.2 %copy-start = (f32[1,4,16,128,128]{4,3,2,1,0:T(8,128)S(1)}, f32[1,4,16,128,128]{4,3,2,1,0:T(8,128)}, u32[]{:S(2)}) copy-start(f32[1,4,16,128,128]{4,3,2,1,0:T(8,128)} %state.5) | copy-start | bytes 12582916
  48.5 9.7 %collective-permute-start.4 = (f32[520,128]{1,0:T(8,128)S(1)}, f32[520,128]{1,0:T(8,128)S(1)}, u32[]{:S(2)}, u32[]{:S(2)}) collective-permute-start(f32[520,128]{1,0:T(8,128)S(1)} %get-tuple-element.24), channel_id=1, source_target_pairs={{0,68},{1,69},{2,70},{3,71},{4,64},{5,65},{6,66},{7,67},{8,76},{9,... | collective-permute-start | bytes 798728 | tf_op jit(solution)/shard_map/ppermute | solution.py:659
  49.6 8.6 %collective-permute-start.5 = (f32[8,128]{1,0:T(8,128)S(1)}, f32[8,128]{1,0:T(8,128)S(1)}, u32[]{:S(2)}, u32[]{:S(2)}) collective-permute-start(f32[8,128]{1,0:T(8,128)S(1)} %get-tuple-element.25), channel_id=1, source_target_pairs={{0,76},{1,77},{2,78},{3,79},{4,72},{5,73},{6,74},{7,75},{8,84},{9,... | collective-permute-start | bytes 12296 | tf_op jit(solution)/shard_map/ppermute | solution.py:659
  51.4 6.8 %collective-permute-start.6 = (f32[8,128]{1,0:T(8,128)S(1)}, f32[8,128]{1,0:T(8,128)S(1)}, u32[]{:S(2)}, u32[]{:S(2)}) collective-permute-start(f32[8,128]{1,0:T(8,128)S(1)} %get-tuple-element.26), channel_id=1, source_target_pairs={{0,124},{1,125},{2,126},{3,127},{4,120},{5,121},{6,122},{7,123},{8... | collective-permute-start | bytes 12296 | tf_op jit(solution)/shard_map/ppermute | solution.py:659

commit v12 on v9

--- a/solution.py
+++ b/solution.py
@@ -236,9 +236,10 @@
     buffer[...] = jnp.zeros_like(buffer)
 
     def clear(i, _):
-        used[i] = 0
+        row = (i ^ MIRROR) * SIZE
+        used[i] = row
         for k in range(CAP):
-            label[i * CAP + k] = 0
+            label[row + k * NV] = 0
         return 0
 
     lax.fori_loop(0, PEERS, clear, 0)
@@ -248,12 +249,13 @@
 
     def place_of(row, f):
         target = dest[f, row]
-        peer = (lax.shift_right_logical(target, 7) & (PEERS - 1)) ^ MIRROR
+        device = lax.shift_right_logical(target, 7) & (PEERS - 1)
         live = f < count[0, row]
-        at = used[peer]
-        used[peer] = at + jnp.where(live, 1, 0)
-        label[jnp.where(live, peer * CAP + at, PEERS * CAP)] = (target & (T - 1)) + 1
-        return jnp.where(live, peer * SIZE + at * NV, PEERS * SIZE)
+        at = used[device]
+        used[device] = jnp.where(live, at + NV, at)
+        place = jnp.where(live, at, PEERS * SIZE)
+        label[place] = (target & (T - 1)) + 1
+        return place
 
     def chunk(c, given, skipped):
         for r in range(0, rows, 2):
@@ -293,7 +295,7 @@
     def name(i, _):
         line = jnp.zeros((1, T), i32)
         for k in range(CAP):
-            line = jnp.where(lane == k, label[i * CAP + k], line)
+            line = jnp.where(lane == k, label[i * SIZE + k * NV], line)
         names[pl.ds(i, 1), :] = line.astype(f32)
         return 0
 
@@ -329,7 +331,7 @@
             pltpu.SMEM((FAN, T), i32),
             pltpu.SMEM((1, T), i32),
             pltpu.SMEM((PEERS,), i32),
-            pltpu.SMEM((PEERS * CAP + 8,), i32),
+            pltpu.SMEM((PEERS * SIZE + 8,), i32),
             pltpu.SemaphoreType.DMA((CHUNKS + 2,)),
         ],
         compiler_params=params(44 * MIB),

time: 61.4 us -> 59.8 us (0.974)
  Pallas kernels: 25.7 us -> 24 us
    pallas_call x1, Pallas kernels: 8.43 us -> 6.78 us  [remap(): pl.pallas_call(remap_kernel, in_specs=[HBM, HBM, VMEM, HBM, VMEM, HBM], o...]
  transfers between devices with their start and end apart: 8 -> 8, of which waited for: 3 -> 3; matrix products, arithmetic and copies ran while one was open for 0% -> 0% of each run, Pallas kernels for 35% -> 33%
where the time goes in v12:
time: 59.8 us; the launch traced here: 59.5 us
  Pallas kernels  24 us (40%)
  starting transfers between devices  20.4 us (34%)
  waiting for transfers between devices  12.7 us (21%)
  local copies, waits for them, and re-layouts  2.21 us (4%)
    all_to_all x1, starting transfers between devices, local(): lax.all_to_all(packed, ('gx', 'gy'), split_axis=0, concat_axis=0, tiled=T...  9.57 us
    pallas_call x1, Pallas kernels, two_steps(): pl.pallas_call(step_kernel, in_specs=[SMEM, HBM] + [VMEM] * 7, out_specs=...  9.38 us
    pallas_call x1, Pallas kernels, remap(): pl.pallas_call(remap_kernel, in_specs=[HBM, HBM, VMEM, HBM, VMEM, HBM], o...  6.78 us
    ppermute x4, starting transfers between devices, shifted(): lax.ppermute(block, axis, [(i, (i + by) % count) for i in range(count)])  6.78 us
    all_to_all x1, waiting for transfers between devices, local(): lax.all_to_all(packed, ('gx', 'gy'), split_axis=0, concat_axis=0, tiled=T...  6.69 us
    ppermute x3, waiting for transfers between devices, crossed(): return lax.ppermute(block, ('comp', 'gx', 'gy'), route)  5.62 us
    ppermute x3, starting transfers between devices, crossed(): return lax.ppermute(block, ('comp', 'gx', 'gy'), route)  4.1 us
    pallas_call x1, Pallas kernels, outer_columns(): pl.pallas_call(column_kernel, in_specs=[HBM] * 4, out_specs=[VMEM] * 5, o...  3.58 us
  transfers between devices with their start and end apart: 8, of which 3 were waited for; matrix products, arithmetic and copies ran while one was open for 0% of the time, Pallas kernels for 33%

profile of v12, /device:TPU:1, one launch (start us, length us, event | category | flops | bytes accessed | tf_op | source)
XLA Modules:
  0.0 59.5 jit_solution(17982371970650796269)
XLA Ops:
  0.0 1.8 %outer_rows.1 = (f32[144,128]{1,0:T(8,128)}, f32[144,128]{1,0:T(8,128)}) custom-call(f32[1,4,16,128,128]{4,3,2,1,0:T(8,128)} %state.5, f32[1,128,128]{2,1,0:T(8,128)} %vert.3, s32[1,128,128]{2,1,0:T(8,128)} %mask.3), custom_call_target="tpu_custom_call" | custom-call | flops 65536 | bytes 524288 | tf_op jit(solution)/shard_map/outer_rows/pallas_call | solution.py:110
  1.8 3.0 %collective-permute-start = (f32[144,128]{1,0:T(8,128)}, f32[144,128]{1,0:T(8,128)S(1)}, u32[]{:S(2)}, u32[]{:S(2)}) collective-permute-start(f32[144,128]{1,0:T(8,128)} %get-tuple-element.20), channel_id=1, source_target_pairs={{0,8},{8,16},{16,24},{24,32},{32,40},{40,48},{48,56},{56,0},{1,9},... | collective-permute-start | bytes 221192 | tf_op jit(solution)/shard_map/ppermute | solution.py:662
  4.9 0.0 collective-permute-start.1
  4.9 3.6 %outer_columns.1 = (f32[384,128]{1,0:T(8,128)S(1)}, f32[512,128]{1,0:T(8,128)S(1)}, f32[128,128]{1,0:T(8,128)S(1)}, f32[128,128]{1,0:T(8,128)S(1)}, bf16[32,4,128,128]{3,2,1,0:T(8,128)(2,1)S(1)}) custom-call(f32[1,4,16,128,128]{4,3,2,1,0:T(8,128)} %state.5, f32[1,128,128]{2,1,0:T(8,128)S(1)} %copy-done.1, s32[1,128,128]{2,1,0:T(8,128)S(1)} %copy-done.2, ...), custom_call_target="tpu_custom_call" | custom-call | flops 6291456 | bytes 9437184 | tf_op jit(solution)/shard_map/outer_columns/pallas_call | solution.py:165
  8.5 0.0 collective-permute-done.top
  8.5 0.4 collective-permute-done.1.bottom
  8.9 0.1 with_corners.1.own.after
  9.0 3.7 %collective-permute-start.3 = (f32[400,128]{1,0:T(8,128)S(1)}, f32[400,128]{1,0:T(8,128)S(1)}, u32[]{:S(2)}, u32[]{:S(2)}) collective-permute-start(f32[400,128]{1,0:T(8,128)S(1)} %with_corners.1.own.after), channel_id=1, source_target_pairs={{0,7},{1,0},{2,1},{3,2},{4,3},{5,4},{6,5},{7,6},{8,15},{9,8},{10,9... | collective-permute-start | bytes 614408 | tf_op jit(solution)/shard_map/ppermute | solution.py:662
  12.7 0.0 collective-permute-start.2
  12.7 6.8 %remap.1.refs_0_ = f32[2112,128]{1,0:T(8,128)} custom-call(s32[4,128]{1,0:T(4,128)S(1)} %bitcast.7, s32[1,128]{1,0:T(1,128)S(1)} %bitcast.8, f32[512,128]{1,0:T(8,128)S(1)} %get-tuple-element.24.surf, bf16[1,128,1,4,128,128]{5,4,3,2,1,0:T(8,128)(2,1)} %weight.3, bf16[32,4,128,128]{3,2,1,0:T(8,128)(2,1)S(1)} %get-tuple-element.25.early, ...), custom_call_target="tpu_custom_call" | custom-call | flops 70254592 | bytes 20971520 | tf_op jit(solution)/shard_map/remap/pallas_call | solution.py:322
  19.5 0.0 copy-start.4
  19.5 0.0 collective-permute-done.3.far.refs_2_
  19.6 0.0 copy-start.6
  19.6 9.6 %all-to-all-start = ((f32[64,33,1,128]{3,2,1,0:T(1,128)}), f32[64,33,1,128]{3,2,1,0:T(1,128)S(1)}, u32[]{:S(2)}, u32[]{:S(2)}) async-start(f32[64,33,1,128]{3,2,1,0:T(1,128)} %bitcast.3), calls=%async_computation | async-start | bytes 2162688 | tf_op jit(solution)/shard_map/all_to_all | solution.py:687
  29.2 0.0 copy-start
  29.2 2.2 %copy-done = f32[1,4,16,128,128]{4,3,2,1,0:T(8,128)S(1)} copy-done((f32[1,4,16,128,128]{4,3,2,1,0:T(8,128)S(1)}, f32[1,4,16,128,128]{4,3,2,1,0:T(8,128)}, u32[]{:S(2)}) %copy-start) | copy-done | bytes 4194328
  31.4 9.4 %two_steps.1 = (f32[1,4,16,128,128]{4,3,2,1,0:T(8,128)}, f32[2064,128]{1,0:T(8,128)S(1)}) custom-call(f32[1,4]{1,0:T(1,128)S(1)} %copy-done.4, f32[1,4,16,128,128]{4,3,2,1,0:T(8,128)S(1)} %copy-done, f32[128,128]{1,0:T(8,128)S(1)} %get-tuple-element.17.coef, f32[128,128]{1,0:T(8,128)S(1)} %get-tuple-element.18.sea, f32[400,128]{1,0:T(8,128)S(1)} %with_corners.1.own.after, ...), custom_call_target="tpu_custom_call" | custom-call | flops 50331648 | bytes 10485760 | tf_op jit(solution)/shard_map/two_steps/pallas_call | solution.py:515
  40.8 6.7 %all-to-all-done = f32[64,33,1,128]{3,2,1,0:T(1,128)S(1)} async-done(((f32[64,33,1,128]{3,2,1,0:T(1,128)}), f32[64,33,1,128]{3,2,1,0:T(1,128)S(1)}, u32[]{:S(2)}, u32[]{:S(2)}) %all-to-all-start) | async-done | bytes 1081376 | tf_op jit(solution)/shard_map/all_to_all | solution.py:687
  47.4 0.7 %unpack.1 = (f32[520,128]{1,0:T(8,128)S(1)}, f32[8,128]{1,0:T(8,128)S(1)}, f32[8,128]{1,0:T(8,128)S(1)}) custom-call(f32[2112,128]{1,0:T(8,128)S(1)} %bitcast.6, f32[2064,128]{1,0:T(8,128)S(1)} %get-tuple-element.23.after.near), custom_call_target="tpu_custom_call" | custom-call | flops 209715200 | bytes 2097152 | tf_op jit(solution)/shard_map/unpack/pallas_call | solution.py:587
  48.1 1.1 %collective-permute-start.4 = (f32[520,128]{1,0:T(8,128)S(1)}, f32[520,128]{1,0:T(8,128)S(1)}, u32[]{:S(2)}, u32[]{:S(2)}) collective-permute-start(f32[520,128]{1,0:T(8,128)S(1)} %get-tuple-element.26), channel_id=1, source_target_pairs={{0,68},{1,69},{2,70},{3,71},{4,64},{5,65},{6,66},{7,67},{8,76},{9,... | collective-permute-start | bytes 798728 | tf_op jit(solution)/shard_map/ppermute | solution.py:673
  49.3 1.8 %collective-permute-start.5 = (f32[8,128]{1,0:T(8,128)S(1)}, f32[8,128]{1,0:T(8,128)S(1)}, u32[]{:S(2)}, u32[]{:S(2)}) collective-permute-start(f32[8,128]{1,0:T(8,128)S(1)} %get-tuple-element.27), channel_id=1, source_target_pairs={{0,76},{1,77},{2,78},{3,79},{4,72},{5,73},{6,74},{7,75},{8,84},{9,... | collective-permute-start | bytes 12296 | tf_op jit(solution)/shard_map/ppermute | solution.py:673
  51.0 1.2 %collective-permute-start.6 = (f32[8,128]{1,0:T(8,128)S(1)}, f32[8,128]{1,0:T(8,128)S(1)}, u32[]{:S(2)}, u32[]{:S(2)}) collective-permute-start(f32[8,128]{1,0:T(8,128)S(1)} %get-tuple-element.28), channel_id=1, source_target_pairs={{0,124},{1,125},{2,126},{3,127},{4,120},{5,121},{6,122},{7,123},{8... | collective-permute-start | bytes 12296 | tf_op jit(solution)/shard_map/ppermute | solution.py:673
  52.2 5.6 %collective-permute-done.5.imp_top = f32[8,128]{1,0:T(8,128)S(1)} collective-permute-done((f32[8,128]{1,0:T(8,128)S(1)}, f32[8,128]{1,0:T(8,128)S(1)}, u32[]{:S(2)}, u32[]{:S(2)}) %collective-permute-start.5) | collective-permute-done | bytes 4128 | tf_op jit(solution)/shard_map/ppermute | solution.py:673
  57.8 1.7 %final.1 = f32[1,4,16,128,128]{4,3,2,1,0:T(8,128)} custom-call(f32[1,4]{1,0:T(1,128)S(1)} %copy-done.4, f32[1,4]{1,0:T(1,128)S(1)} %copy-done.6, f32[1,4,16,128,128]{4,3,2,1,0:T(8,128)} %get-tuple-element.22.mid, f32[2064,128]{1,0:T(8,128)S(1)} %get-tuple-element.23.after.near, ...), custom_call_target="tpu_custom_call", output_to_operand_aliasing={{}: (2, {})} | custom-call | flops 2097152 | bytes 3145728 | tf_op jit(solution)/shard_map/final/pallas_call | solution.py:644
  (14 shorter events, 0.0 us)
Async XLA Ops:
  0.0 4.9 %copy-start.2 = (s32[1,128,128]{2,1,0:T(8,128)S(1)}, s32[1,128,128]{2,1,0:T(8,128)}, u32[]{:S(2)}) copy-start(s32[1,128,128]{2,1,0:T(8,128)} %mask.3) | copy-start | bytes 196612
  0.0 4.9 %copy-start.1 = (f32[1,128,128]{2,1,0:T(8,128)S(1)}, f32[1,128,128]{2,1,0:T(8,128)}, u32[]{:S(2)}) copy-start(f32[1,128,128]{2,1,0:T(8,128)} %vert.3) | copy-start | bytes 196612
  1.8 6.7 %collective-permute-start = (f32[144,128]{1,0:T(8,128)}, f32[144,128]{1,0:T(8,128)S(1)}, u32[]{:S(2)}, u32[]{:S(2)}) collective-permute-start(f32[144,128]{1,0:T(8,128)} %get-tuple-element.20), channel_id=1, source_target_pairs={{0,8},{8,16},{16,24},{24,32},{32,40},{40,48},{48,56},{56,0},{1,9},... | collective-permute-start | bytes 221192 | tf_op jit(solution)/shard_map/ppermute | solution.py:662
  4.9 7.9 %copy-start.3 = (s32[1,128,1,4]{1,3,2,0:T(4,128)S(1)}, s32[1,128,1,4]{1,3,2,0:T(4,128)}, u32[]{:S(2)}) copy-start(s32[1,128,1,4]{1,3,2,0:T(4,128)} %param.13) | copy-start | bytes 6148
  4.9 7.9 %copy-start.5 = (s32[1,128,1]{1,2,0:T(1,128)S(1)}, s32[1,128,1]{1,2,0:T(1,128)}, u32[]{:S(2)}) copy-start(s32[1,128,1]{1,2,0:T(1,128)} %param.14) | copy-start | bytes 1540
  4.9 4.0 %collective-permute-start.1 = (f32[144,128]{1,0:T(8,128)}, f32[144,128]{1,0:T(8,128)S(1)}, u32[]{:S(2)}, u32[]{:S(2)}) collective-permute-start(f32[144,128]{1,0:T(8,128)} %get-tuple-element.21), channel_id=1, source_target_pairs={{0,56},{8,0},{16,8},{24,16},{32,24},{40,32},{48,40},{56,48},{1,57}... | collective-permute-start | bytes 221192 | tf_op jit(solution)/shard_map/ppermute | solution.py:662
  9.0 10.5 %collective-permute-start.3 = (f32[400,128]{1,0:T(8,128)S(1)}, f32[400,128]{1,0:T(8,128)S(1)}, u32[]{:S(2)}, u32[]{:S(2)}) collective-permute-start(f32[400,128]{1,0:T(8,128)S(1)} %with_corners.1.own.after), channel_id=1, source_target_pairs={{0,7},{1,0},{2,1},{3,2},{4,3},{5,4},{6,5},{7,6},{8,15},{9,8},{10,9... | collective-permute-start | bytes 614408 | tf_op jit(solution)/shard_map/ppermute | solution.py:662
  12.7 6.8 %collective-permute-start.2 = (f32[400,128]{1,0:T(8,128)S(1)}, f32[400,128]{1,0:T(8,128)S(1)}, u32[]{:S(2)}, u32[]{:S(2)}) collective-permute-start(f32[400,128]{1,0:T(8,128)S(1)} %with_corners.1.own.after), channel_id=1, source_target_pairs={{0,1},{1,2},{2,3},{3,4},{4,5},{5,6},{6,7},{7,0},{8,9},{9,10},{10,1... | collective-permute-start | bytes 614408 | tf_op jit(solution)/shard_map/ppermute | solution.py:662
  19.5 9.6 %copy-start.4 = (f32[1,4]{1,0:T(1,128)S(1)}, f32[1,4]{1,0:T(1,128)}, u32[]{:S(2)}) copy-start(f32[1,4]{1,0:T(1,128)} %horiz.1) | copy-start | bytes 52
  19.6 38.3 %copy-start.6 = (f32[1,4]{1,0:T(1,128)S(1)}, f32[1,4]{1,0:T(1,128)}, u32[]{:S(2)}) copy-start(f32[1,4]{1,0:T(1,128)} %relax.1) | copy-start | bytes 52
  19.6 27.8 %all-to-all-start = ((f32[64,33,1,128]{3,2,1,0:T(1,128)}), f32[64,33,1,128]{3,2,1,0:T(1,128)S(1)}, u32[]{:S(2)}, u32[]{:S(2)}) async-start(f32[64,33,1,128]{3,2,1,0:T(1,128)} %bitcast.3), calls=%async_computation | async-start | bytes 2162688 | tf_op jit(solution)/shard_map/all_to_all | solution.py:687
  29.2 2.2 %copy-start = (f32[1,4,16,128,128]{4,3,2,1,0:T(8,128)S(1)}, f32[1,4,16,128,128]{4,3,2,1,0:T(8,128)}, u32[]{:S(2)}) copy-start(f32[1,4,16,128,128]{4,3,2,1,0:T(8,128)} %state.5) | copy-start | bytes 12582916
  48.1 9.7 %collective-permute-start.4 = (f32[520,128]{1,0:T(8,128)S(1)}, f32[520,128]{1,0:T(8,128)S(1)}, u32[]{:S(2)}, u32[]{:S(2)}) collective-permute-start(f32[520,128]{1,0:T(8,128)S(1)} %get-tuple-element.26), channel_id=1, source_target_pairs={{0,68},{1,69},{2,70},{3,71},{4,64},{5,65},{6,66},{7,67},{8,76},{9,... | collective-permute-start | bytes 798728 | tf_op jit(solution)/shard_map/ppermute | solution.py:673
  49.3 8.6 %collective-permute-start.5 = (f32[8,128]{1,0:T(8,128)S(1)}, f32[8,128]{1,0:T(8,128)S(1)}, u32[]{:S(2)}, u32[]{:S(2)}) collective-permute-start(f32[8,128]{1,0:T(8,128)S(1)} %get-tuple-element.27), channel_id=1, source_target_pairs={{0,76},{1,77},{2,78},{3,79},{4,72},{5,73},{6,74},{7,75},{8,84},{9,... | collective-permute-start | bytes 12296 | tf_op jit(solution)/shard_map/ppermute | solution.py:673
  51.0 6.8 %collective-permute-start.6 = (f32[8,128]{1,0:T(8,128)S(1)}, f32[8,128]{1,0:T(8,128)S(1)}, u32[]{:S(2)}, u32[]{:S(2)}) collective-permute-start(f32[8,128]{1,0:T(8,128)S(1)} %get-tuple-element.28), channel_id=1, source_target_pairs={{0,124},{1,125},{2,126},{3,127},{4,120},{5,121},{6,122},{7,123},{8... | collective-permute-start | bytes 12296 | tf_op jit(solution)/shard_map/ppermute | solution.py:673

commit v13 on v12

--- a/solution.py
+++ b/solution.py
@@ -25,7 +25,7 @@
 ROW_SIZE = ROW_SEA + 8
 COL_NEXT = T
 COL_COEF = 2 * T
-COL_TOP = 3 * T
+COL_TOP = COL_COEF + 8
 COL_BOTTOM = COL_TOP + 8
 COL_SIZE = COL_BOTTOM + 8
 KEEP_BASE = 0
@@ -156,7 +156,7 @@
     lane = lanes(T)
     wet[...] = sea[...].astype(f32)
     pair = jnp.where(lane < 2, pltpu.roll(coef[...], 1, 1), pltpu.roll(wet[...], 3, 1))
-    cols[COL_COEF : COL_COEF + T, :] = pair * column_keep(T)
+    cols[COL_COEF : COL_COEF + 8, :] = jnp.transpose(pair * column_keep(T))[0:8, :]
     loads[NV + 2].wait()
 
 
@@ -185,15 +185,11 @@
 
 
 def corner_kernel(cols, top, bottom, out):
-    out[0:COL_COEF, :] = cols[0:COL_COEF, :]
+    out[0:COL_TOP, :] = cols[...]
     lane, sub = lanes(PLANES), subl(PLANES)
     keep = column_keep(PLANES)
     for k, rows in enumerate((top, bottom)):
         line = rows[0:PLANES, :]
-        at = COL_COEF + k * PLANES
-        out[at : at + PLANES, :] = jnp.where(
-            (lane == 4) | (lane == 5), pltpu.roll(line, 5, 1) * keep, cols[at : at + PLANES, :]
-        )
         first = jnp.broadcast_to(line[:, 0:1], (PLANES, T))
         last = jnp.broadcast_to(line[:, T - 1 : T], (PLANES, T))
         spread = jnp.where(lane == 2 * sub, last, jnp.where(lane == 2 * sub + 1, first, 0.0))
@@ -378,7 +374,7 @@
     return diffuse(u[l, lo : lo + HALF, :], up, down, spin, rate)
 
 
-def halo_columns(rate, left, right, own):
+def halo_columns(rate, left, right, sides, own):
     lane, sub = lanes(T), subl(T)
     here = merged(left[0:T, :], right[0:T, :])
     outer = merged(pltpu.roll(left[COL_NEXT : COL_NEXT + T, :], 1, 1), right[COL_NEXT : COL_NEXT + T, :], 3)
@@ -393,8 +389,8 @@
     h = here + number * ((north + south) + (outer + inner) - 4.0 * here)
     coef = jnp.where(
         (lane & 1) == 0,
-        jnp.broadcast_to(left[COL_COEF : COL_COEF + T, 0:1], (T, T)),
-        jnp.broadcast_to(right[COL_COEF : COL_COEF + T, 1:2], (T, T)),
+        jnp.broadcast_to(sides[0][:, 0:1], (T, T)),
+        jnp.broadcast_to(sides[1][:, 1:2], (T, T)),
     )
     level = plane % LEV
     above = jnp.where(level < LEV - 1, pltpu.roll(h, T - 2, 1) - h, 0.0)
@@ -406,15 +402,14 @@
     at = v * LEV
     lane, level = lanes(LEV), subl(LEV)
     here = rows[at : at + LEV, :]
-    corner = COL_COEF + k * PLANES + at
-    west = jnp.where(
-        lane == 0, pltpu.roll(left[corner : corner + LEV, :], T - 4, 1), pltpu.roll(here, 1, 1)
-    )
-    east = jnp.where(
-        lane == T - 1,
-        pltpu.roll(right[corner : corner + LEV, :], T - 6, 1),
-        pltpu.roll(here, T - 1, 1),
-    )
+    edge = COL_TOP + 8 * k
+
+    def corner(message, later):
+        line = jnp.broadcast_to(message[edge : edge + 1, :], (LEV, T))
+        return jnp.sum(jnp.where(lane == 2 * (at + level) + later, line, 0.0), axis=1, keepdims=True)
+
+    west = jnp.where(lane == 0, corner(left, 0), pltpu.roll(here, 1, 1))
+    east = jnp.where(lane == T - 1, corner(right, 1), pltpu.roll(here, T - 1, 1))
     outer = rows[PLANES + at : PLANES + at + LEV, :]
     inner = own[at : at + LEV, :]
     h = here + rate[0, v] * ((outer + inner) + (west + east) - 4.0 * here)
@@ -435,7 +430,15 @@
     for load in loads:
         load.start()
     up, down, _, _ = inside()
-    side1[...], side2[...] = halo_columns(rate, near, far, own)
+    rest = jnp.zeros((T - 8, T), f32)
+    sides = [
+        jnp.transpose(jnp.concatenate([x[COL_COEF : COL_COEF + 8, :], rest], axis=0))
+        for x in (near, far)
+    ]
+    side1[...], side2[...] = halo_columns(rate, near, far, sides, own)
+    keep[KEEP_SEA_SIDE : KEEP_SEA_SIDE + T, :] = jnp.where(
+        lanes(T) == 0, pltpu.roll(sides[0], T - 2, 1), pltpu.roll(sides[1], T - 4, 1)
+    )
     for v in range(NV):
         loads[v].wait()
         at = v * LEV
@@ -497,10 +500,6 @@
     keep[KEEP_VERT : KEEP_VERT + T, :] = coef[...]
     keep[KEEP_SEA : KEEP_SEA + T, :] = sea[...]
     keep[KEEP_SIDE : KEEP_SIDE + T, :] = side2[...]
-    coefs = pl.ds(COL_COEF, T)
-    keep[KEEP_SEA_SIDE : KEEP_SEA_SIDE + T, :] = jnp.where(
-        lanes(T) == 0, pltpu.roll(near[coefs, :], T - 2, 1), pltpu.roll(far[coefs, :], T - 4, 1)
-    )
     for k, (rows, line) in enumerate(((top2, top), (bottom2, bottom))):
         for v in range(NV):
             keep[KEEP_ENDS + 8 * k + v : KEEP_ENDS + 8 * k + v + 1, :] = rows[v, 0:1, :]

time: 59.8 us -> 59.8 us (level)
  transfers between devices with their start and end apart: 8 -> 8, of which waited for: 3 -> 3; matrix products, arithmetic and copies ran while one was open for 0% -> 0% of each run, Pallas kernels for 33% -> 34%
where the time goes in v13:
time: 59.8 us; the launch traced here: 59.5 us
  Pallas kernels  24.4 us (41%)
  starting transfers between devices  20.4 us (34%)
  waiting for transfers between devices  12.4 us (21%)
  local copies, waits for them, and re-layouts  2.21 us (4%)
    pallas_call x1, Pallas kernels, two_steps(): pl.pallas_call(step_kernel, in_specs=[SMEM, HBM] + [VMEM] * 7, out_specs=...  9.71 us
    all_to_all x1, starting transfers between devices, local(): lax.all_to_all(packed, ('gx', 'gy'), split_axis=0, concat_axis=0, tiled=T...  9.57 us
    pallas_call x1, Pallas kernels, remap(): pl.pallas_call(remap_kernel, in_specs=[HBM, HBM, VMEM, HBM, VMEM, HBM], o...  6.8 us
    ppermute x4, starting transfers between devices, shifted(): lax.ppermute(block, axis, [(i, (i + by) % count) for i in range(count)])  6.78 us
    all_to_all x1, waiting for transfers between devices, local(): lax.all_to_all(packed, ('gx', 'gy'), split_axis=0, concat_axis=0, tiled=T...  6.36 us
    ppermute x3, waiting for transfers between devices, crossed(): return lax.ppermute(block, ('comp', 'gx', 'gy'), route)  5.62 us
    ppermute x3, starting transfers between devices, crossed(): return lax.ppermute(block, ('comp', 'gx', 'gy'), route)  4.1 us
    pallas_call x1, Pallas kernels, outer_columns(): pl.pallas_call(column_kernel, in_specs=[HBM] * 4, out_specs=[VMEM] * 5, o...  3.58 us
  transfers between devices with their start and end apart: 8, of which 3 were waited for; matrix products, arithmetic and copies ran while one was open for 0% of the time, Pallas kernels for 34%

profile of v13, /device:TPU:1, one launch (start us, length us, event | category | flops | bytes accessed | tf_op | source)
XLA Modules:
  0.0 59.5 jit_solution(3299095168037355028)
XLA Ops:
  0.0 1.8 %outer_rows.1 = (f32[144,128]{1,0:T(8,128)}, f32[144,128]{1,0:T(8,128)}) custom-call(f32[1,4,16,128,128]{4,3,2,1,0:T(8,128)} %state.5, f32[1,128,128]{2,1,0:T(8,128)} %vert.3, s32[1,128,128]{2,1,0:T(8,128)} %mask.3), custom_call_target="tpu_custom_call" | custom-call | flops 65536 | bytes 524288 | tf_op jit(solution)/shard_map/outer_rows/pallas_call | solution.py:110
  1.8 3.0 %collective-permute-start = (f32[144,128]{1,0:T(8,128)}, f32[144,128]{1,0:T(8,128)S(1)}, u32[]{:S(2)}, u32[]{:S(2)}) collective-permute-start(f32[144,128]{1,0:T(8,128)} %get-tuple-element.20), channel_id=1, source_target_pairs={{0,8},{8,16},{16,24},{24,32},{32,40},{40,48},{48,56},{56,0},{1,9},... | collective-permute-start | bytes 221192 | tf_op jit(solution)/shard_map/ppermute | solution.py:661
  4.9 3.6 %outer_columns.1 = (f32[264,128]{1,0:T(8,128)S(1)}, f32[512,128]{1,0:T(8,128)S(1)}, f32[128,128]{1,0:T(8,128)S(1)}, f32[128,128]{1,0:T(8,128)S(1)}, bf16[32,4,128,128]{3,2,1,0:T(8,128)(2,1)S(1)}) custom-call(f32[1,4,16,128,128]{4,3,2,1,0:T(8,128)} %state.5, f32[1,128,128]{2,1,0:T(8,128)S(1)} %copy-done.1, s32[1,128,128]{2,1,0:T(8,128)S(1)} %copy-done.2, ...), custom_call_target="tpu_custom_call" | custom-call | flops 6291456 | bytes 9437184 | tf_op jit(solution)/shard_map/outer_columns/pallas_call | solution.py:165
  8.5 0.0 collective-permute-done.top
  8.5 0.4 collective-permute-done.1.bottom
  8.9 0.1 with_corners.1.own.after
  9.0 3.7 %collective-permute-start.3 = (f32[280,128]{1,0:T(8,128)S(1)}, f32[280,128]{1,0:T(8,128)S(1)}, u32[]{:S(2)}, u32[]{:S(2)}) collective-permute-start(f32[280,128]{1,0:T(8,128)S(1)} %with_corners.1.own.after), channel_id=1, source_target_pairs={{0,7},{1,0},{2,1},{3,2},{4,3},{5,4},{6,5},{7,6},{8,15},{9,8},{10,9... | collective-permute-start | bytes 430088 | tf_op jit(solution)/shard_map/ppermute | solution.py:661
  12.7 0.0 collective-permute-start.2
  12.7 6.8 %remap.1.refs_0_ = f32[2112,128]{1,0:T(8,128)} custom-call(s32[4,128]{1,0:T(4,128)S(1)} %bitcast.7, s32[1,128]{1,0:T(1,128)S(1)} %bitcast.8, f32[512,128]{1,0:T(8,128)S(1)} %get-tuple-element.24.surf, bf16[1,128,1,4,128,128]{5,4,3,2,1,0:T(8,128)(2,1)} %weight.3, bf16[32,4,128,128]{3,2,1,0:T(8,128)(2,1)S(1)} %get-tuple-element.25.early, ...), custom_call_target="tpu_custom_call" | custom-call | flops 70254592 | bytes 20971520 | tf_op jit(solution)/shard_map/remap/pallas_call | solution.py:318
  19.5 0.0 copy-start.3
  19.6 0.0 collective-permute-done.3.far.refs_2_
  19.6 0.0 collective-permute-done.2.near.refs_1_
  19.6 0.0 copy-start.6
  19.6 9.6 %all-to-all-start = ((f32[64,33,1,128]{3,2,1,0:T(1,128)}), f32[64,33,1,128]{3,2,1,0:T(1,128)S(1)}, u32[]{:S(2)}, u32[]{:S(2)}) async-start(f32[64,33,1,128]{3,2,1,0:T(1,128)} %bitcast.3), calls=%async_computation | async-start | bytes 2162688 | tf_op jit(solution)/shard_map/all_to_all | solution.py:686
  29.2 0.0 copy-start
  29.2 2.2 %copy-done = f32[1,4,16,128,128]{4,3,2,1,0:T(8,128)S(1)} copy-done((f32[1,4,16,128,128]{4,3,2,1,0:T(8,128)S(1)}, f32[1,4,16,128,128]{4,3,2,1,0:T(8,128)}, u32[]{:S(2)}) %copy-start) | copy-done | bytes 4194328
  31.4 9.7 %two_steps.1 = (f32[1,4,16,128,128]{4,3,2,1,0:T(8,128)}, f32[2064,128]{1,0:T(8,128)S(1)}) custom-call(f32[1,4]{1,0:T(1,128)S(1)} %copy-done.3, f32[1,4,16,128,128]{4,3,2,1,0:T(8,128)S(1)} %copy-done, f32[128,128]{1,0:T(8,128)S(1)} %get-tuple-element.17.coef, f32[128,128]{1,0:T(8,128)S(1)} %get-tuple-element.18.sea, f32[280,128]{1,0:T(8,128)S(1)} %with_corners.1.own.after, ...), custom_call_target="tpu_custom_call" | custom-call | flops 50331648 | bytes 10485760 | tf_op jit(solution)/shard_map/two_steps/pallas_call | solution.py:514
  41.1 6.4 %all-to-all-done = f32[64,33,1,128]{3,2,1,0:T(1,128)S(1)} async-done(((f32[64,33,1,128]{3,2,1,0:T(1,128)}), f32[64,33,1,128]{3,2,1,0:T(1,128)S(1)}, u32[]{:S(2)}, u32[]{:S(2)}) %all-to-all-start) | async-done | bytes 1081376 | tf_op jit(solution)/shard_map/all_to_all | solution.py:686
  47.4 0.7 %unpack.1 = (f32[520,128]{1,0:T(8,128)S(1)}, f32[8,128]{1,0:T(8,128)S(1)}, f32[8,128]{1,0:T(8,128)S(1)}) custom-call(f32[2112,128]{1,0:T(8,128)S(1)} %bitcast.6, f32[2064,128]{1,0:T(8,128)S(1)} %get-tuple-element.23.after.near), custom_call_target="tpu_custom_call" | custom-call | flops 209715200 | bytes 2097152 | tf_op jit(solution)/shard_map/unpack/pallas_call | solution.py:586
  48.1 1.1 %collective-permute-start.4 = (f32[520,128]{1,0:T(8,128)S(1)}, f32[520,128]{1,0:T(8,128)S(1)}, u32[]{:S(2)}, u32[]{:S(2)}) collective-permute-start(f32[520,128]{1,0:T(8,128)S(1)} %get-tuple-element.26), channel_id=1, source_target_pairs={{0,68},{1,69},{2,70},{3,71},{4,64},{5,65},{6,66},{7,67},{8,76},{9,... | collective-permute-start | bytes 798728 | tf_op jit(solution)/shard_map/ppermute | solution.py:672
  49.3 1.8 %collective-permute-start.5 = (f32[8,128]{1,0:T(8,128)S(1)}, f32[8,128]{1,0:T(8,128)S(1)}, u32[]{:S(2)}, u32[]{:S(2)}) collective-permute-start(f32[8,128]{1,0:T(8,128)S(1)} %get-tuple-element.27), channel_id=1, source_target_pairs={{0,76},{1,77},{2,78},{3,79},{4,72},{5,73},{6,74},{7,75},{8,84},{9,... | collective-permute-start | bytes 12296 | tf_op jit(solution)/shard_map/ppermute | solution.py:672
  51.0 1.2 %collective-permute-start.6 = (f32[8,128]{1,0:T(8,128)S(1)}, f32[8,128]{1,0:T(8,128)S(1)}, u32[]{:S(2)}, u32[]{:S(2)}) collective-permute-start(f32[8,128]{1,0:T(8,128)S(1)} %get-tuple-element.28), channel_id=1, source_target_pairs={{0,124},{1,125},{2,126},{3,127},{4,120},{5,121},{6,122},{7,123},{8... | collective-permute-start | bytes 12296 | tf_op jit(solution)/shard_map/ppermute | solution.py:672
  52.2 5.6 %collective-permute-done.5.imp_top = f32[8,128]{1,0:T(8,128)S(1)} collective-permute-done((f32[8,128]{1,0:T(8,128)S(1)}, f32[8,128]{1,0:T(8,128)S(1)}, u32[]{:S(2)}, u32[]{:S(2)}) %collective-permute-start.5) | collective-permute-done | bytes 4128 | tf_op jit(solution)/shard_map/ppermute | solution.py:672
  57.8 1.7 %final.1 = f32[1,4,16,128,128]{4,3,2,1,0:T(8,128)} custom-call(f32[1,4]{1,0:T(1,128)S(1)} %copy-done.3, f32[1,4]{1,0:T(1,128)S(1)} %copy-done.6, f32[1,4,16,128,128]{4,3,2,1,0:T(8,128)} %get-tuple-element.22.mid, f32[2064,128]{1,0:T(8,128)S(1)} %get-tuple-element.23.after.near, ...), custom_call_target="tpu_custom_call", output_to_operand_aliasing={{}: (2, {})} | custom-call | flops 2097152 | bytes 3145728 | tf_op jit(solution)/shard_map/final/pallas_call | solution.py:643
  (14 shorter events, 0.0 us)
Async XLA Ops:
  0.0 4.9 %copy-start.2 = (s32[1,128,128]{2,1,0:T(8,128)S(1)}, s32[1,128,128]{2,1,0:T(8,128)}, u32[]{:S(2)}) copy-start(s32[1,128,128]{2,1,0:T(8,128)} %mask.3) | copy-start | bytes 196612
  0.0 4.9 %copy-start.1 = (f32[1,128,128]{2,1,0:T(8,128)S(1)}, f32[1,128,128]{2,1,0:T(8,128)}, u32[]{:S(2)}) copy-start(f32[1,128,128]{2,1,0:T(8,128)} %vert.3) | copy-start | bytes 196612
  1.8 6.7 %collective-permute-start = (f32[144,128]{1,0:T(8,128)}, f32[144,128]{1,0:T(8,128)S(1)}, u32[]{:S(2)}, u32[]{:S(2)}) collective-permute-start(f32[144,128]{1,0:T(8,128)} %get-tuple-element.20), channel_id=1, source_target_pairs={{0,8},{8,16},{16,24},{24,32},{32,40},{40,48},{48,56},{56,0},{1,9},... | collective-permute-start | bytes 221192 | tf_op jit(solution)/shard_map/ppermute | solution.py:661
  4.9 7.8 %copy-start.4 = (s32[1,128,1,4]{1,3,2,0:T(4,128)S(1)}, s32[1,128,1,4]{1,3,2,0:T(4,128)}, u32[]{:S(2)}) copy-start(s32[1,128,1,4]{1,3,2,0:T(4,128)} %param.13) | copy-start | bytes 6148
  4.9 7.8 %copy-start.5 = (s32[1,128,1]{1,2,0:T(1,128)S(1)}, s32[1,128,1]{1,2,0:T(1,128)}, u32[]{:S(2)}) copy-start(s32[1,128,1]{1,2,0:T(1,128)} %param.14) | copy-start | bytes 1540
  4.9 4.0 %collective-permute-start.1 = (f32[144,128]{1,0:T(8,128)}, f32[144,128]{1,0:T(8,128)S(1)}, u32[]{:S(2)}, u32[]{:S(2)}) collective-permute-start(f32[144,128]{1,0:T(8,128)} %get-tuple-element.21), channel_id=1, source_target_pairs={{0,56},{8,0},{16,8},{24,16},{32,24},{40,32},{48,40},{56,48},{1,57}... | collective-permute-start | bytes 221192 | tf_op jit(solution)/shard_map/ppermute | solution.py:661
  9.0 10.6 %collective-permute-start.3 = (f32[280,128]{1,0:T(8,128)S(1)}, f32[280,128]{1,0:T(8,128)S(1)}, u32[]{:S(2)}, u32[]{:S(2)}) collective-permute-start(f32[280,128]{1,0:T(8,128)S(1)} %with_corners.1.own.after), channel_id=1, source_target_pairs={{0,7},{1,0},{2,1},{3,2},{4,3},{5,4},{6,5},{7,6},{8,15},{9,8},{10,9... | collective-permute-start | bytes 430088 | tf_op jit(solution)/shard_map/ppermute | solution.py:661
  12.7 6.8 %collective-permute-start.2 = (f32[280,128]{1,0:T(8,128)S(1)}, f32[280,128]{1,0:T(8,128)S(1)}, u32[]{:S(2)}, u32[]{:S(2)}) collective-permute-start(f32[280,128]{1,0:T(8,128)S(1)} %with_corners.1.own.after), channel_id=1, source_target_pairs={{0,1},{1,2},{2,3},{3,4},{4,5},{5,6},{6,7},{7,0},{8,9},{9,10},{10,1... | collective-permute-start | bytes 430088 | tf_op jit(solution)/shard_map/ppermute | solution.py:661
  19.5 9.6 %copy-start.3 = (f32[1,4]{1,0:T(1,128)S(1)}, f32[1,4]{1,0:T(1,128)}, u32[]{:S(2)}) copy-start(f32[1,4]{1,0:T(1,128)} %horiz.1) | copy-start | bytes 52
  19.6 38.3 %copy-start.6 = (f32[1,4]{1,0:T(1,128)S(1)}, f32[1,4]{1,0:T(1,128)}, u32[]{:S(2)}) copy-start(f32[1,4]{1,0:T(1,128)} %relax.1) | copy-start | bytes 52
  19.6 27.8 %all-to-all-start = ((f32[64,33,1,128]{3,2,1,0:T(1,128)}), f32[64,33,1,128]{3,2,1,0:T(1,128)S(1)}, u32[]{:S(2)}, u32[]{:S(2)}) async-start(f32[64,33,1,128]{3,2,1,0:T(1,128)} %bitcast.3), calls=%async_computation | async-start | bytes 2162688 | tf_op jit(solution)/shard_map/all_to_all | solution.py:686
  29.2 2.2 %copy-start = (f32[1,4,16,128,128]{4,3,2,1,0:T(8,128)S(1)}, f32[1,4,16,128,128]{4,3,2,1,0:T(8,128)}, u32[]{:S(2)}) copy-start(f32[1,4,16,128,128]{4,3,2,1,0:T(8,128)} %state.5) | copy-start | bytes 12582916
  48.1 9.7 %collective-permute-start.4 = (f32[520,128]{1,0:T(8,128)S(1)}, f32[520,128]{1,0:T(8,128)S(1)}, u32[]{:S(2)}, u32[]{:S(2)}) collective-permute-start(f32[520,128]{1,0:T(8,128)S(1)} %get-tuple-element.26), channel_id=1, source_target_pairs={{0,68},{1,69},{2,70},{3,71},{4,64},{5,65},{6,66},{7,67},{8,76},{9,... | collective-permute-start | bytes 798728 | tf_op jit(solution)/shard_map/ppermute | solution.py:672
  49.3 8.6 %collective-permute-start.5 = (f32[8,128]{1,0:T(8,128)S(1)}, f32[8,128]{1,0:T(8,128)S(1)}, u32[]{:S(2)}, u32[]{:S(2)}) collective-permute-start(f32[8,128]{1,0:T(8,128)S(1)} %get-tuple-element.27), channel_id=1, source_target_pairs={{0,76},{1,77},{2,78},{3,79},{4,72},{5,73},{6,74},{7,75},{8,84},{9,... | collective-permute-start | bytes 12296 | tf_op jit(solution)/shard_map/ppermute | solution.py:672
  51.0 6.8 %collective-permute-start.6 = (f32[8,128]{1,0:T(8,128)S(1)}, f32[8,128]{1,0:T(8,128)S(1)}, u32[]{:S(2)}, u32[]{:S(2)}) collective-permute-start(f32[8,128]{1,0:T(8,128)S(1)} %get-tuple-element.28), channel_id=1, source_target_pairs={{0,124},{1,125},{2,126},{3,127},{4,120},{5,121},{6,122},{7,123},{8... | collective-permute-start | bytes 12296 | tf_op jit(solution)/shard_map/ppermute | solution.py:672
